TPU v7x, 256 devices: a whole 4x4x8 slice. The times are simulated.
256 devices in a mesh: group: 4 (over y_lo, core), seq: 2 (over y_hi), tensor: 32 (over z, x).
Axes of the slice: x: 4, y: 4 (y_hi: 2, y_lo: 2; y = y_hi * 2 + y_lo), z: 8, core: 2. Of those that a mesh axis runs over, the one named last changes fastest.
Arguments:
- teacher_heads: bfloat16 [512, 8192], P(('group', 'seq'), 'tensor'), may hold values from -6 to 6
- teacher_out: bfloat16 [8192, 16384], P('tensor', 'seq'), may hold values from -0.0625 to 0.0625
- teacher_resid: bfloat16 [512, 16384], P('group', ('seq', 'tensor')), may hold values from -6 to 6
- matches: int32 [1024], P('group'), may hold values from 0 to 127
- projector: bfloat16 [16384, 8192], P(('seq', 'tensor')), may hold values from -0.046875 to 0.046875
- student_heads: bfloat16 [1024, 4096], P(('group', 'seq'), 'tensor'), may hold values from -6 to 6
- student_out: bfloat16 [4096, 8192], P('tensor'), may hold values from -0.09375 to 0.09375
- student_resid: bfloat16 [1024, 8192], P(('group', 'seq', 'tensor')), may hold values from -36 to 36
Outputs:
- loss: float32 [1], replicated
- grad_heads: bfloat16 [1024, 4096], P(('group', 'seq'), 'tensor')
- grad_weight: bfloat16 [4096, 8192], P('tensor', ('group', 'seq'))
Inputs may be any that keep to these rules, and one draw needn't show every extreme that they name: `matches`: each student row names a teacher row of its own window by its index within that window.
All inputs are finite; a program needn't handle non-finite values.
Results may differ from a plain program's by a relative error of at most 0.023.
Values may be sent and summed in bfloat16 or wider, within the bound.
No kernel may reach another device: no remote copies, remote signals or barrier semaphores. Data moves between devices by JAX's collectives and lax.ppermute only.
A program may use at most 128 MiB of HBM per device.

v0:
```python
import jax
import jax.numpy as jnp
from jax import lax
from jax.sharding import PartitionSpec as P

S_WIN = 256


def local(
    teacher_heads,
    teacher_out,
    teacher_resid,
    matches,
    projector,
    student_heads,
    student_out,
    student_resid,
):
    partial_value = jnp.dot(
        lax.all_gather(teacher_heads, "seq", axis=0, tiled=True),
        teacher_out,
        preferred_element_type=jnp.float32,
    )
    summed = lax.psum_scatter(
        partial_value.astype(jnp.bfloat16), "tensor", scatter_dimension=1, tiled=True
    ).astype(jnp.float32)
    hidden = (teacher_resid.astype(jnp.float32) + summed).astype(jnp.bfloat16)
    selected = jnp.take(hidden, matches, axis=0)
    block = selected
    projected = lax.psum_scatter(
        jnp.dot(block, projector, preferred_element_type=jnp.float32),
        ("seq", "tensor"),
        scatter_dimension=0,
        tiled=True,
    )
    block = student_heads
    student_sum = lax.psum_scatter(
        jnp.dot(block, student_out, preferred_element_type=jnp.float32).astype(jnp.bfloat16),
        "tensor",
        scatter_dimension=0,
        tiled=True,
    ).astype(jnp.float32)
    difference = student_resid.astype(jnp.float32) + student_sum - projected
    squared = jnp.sum(difference * difference)
    total = lax.psum(squared, ("group", "seq", "tensor"))
    count = lax.axis_size("group") * S_WIN * difference.shape[1]
    loss = (total / count).reshape(1)
    grad_hidden = (difference * 0.125).astype(jnp.bfloat16)
    grad_all = lax.all_gather(grad_hidden, "tensor", axis=0, tiled=True)
    grad_heads = lax.dot_general(
        grad_all, student_out, (((1,), (1,)), ((), ())), preferred_element_type=jnp.float32
    ).astype(jnp.bfloat16)
    weight_part = lax.dot_general(
        student_heads, grad_all, (((0,), (0,)), ((), ())), preferred_element_type=jnp.float32
    )
    grad_weight = lax.psum_scatter(
        weight_part.astype(jnp.bfloat16), ("group", "seq"), scatter_dimension=1, tiled=True
    )
    return (loss, grad_heads, grad_weight)


def solution(mesh):
    return jax.shard_map(
        local,
        mesh=mesh,
        in_specs=(
            P(("group", "seq"), "tensor"),
            P("tensor", "seq"),
            P("group", ("seq", "tensor")),
            P("group"),
            P(("seq", "tensor"), None),
            P(("group", "seq"), "tensor"),
            P("tensor", None),
            P(("group", "seq", "tensor"), None),
        ),
        out_specs=(P(), P(("group", "seq"), "tensor"), P("tensor", ("group", "seq"))),
        check_vma=False,
    )
```

profile of v0, /device:TPU:1, one launch (start us, length us, event | category | flops | bytes accessed | tf_op | source)
XLA Modules:
  0.0 1303.2 jit_solution(2776759514324073713)
XLA Ops:
  7.2 6.1 all_gather.6
  13.3 4.3 convolution_convert_fusion
  17.6 0.0 all-reduce.5.cloned.1.call-start
  17.7 0.7 copy-done.1
  18.4 2.0 convolution_convert_fusion.2
  20.4 0.0 all-reduce.7.cloned.1.call-start
  20.4 0.6 copy-done.4
  21.1 211.9 %reduce-scatter.3.cloned.1.call-done = bf16[128,256]{1,0:T(8,128)(2,1)} async-done(((bf16[128,8192]{1,0:T(8,128)(2,1)}), bf16[128,256]{1,0:T(8,128)(2,1)}) %reduce-scatter.3.cloned.1.call-update) | async-done | bytes 65552 | tf_op jit(solution)/shard_map/reduce_scatter | solution.py:24
  233.0 0.9 add_convert_fusion
  233.8 1.2 gather_fusion
  235.0 6.7 fusion.1
  241.7 0.0 all-gather.3.cloned.1.call-start
  241.8 0.6 copy-done.6
  242.4 0.6 dynamic-slice.2
  243.0 0.6 dynamic-slice
  244.8 145.3 %all-reduce.5.cloned.1.call-done = bf16[128,8192]{1,0:T(8,128)(2,1)} async-done(((bf16[128,8192]{1,0:T(8,128)(2,1)}), bf16[128,8192]{1,0:T(8,128)(2,1)}) %all-reduce.5.cloned.1.call-update) | async-done | bytes 2097168
  390.2 683.6 %all-reduce.7.cloned.1.call-done = f32[256,8192]{1,0:T(8,128)} async-done(((f32[256,8192]{1,0:T(8,128)}), f32[256,8192]{1,0:T(8,128)}) %all-reduce.7.cloned.1.call-update) | async-done | bytes 8388624
  1073.8 2.3 fusion.4
  1076.2 115.3 %all-gather.3.cloned.1.call-done = bf16[32,4,8192]{2,1,0:T(4,128)(2,1)} async-done(((bf16[1,4,8192]{2,1,0:T(4,128)(2,1)}), bf16[32,4,8192]{2,1,0:T(4,128)(2,1)}) %all-gather.3.cloned.1.call-update) | async-done | bytes 2097168 | tf_op jit(solution)/shard_map/all_gather | solution.py:49
  1191.5 3.9 reshape.25
  1195.4 3.6 fusion
  1199.1 91.0 %psum.7 = f32[]{:T(128)} all-reduce(f32[]{:T(128)} %get-tuple-element.10), channel_id=1, replica_groups=mesh['group'=4,'seq'=2,'tensor'=32] {'group','seq','tensor'}, use_global_device_ids=true, to_apply=%region_4.5 | all-reduce | flops 1 | bytes 8 | tf_op jit(solution)/shard_map/psum | solution.py:45
  1290.8 2.9 convolution_convert_fusion.3
  1293.7 1.8 copy.12
  (22 shorter events, 0.2 us)
Async XLA Ops:
  7.2 10.5 copy-start
  7.2 225.8 %reduce-scatter.3.cloned.1.call-start = ((), (), s32[]{:S(2)}) async-start(), calls=%async_computation.2 | async-start | bytes 2162688 | tf_op jit(solution)/shard_map/reduce_scatter | solution.py:24
  17.6 0.8 copy-start.1
  17.6 372.5 %all-reduce.5.cloned.1.call-start = ((), (), s32[]{:S(2)}) async-start(), calls=%async_computation.5 | async-start | bytes 4194304
  20.3 0.7 copy-start.4
  20.4 212.6 %copy-start.2 = (bf16[128,256]{1,0:T(8,128)(2,1)S(1)}, bf16[128,256]{1,0:T(8,128)(2,1)}, u32[]{:S(2)}) copy-start(bf16[128,256]{1,0:T(8,128)(2,1)} %param.10) | copy-start | bytes 196612
  20.4 1053.4 %all-reduce.7.cloned.1.call-start = ((), (), s32[]{:S(2)}) async-start(), calls=%async_computation.6 | async-start | bytes 16777216
  241.7 0.7 copy-start.6
  241.7 1.3 copy-start.5
  241.7 832.1 %copy-start.3 = (bf16[4,8192]{1,0:T(4,128)(2,1)S(1)}, bf16[4,8192]{1,0:T(4,128)(2,1)}, u32[]{:S(2)}) copy-start(bf16[4,8192]{1,0:T(4,128)(2,1)} %param.15) | copy-start | bytes 196612
  241.7 949.8 %all-gather.3.cloned.1.call-start = ((), (), s32[]{:S(2)}) async-start(), calls=%async_computation.4 | async-start | bytes 2162688 | tf_op jit(solution)/shard_map/all_gather | solution.py:49
  1076.1 217.6 %reduce-scatter.5.cloned.1.call-start = ((), (), s32[]{:S(2)}) async-start(), calls=%async_computation.3 | async-start | bytes 2359296 | tf_op jit(solution)/shard_map/reduce_scatter | solution.py:56
Sparse Core Ops, SparseCore 0:
  17.7 215.1 reduce-scatter.2
  236.9 153.2 all-reduce.4
  392.8 680.8 all-reduce.6
  1076.8 114.6 all-gather.2
  1199.2 61.3 reduce-scatter.4
where the time goes:
time: 1300 us
  waiting for transfers between devices  1160 us (89%)
  blocking collectives  97.2 us (7%)
  matrix products  19.5 us (2%)
  between operations  16.9 us (1%)
    unnamed x7, waiting for transfers between devices  829 us
    reduce_scatter x1, waiting for transfers between devices, local(): lax.psum_scatter(partial_value.astype(jnp.bfloat16), 'tensor', scatter_di...  212 us
    all_gather x1, waiting for transfers between devices, local(): grad_all = lax.all_gather(grad_hidden, 'tensor', axis=0, tiled=True)  115 us
    psum x1, blocking collectives, local(): total = lax.psum(squared, ('group', 'seq', 'tensor'))  91 us
  transfers between devices with their start and end apart: 5, of which 4 were waited for; matrix products, arithmetic and copies ran while one was open for 1% of the time, Pallas kernels for 0%

commit v1 on v0

v1 whole, which is shorter than its diff:
```python
import jax
import jax.numpy as jnp
from jax import lax
from jax.sharding import Mesh, PartitionSpec as P

B16 = jnp.bfloat16
F32 = jnp.float32
NY, NZ, NX = 8, 8, 4
GROUP = ("ylo", "core")
COLUMN = ("ylo", "core", "seq")
PLANE = ("z", "x")
ROWS = 1024
COLS = 1024


def dot(a, b, dims):
    return lax.dot_general(a, b, (dims, ((), ())), preferred_element_type=F32)


def spread(block, axis, parts):
    return lax.all_to_all(jnp.broadcast_to(block[None], (parts,) + block.shape), axis, 0, 0)


def scatter_sum(parts):
    over_x = lax.all_to_all(parts, "x", 0, 0)
    summed = jnp.sum(over_x.astype(F32), axis=0).astype(B16)
    over_z = lax.all_to_all(summed, "z", 0, 0)
    return jnp.sum(over_z.astype(F32), axis=0)


def own_order(rows):
    rest = rows.shape[2:]
    parts = rows.reshape((NY, NZ, NX, 4) + rest)
    return jnp.transpose(parts, (2, 1, 0, 3) + tuple(range(4, parts.ndim))).reshape((ROWS,) + rest)


def block_order(rows):
    rest = rows.shape[1:]
    parts = rows.reshape((NX, NZ, NY, 4) + rest)
    return jnp.transpose(parts, (2, 1, 0, 3) + tuple(range(4, parts.ndim))).reshape((NY, 128) + rest)


def local(
    teacher_heads,
    teacher_out,
    teacher_resid,
    matches,
    projector,
    student_heads,
    student_out,
    student_resid,
):
    seq = lax.axis_index("seq")
    member = lax.axis_index(COLUMN)

    away = lax.dynamic_slice(projector, (0, (member + 1 - 2 * seq) * COLS), (256, COLS))
    home = lax.dynamic_slice(projector, (0, member * COLS), (256, COLS))
    other = lax.ppermute(away, "seq", [(0, 1), (1, 0)])
    first = jnp.where(seq == 0, home, other)
    second = jnp.where(seq == 0, other, home)
    out_cols = lax.dynamic_slice(student_out, (0, member * COLS), (128, COLS))

    own_matches = lax.dynamic_slice(matches, (seq * 128,), (128,)).astype(B16)
    shared = jnp.concatenate(
        [
            student_heads,
            teacher_heads[:, :128],
            teacher_heads[:, 128:],
            jnp.broadcast_to(own_matches[None], (16, 128)),
        ],
        axis=0,
    )
    resid_parts = jnp.transpose(student_resid.reshape(4, NY, 8, 128), (1, 0, 2, 3)).reshape(NY, 32, 128)
    sent = jnp.concatenate(
        [jnp.broadcast_to(shared[None], (NY,) + shared.shape), resid_parts], axis=1
    )
    got = lax.all_to_all(sent, COLUMN, 0, 0)
    heads = own_order(got[:, :128])
    pair = lax.dynamic_slice(got, (member - seq, 128, 0), (2, 128, 128))
    window = jnp.concatenate([pair[:, :64], pair[:, 64:]], axis=2).reshape(128, 256)
    base = (jnp.arange(NY, dtype=jnp.int32) // 2 * 128)[:, None]
    picked = own_order(got[:, 256].astype(jnp.int32) + base)
    resid = got[:, 272:].reshape(32, COLS)

    product = dot(window, teacher_out, ((1,), (0,))).astype(B16)
    parts = jnp.transpose(product.reshape(128, NZ, NX, 256), (2, 1, 0, 3))
    hidden = (teacher_resid.astype(F32) + scatter_sum(parts)).astype(B16)

    every = spread(hidden, COLUMN, NY).reshape(4, 2, 128, 256)
    low = every[:, 0].reshape(512, 256)
    high = every[:, 1].reshape(512, 256)
    choose = (picked[:, None] == jnp.arange(512, dtype=jnp.int32)[None]).astype(B16)
    low = dot(choose, low, ((1,), (0,))).astype(B16)
    high = dot(choose, high, ((1,), (0,))).astype(B16)
    partial = (
        dot(heads, out_cols, ((1,), (0,)))
        - dot(low, first, ((1,), (0,)))
        - dot(high, second, ((1,), (0,)))
    ).astype(B16)
    difference = resid.astype(F32) + scatter_sum(partial.reshape(NX, NZ, 32, COLS))
    grad = (difference * 0.125).astype(B16)

    tall = spread(grad, "z", NZ).reshape(256, COLS)
    grad_all = lax.all_gather(tall, "x", axis=0, tiled=True)

    grad_weight = dot(heads, grad_all, ((0,), (0,))).astype(B16)
    heads_part = block_order(dot(grad_all, out_cols, ((1,), (1,))).astype(B16))
    wide = grad_all.astype(F32)
    squares = jnp.sum(wide * wide)
    top = lax.reduce_precision(squares, 8, 7)
    middle = lax.reduce_precision(squares - top, 8, 7)
    bottom = squares - top - middle
    scalars = jnp.stack([top, middle, bottom]).astype(B16)
    extra = jnp.broadcast_to(jnp.pad(scalars, (0, 125))[None, None], (NY, 16, 128))
    back = lax.all_to_all(jnp.concatenate([heads_part, extra], axis=1), COLUMN, 0, 0).astype(F32)
    grad_heads = jnp.sum(back[:, :128], axis=0).astype(B16)
    total = jnp.sum(back[:, 128, :3])
    loss = (total * (64.0 / (ROWS * 8192))).reshape(1)
    return (loss, grad_heads, grad_weight)


def solution(mesh):
    cut = Mesh(mesh.devices.reshape(2, 2, 2, NZ, NX), COLUMN + PLANE)
    every = COLUMN + PLANE
    return jax.shard_map(
        local,
        mesh=cut,
        in_specs=(
            P(COLUMN, PLANE),
            P(PLANE, "seq"),
            P(GROUP, ("seq",) + PLANE),
            P(GROUP),
            P(("seq",) + PLANE, None),
            P(COLUMN, PLANE),
            P(PLANE, None),
            P(every, None),
        ),
        out_specs=(P(), P(COLUMN, PLANE), P(PLANE, COLUMN)),
        check_vma=False,
    )
```

time: 1300 us -> 258 us (0.20)
  waiting for transfers between devices: 1160 us -> 76.4 us
  starting transfers between devices: 0.2 us -> 30.2 us
  blocking collectives: 97.2 us -> 77.8 us
    unnamed x7 -> x1, waiting for transfers between devices: 829 us -> 0.02 us
    reduce_scatter x2 -> x0, waiting for transfers between devices: 212 us -> none  [the longest x1 212 us: local(): lax.psum_scatter(partial_value.astype(jnp.bfloat16), 'tensor', scatter_di...]
    psum x1 -> x0, blocking collectives: 91 us -> none  [local(): total = lax.psum(squared, ('group', 'seq', 'tensor'))]
    all_gather x1, waiting for transfers between devices: 115 us -> 28.3 us  [local(): grad_all = lax.all_gather(tall, 'x', axis=0, tiled=True)]
    all_to_all x0 -> x3, blocking collectives: none -> 77.8 us  [the longest x2 59.2 us: scatter_sum(): over_x = lax.all_to_all(parts, 'x', 0, 0)]
    all_to_all x0 -> x5, waiting for transfers between devices: none -> 48.1 us  [the longest x2 28.2 us: scatter_sum(): over_z = lax.all_to_all(summed, 'z', 0, 0)]
    all_to_all x0 -> x5, starting transfers between devices: none -> 29.4 us  [the longest x2 11.6 us: scatter_sum(): over_z = lax.all_to_all(summed, 'z', 0, 0)]
  transfers between devices with their start and end apart: 5 -> 7, of which waited for: 4 -> 6; matrix products, arithmetic and copies ran while one was open for 1% -> 5% of each run, Pallas kernels for 0% -> 0%
where the time goes in v1:
time: 258 us; the launch traced here: 257 us
  blocking collectives  77.8 us (30%)
  waiting for transfers between devices  76.4 us (30%)
  starting transfers between devices  30.2 us (12%)
  matrix products  22.3 us (9%)
  between operations  20.9 us (8%)
  local copies, waits for them, and re-layouts  15.9 us (6%)
  other arithmetic  13.2 us (5%)
    all_to_all x2, blocking collectives, scatter_sum(): over_x = lax.all_to_all(parts, 'x', 0, 0)  59.2 us
    all_gather x1, waiting for transfers between devices, local(): grad_all = lax.all_gather(tall, 'x', axis=0, tiled=True)  28.3 us
    all_to_all x2, waiting for transfers between devices, scatter_sum(): over_z = lax.all_to_all(summed, 'z', 0, 0)  28.2 us
    dot_general x6, matrix products, dot(): return lax.dot_general(a, b, (dims, ((), ())), preferred_element_type=F32)  22.3 us
    all_to_all x1, blocking collectives, spread(): lax.all_to_all(jnp.broadcast_to(block[None], (parts,) + block.shape), axi...  18.5 us
    all_to_all x2, starting transfers between devices, scatter_sum(): over_z = lax.all_to_all(summed, 'z', 0, 0)  11.6 us
    all_to_all x1, waiting for transfers between devices, local(): got = lax.all_to_all(sent, COLUMN, 0, 0)  10.4 us
    all_to_all x1, starting transfers between devices, local(): got = lax.all_to_all(sent, COLUMN, 0, 0)  6.69 us
  transfers between devices with their start and end apart: 7, of which 6 were waited for; matrix products, arithmetic and copies ran while one was open for 5% of the time, Pallas kernels for 0%

profile of v1, /device:TPU:1, one launch (start us, length us, event | category | flops | bytes accessed | tf_op | source)
XLA Modules:
  0.0 256.7 jit_solution(1486990469710368165)
XLA Ops:
  11.4 6.7 %all-to-all-start = ((bf16[8,304,128]{2,1,0:T(8,128)(2,1)}), bf16[8,304,128]{2,1,0:T(8,128)(2,1)S(1)}, u32[]{:S(2)}, u32[]{:S(2)}) async-start(bf16[8,304,128]{2,1,0:T(8,128)(2,1)} %pad_maximum_fusion), calls=%async_computation | async-start | bytes 1245184 | tf_op jit(solution)/shard_map/all_to_all | solution.py:77
  18.1 10.4 %all-to-all-done = bf16[8,304,128]{2,1,0:T(8,128)(2,1)S(1)} async-done(((bf16[8,304,128]{2,1,0:T(8,128)(2,1)}), bf16[8,304,128]{2,1,0:T(8,128)(2,1)S(1)}, u32[]{:S(2)}, u32[]{:S(2)}) %all-to-all-start) | async-done | bytes 622624 | tf_op jit(solution)/shard_map/all_to_all | solution.py:77
  28.6 4.5 %convolution_convert_fusion = bf16[128,8192]{1,0:T(8,128)(2,1)} fusion(bf16[128,256]{1,0:T(8,128)(2,1)S(1)} %bitcast.56, bf16[256,8192]{1,0:T(8,128)(2,1)} %param.9), kind=kOutput, calls=%fused_computation | convolution fusion | flops 537919488 | bytes 6356992 | tf_op jit(solution)/shard_map/dot_general | solution.py:17
  33.0 4.5 %reshape.88 = bf16[128,8,4,256]{3,2,1,0:T(4,128)(2,1)} reshape(bf16[128,8192]{1,0:T(8,128)(2,1)} %convolution_convert_fusion) | data formatting | bytes 4194304 | tf_op jit(solution)/shard_map/reshape | solution.py:86
  39.4 28.8 %all_to_all.40 = bf16[4,8,128,256]{3,1,2,0:T(8,128)(2,1)} all-to-all(bf16[4,8,128,256]{3,1,2,0:T(8,128)(2,1)S(1)} %bitcast.45), channel_id=1, replica_groups=mesh['ylo'=2,'core'=2,'seq'=2,'z'=8,'x'=4] {'x'}, dimensions={0} | all-to-all | bytes 4194304 | tf_op jit(solution)/shard_map/all_to_all | solution.py:25
  68.2 2.2 reduce_sum.69
  71.2 8.1 %all-to-all-start.2 = ((bf16[8,128,256]{2,1,0:T(8,128)(2,1)}), bf16[8,128,256]{2,1,0:T(8,128)(2,1)S(1)}, u32[]{:S(2)}, u32[]{:S(2)}) async-start(bf16[8,128,256]{2,1,0:T(8,128)(2,1)} %copy.45), calls=%async_computation.2 | async-start | bytes 1048576 | tf_op jit(solution)/shard_map/all_to_all | solution.py:27
  82.8 12.2 %all-to-all-done.2 = bf16[8,128,256]{2,1,0:T(8,128)(2,1)S(1)} async-done(((bf16[8,128,256]{2,1,0:T(8,128)(2,1)}), bf16[8,128,256]{2,1,0:T(8,128)(2,1)S(1)}, u32[]{:S(2)}, u32[]{:S(2)}) %all-to-all-start.2) | async-done | bytes 524320 | tf_op jit(solution)/shard_map/all_to_all | solution.py:27
  96.0 6.2 %all-to-all-start.3 = ((bf16[8,128,256]{2,1,0:T(8,128)(2,1)}), bf16[8,128,256]{2,1,0:T(8,128)(2,1)S(1)}, u32[]{:S(2)}, u32[]{:S(2)}) async-start(bf16[8,128,256]{2,1,0:T(8,128)(2,1)} %broadcast_in_dim.12), calls=%async_computation.3 | async-start | bytes 1048576 | tf_op jit(solution)/shard_map/all_to_all | solution.py:21
  103.6 2.6 %fusion.16 = f32[1024,1024]{1,0:T(8,128)} fusion(bf16[1024,128]{1,0:T(8,128)(2,1)S(1)} %bitcast.47, bf16[128,8192]{1,0:T(8,128)(2,1)S(1)} %copy-done, s32[]{:T(128)S(6)} %select_n.35), kind=kOutput, calls=%fused_computation.26 | convolution fusion | flops 268435456 | bytes 4718596 | tf_op jit(solution)/shard_map/dot_general | solution.py:17
  106.3 5.3 %all-to-all-done.3 = bf16[8,128,256]{2,1,0:T(8,128)(2,1)S(1)} async-done(((bf16[8,128,256]{2,1,0:T(8,128)(2,1)}), bf16[8,128,256]{2,1,0:T(8,128)(2,1)S(1)}, u32[]{:S(2)}, u32[]{:S(2)}) %all-to-all-start.3) | async-done | bytes 524320 | tf_op jit(solution)/shard_map/all_to_all | solution.py:21
  112.4 4.5 %fusion.4 = f32[1024,1024]{1,0:T(8,128)} fusion(bf16[512,256]{1,0:T(8,128)(2,1)} %bitcast.55, s32[1024]{0:T(1024)S(1)} %eq.19, bf16[256,1024]{1,0:T(8,128)(2,1)S(1)} %collective-permute-done, pred[]{:T(512)S(6)} %eq.23, bf16[256,8192]{1,0:T(8,128)(2,1)} %param.12, s32[]{:T(128)S(6)} %select_n.35), kind=kOutput, calls=%fused_computation.9 | convolution fusion | flops 806354944 | bytes 5509125 | tf_op jit(solution)/shard_map/dot_general | solution.py:17
  116.9 5.6 %subtract_convert_fusion = bf16[1024,1024]{1,0:T(8,128)(2,1)} fusion(f32[1024,1024]{1,0:T(8,128)} %fusion.16, f32[1024,1024]{1,0:T(8,128)} %fusion.4, bf16[512,256]{1,0:T(8,128)(2,1)S(1)} %bitcast.51, s32[1024]{0:T(1024)S(1)} %eq.19, bf16[256,1024]{1,0:T(8,128)(2,1)S(1)} %collective-permute-done, pred[]{:T(512)S(6)} %eq.23, bf16[256,8192]{1,0:T(8,128)(2,1)} %param.12, ...), kind=kOutput, calls=%fused_computation.2 | convolution fusion | flops 809500672 | bytes 11800581 | tf_op jit(solution)/shard_map/dot_general | solution.py:17
  122.5 30.5 %all_to_all.41 = bf16[4,8,32,1024]{3,2,1,0:T(8,128)(2,1)} all-to-all(bf16[4,8,32,1024]{3,2,1,0:T(8,128)(2,1)} %bitcast.46), channel_id=1, replica_groups=mesh['ylo'=2,'core'=2,'seq'=2,'z'=8,'x'=4] {'x'}, dimensions={0} | all-to-all | bytes 4194304 | tf_op jit(solution)/shard_map/all_to_all | solution.py:25
  153.0 2.9 %reduce_sum.71 = bf16[8,32,1024]{2,1,0:T(8,128)(2,1)} reduce(bf16[4,8,32,1024]{3,2,1,0:T(8,128)(2,1)} %all_to_all.41, bf16[]{:T(256)} %constant.52.clone.1), dimensions={0}, to_apply=%region_2.3 | reduce | flops 786432 | bytes 2621442 | tf_op jit(solution)/shard_map/reduce_sum | solution.py:26
  155.9 3.5 %all-to-all-start.5 = ((bf16[8,32,1024]{2,1,0:T(8,128)(2,1)}), bf16[8,32,1024]{2,1,0:T(8,128)(2,1)S(1)}, u32[]{:S(2)}, u32[]{:S(2)}) async-start(bf16[8,32,1024]{2,1,0:T(8,128)(2,1)} %reduce_sum.71), calls=%async_computation.5 | async-start | bytes 1048576 | tf_op jit(solution)/shard_map/all_to_all | solution.py:27
  160.4 16.0 %all-to-all-done.5 = bf16[8,32,1024]{2,1,0:T(8,128)(2,1)S(1)} async-done(((bf16[8,32,1024]{2,1,0:T(8,128)(2,1)}), bf16[8,32,1024]{2,1,0:T(8,128)(2,1)S(1)}, u32[]{:S(2)}, u32[]{:S(2)}) %all-to-all-start.5) | async-done | bytes 524320 | tf_op jit(solution)/shard_map/all_to_all | solution.py:27
  176.6 18.5 %all_to_all.42 = bf16[8,32,1024]{2,1,0:T(8,128)(2,1)} all-to-all(bf16[8,32,1024]{2,1,0:T(8,128)(2,1)S(1)} %broadcast_in_dim.13), channel_id=1, replica_groups=mesh['ylo'=2,'core'=2,'seq'=2,'z'=8,'x'=4] {'z'}, dimensions={0} | all-to-all | bytes 1048576 | tf_op jit(solution)/shard_map/all_to_all | solution.py:21
  195.1 28.3 %all-gather.2.cloned.1.call-done = bf16[1024,1024]{1,0:T(8,128)(2,1)} async-done(((bf16[256,1024]{1,0:T(8,128)(2,1)}), bf16[1024,1024]{1,0:T(8,128)(2,1)}) %all-gather.2.cloned.1.call-update) | async-done | bytes 2097168 | tf_op jit(solution)/shard_map/all_gather | solution.py:104
  223.5 3.3 %multiply_reduce_fusion = f32[]{:T(128)} fusion(bf16[1024,1024]{1,0:T(8,128)(2,1)} %all-gather.2.cloned.1.call-done), kind=kLoop, calls=%fused_computation.1 | loop fusion | flops 3145727 | bytes 2097156 | tf_op jit(solution)/shard_map/reduce_sum | solution.py:109
  231.7 2.3 convolution_convert_fusion.2
  234.9 5.0 %all-to-all-start.7 = ((bf16[8,144,128]{2,1,0:T(8,128)(2,1)}), bf16[8,144,128]{2,1,0:T(8,128)(2,1)S(1)}, u32[]{:S(2)}, u32[]{:S(2)}) async-start(bf16[8,144,128]{2,1,0:T(8,128)(2,1)} %copy.47), calls=%async_computation.7 | async-start | bytes 589824 | tf_op jit(solution)/shard_map/all_to_all | solution.py:115
  239.9 2.8 %convolution_convert_fusion.1 = bf16[128,1024]{1,0:T(8,128)(2,1)} fusion(bf16[1024,128]{1,0:T(8,128)(2,1)S(1)} %bitcast.48, bf16[1024,1024]{1,0:T(8,128)(2,1)} %all-gather.2.cloned.1.call-done), kind=kOutput, calls=%fused_computation.10 | convolution fusion | flops 268566528 | bytes 2621440 | tf_op jit(solution)/shard_map/dot_general | solution.py:17
  242.7 4.1 %all-to-all-done.7 = bf16[8,144,128]{2,1,0:T(8,128)(2,1)S(1)} async-done(((bf16[8,144,128]{2,1,0:T(8,128)(2,1)}), bf16[8,144,128]{2,1,0:T(8,128)(2,1)S(1)}, u32[]{:S(2)}, u32[]{:S(2)}) %all-to-all-start.7) | async-done | bytes 294944 | tf_op jit(solution)/shard_map/all_to_all | solution.py:115
  (49 shorter events, 17.0 us)
Async XLA Ops:
  7.2 96.5 %copy-start = (bf16[128,8192]{1,0:T(8,128)(2,1)S(1)}, bf16[128,8192]{1,0:T(8,128)(2,1)}, u32[]{:S(2)}) copy-start(bf16[128,8192]{1,0:T(8,128)(2,1)} %param.14) | copy-start | bytes 6291460
  11.4 17.1 %all-to-all-start = ((bf16[8,304,128]{2,1,0:T(8,128)(2,1)}), bf16[8,304,128]{2,1,0:T(8,128)(2,1)S(1)}, u32[]{:S(2)}, u32[]{:S(2)}) async-start(bf16[8,304,128]{2,1,0:T(8,128)(2,1)} %pad_maximum_fusion), calls=%async_computation | async-start | bytes 1245184 | tf_op jit(solution)/shard_map/all_to_all | solution.py:77
  28.5 4.5 %copy-start.1 = (bf16[8,304,128]{2,1,0:T(8,128)(2,1)}, bf16[8,304,128]{2,1,0:T(8,128)(2,1)S(1)}, u32[]{:S(2)}) copy-start(bf16[8,304,128]{2,1,0:T(8,128)(2,1)S(1)} %all-to-all-done) | copy-start | bytes 1867780
  70.3 24.8 %copy-start.3 = (bf16[128,256]{1,0:T(8,128)(2,1)S(1)}, bf16[128,256]{1,0:T(8,128)(2,1)}, u32[]{:S(2)}) copy-start(bf16[128,256]{1,0:T(8,128)(2,1)} %param.10) | copy-start | bytes 196612
  71.2 23.8 %all-to-all-start.2 = ((bf16[8,128,256]{2,1,0:T(8,128)(2,1)}), bf16[8,128,256]{2,1,0:T(8,128)(2,1)S(1)}, u32[]{:S(2)}, u32[]{:S(2)}) async-start(bf16[8,128,256]{2,1,0:T(8,128)(2,1)} %copy.45), calls=%async_computation.2 | async-start | bytes 1048576 | tf_op jit(solution)/shard_map/all_to_all | solution.py:27
  81.2 31.2 %collective-permute-start = (bf16[256,1024]{1,0:T(8,128)(2,1)}, bf16[256,1024]{1,0:T(8,128)(2,1)S(1)}, u32[]{:S(2)}, u32[]{:S(2)}) collective-permute-start(bf16[256,1024]{1,0:T(8,128)(2,1)} %constant_dynamic-slice_fusion.1), channel_id=1, source_target_pairs={{0,32},{32,0},{1,33},{33,1},{2,34},{34,2},{3,35},{35,3},{4,36},{36... | collective-permute-start | bytes 1572872 | tf_op jit(solution)/shard_map/ppermute | solution.py:58
  96.0 15.6 %all-to-all-start.3 = ((bf16[8,128,256]{2,1,0:T(8,128)(2,1)}), bf16[8,128,256]{2,1,0:T(8,128)(2,1)S(1)}, u32[]{:S(2)}, u32[]{:S(2)}) async-start(bf16[8,128,256]{2,1,0:T(8,128)(2,1)} %broadcast_in_dim.12), calls=%async_computation.3 | async-start | bytes 1048576 | tf_op jit(solution)/shard_map/all_to_all | solution.py:21
  112.4 4.5 %copy-start.2 = (bf16[4,1,128,256]{3,2,1,0:T(8,128)(2,1)S(1)}, bf16[4,1,128,256]{3,2,1,0:T(8,128)(2,1)}, u32[]{:S(2)}) copy-start(bf16[4,1,128,256]{3,2,1,0:T(8,128)(2,1)} %get-tuple-element.5) | copy-start | bytes 786436
  155.9 20.5 %all-to-all-start.5 = ((bf16[8,32,1024]{2,1,0:T(8,128)(2,1)}), bf16[8,32,1024]{2,1,0:T(8,128)(2,1)S(1)}, u32[]{:S(2)}, u32[]{:S(2)}) async-start(bf16[8,32,1024]{2,1,0:T(8,128)(2,1)} %reduce_sum.71), calls=%async_computation.5 | async-start | bytes 1048576 | tf_op jit(solution)/shard_map/all_to_all | solution.py:27
  159.4 64.0 %all-gather.2.cloned.1.call-start = ((), (), s32[]{:S(2)}) async-start(), calls=%async_computation.8 | async-start | bytes 2621440 | tf_op jit(solution)/shard_map/all_gather | solution.py:104
  234.9 11.9 %all-to-all-start.7 = ((bf16[8,144,128]{2,1,0:T(8,128)(2,1)}), bf16[8,144,128]{2,1,0:T(8,128)(2,1)S(1)}, u32[]{:S(2)}, u32[]{:S(2)}) async-start(bf16[8,144,128]{2,1,0:T(8,128)(2,1)} %copy.47), calls=%async_computation.7 | async-start | bytes 589824 | tf_op jit(solution)/shard_map/all_to_all | solution.py:115
Sparse Core Ops, SparseCore 0:
  195.2 28.1 all-gather.1

commit v2 on v1

v2 whole, which is shorter than its diff:
```python
import jax
import jax.numpy as jnp
from jax import lax
from jax.experimental import pallas as pl
from jax.experimental.pallas import tpu as pltpu
from jax.sharding import Mesh, PartitionSpec as P

B16 = jnp.bfloat16
F32 = jnp.float32
NY, NZ, NX = 8, 8, 4
GROUP = ("ylo", "core")
COLUMN = ("ylo", "core", "seq")
PLANE = ("z", "x")
ROWS = 1024
COLS = 1024
PARAMS = pltpu.CompilerParams(vmem_limit_bytes=40 * 1024 * 1024)


def dot(a, b, dims):
    return lax.dot_general(a, b, (dims, ((), ())), preferred_element_type=F32)


def spread(block, axis, parts):
    return lax.all_to_all(jnp.broadcast_to(block[None], (parts,) + block.shape), axis, 0, 0)


def scatter_sum(parts):
    over_x = lax.all_to_all(parts, "x", 0, 0)
    summed = jnp.sum(over_x.astype(F32), axis=0).astype(B16)
    over_z = lax.all_to_all(summed, "z", 0, 0)
    return jnp.sum(over_z.astype(F32), axis=0)


def own_order(rows):
    rest = rows.shape[2:]
    parts = rows.reshape((NY, NZ, NX, 4) + rest)
    return jnp.transpose(parts, (2, 1, 0, 3) + tuple(range(4, parts.ndim))).reshape((ROWS,) + rest)


def block_order(rows):
    rest = rows.shape[1:]
    parts = rows.reshape((NX, NZ, NY, 4) + rest)
    return jnp.transpose(parts, (2, 1, 0, 3) + tuple(range(4, parts.ndim))).reshape((NY, 128) + rest)


def teacher_kernel(heads_ref, out_ref, parts_ref):
    product = dot(heads_ref[...], out_ref[...], ((1,), (0,))).astype(B16)
    for x in range(NX):
        parts_ref[x, 0] = product[:, x * 256 : (x + 1) * 256]


def teacher_parts(window, teacher_out):
    return pl.pallas_call(
        teacher_kernel,
        grid=(NZ,),
        in_specs=[
            pl.BlockSpec((128, 256), lambda i: (0, 0)),
            pl.BlockSpec((256, 1024), lambda i: (0, i)),
        ],
        out_specs=pl.BlockSpec((NX, 1, 128, 256), lambda i: (0, i, 0, 0)),
        out_shape=jax.ShapeDtypeStruct((NX, NZ, 128, 256), B16),
        compiler_params=PARAMS,
        cost_estimate=pl.CostEstimate(flops=2 * 128 * 256 * 8192, bytes_accessed=6 << 20, transcendentals=0),
    )(window, teacher_out)


def combine_kernel(place_ref, picked_ref, got_ref, heads_ref, out_ref, home_ref, other_ref, parts_ref, hidden_ref):
    seq = place_ref[1]

    @pl.when(pl.program_id(0) == 0)
    def _():
        for g in range(4):
            rows = slice(g * 128, (g + 1) * 128)
            hidden_ref[rows, 0:128] = got_ref[2 * g + seq, 0:128, :]
            hidden_ref[rows, 128:256] = got_ref[2 * g + seq, 128:256, :]
            hidden_ref[rows, 256:384] = got_ref[2 * g + 1 - seq, 0:128, :]
            hidden_ref[rows, 384:512] = got_ref[2 * g + 1 - seq, 128:256, :]

    row = lax.broadcasted_iota(jnp.int32, (512, 256), 0)
    choose = (row == picked_ref[0]).astype(F32).astype(B16)
    selected = dot(choose, hidden_ref[...], ((0,), (0,))).astype(B16)
    total = dot(heads_ref[...], out_ref[...], ((1,), (0,)))
    total -= dot(selected[:, :256], home_ref[...], ((1,), (0,)))
    total -= dot(selected[:, 256:], other_ref[...], ((1,), (0,)))
    parts_ref[...] = total.astype(B16)


def combined_parts(place, picked, got, heads, student_out, projector, other):
    return pl.pallas_call(
        combine_kernel,
        grid_spec=pltpu.PrefetchScalarGridSpec(
            num_scalar_prefetch=1,
            grid=(NX,),
            in_specs=[
                pl.BlockSpec((1, 1, 256), lambda i, m: (i, 0, 0)),
                pl.BlockSpec(got.shape, lambda i, m: (0, 0, 0)),
                pl.BlockSpec((256, 128), lambda i, m: (i, 0)),
                pl.BlockSpec((128, COLS), lambda i, m: (0, m[0])),
                pl.BlockSpec((256, COLS), lambda i, m: (0, m[0])),
                pl.BlockSpec((256, COLS), lambda i, m: (0, 0)),
            ],
            out_specs=pl.BlockSpec((256, COLS), lambda i, m: (i, 0)),
            scratch_shapes=[pltpu.VMEM((512, 512), B16)],
        ),
        out_shape=jax.ShapeDtypeStruct((ROWS, COLS), B16),
        compiler_params=PARAMS,
        cost_estimate=pl.CostEstimate(flops=2 * 1024 * 1024 * 900, bytes_accessed=5 << 20, transcendentals=0),
    )(place, picked, got, heads, student_out, projector, other)


def heads_kernel(place_ref, grad_ref, out_ref, part_ref, squares_ref):
    grad = grad_ref[...]
    part_ref[...] = dot(grad, out_ref[...], ((1,), (1,))).astype(B16)
    wide = grad.astype(F32)
    squares = jnp.sum(wide * wide)

    @pl.when(pl.program_id(0) == 0)
    def _():
        squares_ref[0, 0] = squares

    @pl.when(pl.program_id(0) > 0)
    def _():
        squares_ref[0, 0] += squares


def heads_parts(place, grad_all, student_out):
    return pl.pallas_call(
        heads_kernel,
        grid_spec=pltpu.PrefetchScalarGridSpec(
            num_scalar_prefetch=1,
            grid=(NX,),
            in_specs=[
                pl.BlockSpec((256, COLS), lambda i, m: (i, 0)),
                pl.BlockSpec((128, COLS), lambda i, m: (0, m[0])),
            ],
            out_specs=[
                pl.BlockSpec((256, 128), lambda i, m: (i, 0)),
                pl.BlockSpec(memory_space=pltpu.SMEM),
            ],
        ),
        out_shape=[
            jax.ShapeDtypeStruct((ROWS, 128), B16),
            jax.ShapeDtypeStruct((1, 1), F32),
        ],
        compiler_params=PARAMS,
        cost_estimate=pl.CostEstimate(flops=2 * 1024 * 1024 * 128, bytes_accessed=3 << 20, transcendentals=0),
    )(place, grad_all, student_out)


def local(
    teacher_heads,
    teacher_out,
    teacher_resid,
    matches,
    projector,
    student_heads,
    student_out,
    student_resid,
):
    seq = lax.axis_index("seq")
    member = lax.axis_index(COLUMN)
    place = jnp.stack([member, seq]).astype(jnp.int32)
    swap = [(0, 1), (1, 0)]

    there = lax.ppermute(teacher_heads, "seq", swap)
    window = jnp.where(
        seq == 0,
        jnp.concatenate([teacher_heads, there], axis=0),
        jnp.concatenate([there, teacher_heads], axis=0),
    )
    parts = teacher_parts(window, teacher_out)
    hidden = (teacher_resid.astype(F32) + scatter_sum(parts)).astype(B16)

    away = lax.dynamic_slice(projector, (0, (member + 1 - 2 * seq) * COLS), (256, COLS))
    other = lax.ppermute(away, "seq", swap)

    own_matches = lax.dynamic_slice(matches, (seq * 128,), (128,)).astype(B16)
    shared = jnp.concatenate(
        [hidden[:, :128], hidden[:, 128:], student_heads, jnp.broadcast_to(own_matches[None], (16, 128))],
        axis=0,
    )
    resid_parts = jnp.transpose(student_resid.reshape(4, NY, 8, 128), (1, 0, 2, 3)).reshape(NY, 32, 128)
    sent = jnp.concatenate(
        [jnp.broadcast_to(shared[None], (NY,) + shared.shape), resid_parts], axis=1
    )
    got = lax.all_to_all(sent, COLUMN, 0, 0)
    heads = own_order(got[:, 256:384])
    base = (jnp.arange(NY, dtype=jnp.int32) // 2 * 128)[:, None]
    picked = own_order(got[:, 384].astype(jnp.int32) + base).reshape(NX, 1, 256)
    resid = got[:, 400:].reshape(32, COLS)

    partial = combined_parts(place, picked, got, heads, student_out, projector, other)
    difference = resid.astype(F32) + scatter_sum(partial.reshape(NX, NZ, 32, COLS))
    grad = (difference * 0.125).astype(B16)

    tall = spread(grad, "z", NZ).reshape(256, COLS)
    grad_all = spread(tall, "x", NX).reshape(ROWS, COLS)

    heads_part, squares = heads_parts(place, grad_all, student_out)
    squares = squares[0, 0]
    top = lax.reduce_precision(squares, 8, 7)
    middle = lax.reduce_precision(squares - top, 8, 7)
    bottom = squares - top - middle
    scalars = jnp.stack([top, middle, bottom]).astype(B16)
    extra = jnp.broadcast_to(jnp.pad(scalars, (0, 125))[None, None], (NY, 16, 128))
    back = lax.all_to_all(
        jnp.concatenate([block_order(heads_part), extra], axis=1), COLUMN, 0, 0
    ).astype(F32)
    grad_weight = dot(heads, grad_all, ((0,), (0,))).astype(B16)
    grad_heads = jnp.sum(back[:, :128], axis=0).astype(B16)
    total = jnp.sum(back[:, 128, :3])
    loss = (total * (64.0 / (ROWS * 8192))).reshape(1)
    return (loss, grad_heads, grad_weight)


def solution(mesh):
    cut = Mesh(mesh.devices.reshape(2, 2, 2, NZ, NX), COLUMN + PLANE)
    every = COLUMN + PLANE
    return jax.shard_map(
        local,
        mesh=cut,
        in_specs=(
            P(COLUMN, PLANE),
            P(PLANE, "seq"),
            P(GROUP, ("seq",) + PLANE),
            P(GROUP),
            P(("seq",) + PLANE, None),
            P(COLUMN, PLANE),
            P(PLANE, None),
            P(every, None),
        ),
        out_specs=(P(), P(COLUMN, PLANE), P(PLANE, COLUMN)),
        check_vma=False,
    )
```

time: 258 us -> 224 us (0.87)
  matrix products: 22.3 us -> 1.18 us
  waiting for transfers between devices: 76.4 us -> 56.3 us
  blocking collectives: 77.8 us -> 97.6 us
  between operations: 20.9 us -> 7.53 us
  Pallas kernels: 0 us -> 10.2 us
  local copies, waits for them, and re-layouts: 15.9 us -> 8.14 us
  other arithmetic: 13.2 us -> 6.18 us
  starting transfers between devices: 30.2 us -> 35.5 us
    all_gather x1 -> x0, waiting for transfers between devices: 28.3 us -> none  [local(): grad_all = lax.all_gather(tall, 'x', axis=0, tiled=True)]
    all_to_all x1 -> x2, blocking collectives: 18.5 us -> 41.8 us  [spread(): lax.all_to_all(jnp.broadcast_to(block[None], (parts,) + block.shape), axi...]
    dot_general x6 -> x1, matrix products: 22.3 us -> 1.18 us  [dot(): return lax.dot_general(a, b, (dims, ((), ())), preferred_element_type=F32)]
    ppermute x1 -> x2, waiting for transfers between devices: 0.01 us -> 12.3 us  [the longest x1 10.8 us: local(): other = lax.ppermute(away, 'seq', swap)]
    pallas_call x0 -> x3, Pallas kernels: none -> 10.2 us  [the longest x1 4.79 us: combined_parts(): pl.pallas_call(combine_kernel, grid_spec=pltpu.PrefetchScalarGridSpec(num...]
    reshape x2 -> x0, local copies, waits for them, and re-layouts: 6.37 us -> none  [local(): parts = jnp.transpose(product.reshape(128, NZ, NX, 256), (2, 1, 0, 3))]
    ppermute x1 -> x2, starting transfers between devices: 0.78 us -> 6.72 us  [the longest x1 3.83 us: local(): there = lax.ppermute(teacher_heads, 'seq', swap)]
    unnamed x8 -> x16, local copies, waits for them, and re-layouts: 0.02 us -> 4.4 us
  transfers between devices with their start and end apart: 7 -> 6, of which waited for: 6 -> 6; matrix products, arithmetic and copies ran while one was open for 5% -> 2% of each run, Pallas kernels for 0% -> 0%
where the time goes in v2:
time: 224 us; the launch traced here: 223 us
  blocking collectives  97.6 us (44%)
  waiting for transfers between devices  56.3 us (25%)
  starting transfers between devices  35.5 us (16%)
  Pallas kernels  10.2 us (5%)
  local copies, waits for them, and re-layouts  8.14 us (4%)
  between operations  7.53 us (3%)
  other arithmetic  6.18 us (3%)
    all_to_all x2, blocking collectives, scatter_sum(): over_x = lax.all_to_all(parts, 'x', 0, 0)  55.8 us
    all_to_all x2, blocking collectives, spread(): lax.all_to_all(jnp.broadcast_to(block[None], (parts,) + block.shape), axi...  41.8 us
    all_to_all x2, waiting for transfers between devices, scatter_sum(): over_z = lax.all_to_all(summed, 'z', 0, 0)  29.8 us
    all_to_all x2, starting transfers between devices, scatter_sum(): over_z = lax.all_to_all(summed, 'z', 0, 0)  11.6 us
    ppermute x1, waiting for transfers between devices, local(): other = lax.ppermute(away, 'seq', swap)  10.8 us
    all_to_all x1, starting transfers between devices, local(): got = lax.all_to_all(sent, COLUMN, 0, 0)  8.94 us
    all_to_all x1, waiting for transfers between devices, local(): got = lax.all_to_all(sent, COLUMN, 0, 0)  8.47 us
    all_to_all x1, starting transfers between devices, local(): lax.all_to_all(jnp.concatenate([block_order(heads_part), extra], axis=1),...  8.21 us
  transfers between devices with their start and end apart: 6, of which 6 were waited for; matrix products, arithmetic and copies ran while one was open for 2% of the time, Pallas kernels for 0%

profile of v2, /device:TPU:1, one launch (start us, length us, event | category | flops | bytes accessed | tf_op | source)
XLA Modules:
  0.0 222.7 jit_solution(5965232874100801909)
XLA Ops:
  0.6 3.8 %collective-permute-start = (bf16[64,256]{1,0:T(8,128)(2,1)}, bf16[64,256]{1,0:T(8,128)(2,1)S(1)}, u32[]{:S(2)}, u32[]{:S(2)}) collective-permute-start(bf16[64,256]{1,0:T(8,128)(2,1)} %param.8), channel_id=1, source_target_pairs={{0,32},{32,0},{1,33},{33,1},{2,34},{34,2},{3,35},{35,3},{4,36},{36... | collective-permute-start | bytes 98312 | tf_op jit(solution)/shard_map/ppermute | solution.py:165
  4.5 1.5 collective-permute-done
  6.8 2.2 copy-done.3
  9.0 2.3 %shard_map.103 = bf16[4,8,128,256]{3,2,1,0:T(8,128)(2,1)S(1)} custom-call(bf16[128,256]{1,0:T(8,128)(2,1)S(1)} %maximum_select_fusion.heads_ref, bf16[256,8192]{1,0:T(8,128)(2,1)S(1)} %copy-done.3), custom_call_target="tpu_custom_call" | custom-call | flops 536870912 | bytes 6291456 | tf_op jit(solution)/shard_map/pallas_call | solution.py:53
  11.3 27.9 %all_to_all.40 = bf16[4,8,128,256]{3,2,1,0:T(8,128)(2,1)S(1)} all-to-all(bf16[4,8,128,256]{3,2,1,0:T(8,128)(2,1)S(1)} %shard_map.103), channel_id=1, replica_groups=mesh['ylo'=2,'core'=2,'seq'=2,'z'=8,'x'=4] {'x'}, dimensions={0} | all-to-all | bytes 4194304 | tf_op jit(solution)/shard_map/all_to_all | solution.py:28
  39.2 1.3 reduce_sum.60
  40.5 8.1 %all-to-all-start.1 = ((bf16[8,128,256]{2,1,0:T(8,128)(2,1)}), bf16[8,128,256]{2,1,0:T(8,128)(2,1)S(1)}, u32[]{:S(2)}, u32[]{:S(2)}) async-start(bf16[8,128,256]{2,1,0:T(8,128)(2,1)} %reduce_sum.60), calls=%async_computation.1 | async-start | bytes 1048576 | tf_op jit(solution)/shard_map/all_to_all | solution.py:30
  48.8 14.0 %all-to-all-done.1 = bf16[8,128,256]{2,1,0:T(8,128)(2,1)S(1)} async-done(((bf16[8,128,256]{2,1,0:T(8,128)(2,1)}), bf16[8,128,256]{2,1,0:T(8,128)(2,1)S(1)}, u32[]{:S(2)}, u32[]{:S(2)}) %all-to-all-start.1) | async-done | bytes 524320 | tf_op jit(solution)/shard_map/all_to_all | solution.py:30
  64.0 8.9 %all-to-all-start.2 = ((bf16[8,432,128]{2,1,0:T(8,128)(2,1)}), bf16[8,432,128]{2,1,0:T(8,128)(2,1)S(1)}, u32[]{:S(2)}, u32[]{:S(2)}) async-start(bf16[8,432,128]{2,1,0:T(8,128)(2,1)} %pad_maximum_fusion), calls=%async_computation.2 | async-start | bytes 1769472 | tf_op jit(solution)/shard_map/all_to_all | solution.py:186
  72.9 1.9 constant_dynamic-slice_fusion
  74.8 2.9 %collective-permute-start.1 = (bf16[256,1024]{1,0:T(8,128)(2,1)}, bf16[256,1024]{1,0:T(8,128)(2,1)}, u32[]{:S(2)}, u32[]{:S(2)}) collective-permute-start(bf16[256,1024]{1,0:T(8,128)(2,1)} %constant_dynamic-slice_fusion), channel_id=1, source_target_pairs={{0,32},{32,0},{1,33},{33,1},{2,34},{34,2},{3,35},{35,3},{4,36},{36... | collective-permute-start | bytes 1572872 | tf_op jit(solution)/shard_map/ppermute | solution.py:175
  77.8 8.5 %all-to-all-done.2.got_ref = bf16[8,432,128]{2,1,0:T(8,128)(2,1)S(1)} async-done(((bf16[8,432,128]{2,1,0:T(8,128)(2,1)}), bf16[8,432,128]{2,1,0:T(8,128)(2,1)S(1)}, u32[]{:S(2)}, u32[]{:S(2)}) %all-to-all-start.2) | async-done | bytes 884768 | tf_op jit(solution)/shard_map/all_to_all | solution.py:186
  86.9 10.8 %collective-permute-done.1.other_ref = bf16[256,1024]{1,0:T(8,128)(2,1)} collective-permute-done((bf16[256,1024]{1,0:T(8,128)(2,1)}, bf16[256,1024]{1,0:T(8,128)(2,1)}, u32[]{:S(2)}, u32[]{:S(2)}) %collective-permute-start.1) | collective-permute-done | bytes 524320 | tf_op jit(solution)/shard_map/ppermute | solution.py:175
  97.7 2.2 copy-done.2
  99.9 4.8 %shard_map.104 = bf16[1024,1024]{1,0:T(8,128)(2,1)S(1)} custom-call(s32[2]{0:T(128)S(1)} %pad_add_fusion.place_ref, s32[4,1,256]{2,1,0:T(1,128)S(1)} %reshape_reshape.4.picked_ref, bf16[8,432,128]{2,1,0:T(8,128)(2,1)S(1)} %all-to-all-done.2.got_ref, bf16[1024,128]{1,0:T(8,128)(2,1)S(1)} %bitcast.37, bf16[128,8192]{1,0:T(8,128)(2,1)S(1)} %copy-done, ...), custom_call_target="tpu_custom_call" | custom-call | flops 1887436800 | bytes 5242880 | tf_op jit(solution)/shard_map/pallas_call | solution.py:89
  104.7 27.9 %all_to_all.41 = bf16[4,8,32,1024]{3,2,1,0:T(8,128)(2,1)S(1)} all-to-all(bf16[4,8,32,1024]{3,2,1,0:T(8,128)(2,1)S(1)} %bitcast.36), channel_id=1, replica_groups=mesh['ylo'=2,'core'=2,'seq'=2,'z'=8,'x'=4] {'x'}, dimensions={0} | all-to-all | bytes 4194304 | tf_op jit(solution)/shard_map/all_to_all | solution.py:28
  132.6 1.3 reduce_sum.62
  133.9 3.5 %all-to-all-start.4 = ((bf16[8,32,1024]{2,1,0:T(8,128)(2,1)}), bf16[8,32,1024]{2,1,0:T(8,128)(2,1)S(1)}, u32[]{:S(2)}, u32[]{:S(2)}) async-start(bf16[8,32,1024]{2,1,0:T(8,128)(2,1)} %reduce_sum.62), calls=%async_computation.4 | async-start | bytes 1048576 | tf_op jit(solution)/shard_map/all_to_all | solution.py:30
  137.5 15.8 %all-to-all-done.4 = bf16[8,32,1024]{2,1,0:T(8,128)(2,1)S(1)} async-done(((bf16[8,32,1024]{2,1,0:T(8,128)(2,1)}), bf16[8,32,1024]{2,1,0:T(8,128)(2,1)S(1)}, u32[]{:S(2)}, u32[]{:S(2)}) %all-to-all-start.4) | async-done | bytes 524320 | tf_op jit(solution)/shard_map/all_to_all | solution.py:30
  153.4 16.9 %all_to_all.42 = bf16[8,32,1024]{2,1,0:T(8,128)(2,1)S(1)} all-to-all(bf16[8,32,1024]{2,1,0:T(8,128)(2,1)S(1)} %broadcast_in_dim.14), channel_id=1, replica_groups=mesh['ylo'=2,'core'=2,'seq'=2,'z'=8,'x'=4] {'z'}, dimensions={0} | all-to-all | bytes 1048576 | tf_op jit(solution)/shard_map/all_to_all | solution.py:24
  170.6 25.0 %all_to_all.43 = bf16[4,256,1024]{2,1,0:T(8,128)(2,1)S(1)} all-to-all(bf16[4,256,1024]{2,1,0:T(8,128)(2,1)S(1)} %broadcast_in_dim.16), channel_id=1, replica_groups=mesh['ylo'=2,'core'=2,'seq'=2,'z'=8,'x'=4] {'x'}, dimensions={0} | all-to-all | bytes 4194304 | tf_op jit(solution)/shard_map/all_to_all | solution.py:24
  195.6 3.1 %shard_map.105 = (bf16[1024,128]{1,0:T(8,128)(2,1)S(1)}, f32[1,1]{1,0:T(1,128)}) custom-call(s32[2]{0:T(128)S(1)} %pad_add_fusion.place_ref, bf16[1024,1024]{1,0:T(8,128)(2,1)S(1)} %bitcast.34, bf16[128,8192]{1,0:T(8,128)(2,1)S(1)} %copy-done.1), custom_call_target="tpu_custom_call" | custom-call | flops 268435456 | bytes 3145728 | tf_op jit(solution)/shard_map/pallas_call | solution.py:127
  204.5 8.2 %all-to-all-start.7 = ((bf16[8,144,128]{2,1,0:T(8,128)(2,1)}), bf16[8,144,128]{2,1,0:T(8,128)(2,1)S(1)}, u32[]{:S(2)}, u32[]{:S(2)}) async-start(bf16[8,144,128]{2,1,0:T(8,128)(2,1)} %copy.40), calls=%async_computation.7 | async-start | bytes 589824 | tf_op jit(solution)/shard_map/all_to_all | solution.py:206
  213.9 5.7 %all-to-all-done.7 = bf16[8,144,128]{2,1,0:T(8,128)(2,1)S(1)} async-done(((bf16[8,144,128]{2,1,0:T(8,128)(2,1)}), bf16[8,144,128]{2,1,0:T(8,128)(2,1)S(1)}, u32[]{:S(2)}, u32[]{:S(2)}) %all-to-all-start.7) | async-done | bytes 294944 | tf_op jit(solution)/shard_map/all_to_all | solution.py:206
  (48 shorter events, 6.7 us)
Async XLA Ops:
  0.6 5.3 %collective-permute-start = (bf16[64,256]{1,0:T(8,128)(2,1)}, bf16[64,256]{1,0:T(8,128)(2,1)S(1)}, u32[]{:S(2)}, u32[]{:S(2)}) collective-permute-start(bf16[64,256]{1,0:T(8,128)(2,1)} %param.8), channel_id=1, source_target_pairs={{0,32},{32,0},{1,33},{33,1},{2,34},{34,2},{3,35},{35,3},{4,36},{36... | collective-permute-start | bytes 98312 | tf_op jit(solution)/shard_map/ppermute | solution.py:165
  6.8 2.2 copy-start.3
  39.2 9.4 %copy-start.7 = (s32[256]{0:T(256)S(1)}, s32[256]{0:T(256)}, u32[]{:S(2)}) copy-start(s32[256]{0:T(256)} %param.11) | copy-start | bytes 3076
  39.2 9.5 %copy-start.4 = (bf16[4,8192]{1,0:T(4,128)(2,1)S(1)}, bf16[4,8192]{1,0:T(4,128)(2,1)}, u32[]{:S(2)}) copy-start(bf16[4,8192]{1,0:T(4,128)(2,1)} %param.15) | copy-start | bytes 196612
  39.2 23.6 %copy-start.5 = (bf16[128,256]{1,0:T(8,128)(2,1)S(1)}, bf16[128,256]{1,0:T(8,128)(2,1)}, u32[]{:S(2)}) copy-start(bf16[128,256]{1,0:T(8,128)(2,1)} %param.10) | copy-start | bytes 196612
  39.2 23.6 %copy-start.6 = (bf16[128,128]{1,0:T(8,128)(2,1)S(1)}, bf16[128,128]{1,0:T(8,128)(2,1)}, u32[]{:S(2)}) copy-start(bf16[128,128]{1,0:T(8,128)(2,1)} %param.13) | copy-start | bytes 98308
  40.5 22.2 %all-to-all-start.1 = ((bf16[8,128,256]{2,1,0:T(8,128)(2,1)}), bf16[8,128,256]{2,1,0:T(8,128)(2,1)S(1)}, u32[]{:S(2)}, u32[]{:S(2)}) async-start(bf16[8,128,256]{2,1,0:T(8,128)(2,1)} %reduce_sum.60), calls=%async_computation.1 | async-start | bytes 1048576 | tf_op jit(solution)/shard_map/all_to_all | solution.py:30
  64.0 33.7 %copy-start = (bf16[128,8192]{1,0:T(8,128)(2,1)S(1)}, bf16[128,8192]{1,0:T(8,128)(2,1)}, u32[]{:S(2)}) copy-start(bf16[128,8192]{1,0:T(8,128)(2,1)} %out_ref.5) | copy-start | bytes 6291460
  64.0 22.3 %all-to-all-start.2 = ((bf16[8,432,128]{2,1,0:T(8,128)(2,1)}), bf16[8,432,128]{2,1,0:T(8,128)(2,1)S(1)}, u32[]{:S(2)}, u32[]{:S(2)}) async-start(bf16[8,432,128]{2,1,0:T(8,128)(2,1)} %pad_maximum_fusion), calls=%async_computation.2 | async-start | bytes 1769472 | tf_op jit(solution)/shard_map/all_to_all | solution.py:186
  74.8 22.9 %collective-permute-start.1 = (bf16[256,1024]{1,0:T(8,128)(2,1)}, bf16[256,1024]{1,0:T(8,128)(2,1)}, u32[]{:S(2)}, u32[]{:S(2)}) collective-permute-start(bf16[256,1024]{1,0:T(8,128)(2,1)} %constant_dynamic-slice_fusion), channel_id=1, source_target_pairs={{0,32},{32,0},{1,33},{33,1},{2,34},{34,2},{3,35},{35,3},{4,36},{36... | collective-permute-start | bytes 1572872 | tf_op jit(solution)/shard_map/ppermute | solution.py:175
  97.7 2.2 copy-start.2
  133.9 19.3 %all-to-all-start.4 = ((bf16[8,32,1024]{2,1,0:T(8,128)(2,1)}), bf16[8,32,1024]{2,1,0:T(8,128)(2,1)S(1)}, u32[]{:S(2)}, u32[]{:S(2)}) async-start(bf16[8,32,1024]{2,1,0:T(8,128)(2,1)} %reduce_sum.62), calls=%async_computation.4 | async-start | bytes 1048576 | tf_op jit(solution)/shard_map/all_to_all | solution.py:30
  170.6 25.0 %copy-start.1 = (bf16[128,8192]{1,0:T(8,128)(2,1)S(1)}, bf16[128,8192]{1,0:T(8,128)(2,1)}, u32[]{:S(2)}) copy-start(bf16[128,8192]{1,0:T(8,128)(2,1)} %out_ref.5) | copy-start | bytes 6291460
  204.5 15.1 %all-to-all-start.7 = ((bf16[8,144,128]{2,1,0:T(8,128)(2,1)}), bf16[8,144,128]{2,1,0:T(8,128)(2,1)S(1)}, u32[]{:S(2)}, u32[]{:S(2)}) async-start(bf16[8,144,128]{2,1,0:T(8,128)(2,1)} %copy.40), calls=%async_computation.7 | async-start | bytes 589824 | tf_op jit(solution)/shard_map/all_to_all | solution.py:206

commit v3 on v2

v3 whole, which is shorter than its diff:
```python
import jax
import jax.numpy as jnp
from jax import lax
from jax.experimental import pallas as pl
from jax.experimental.pallas import tpu as pltpu
from jax.sharding import Mesh, PartitionSpec as P

B16 = jnp.bfloat16
F32 = jnp.float32
NY, NZ, NX = 8, 8, 4
GROUP = ("ylo", "core")
COLUMN = ("ylo", "core", "seq")
PLANE = ("z", "x")
ROWS = 1024
COLS = 1024
HALF = COLS // 2
PARAMS = pltpu.CompilerParams(vmem_limit_bytes=56 * 1024 * 1024)


def dot(a, b, dims):
    return lax.dot_general(a, b, (dims, ((), ())), preferred_element_type=F32)


def add(a, b):
    return (a.astype(F32) + b.astype(F32)).astype(B16)


def across(block, flip):
    return lax.ppermute(block, "x", [(i, i ^ flip) for i in range(NX)])


def reduce_x(first, second):
    from_one = across(first[1:3], 1)
    from_three = across(second[2:4], 3)
    mine = first[0].astype(F32) + from_one[0].astype(F32)
    pass_on = add(first[3], from_one[1])
    last_three = across(pass_on, 3)
    theirs = second[0].astype(F32) + from_three[1].astype(F32)
    pass_back = add(second[1], from_three[0])
    last_one = across(pass_back, 1)
    return (
        (mine + last_three.astype(F32)).astype(B16),
        (theirs + last_one.astype(F32)).astype(B16),
    )


def gather_x(first, second):
    pair = jnp.stack([first, across(first, 3)])
    other = jnp.stack([second, across(second, 1)])
    return pair, across(pair, 1), other, across(other, 3)


def reduce_z(parts):
    moved = lax.all_to_all(parts, "z", 0, 0)
    return jnp.sum(moved.astype(F32), axis=0)


def own_order(rows):
    rest = rows.shape[2:]
    parts = rows.reshape((NY, NZ, NX, 4) + rest)
    return jnp.transpose(parts, (2, 1, 0, 3) + tuple(range(4, parts.ndim))).reshape((ROWS,) + rest)


def block_order(rows):
    rest = rows.shape[1:]
    parts = rows.reshape((NX, NZ, NY, 4) + rest)
    return jnp.transpose(parts, (2, 1, 0, 3) + tuple(range(4, parts.ndim))).reshape((NY, 128) + rest)


def teacher_kernel(place_ref, own_ref, there_ref, out_ref, first_ref, second_ref, window_ref):
    seq, x = place_ref[1], place_ref[2]

    @pl.when(pl.program_id(0) == 0)
    def _():
        window_ref[pl.ds(pl.multiple_of(seq * 64, 64), 64), :] = own_ref[...]
        window_ref[pl.ds(pl.multiple_of(64 - seq * 64, 64), 64), :] = there_ref[...]

    product = dot(window_ref[...], out_ref[...], ((1,), (0,))).astype(B16)
    for to in range(NX):
        first_ref[to ^ x, 0] = product[:, to * 256 : to * 256 + 128]
        second_ref[to ^ x, 0] = product[:, to * 256 + 128 : to * 256 + 256]


def teacher_parts(place, own, there, teacher_out):
    half = pl.BlockSpec((NX, 1, 128, 128), lambda i, m: (0, i, 0, 0))
    return pl.pallas_call(
        teacher_kernel,
        grid_spec=pltpu.PrefetchScalarGridSpec(
            num_scalar_prefetch=1,
            grid=(NZ,),
            in_specs=[
                pl.BlockSpec((64, 256), lambda i, m: (0, 0)),
                pl.BlockSpec((64, 256), lambda i, m: (0, 0)),
                pl.BlockSpec((256, 1024), lambda i, m: (0, i)),
            ],
            out_specs=[half, half],
            scratch_shapes=[pltpu.VMEM((128, 256), B16)],
        ),
        out_shape=[jax.ShapeDtypeStruct((NX, NZ, 128, 128), B16)] * 2,
        compiler_params=PARAMS,
        cost_estimate=pl.CostEstimate(flops=2 * 128 * 256 * 8192, bytes_accessed=6 << 20, transcendentals=0),
    )(place, own, there, teacher_out)


def combine_kernel(
    place_ref, picked_ref, got_ref, heads_ref, out_ref, home_ref, other_ref, first_ref, second_ref, hidden_ref
):
    seq = place_ref[1]

    @pl.when(pl.program_id(0) == 0)
    def _():
        for g in range(4):
            rows = slice(g * 128, (g + 1) * 128)
            hidden_ref[rows, 0:128] = got_ref[2 * g + seq, 0:128, :]
            hidden_ref[rows, 128:256] = got_ref[2 * g + seq, 128:256, :]
            hidden_ref[rows, 256:384] = got_ref[2 * g + 1 - seq, 0:128, :]
            hidden_ref[rows, 384:512] = got_ref[2 * g + 1 - seq, 128:256, :]

    row = lax.broadcasted_iota(jnp.int32, (512, 256), 0)
    choose = (row == picked_ref[0]).astype(F32).astype(B16)
    selected = dot(choose, hidden_ref[...], ((0,), (0,))).astype(B16)
    total = dot(heads_ref[...], out_ref[...], ((1,), (0,)))
    total -= dot(selected[:, :256], home_ref[...], ((1,), (0,)))
    total -= dot(selected[:, 256:], other_ref[...], ((1,), (0,)))
    first_ref[0] = total[:, :HALF].astype(B16)
    second_ref[0] = total[:, HALF:].astype(B16)


def combined_parts(place, picked, got, heads, student_out, projector, other):
    half = pl.BlockSpec((1, 256, HALF), lambda i, m: (i, 0, 0))
    return pl.pallas_call(
        combine_kernel,
        grid_spec=pltpu.PrefetchScalarGridSpec(
            num_scalar_prefetch=1,
            grid=(NX,),
            in_specs=[
                pl.BlockSpec((1, 1, 256), lambda i, m: (i ^ m[2], 0, 0)),
                pl.BlockSpec(got.shape, lambda i, m: (0, 0, 0)),
                pl.BlockSpec((256, 128), lambda i, m: (i ^ m[2], 0)),
                pl.BlockSpec((128, COLS), lambda i, m: (0, m[0])),
                pl.BlockSpec((256, COLS), lambda i, m: (0, m[0])),
                pl.BlockSpec((256, COLS), lambda i, m: (0, 0)),
            ],
            out_specs=[half, half],
            scratch_shapes=[pltpu.VMEM((512, 512), B16)],
        ),
        out_shape=[jax.ShapeDtypeStruct((NX, 256, HALF), B16)] * 2,
        compiler_params=PARAMS,
        cost_estimate=pl.CostEstimate(flops=2 * 1024 * 1024 * 900, bytes_accessed=5 << 20, transcendentals=0),
    )(place, picked, got, heads, student_out, projector, other)


def gradient_parts(pair_ref, far_ref, other_ref, off_ref):
    return (
        (0, pair_ref[0], other_ref[0]),
        (1, far_ref[0], other_ref[1]),
        (2, far_ref[1], off_ref[1]),
        (3, pair_ref[1], off_ref[0]),
    )


def heads_kernel(place_ref, pair_ref, far_ref, other_ref, off_ref, out_ref, part_ref, squares_ref, sums_ref):
    x = place_ref[2]
    for k, first, second in gradient_parts(pair_ref, far_ref, other_ref, off_ref):
        part = dot(first, out_ref[:, :HALF], ((1,), (1,))) + dot(second, out_ref[:, HALF:], ((1,), (1,)))
        part_ref[k ^ x] = part.astype(B16)
        wide = first.astype(F32)
        more = second.astype(F32)
        line = jnp.sum(wide * wide + more * more, axis=0, keepdims=True)
        sums_ref[k ^ x] = line[:, :128] + line[:, 128:256] + line[:, 256:384] + line[:, 384:]
    total = sums_ref[0] + sums_ref[1] + sums_ref[2] + sums_ref[3]
    top = total.astype(B16).astype(F32)
    middle = (total - top).astype(B16).astype(F32)
    bottom = total - top - middle
    row = lax.broadcasted_iota(jnp.int32, (16, 128), 0)
    lines = jnp.where(row == 0, top, jnp.where(row == 1, middle, jnp.where(row == 2, bottom, 0.0)))
    squares_ref[...] = lines.astype(B16)


def weight_kernel(place_ref, pair_ref, far_ref, other_ref, off_ref, heads_ref, weight_ref):
    x = place_ref[2]
    left = jnp.zeros((128, HALF), F32)
    right = jnp.zeros((128, HALF), F32)
    for k, first, second in gradient_parts(pair_ref, far_ref, other_ref, off_ref):
        heads = heads_ref[k ^ x]
        left += dot(heads, first, ((0,), (0,)))
        right += dot(heads, second, ((0,), (0,)))
    weight_ref[:, :HALF] = left.astype(B16)
    weight_ref[:, HALF:] = right.astype(B16)


QUARTERS = pl.BlockSpec((2, 256, HALF), lambda i, m: (0, 0, 0))


def heads_parts(place, gathered, student_out):
    return pl.pallas_call(
        heads_kernel,
        grid_spec=pltpu.PrefetchScalarGridSpec(
            num_scalar_prefetch=1,
            grid=(1,),
            in_specs=[QUARTERS] * 4 + [pl.BlockSpec((128, COLS), lambda i, m: (0, m[0]))],
            out_specs=[
                pl.BlockSpec((NX, 256, 128), lambda i, m: (0, 0, 0)),
                pl.BlockSpec((16, 128), lambda i, m: (0, 0)),
            ],
            scratch_shapes=[pltpu.VMEM((NX, 1, 128), F32)],
        ),
        out_shape=[
            jax.ShapeDtypeStruct((NX, 256, 128), B16),
            jax.ShapeDtypeStruct((16, 128), B16),
        ],
        compiler_params=pltpu.CompilerParams(vmem_limit_bytes=24 * 1024 * 1024),
        cost_estimate=pl.CostEstimate(flops=2 * 1024 * 1024 * 128, bytes_accessed=3 << 20, transcendentals=0),
    )(place, *gathered, student_out)


def weight_grad(place, gathered, heads):
    return pl.pallas_call(
        weight_kernel,
        grid_spec=pltpu.PrefetchScalarGridSpec(
            num_scalar_prefetch=1,
            grid=(1,),
            in_specs=[QUARTERS] * 4 + [pl.BlockSpec((NX, 256, 128), lambda i, m: (0, 0, 0))],
            out_specs=pl.BlockSpec((128, COLS), lambda i, m: (0, 0)),
        ),
        out_shape=jax.ShapeDtypeStruct((128, COLS), B16),
        compiler_params=pltpu.CompilerParams(vmem_limit_bytes=24 * 1024 * 1024),
        cost_estimate=pl.CostEstimate(flops=2 * 1024 * 1024 * 128, bytes_accessed=3 << 20, transcendentals=0),
    )(place, *gathered, heads)


def local(
    teacher_heads,
    teacher_out,
    teacher_resid,
    matches,
    projector,
    student_heads,
    student_out,
    student_resid,
):
    seq = lax.axis_index("seq")
    member = lax.axis_index(COLUMN)
    place = jnp.stack([member, seq, lax.axis_index("x")]).astype(jnp.int32)
    swap = [(0, 1), (1, 0)]

    there = lax.ppermute(teacher_heads, "seq", swap)
    first, second = reduce_x(*teacher_parts(place, teacher_heads, there, teacher_out))
    halves = jnp.concatenate([first, second], axis=1)

    away = lax.dynamic_slice(projector, (0, (member + 1 - 2 * seq) * COLS), (256, COLS))
    other = lax.ppermute(away, "seq", swap)
    halves, other = lax.optimization_barrier((halves, other))
    resid_halves = jnp.concatenate([teacher_resid[:, :128], teacher_resid[:, 128:]], axis=0)
    hidden = (resid_halves.astype(F32) + reduce_z(halves)).astype(B16)

    own_matches = lax.dynamic_slice(matches, (seq * 128,), (128,)).astype(B16)
    shared = jnp.concatenate(
        [hidden, student_heads, jnp.broadcast_to(own_matches[None], (16, 128))], axis=0
    )
    resid_parts = jnp.transpose(student_resid.reshape(4, NY, 8, 128), (1, 0, 2, 3)).reshape(NY, 32, 128)
    sent = jnp.concatenate(
        [jnp.broadcast_to(shared[None], (NY,) + shared.shape), resid_parts], axis=1
    )
    got = lax.all_to_all(sent, COLUMN, 0, 0)
    heads = own_order(got[:, 256:384])
    base = (jnp.arange(NY, dtype=jnp.int32) // 2 * 128)[:, None]
    picked = own_order(got[:, 384].astype(jnp.int32) + base).reshape(NX, 1, 256)
    resid = got[:, 400:].reshape(32, 2, HALF)
    resid = jnp.concatenate([resid[:, 0], resid[:, 1]], axis=0)

    first, second = combined_parts(place, picked, got, heads, student_out, projector, other)
    first, second = reduce_x(
        first.reshape(NX, NZ, 32, HALF), second.reshape(NX, NZ, 32, HALF)
    )
    summed = reduce_z(jnp.concatenate([first, second], axis=1))
    difference = resid.astype(F32) + summed
    grad = (difference * 0.125).astype(B16)

    tall = lax.all_to_all(jnp.broadcast_to(grad[None], (NZ, 64, HALF)), "z", 0, 0)
    gathered = gather_x(tall[:, :32].reshape(256, HALF), tall[:, 32:].reshape(256, HALF))

    heads_part, squares = heads_parts(place, gathered, student_out)
    sent = jnp.concatenate(
        [block_order(heads_part.reshape(ROWS, 128)), jnp.broadcast_to(squares[None], (NY, 16, 128))], axis=1
    )
    back = lax.all_to_all(sent, COLUMN, 0, 0).astype(F32)
    grad_weight = weight_grad(place, gathered, heads.reshape(NX, 256, 128))
    grad_heads = jnp.sum(back[:, :128], axis=0).astype(B16)
    total = jnp.sum(back[:, 128:])
    loss = (total * (64.0 / (ROWS * 8192))).reshape(1)
    return (loss, grad_heads, grad_weight)


def solution(mesh):
    cut = Mesh(mesh.devices.reshape(2, 2, 2, NZ, NX), COLUMN + PLANE)
    every = COLUMN + PLANE
    return jax.shard_map(
        local,
        mesh=cut,
        in_specs=(
            P(COLUMN, PLANE),
            P(PLANE, "seq"),
            P(GROUP, ("seq",) + PLANE),
            P(GROUP),
            P(("seq",) + PLANE, None),
            P(COLUMN, PLANE),
            P(PLANE, None),
            P(every, None),
        ),
        out_specs=(P(), P(COLUMN, PLANE), P(PLANE, COLUMN)),
        check_vma=False,
    )
```

time: 224 us -> 201 us (0.90)
  blocking collectives: 97.6 us -> 15.7 us
  waiting for transfers between devices: 56.3 us -> 90.5 us
  starting transfers between devices: 35.5 us -> 56.5 us
  Pallas kernels: 10.2 us -> 17 us
  between operations: 7.53 us -> 2.76 us
  local copies, waits for them, and re-layouts: 8.14 us -> 11.3 us
    all_to_all x4 -> x1, blocking collectives: 97.6 us -> 15.7 us  [local(): lax.all_to_all(jnp.broadcast_to(grad[None], (NZ, 64, HALF)), 'z', 0, 0)]
    ppermute x0 -> x12, waiting for transfers between devices: none -> 41.1 us  [across(): return lax.ppermute(block, 'x', [(i, i ^ flip) for i in range(NX)])]
    ppermute x0 -> x12, starting transfers between devices: none -> 13.9 us  [across(): return lax.ppermute(block, 'x', [(i, i ^ flip) for i in range(NX)])]
    ppermute x1, waiting for transfers between devices: 10.8 us -> 3.33 us  [local(): other = lax.ppermute(away, 'seq', swap)]
    pallas_call x1 -> x2, Pallas kernels: 2.32 us -> 9.28 us  [the longest x1 7.56 us: teacher_parts(): pl.pallas_call(teacher_kernel, grid_spec=pltpu.PrefetchScalarGridSpec(num...]
    slice x1 -> x10, local copies, waits for them, and re-layouts: 0.01 us -> 6.44 us  [the longest x2 3.25 us: reduce_x(): from_one = across(first[1:3], 1)]
    all_to_all x1, waiting for transfers between devices: 8.47 us -> 13.2 us  [local(): got = lax.all_to_all(sent, COLUMN, 0, 0)]
    unnamed x16 -> x30, local copies, waits for them, and re-layouts: 4.4 us -> 0.68 us
  transfers between devices with their start and end apart: 6 -> 18, of which waited for: 6 -> 16; matrix products, arithmetic and copies ran while one was open for 2% -> 4% of each run, Pallas kernels for 0% -> 1%
where the time goes in v3:
time: 201 us; the launch traced here: 200 us
  waiting for transfers between devices  90.5 us (45%)
  starting transfers between devices  56.5 us (28%)
  Pallas kernels  17 us (8%)
  blocking collectives  15.7 us (8%)
  local copies, waits for them, and re-layouts  11.3 us (6%)
  other arithmetic  6.55 us (3%)
  between operations  2.76 us (1%)
    ppermute x12, waiting for transfers between devices, across(): return lax.ppermute(block, 'x', [(i, i ^ flip) for i in range(NX)])  41.1 us
    all_to_all x2, waiting for transfers between devices, reduce_z(): moved = lax.all_to_all(parts, 'z', 0, 0)  26.7 us
    all_to_all x1, blocking collectives, local(): lax.all_to_all(jnp.broadcast_to(grad[None], (NZ, 64, HALF)), 'z', 0, 0)  15.7 us
    ppermute x12, starting transfers between devices, across(): return lax.ppermute(block, 'x', [(i, i ^ flip) for i in range(NX)])  13.9 us
    all_to_all x1, waiting for transfers between devices, local(): got = lax.all_to_all(sent, COLUMN, 0, 0)  13.2 us
    all_to_all x1, starting transfers between devices, local(): got = lax.all_to_all(sent, COLUMN, 0, 0)  12.5 us
    all_to_all x2, starting transfers between devices, reduce_z(): moved = lax.all_to_all(parts, 'z', 0, 0)  11.7 us
    all_to_all x1, starting transfers between devices, local(): back = lax.all_to_all(sent, COLUMN, 0, 0).astype(F32)  11.3 us
  transfers between devices with their start and end apart: 18, of which 16 were waited for; matrix products, arithmetic and copies ran while one was open for 4% of the time, Pallas kernels for 1%

profile of v3, /device:TPU:1, one launch (start us, length us, event | category | flops | bytes accessed | tf_op | source)
XLA Modules:
  0.0 200.3 jit_solution(10603118141128211375)
XLA Ops:
  0.6 3.8 %collective-permute-start = (bf16[64,256]{1,0:T(8,128)(2,1)}, bf16[64,256]{1,0:T(8,128)(2,1)S(1)}, u32[]{:S(2)}, u32[]{:S(2)}) collective-permute-start(bf16[64,256]{1,0:T(8,128)(2,1)} %own_ref.1), channel_id=1, source_target_pairs={{0,32},{32,0},{1,33},{33,1},{2,34},{34,2},{3,35},{35,3},{4,36},{36... | collective-permute-start | bytes 98312 | tf_op jit(solution)/shard_map/ppermute | solution.py:247
  6.6 7.6 %shard_map.103 = (bf16[4,8,128,128]{3,2,1,0:T(8,128)(2,1)}, bf16[4,8,128,128]{3,2,1,0:T(8,128)(2,1)}) custom-call(s32[3]{0:T(128)} %pad_add_fusion.place_ref, bf16[64,256]{1,0:T(8,128)(2,1)} %own_ref.1, bf16[64,256]{1,0:T(8,128)(2,1)} %copy-done.12, bf16[256,8192]{1,0:T(8,128)(2,1)} %out_ref.3), custom_call_target="tpu_custom_call" | custom-call | flops 536870912 | bytes 6291456 | tf_op jit(solution)/shard_map/pallas_call | solution.py:86
  14.2 2.0 %slice.106 = bf16[2,8,128,128]{3,2,1,0:T(8,128)(2,1)} slice(bf16[4,8,128,128]{3,2,1,0:T(8,128)(2,1)} %get-tuple-element.11), slice={[1:3], [0:8], [0:128], [0:128]} | slice | bytes 1048576 | tf_op jit(solution)/shard_map/slice | solution.py:33
  17.4 1.9 slice.111
  19.3 1.8 collective-permute-start.3
  21.2 5.7 %collective-permute-done.1 = bf16[2,8,128,128]{3,2,1,0:T(8,128)(2,1)S(1)} collective-permute-done((bf16[2,8,128,128]{3,2,1,0:T(8,128)(2,1)}, bf16[2,8,128,128]{3,2,1,0:T(8,128)(2,1)S(1)}, u32[]{:S(2)}, u32[]{:S(2)}) %collective-permute-start.1) | collective-permute-done | bytes 524320 | tf_op jit(solution)/shard_map/ppermute | solution.py:29
  27.0 3.7 %collective-permute-start.2 = (bf16[8,128,128]{2,1,0:T(8,128)(2,1)S(1)}, bf16[8,128,128]{2,1,0:T(8,128)(2,1)S(1)}, u32[]{:S(2)}, u32[]{:S(2)}) collective-permute-start(bf16[8,128,128]{2,1,0:T(8,128)(2,1)S(1)} %fusion.8), channel_id=1, source_target_pairs={{0,3},{1,2},{2,1},{3,0},{4,7},{5,6},{6,5},{7,4},{8,11},{9,10},{10,... | collective-permute-start | bytes 786440 | tf_op jit(solution)/shard_map/ppermute | solution.py:29
  33.1 3.2 %collective-permute-start.5 = (bf16[256,1024]{1,0:T(8,128)(2,1)S(1)}, bf16[256,1024]{1,0:T(8,128)(2,1)S(1)}, u32[]{:S(2)}, u32[]{:S(2)}) collective-permute-start(bf16[256,1024]{1,0:T(8,128)(2,1)S(1)} %constant_dynamic-slice_fusion), channel_id=1, source_target_pairs={{0,32},{32,0},{1,33},{33,1},{2,34},{34,2},{3,35},{35,3},{4,36},{36... | collective-permute-start | bytes 1572872 | tf_op jit(solution)/shard_map/ppermute | solution.py:252
  39.6 3.3 %collective-permute-done.5.other_ref = bf16[256,1024]{1,0:T(8,128)(2,1)S(1)} collective-permute-done((bf16[256,1024]{1,0:T(8,128)(2,1)S(1)}, bf16[256,1024]{1,0:T(8,128)(2,1)S(1)}, u32[]{:S(2)}, u32[]{:S(2)}) %collective-permute-start.5) | collective-permute-done | bytes 524320 | tf_op jit(solution)/shard_map/ppermute | solution.py:252
  43.0 8.2 %all-to-all-start = ((bf16[8,256,128]{2,1,0:T(8,128)(2,1)}), bf16[8,256,128]{2,1,0:T(8,128)(2,1)S(1)}, u32[]{:S(2)}, u32[]{:S(2)}) async-start(bf16[8,256,128]{2,1,0:T(8,128)(2,1)} %pad_maximum_fusion.1), calls=%async_computation | async-start | bytes 1048576 | tf_op jit(solution)/shard_map/all_to_all | solution.py:54
  51.3 12.1 %all-to-all-done = bf16[8,256,128]{2,1,0:T(8,128)(2,1)S(1)} async-done(((bf16[8,256,128]{2,1,0:T(8,128)(2,1)}), bf16[8,256,128]{2,1,0:T(8,128)(2,1)S(1)}, u32[]{:S(2)}, u32[]{:S(2)}) %all-to-all-start) | async-done | bytes 524320 | tf_op jit(solution)/shard_map/all_to_all | solution.py:54
  64.7 12.5 %all-to-all-start.1 = ((bf16[8,432,128]{2,1,0:T(8,128)(2,1)}), bf16[8,432,128]{2,1,0:T(8,128)(2,1)S(1)}, u32[]{:S(2)}, u32[]{:S(2)}) async-start(bf16[8,432,128]{2,1,0:T(8,128)(2,1)} %pad_maximum_fusion), calls=%async_computation.1 | async-start | bytes 1769472 | tf_op jit(solution)/shard_map/all_to_all | solution.py:265
  77.2 13.2 %all-to-all-done.1.got_ref = bf16[8,432,128]{2,1,0:T(8,128)(2,1)S(1)} async-done(((bf16[8,432,128]{2,1,0:T(8,128)(2,1)}), bf16[8,432,128]{2,1,0:T(8,128)(2,1)S(1)}, u32[]{:S(2)}, u32[]{:S(2)}) %all-to-all-start.1) | async-done | bytes 884768 | tf_op jit(solution)/shard_map/all_to_all | solution.py:265
  92.5 6.4 %shard_map.104 = (bf16[4,256,512]{2,1,0:T(8,128)(2,1)}, bf16[4,256,512]{2,1,0:T(8,128)(2,1)}) custom-call(s32[3]{0:T(128)} %pad_add_fusion.place_ref, s32[4,1,256]{2,1,0:T(1,128)} %reshape_reshape.12.picked_ref, bf16[8,432,128]{2,1,0:T(8,128)(2,1)} %copy-done.3, bf16[1024,128]{1,0:T(8,128)(2,1)} %bitcast.80, bf16[128,8192]{1,0:T(8,128)(2,1)} %out_ref.5, ...), custom_call_target="tpu_custom_call" | custom-call | flops 1887436800 | bytes 5242880 | tf_op jit(solution)/shard_map/pallas_call | solution.py:131
  104.3 9.6 %collective-permute-done.6 = bf16[2,8,32,512]{3,2,1,0:T(8,128)(2,1)S(1)} collective-permute-done((bf16[2,8,32,512]{3,2,1,0:T(8,128)(2,1)S(1)}, bf16[2,8,32,512]{3,2,1,0:T(8,128)(2,1)S(1)}, u32[]{:S(2)}, u32[]{:S(2)}) %collective-permute-start.6) | collective-permute-done | bytes 524320 | tf_op jit(solution)/shard_map/ppermute | solution.py:29
  115.0 2.1 %collective-permute-done.8 = bf16[2,8,32,512]{3,2,1,0:T(8,128)(2,1)S(1)} collective-permute-done((bf16[2,8,32,512]{3,2,1,0:T(8,128)(2,1)S(1)}, bf16[2,8,32,512]{3,2,1,0:T(8,128)(2,1)S(1)}, u32[]{:S(2)}, u32[]{:S(2)}) %collective-permute-start.8) | collective-permute-done | bytes 524320 | tf_op jit(solution)/shard_map/ppermute | solution.py:29
  117.3 5.4 %collective-permute-done.7 = bf16[8,32,512]{2,1,0:T(8,128)(2,1)S(1)} collective-permute-done((bf16[8,32,512]{2,1,0:T(8,128)(2,1)S(1)}, bf16[8,32,512]{2,1,0:T(8,128)(2,1)S(1)}, u32[]{:S(2)}, u32[]{:S(2)}) %collective-permute-start.7) | collective-permute-done | bytes 262176 | tf_op jit(solution)/shard_map/ppermute | solution.py:29
  124.3 3.5 %all-to-all-start.2 = ((bf16[8,64,512]{2,1,0:T(8,128)(2,1)}), bf16[8,64,512]{2,1,0:T(8,128)(2,1)S(1)}, u32[]{:S(2)}, u32[]{:S(2)}) async-start(bf16[8,64,512]{2,1,0:T(8,128)(2,1)} %pad_maximum_fusion.2), calls=%async_computation.2 | async-start | bytes 1048576 | tf_op jit(solution)/shard_map/all_to_all | solution.py:54
  128.0 14.6 %all-to-all-done.2 = bf16[8,64,512]{2,1,0:T(8,128)(2,1)S(1)} async-done(((bf16[8,64,512]{2,1,0:T(8,128)(2,1)}), bf16[8,64,512]{2,1,0:T(8,128)(2,1)S(1)}, u32[]{:S(2)}, u32[]{:S(2)}) %all-to-all-start.2) | async-done | bytes 524320 | tf_op jit(solution)/shard_map/all_to_all | solution.py:54
  142.7 15.7 %all_to_all.25 = bf16[8,64,512]{2,1,0:T(8,128)(2,1)S(1)} all-to-all(bf16[8,64,512]{2,1,0:T(8,128)(2,1)S(1)} %broadcast_in_dim.10), channel_id=1, replica_groups=mesh['ylo'=2,'core'=2,'seq'=2,'z'=8,'x'=4] {'z'}, dimensions={0} | all-to-all | bytes 1048576 | tf_op jit(solution)/shard_map/all_to_all | solution.py:280
  160.6 3.2 %collective-permute-done.12 = bf16[256,512]{1,0:T(8,128)(2,1)S(1)} collective-permute-done((bf16[256,512]{1,0:T(8,128)(2,1)S(1)}, bf16[256,512]{1,0:T(8,128)(2,1)S(1)}, u32[]{:S(2)}, u32[]{:S(2)}) %collective-permute-start.12) | collective-permute-done | bytes 262176 | tf_op jit(solution)/shard_map/ppermute | solution.py:29
  166.3 10.4 %collective-permute-done.13.off_ref = bf16[2,256,512]{2,1,0:T(8,128)(2,1)S(1)} collective-permute-done((bf16[2,256,512]{2,1,0:T(8,128)(2,1)S(1)}, bf16[2,256,512]{2,1,0:T(8,128)(2,1)S(1)}, u32[]{:S(2)}, u32[]{:S(2)}) %collective-permute-start.13) | collective-permute-done | bytes 524320 | tf_op jit(solution)/shard_map/ppermute | solution.py:29
  178.9 11.3 %all-to-all-start.4 = ((bf16[8,144,128]{2,1,0:T(8,128)(2,1)}), bf16[8,144,128]{2,1,0:T(8,128)(2,1)S(1)}, u32[]{:S(2)}, u32[]{:S(2)}) async-start(bf16[8,144,128]{2,1,0:T(8,128)(2,1)} %copy.40), calls=%async_computation.4 | async-start | bytes 589824 | tf_op jit(solution)/shard_map/all_to_all | solution.py:287
  192.0 5.2 %all-to-all-done.4 = bf16[8,144,128]{2,1,0:T(8,128)(2,1)S(1)} async-done(((bf16[8,144,128]{2,1,0:T(8,128)(2,1)}), bf16[8,144,128]{2,1,0:T(8,128)(2,1)S(1)}, u32[]{:S(2)}, u32[]{:S(2)}) %all-to-all-start.4) | async-done | bytes 294944 | tf_op jit(solution)/shard_map/all_to_all | solution.py:287
  (99 shorter events, 30.8 us)
Async XLA Ops:
  0.6 5.3 %collective-permute-start = (bf16[64,256]{1,0:T(8,128)(2,1)}, bf16[64,256]{1,0:T(8,128)(2,1)S(1)}, u32[]{:S(2)}, u32[]{:S(2)}) collective-permute-start(bf16[64,256]{1,0:T(8,128)(2,1)} %own_ref.1), channel_id=1, source_target_pairs={{0,32},{32,0},{1,33},{33,1},{2,34},{34,2},{3,35},{35,3},{4,36},{36... | collective-permute-start | bytes 98312 | tf_op jit(solution)/shard_map/ppermute | solution.py:247
  16.2 10.7 %collective-permute-start.1 = (bf16[2,8,128,128]{3,2,1,0:T(8,128)(2,1)}, bf16[2,8,128,128]{3,2,1,0:T(8,128)(2,1)S(1)}, u32[]{:S(2)}, u32[]{:S(2)}) collective-permute-start(bf16[2,8,128,128]{3,2,1,0:T(8,128)(2,1)} %slice.106), channel_id=1, source_target_pairs={{0,1},{1,0},{2,3},{3,2},{4,5},{5,4},{6,7},{7,6},{8,9},{9,8},{10,11... | collective-permute-start | bytes 1572872 | tf_op jit(solution)/shard_map/ppermute | solution.py:29
  19.3 12.5 %collective-permute-start.3 = (bf16[2,8,128,128]{3,2,1,0:T(8,128)(2,1)}, bf16[2,8,128,128]{3,2,1,0:T(8,128)(2,1)S(1)}, u32[]{:S(2)}, u32[]{:S(2)}) collective-permute-start(bf16[2,8,128,128]{3,2,1,0:T(8,128)(2,1)} %slice.111), channel_id=1, source_target_pairs={{0,3},{1,2},{2,1},{3,0},{4,7},{5,6},{6,5},{7,4},{8,11},{9,10},{10,... | collective-permute-start | bytes 1572872 | tf_op jit(solution)/shard_map/ppermute | solution.py:29
  27.0 10.6 %collective-permute-start.2 = (bf16[8,128,128]{2,1,0:T(8,128)(2,1)S(1)}, bf16[8,128,128]{2,1,0:T(8,128)(2,1)S(1)}, u32[]{:S(2)}, u32[]{:S(2)}) collective-permute-start(bf16[8,128,128]{2,1,0:T(8,128)(2,1)S(1)} %fusion.8), channel_id=1, source_target_pairs={{0,3},{1,2},{2,1},{3,0},{4,7},{5,6},{6,5},{7,4},{8,11},{9,10},{10,... | collective-permute-start | bytes 786440 | tf_op jit(solution)/shard_map/ppermute | solution.py:29
  31.9 6.8 %collective-permute-start.4 = (bf16[8,128,128]{2,1,0:T(8,128)(2,1)S(1)}, bf16[8,128,128]{2,1,0:T(8,128)(2,1)S(1)}, u32[]{:S(2)}, u32[]{:S(2)}) collective-permute-start(bf16[8,128,128]{2,1,0:T(8,128)(2,1)S(1)} %fusion.9), channel_id=1, source_target_pairs={{0,1},{1,0},{2,3},{3,2},{4,5},{5,4},{6,7},{7,6},{8,9},{9,8},{10,11... | collective-permute-start | bytes 786440 | tf_op jit(solution)/shard_map/ppermute | solution.py:29
  33.1 18.2 %copy-start.10 = (bf16[128,256]{1,0:T(8,128)(2,1)S(1)}, bf16[128,256]{1,0:T(8,128)(2,1)}, u32[]{:S(2)}) copy-start(bf16[128,256]{1,0:T(8,128)(2,1)} %param.10) | copy-start | bytes 196612
  33.1 18.2 %copy-start.11 = (bf16[4,8192]{1,0:T(4,128)(2,1)S(1)}, bf16[4,8192]{1,0:T(4,128)(2,1)}, u32[]{:S(2)}) copy-start(bf16[4,8192]{1,0:T(4,128)(2,1)} %param.15) | copy-start | bytes 196612
  33.1 9.8 %collective-permute-start.5 = (bf16[256,1024]{1,0:T(8,128)(2,1)S(1)}, bf16[256,1024]{1,0:T(8,128)(2,1)S(1)}, u32[]{:S(2)}, u32[]{:S(2)}) collective-permute-start(bf16[256,1024]{1,0:T(8,128)(2,1)S(1)} %constant_dynamic-slice_fusion), channel_id=1, source_target_pairs={{0,32},{32,0},{1,33},{33,1},{2,34},{34,2},{3,35},{35,3},{4,36},{36... | collective-permute-start | bytes 1572872 | tf_op jit(solution)/shard_map/ppermute | solution.py:252
  38.7 24.9 %copy-start.13 = (bf16[128,128]{1,0:T(8,128)(2,1)S(1)}, bf16[128,128]{1,0:T(8,128)(2,1)}, u32[]{:S(2)}) copy-start(bf16[128,128]{1,0:T(8,128)(2,1)} %param.13) | copy-start | bytes 98308
  43.0 21.7 %copy-start.8 = (bf16[256,1024]{1,0:T(8,128)(2,1)}, bf16[256,1024]{1,0:T(8,128)(2,1)S(1)}, u32[]{:S(2)}) copy-start(bf16[256,1024]{1,0:T(8,128)(2,1)S(1)} %collective-permute-done.5.other_ref) | copy-start | bytes 1572868
  43.0 20.5 %all-to-all-start = ((bf16[8,256,128]{2,1,0:T(8,128)(2,1)}), bf16[8,256,128]{2,1,0:T(8,128)(2,1)S(1)}, u32[]{:S(2)}, u32[]{:S(2)}) async-start(bf16[8,256,128]{2,1,0:T(8,128)(2,1)} %pad_maximum_fusion.1), calls=%async_computation | async-start | bytes 1048576 | tf_op jit(solution)/shard_map/all_to_all | solution.py:54
  64.7 25.7 %all-to-all-start.1 = ((bf16[8,432,128]{2,1,0:T(8,128)(2,1)}), bf16[8,432,128]{2,1,0:T(8,128)(2,1)S(1)}, u32[]{:S(2)}, u32[]{:S(2)}) async-start(bf16[8,432,128]{2,1,0:T(8,128)(2,1)} %pad_maximum_fusion), calls=%async_computation.1 | async-start | bytes 1769472 | tf_op jit(solution)/shard_map/all_to_all | solution.py:265
  100.1 13.8 %collective-permute-start.6 = (bf16[2,8,32,512]{3,2,1,0:T(8,128)(2,1)S(1)}, bf16[2,8,32,512]{3,2,1,0:T(8,128)(2,1)S(1)}, u32[]{:S(2)}, u32[]{:S(2)}) collective-permute-start(bf16[2,8,32,512]{3,2,1,0:T(8,128)(2,1)S(1)} %bitcast.94), channel_id=1, source_target_pairs={{0,1},{1,0},{2,3},{3,2},{4,5},{5,4},{6,7},{7,6},{8,9},{9,8},{10,11... | collective-permute-start | bytes 1572872 | tf_op jit(solution)/shard_map/ppermute | solution.py:29
  103.0 14.1 %collective-permute-start.8 = (bf16[2,8,32,512]{3,2,1,0:T(8,128)(2,1)S(1)}, bf16[2,8,32,512]{3,2,1,0:T(8,128)(2,1)S(1)}, u32[]{:S(2)}, u32[]{:S(2)}) collective-permute-start(bf16[2,8,32,512]{3,2,1,0:T(8,128)(2,1)S(1)} %bitcast.93), channel_id=1, source_target_pairs={{0,3},{1,2},{2,1},{3,0},{4,7},{5,6},{6,5},{7,4},{8,11},{9,10},{10,... | collective-permute-start | bytes 1572872 | tf_op jit(solution)/shard_map/ppermute | solution.py:29
  114.0 8.7 %collective-permute-start.7 = (bf16[8,32,512]{2,1,0:T(8,128)(2,1)S(1)}, bf16[8,32,512]{2,1,0:T(8,128)(2,1)S(1)}, u32[]{:S(2)}, u32[]{:S(2)}) collective-permute-start(bf16[8,32,512]{2,1,0:T(8,128)(2,1)S(1)} %fusion.3), channel_id=1, source_target_pairs={{0,3},{1,2},{2,1},{3,0},{4,7},{5,6},{6,5},{7,4},{8,11},{9,10},{10,... | collective-permute-start | bytes 786440 | tf_op jit(solution)/shard_map/ppermute | solution.py:29
  117.2 6.2 %collective-permute-start.9 = (bf16[8,32,512]{2,1,0:T(8,128)(2,1)S(1)}, bf16[8,32,512]{2,1,0:T(8,128)(2,1)S(1)}, u32[]{:S(2)}, u32[]{:S(2)}) collective-permute-start(bf16[8,32,512]{2,1,0:T(8,128)(2,1)S(1)} %fusion), channel_id=1, source_target_pairs={{0,1},{1,0},{2,3},{3,2},{4,5},{5,4},{6,7},{7,6},{8,9},{9,8},{10,11... | collective-permute-start | bytes 786440 | tf_op jit(solution)/shard_map/ppermute | solution.py:29
  124.3 18.3 %all-to-all-start.2 = ((bf16[8,64,512]{2,1,0:T(8,128)(2,1)}), bf16[8,64,512]{2,1,0:T(8,128)(2,1)S(1)}, u32[]{:S(2)}, u32[]{:S(2)}) async-start(bf16[8,64,512]{2,1,0:T(8,128)(2,1)} %pad_maximum_fusion.2), calls=%async_computation.2 | async-start | bytes 1048576 | tf_op jit(solution)/shard_map/all_to_all | solution.py:54
  142.7 34.0 %copy-start = (bf16[128,8192]{1,0:T(8,128)(2,1)S(1)}, bf16[128,8192]{1,0:T(8,128)(2,1)}, u32[]{:S(2)}) copy-start(bf16[128,8192]{1,0:T(8,128)(2,1)} %out_ref.5) | copy-start | bytes 6291460
  142.7 34.0 %copy-start.2 = (s32[3]{0:T(128)S(1)}, s32[3]{0:T(128)}, u32[]{:S(2)}) copy-start(s32[3]{0:T(128)} %pad_add_fusion.place_ref) | copy-start | bytes 40
  158.5 5.3 %collective-permute-start.12 = (bf16[256,512]{1,0:T(8,128)(2,1)S(1)}, bf16[256,512]{1,0:T(8,128)(2,1)S(1)}, u32[]{:S(2)}, u32[]{:S(2)}) collective-permute-start(bf16[256,512]{1,0:T(8,128)(2,1)S(1)} %bitcast.88), channel_id=1, source_target_pairs={{0,1},{1,0},{2,3},{3,2},{4,5},{5,4},{6,7},{7,6},{8,9},{9,8},{10,11... | collective-permute-start | bytes 786440 | tf_op jit(solution)/shard_map/ppermute | solution.py:29
  159.7 6.4 %collective-permute-start.10 = (bf16[256,512]{1,0:T(8,128)(2,1)S(1)}, bf16[256,512]{1,0:T(8,128)(2,1)S(1)}, u32[]{:S(2)}, u32[]{:S(2)}) collective-permute-start(bf16[256,512]{1,0:T(8,128)(2,1)S(1)} %bitcast.85), channel_id=1, source_target_pairs={{0,3},{1,2},{2,1},{3,0},{4,7},{5,6},{6,5},{7,4},{8,11},{9,10},{10,... | collective-permute-start | bytes 786440 | tf_op jit(solution)/shard_map/ppermute | solution.py:29
  163.9 12.9 %collective-permute-start.13 = (bf16[2,256,512]{2,1,0:T(8,128)(2,1)S(1)}, bf16[2,256,512]{2,1,0:T(8,128)(2,1)S(1)}, u32[]{:S(2)}, u32[]{:S(2)}) collective-permute-start(bf16[2,256,512]{2,1,0:T(8,128)(2,1)S(1)} %pad_maximum_fusion.4.other_ref), channel_id=1, source_target_pairs={{0,3},{1,2},{2,1},{3,0},{4,7},{5,6},{6,5},{7,4},{8,11},{9,10},{10,... | collective-permute-start | bytes 1572872 | tf_op jit(solution)/shard_map/ppermute | solution.py:29
  166.2 10.5 %collective-permute-start.11 = (bf16[2,256,512]{2,1,0:T(8,128)(2,1)S(1)}, bf16[2,256,512]{2,1,0:T(8,128)(2,1)S(1)}, u32[]{:S(2)}, u32[]{:S(2)}) collective-permute-start(bf16[2,256,512]{2,1,0:T(8,128)(2,1)S(1)} %pad_maximum_fusion.3.pair_ref), channel_id=1, source_target_pairs={{0,1},{1,0},{2,3},{3,2},{4,5},{5,4},{6,7},{7,6},{8,9},{9,8},{10,11... | collective-permute-start | bytes 1572872 | tf_op jit(solution)/shard_map/ppermute | solution.py:29
  178.9 18.2 %all-to-all-start.4 = ((bf16[8,144,128]{2,1,0:T(8,128)(2,1)}), bf16[8,144,128]{2,1,0:T(8,128)(2,1)S(1)}, u32[]{:S(2)}, u32[]{:S(2)}) async-start(bf16[8,144,128]{2,1,0:T(8,128)(2,1)} %copy.40), calls=%async_computation.4 | async-start | bytes 589824 | tf_op jit(solution)/shard_map/all_to_all | solution.py:287
  (10 other events, 84.4 us)

commit v4 on v1

v4 whole, which is shorter than its diff:
```python
import functools

import jax
import jax.numpy as jnp
from jax import lax
from jax.experimental import pallas as pl
from jax.experimental.pallas import tpu as pltpu
from jax.sharding import Mesh, PartitionSpec as P

B16 = jnp.bfloat16
F32 = jnp.float32
NY, NZ, NX = 8, 8, 4
GROUP = ("ylo", "core")
COLUMN = ("ylo", "core", "seq")
PLANE = ("z", "x")
ROWS = 1024
COLS = 1024
HALF = COLS // 2
PARAMS = pltpu.CompilerParams(vmem_limit_bytes=32 * 1024 * 1024)


def dot(a, b, dims):
    return lax.dot_general(a, b, (dims, ((), ())), preferred_element_type=F32)


def add(*terms):
    total = terms[0].astype(F32)
    for term in terms[1:]:
        total += term.astype(F32)
    return total.astype(B16)


def across(block, flip):
    return lax.ppermute(block, "x", [(i, i ^ flip) for i in range(NX)])


def reduce_x(first, second, tie=()):
    first_far = across(first[2], 1)
    second_far = across(second[2], 3)
    first_near = across(first[1], 1)
    second_near = across(second[3], 3)
    if tie:
        first_far, second_far, *tie = lax.optimization_barrier((first_far, second_far, *tie))
    first_last = across(add(first[3], first_far), 3)
    second_last = across(add(second[1], second_far), 1)
    return (
        add(first[0], first_near, first_last),
        add(second[0], second_near, second_last),
        *tie,
    )


def gather_x(first, second):
    first_three = across(first, 3)
    second_one = across(second, 1)
    first_one = across(first, 1)
    second_three = across(second, 3)
    first_two = across(first_three, 1)
    second_two = across(second_one, 3)
    return first, first_one, first_two, first_three, second, second_one, second_two, second_three


def reduce_z(parts):
    moved = lax.all_to_all(parts, "z", 0, 0)
    return jnp.sum(moved.astype(F32), axis=0)


def own_order(rows):
    rest = rows.shape[2:]
    parts = rows.reshape((NY, NZ, NX, 4) + rest)
    return jnp.transpose(parts, (2, 1, 0, 3) + tuple(range(4, parts.ndim))).reshape((ROWS,) + rest)


def block_order(rows):
    rest = rows.shape[1:]
    parts = rows.reshape((NX, NZ, NY, 4) + rest)
    return jnp.transpose(parts, (2, 1, 0, 3) + tuple(range(4, parts.ndim))).reshape((NY, 128) + rest)


def whole(*shape):
    return pl.BlockSpec(shape, lambda i, m: (0,) * len(shape))


def call(kernel, in_specs, outs, flops, scratch=()):
    return pl.pallas_call(
        kernel,
        grid_spec=pltpu.PrefetchScalarGridSpec(
            num_scalar_prefetch=1,
            grid=(1,),
            in_specs=in_specs,
            out_specs=[whole(*out.shape) for out in outs],
            scratch_shapes=scratch,
        ),
        out_shape=outs,
        compiler_params=PARAMS,
        cost_estimate=pl.CostEstimate(flops=flops, bytes_accessed=5 << 20, transcendentals=0),
    )


def teacher_kernel(place_ref, rows_ref, out_ref, *parts):
    x = place_ref[2]
    rows = rows_ref[...]
    for z in range(NZ):
        for k in range(NX):
            columns = pl.ds(pl.multiple_of(z * 1024 + (k ^ x) * 256, 256), 256)
            parts[k][z] = dot(rows, out_ref[:, columns], ((1,), (0,))).astype(B16)


def teacher_parts(place, rows, teacher_out):
    outs = [jax.ShapeDtypeStruct((NZ, 64, 256), B16)] * NX
    return call(teacher_kernel, [whole(64, 256), whole(256, 8192)], outs, 2 * 64 * 256 * 8192)(
        place, rows, teacher_out
    )


def gather_hidden(place_ref, got_ref, hidden_ref):
    seq = place_ref[1]
    for g in range(4):
        near = pl.ds(pl.multiple_of(g * 128 + seq * 64, 64), 64)
        far = pl.ds(pl.multiple_of(g * 128 + 64 - seq * 64, 64), 64)
        hidden_ref[near, 0:256] = got_ref[2 * g + seq, 0:64, :]
        hidden_ref[far, 0:256] = got_ref[2 * g + seq, 64:128, :]
        hidden_ref[far, 256:512] = got_ref[2 * g + 1 - seq, 0:64, :]
        hidden_ref[near, 256:512] = got_ref[2 * g + 1 - seq, 64:128, :]


def combine_kernel(jobs, place_ref, picked_ref, got_ref, heads_ref, out_ref, home_ref, other_ref, *refs):
    x = place_ref[2]
    parts, hidden_ref = refs[:-1], refs[-1]
    gather_hidden(place_ref, got_ref, hidden_ref)
    row = lax.broadcasted_iota(jnp.int32, (512, 256), 0)
    for k, halves in jobs:
        choose = (row == picked_ref[k ^ x]).astype(F32).astype(B16)
        selected = dot(choose, hidden_ref[...], ((0,), (0,))).astype(B16)
        heads = heads_ref[k ^ x]
        for half, to in halves:
            columns = slice(half * HALF, (half + 1) * HALF)
            total = dot(heads, out_ref[:, columns], ((1,), (0,)))
            total -= dot(selected[:, :256], home_ref[:, columns], ((1,), (0,)))
            total -= dot(selected[:, 256:], other_ref[:, columns], ((1,), (0,)))
            parts[to][...] = total.astype(B16)


SENT = ((2, ((0, 1), (1, 2))), (1, ((0, 0),)), (3, ((1, 3),)))
KEPT = ((3, ((0, 1),)), (1, ((1, 3),)), (0, ((0, 0), (1, 2))))


def combined_parts(jobs, place, picked, got, heads, student_out, projector, other):
    specs = [
        whole(NX, 1, 256),
        whole(NY, 128, 256),
        whole(NX, 256, 128),
        pl.BlockSpec((128, COLS), lambda i, m: (0, m[0])),
        pl.BlockSpec((256, COLS), lambda i, m: (0, m[0])),
        whole(256, COLS),
    ]
    outs = [jax.ShapeDtypeStruct((256, HALF), B16)] * 4
    return call(
        functools.partial(combine_kernel, jobs), specs, outs, 2 * 512 * 1024 * 900, [pltpu.VMEM((512, 512), B16)]
    )(place, picked, got, heads, student_out, projector, other)


def heads_kernel(place_ref, *refs):
    x = place_ref[2]
    first, second = refs[:4], refs[4:8]
    out_ref, part_ref, squares_ref, sums_ref = refs[8:]
    for k in range(NX):
        near, far = first[k][...], second[k][...]
        part = dot(near, out_ref[:, :HALF], ((1,), (1,))) + dot(far, out_ref[:, HALF:], ((1,), (1,)))
        part_ref[k ^ x] = part.astype(B16)
        near, far = near.astype(F32), far.astype(F32)
        line = jnp.sum(near * near + far * far, axis=0, keepdims=True)
        sums_ref[k ^ x] = line[:, :128] + line[:, 128:256] + line[:, 256:384] + line[:, 384:]
    total = sums_ref[0] + sums_ref[1] + sums_ref[2] + sums_ref[3]
    top = total.astype(B16).astype(F32)
    middle = (total - top).astype(B16).astype(F32)
    bottom = total - top - middle
    row = lax.broadcasted_iota(jnp.int32, (16, 128), 0)
    lines = jnp.where(row == 0, top, jnp.where(row == 1, middle, jnp.where(row == 2, bottom, 0.0)))
    squares_ref[...] = lines.astype(B16)


def weight_kernel(place_ref, *refs):
    x = place_ref[2]
    first, second = refs[:4], refs[4:8]
    heads_ref, weight_ref = refs[8:]
    left = jnp.zeros((128, HALF), F32)
    right = jnp.zeros((128, HALF), F32)
    for k in range(NX):
        heads = heads_ref[k ^ x]
        left += dot(heads, first[k][...], ((0,), (0,)))
        right += dot(heads, second[k][...], ((0,), (0,)))
    weight_ref[:, :HALF] = left.astype(B16)
    weight_ref[:, HALF:] = right.astype(B16)


def heads_parts(place, gathered, student_out):
    specs = [whole(256, HALF)] * 8 + [pl.BlockSpec((128, COLS), lambda i, m: (0, m[0]))]
    outs = [jax.ShapeDtypeStruct((NX, 256, 128), B16), jax.ShapeDtypeStruct((16, 128), B16)]
    return call(heads_kernel, specs, outs, 2 * 1024 * 1024 * 128, [pltpu.VMEM((NX, 1, 128), F32)])(
        place, *gathered, student_out
    )


def weight_grad(place, gathered, heads):
    specs = [whole(256, HALF)] * 8 + [whole(NX, 256, 128)]
    outs = [jax.ShapeDtypeStruct((128, COLS), B16)]
    return call(weight_kernel, specs, outs, 2 * 1024 * 1024 * 128)(place, *gathered, heads)[0]


def local(
    teacher_heads,
    teacher_out,
    teacher_resid,
    matches,
    projector,
    student_heads,
    student_out,
    student_resid,
):
    seq = lax.axis_index("seq")
    member = lax.axis_index(COLUMN)
    place = jnp.stack([member, seq, lax.axis_index("x")]).astype(jnp.int32)
    swap = [(0, 1), (1, 0)]

    away = lax.dynamic_slice(projector, (0, (member + 1 - 2 * seq) * COLS), (256, COLS))
    other = lax.ppermute(away, "seq", swap)

    own_matches = lax.dynamic_slice(matches, (seq * 128,), (128,)).astype(B16)
    shared = jnp.concatenate([student_heads, jnp.broadcast_to(own_matches[None], (16, 128))], axis=0)
    resid_parts = jnp.transpose(student_resid.reshape(4, NY, 8, 128), (1, 0, 2, 3)).reshape(NY, 32, 128)
    early = jnp.concatenate([jnp.broadcast_to(shared[None], (NY,) + shared.shape), resid_parts], axis=1)
    early = lax.all_to_all(early, COLUMN, 0, 0)

    there = lax.ppermute(teacher_heads, "seq", swap)
    first, second, other = reduce_x(
        teacher_parts(place, teacher_heads, teacher_out),
        teacher_parts(place, there, teacher_out),
        (other,),
    )
    summed = jnp.concatenate([first, second], axis=1)
    summed, early = lax.optimization_barrier((summed, early))
    heads = own_order(early[:, :128]).reshape(NX, 256, 128)
    base = (jnp.arange(NY, dtype=jnp.int32) // 2 * 128)[:, None]
    picked = own_order(early[:, 128].astype(jnp.int32) + base).reshape(NX, 1, 256)
    resid = early[:, 144:].reshape(32, 2, HALF)
    resid = jnp.concatenate([resid[:, 0], resid[:, 1]], axis=0)
    near = lax.dynamic_slice(teacher_resid, (seq * 64, 0), (64, 256))
    far = lax.dynamic_slice(teacher_resid, (64 - seq * 64, 0), (64, 256))
    hidden = (jnp.concatenate([near, far], axis=0).astype(F32) + reduce_z(summed)).astype(B16)

    got = lax.all_to_all(jnp.broadcast_to(hidden[None], (NY, 128, 256)), COLUMN, 0, 0)
    operands = (place, picked, got, heads, student_out, projector, other)
    sent = combined_parts(SENT, *operands)
    kept = combined_parts(KEPT, *operands)
    sent = [part.reshape(NZ, 32, HALF) for part in sent]
    kept = [part.reshape(NZ, 32, HALF) for part in kept]
    first, second = reduce_x(
        (kept[0], sent[0], sent[1], kept[1]), (kept[2], kept[3], sent[2], sent[3])
    )
    summed = reduce_z(jnp.concatenate([first, second], axis=1))
    difference = resid.astype(F32) + summed
    grad = (difference * 0.125).astype(B16)

    tall = lax.all_to_all(jnp.broadcast_to(grad[None], (NZ, 64, HALF)), "z", 0, 0)
    gathered = gather_x(tall[:, :32].reshape(256, HALF), tall[:, 32:].reshape(256, HALF))

    heads_part, squares = heads_parts(place, gathered, student_out)
    sent = jnp.concatenate(
        [block_order(heads_part.reshape(ROWS, 128)), jnp.broadcast_to(squares[None], (NY, 16, 128))], axis=1
    )
    back = lax.all_to_all(sent, COLUMN, 0, 0).astype(F32)
    grad_weight = weight_grad(place, gathered, heads)
    grad_heads = jnp.sum(back[:, :128], axis=0).astype(B16)
    total = jnp.sum(back[:, 128:])
    loss = (total * (64.0 / (ROWS * 8192))).reshape(1)
    return (loss, grad_heads, grad_weight)


def solution(mesh):
    cut = Mesh(mesh.devices.reshape(2, 2, 2, NZ, NX), COLUMN + PLANE)
    every = COLUMN + PLANE
    return jax.shard_map(
        local,
        mesh=cut,
        in_specs=(
            P(COLUMN, PLANE),
            P(PLANE, "seq"),
            P(GROUP, ("seq",) + PLANE),
            P(GROUP),
            P(("seq",) + PLANE, None),
            P(COLUMN, PLANE),
            P(PLANE, None),
            P(every, None),
        ),
        out_specs=(P(), P(COLUMN, PLANE), P(PLANE, COLUMN)),
        check_vma=False,
    )
```

time: 258 us -> 185 us (0.72)
  blocking collectives: 77.8 us -> 15.4 us
  starting transfers between devices: 30.2 us -> 59.2 us
  matrix products: 22.3 us -> 0 us
  between operations: 20.9 us -> 2.73 us
  Pallas kernels: 0 us -> 10.5 us
  waiting for transfers between devices: 76.4 us -> 69.5 us
  other arithmetic: 13.2 us -> 6.96 us
  local copies, waits for them, and re-layouts: 15.9 us -> 19.8 us
    all_to_all x3 -> x1, blocking collectives: 77.8 us -> 15.4 us  [local(): lax.all_to_all(jnp.broadcast_to(grad[None], (NZ, 64, HALF)), 'z', 0, 0)]
    all_gather x1 -> x0, waiting for transfers between devices: 28.3 us -> none  [local(): grad_all = lax.all_gather(tall, 'x', axis=0, tiled=True)]
    ppermute x1 -> x20, waiting for transfers between devices: 0.01 us -> 27.1 us  [the longest x18 27.1 us: across(): return lax.ppermute(block, 'x', [(i, i ^ flip) for i in range(NX)])]
    dot_general x6 -> x0, matrix products: 22.3 us -> none  [dot(): return lax.dot_general(a, b, (dims, ((), ())), preferred_element_type=F32)]
    ppermute x1 -> x20, starting transfers between devices: 0.78 us -> 22.8 us  [the longest x18 18.8 us: across(): return lax.ppermute(block, 'x', [(i, i ^ flip) for i in range(NX)])]
    unnamed x8 -> x35, local copies, waits for them, and re-layouts: 0.02 us -> 11.9 us
    pallas_call x0 -> x6, Pallas kernels: none -> 10.5 us  [the longest x2 4.03 us: combined_parts(): call(functools.partial(combine_kernel, jobs), specs, outs, 2 * 512 * 1024...]
    reduce_sum x6 -> x3, other arithmetic: 9.14 us -> 0.75 us  [the longest x1 0.61 us: local(): total = jnp.sum(back[:, 128:])]
  transfers between devices with their start and end apart: 7 -> 25, of which waited for: 6 -> 16; matrix products, arithmetic and copies ran while one was open for 5% -> 6% of each run, Pallas kernels for 0% -> 4%
where the time goes in v4:
time: 185 us; the launch traced here: 184 us
  waiting for transfers between devices  69.5 us (38%)
  starting transfers between devices  59.2 us (32%)
  local copies, waits for them, and re-layouts  19.8 us (11%)
  blocking collectives  15.4 us (8%)
  Pallas kernels  10.5 us (6%)
  other arithmetic  6.96 us (4%)
  between operations  2.73 us (1%)
    all_to_all x2, waiting for transfers between devices, reduce_z(): moved = lax.all_to_all(parts, 'z', 0, 0)  31.4 us
    ppermute x18, waiting for transfers between devices, across(): return lax.ppermute(block, 'x', [(i, i ^ flip) for i in range(NX)])  27.1 us
    ppermute x18, starting transfers between devices, across(): return lax.ppermute(block, 'x', [(i, i ^ flip) for i in range(NX)])  18.8 us
    all_to_all x1, blocking collectives, local(): lax.all_to_all(jnp.broadcast_to(grad[None], (NZ, 64, HALF)), 'z', 0, 0)  15.4 us
    unnamed x35, local copies, waits for them, and re-layouts  11.9 us
    all_to_all x2, starting transfers between devices, reduce_z(): moved = lax.all_to_all(parts, 'z', 0, 0)  11.7 us
    all_to_all x1, starting transfers between devices, local(): back = lax.all_to_all(sent, COLUMN, 0, 0).astype(F32)  11.5 us
    all_to_all x1, starting transfers between devices, local(): early = lax.all_to_all(early, COLUMN, 0, 0)  9.29 us
  transfers between devices with their start and end apart: 25, of which 16 were waited for; matrix products, arithmetic and copies ran while one was open for 6% of the time, Pallas kernels for 4%

profile of v4, /device:TPU:1, one launch (start us, length us, event | category | flops | bytes accessed | tf_op | source)
XLA Modules:
  0.0 184.0 jit_solution(193588512740280504)
XLA Ops:
  0.6 3.8 %collective-permute-start.2 = (bf16[64,256]{1,0:T(8,128)(2,1)}, bf16[64,256]{1,0:T(8,128)(2,1)S(1)}, u32[]{:S(2)}, u32[]{:S(2)}) collective-permute-start(bf16[64,256]{1,0:T(8,128)(2,1)} %rows_ref.1), channel_id=1, source_target_pairs={{0,32},{32,0},{1,33},{33,1},{2,34},{34,2},{3,35},{35,3},{4,36},{36... | collective-permute-start | bytes 98312 | tf_op jit(solution)/shard_map/ppermute | solution.py:235
  5.8 2.2 %copy-done.2 = bf16[256,8192]{1,0:T(8,128)(2,1)S(1)} copy-done((bf16[256,8192]{1,0:T(8,128)(2,1)S(1)}, bf16[256,8192]{1,0:T(8,128)(2,1)}, u32[]{:S(2)}) %copy-start.2) | copy-done | bytes 4194328
  12.3 2.2 %copy-done.3 = bf16[256,8192]{1,0:T(8,128)(2,1)S(1)} copy-done((bf16[256,8192]{1,0:T(8,128)(2,1)S(1)}, bf16[256,8192]{1,0:T(8,128)(2,1)}, u32[]{:S(2)}) %copy-start.3) | copy-done | bytes 4194328
  15.9 2.6 %collective-permute-start.3 = (bf16[8,64,256]{2,1,0:T(8,128)(2,1)S(1)}, bf16[8,64,256]{2,1,0:T(8,128)(2,1)S(1)}, u32[]{:S(2)}, u32[]{:S(2)}) collective-permute-start(bf16[8,64,256]{2,1,0:T(8,128)(2,1)S(1)} %get-tuple-element.30), channel_id=1, source_target_pairs={{0,3},{1,2},{2,1},{3,0},{4,7},{5,6},{6,5},{7,4},{8,11},{9,10},{10,... | collective-permute-start | bytes 786440 | tf_op jit(solution)/shard_map/ppermute | solution.py:34
  18.8 3.1 %collective-permute-done.1 = bf16[8,64,256]{2,1,0:T(8,128)(2,1)S(1)} collective-permute-done((bf16[8,64,256]{2,1,0:T(8,128)(2,1)S(1)}, bf16[8,64,256]{2,1,0:T(8,128)(2,1)S(1)}, u32[]{:S(2)}, u32[]{:S(2)}) %collective-permute-start.1) | collective-permute-done | bytes 262176 | tf_op jit(solution)/shard_map/ppermute | solution.py:34
  24.4 2.2 %collective-permute-start.5 = (bf16[8,64,256]{2,1,0:T(8,128)(2,1)S(1)}, bf16[8,64,256]{2,1,0:T(8,128)(2,1)}, u32[]{:S(2)}, u32[]{:S(2)}) collective-permute-start(bf16[8,64,256]{2,1,0:T(8,128)(2,1)S(1)} %add_convert_fusion.3), channel_id=1, source_target_pairs={{0,3},{1,2},{2,1},{3,0},{4,7},{5,6},{6,5},{7,4},{8,11},{9,10},{10,... | collective-permute-start | bytes 786440 | tf_op jit(solution)/shard_map/ppermute | solution.py:34
  27.4 9.3 %all-to-all-start = ((bf16[8,176,128]{2,1,0:T(8,128)(2,1)}), bf16[8,176,128]{2,1,0:T(8,128)(2,1)S(1)}, u32[]{:S(2)}, u32[]{:S(2)}) async-start(bf16[8,176,128]{2,1,0:T(8,128)(2,1)} %pad_maximum_fusion.2), calls=%async_computation | async-start | bytes 720896 | tf_op jit(solution)/shard_map/all_to_all | solution.py:233
  39.9 4.4 %all-to-all-done = bf16[8,176,128]{2,1,0:T(8,128)(2,1)S(1)} async-done(((bf16[8,176,128]{2,1,0:T(8,128)(2,1)}), bf16[8,176,128]{2,1,0:T(8,128)(2,1)S(1)}, u32[]{:S(2)}, u32[]{:S(2)}) %all-to-all-start) | async-done | bytes 360480 | tf_op jit(solution)/shard_map/all_to_all | solution.py:233
  45.0 8.2 %all-to-all-start.1 = ((bf16[8,128,256]{2,1,0:T(8,128)(2,1)}), bf16[8,128,256]{2,1,0:T(8,128)(2,1)S(1)}, u32[]{:S(2)}, u32[]{:S(2)}) async-start(bf16[8,128,256]{2,1,0:T(8,128)(2,1)} %pad_maximum_fusion), calls=%async_computation.1 | async-start | bytes 1048576 | tf_op jit(solution)/shard_map/all_to_all | solution.py:64
  54.0 17.2 %all-to-all-done.1 = bf16[8,128,256]{2,1,0:T(8,128)(2,1)S(1)} async-done(((bf16[8,128,256]{2,1,0:T(8,128)(2,1)}), bf16[8,128,256]{2,1,0:T(8,128)(2,1)S(1)}, u32[]{:S(2)}, u32[]{:S(2)}) %all-to-all-start.1) | async-done | bytes 524320 | tf_op jit(solution)/shard_map/all_to_all | solution.py:64
  72.1 3.9 %all-to-all-start.2 = ((bf16[8,128,256]{2,1,0:T(8,128)(2,1)}), bf16[8,128,256]{2,1,0:T(8,128)(2,1)S(1)}, u32[]{:S(2)}, u32[]{:S(2)}) async-start(bf16[8,128,256]{2,1,0:T(8,128)(2,1)} %broadcast_in_dim.12), calls=%async_computation.2 | async-start | bytes 1048576 | tf_op jit(solution)/shard_map/all_to_all | solution.py:252
  80.2 5.2 %all-to-all-done.2.got_ref = bf16[8,128,256]{2,1,0:T(8,128)(2,1)S(1)} async-done(((bf16[8,128,256]{2,1,0:T(8,128)(2,1)}), bf16[8,128,256]{2,1,0:T(8,128)(2,1)S(1)}, u32[]{:S(2)}, u32[]{:S(2)}) %all-to-all-start.2) | async-done | bytes 524320 | tf_op jit(solution)/shard_map/all_to_all | solution.py:252
  85.4 2.2 %copy-done = bf16[256,8192]{1,0:T(8,128)(2,1)S(1)} copy-done((bf16[256,8192]{1,0:T(8,128)(2,1)S(1)}, bf16[256,8192]{1,0:T(8,128)(2,1)}, u32[]{:S(2)}) %copy-start) | copy-done | bytes 4194328
  93.7 3.5 %collective-permute-done.9 = bf16[8,32,512]{2,1,0:T(8,128)(2,1)S(1)} collective-permute-done((bf16[8,32,512]{2,1,0:T(8,128)(2,1)S(1)}, bf16[8,32,512]{2,1,0:T(8,128)(2,1)S(1)}, u32[]{:S(2)}, u32[]{:S(2)}) %collective-permute-start.9) | collective-permute-done | bytes 262176 | tf_op jit(solution)/shard_map/ppermute | solution.py:34
  97.8 2.2 %collective-permute-start.11 = (bf16[8,32,512]{2,1,0:T(8,128)(2,1)S(1)}, bf16[8,32,512]{2,1,0:T(8,128)(2,1)S(1)}, u32[]{:S(2)}, u32[]{:S(2)}) collective-permute-start(bf16[8,32,512]{2,1,0:T(8,128)(2,1)S(1)} %bitcast.62), channel_id=1, source_target_pairs={{0,3},{1,2},{2,1},{3,0},{4,7},{5,6},{6,5},{7,4},{8,11},{9,10},{10,... | collective-permute-start | bytes 786440 | tf_op jit(solution)/shard_map/ppermute | solution.py:34
  100.2 2.6 %collective-permute-done.8 = bf16[8,32,512]{2,1,0:T(8,128)(2,1)S(1)} collective-permute-done((bf16[8,32,512]{2,1,0:T(8,128)(2,1)S(1)}, bf16[8,32,512]{2,1,0:T(8,128)(2,1)S(1)}, u32[]{:S(2)}, u32[]{:S(2)}) %collective-permute-start.8) | collective-permute-done | bytes 262176 | tf_op jit(solution)/shard_map/ppermute | solution.py:34
  104.5 5.5 %collective-permute-done.11 = bf16[8,32,512]{2,1,0:T(8,128)(2,1)S(1)} collective-permute-done((bf16[8,32,512]{2,1,0:T(8,128)(2,1)S(1)}, bf16[8,32,512]{2,1,0:T(8,128)(2,1)S(1)}, u32[]{:S(2)}, u32[]{:S(2)}) %collective-permute-start.11) | collective-permute-done | bytes 262176 | tf_op jit(solution)/shard_map/ppermute | solution.py:34
  110.9 3.5 %all-to-all-start.3 = ((bf16[8,64,512]{2,1,0:T(8,128)(2,1)}), bf16[8,64,512]{2,1,0:T(8,128)(2,1)S(1)}, u32[]{:S(2)}, u32[]{:S(2)}) async-start(bf16[8,64,512]{2,1,0:T(8,128)(2,1)} %pad_maximum_fusion.1), calls=%async_computation.3 | async-start | bytes 1048576 | tf_op jit(solution)/shard_map/all_to_all | solution.py:64
  114.6 14.2 %all-to-all-done.3 = bf16[8,64,512]{2,1,0:T(8,128)(2,1)S(1)} async-done(((bf16[8,64,512]{2,1,0:T(8,128)(2,1)}), bf16[8,64,512]{2,1,0:T(8,128)(2,1)S(1)}, u32[]{:S(2)}, u32[]{:S(2)}) %all-to-all-start.3) | async-done | bytes 524320 | tf_op jit(solution)/shard_map/all_to_all | solution.py:64
  128.9 15.4 %all_to_all.30 = bf16[8,64,512]{2,1,0:T(8,128)(2,1)S(1)} all-to-all(bf16[8,64,512]{2,1,0:T(8,128)(2,1)S(1)} %broadcast_in_dim.13), channel_id=1, replica_groups=mesh['ylo'=2,'core'=2,'seq'=2,'z'=8,'x'=4] {'z'}, dimensions={0} | all-to-all | bytes 1048576 | tf_op jit(solution)/shard_map/all_to_all | solution.py:265
  146.4 2.1 %collective-permute-start.19 = (bf16[256,512]{1,0:T(8,128)(2,1)S(1)}, bf16[256,512]{1,0:T(8,128)(2,1)S(1)}, u32[]{:S(2)}, u32[]{:S(2)}) collective-permute-start(bf16[256,512]{1,0:T(8,128)(2,1)S(1)} %bitcast.50), channel_id=1, source_target_pairs={{0,3},{1,2},{2,1},{3,0},{4,7},{5,6},{6,5},{7,4},{8,11},{9,10},{10,... | collective-permute-start | bytes 786440 | tf_op jit(solution)/shard_map/ppermute | solution.py:34
  148.5 2.3 %collective-permute-done.15.refs_3_ = bf16[256,512]{1,0:T(8,128)(2,1)S(1)} collective-permute-done((bf16[256,512]{1,0:T(8,128)(2,1)S(1)}, bf16[256,512]{1,0:T(8,128)(2,1)S(1)}, u32[]{:S(2)}, u32[]{:S(2)}) %collective-permute-start.15) | collective-permute-done | bytes 262176 | tf_op jit(solution)/shard_map/ppermute | solution.py:34
  153.6 5.3 %collective-permute-done.16.refs_2_ = bf16[256,512]{1,0:T(8,128)(2,1)S(1)} collective-permute-done((bf16[256,512]{1,0:T(8,128)(2,1)S(1)}, bf16[256,512]{1,0:T(8,128)(2,1)S(1)}, u32[]{:S(2)}, u32[]{:S(2)}) %collective-permute-start.16) | collective-permute-done | bytes 262176 | tf_op jit(solution)/shard_map/ppermute | solution.py:34
  162.5 11.5 %all-to-all-start.5 = ((bf16[8,144,128]{2,1,0:T(8,128)(2,1)}), bf16[8,144,128]{2,1,0:T(8,128)(2,1)S(1)}, u32[]{:S(2)}, u32[]{:S(2)}) async-start(bf16[8,144,128]{2,1,0:T(8,128)(2,1)} %copy.46), calls=%async_computation.5 | async-start | bytes 589824 | tf_op jit(solution)/shard_map/all_to_all | solution.py:272
  (114 shorter events, 46.7 us)
Async XLA Ops:
  0.6 11.7 %collective-permute-start.2 = (bf16[64,256]{1,0:T(8,128)(2,1)}, bf16[64,256]{1,0:T(8,128)(2,1)S(1)}, u32[]{:S(2)}, u32[]{:S(2)}) collective-permute-start(bf16[64,256]{1,0:T(8,128)(2,1)} %rows_ref.1), channel_id=1, source_target_pairs={{0,32},{32,0},{1,33},{33,1},{2,34},{34,2},{3,35},{35,3},{4,36},{36... | collective-permute-start | bytes 98312 | tf_op jit(solution)/shard_map/ppermute | solution.py:235
  5.5 16.9 %collective-permute-start.4 = (bf16[256,1024]{1,0:T(8,128)(2,1)S(1)}, bf16[256,1024]{1,0:T(8,128)(2,1)S(1)}, u32[]{:S(2)}, u32[]{:S(2)}) collective-permute-start(bf16[256,1024]{1,0:T(8,128)(2,1)S(1)} %constant_dynamic-slice_fusion.2), channel_id=1, source_target_pairs={{0,32},{32,0},{1,33},{33,1},{2,34},{34,2},{3,35},{35,3},{4,36},{36... | collective-permute-start | bytes 1572872 | tf_op jit(solution)/shard_map/ppermute | solution.py:227
  10.8 27.0 %collective-permute-start = (bf16[8,64,256]{2,1,0:T(8,128)(2,1)}, bf16[8,64,256]{2,1,0:T(8,128)(2,1)}, u32[]{:S(2)}, u32[]{:S(2)}) collective-permute-start(bf16[8,64,256]{2,1,0:T(8,128)(2,1)} %get-tuple-element.27), channel_id=1, source_target_pairs={{0,1},{1,0},{2,3},{3,2},{4,5},{5,4},{6,7},{7,6},{8,9},{9,8},{10,11... | collective-permute-start | bytes 786440 | tf_op jit(solution)/shard_map/ppermute | solution.py:34
  12.0 9.9 %collective-permute-start.1 = (bf16[8,64,256]{2,1,0:T(8,128)(2,1)S(1)}, bf16[8,64,256]{2,1,0:T(8,128)(2,1)S(1)}, u32[]{:S(2)}, u32[]{:S(2)}) collective-permute-start(bf16[8,64,256]{2,1,0:T(8,128)(2,1)S(1)} %get-tuple-element.29), channel_id=1, source_target_pairs={{0,1},{1,0},{2,3},{3,2},{4,5},{5,4},{6,7},{7,6},{8,9},{9,8},{10,11... | collective-permute-start | bytes 786440 | tf_op jit(solution)/shard_map/ppermute | solution.py:34
  15.9 6.5 %collective-permute-start.3 = (bf16[8,64,256]{2,1,0:T(8,128)(2,1)S(1)}, bf16[8,64,256]{2,1,0:T(8,128)(2,1)S(1)}, u32[]{:S(2)}, u32[]{:S(2)}) collective-permute-start(bf16[8,64,256]{2,1,0:T(8,128)(2,1)S(1)} %get-tuple-element.30), channel_id=1, source_target_pairs={{0,3},{1,2},{2,1},{3,0},{4,7},{5,6},{6,5},{7,4},{8,11},{9,10},{10,... | collective-permute-start | bytes 786440 | tf_op jit(solution)/shard_map/ppermute | solution.py:34
  18.5 18.1 %collective-permute-start.6 = (bf16[8,64,256]{2,1,0:T(8,128)(2,1)S(1)}, bf16[8,64,256]{2,1,0:T(8,128)(2,1)}, u32[]{:S(2)}, u32[]{:S(2)}) collective-permute-start(bf16[8,64,256]{2,1,0:T(8,128)(2,1)S(1)} %get-tuple-element.33), channel_id=1, source_target_pairs={{0,3},{1,2},{2,1},{3,0},{4,7},{5,6},{6,5},{7,4},{8,11},{9,10},{10,... | collective-permute-start | bytes 786440 | tf_op jit(solution)/shard_map/ppermute | solution.py:34
  22.5 14.2 %collective-permute-start.7 = (bf16[8,64,256]{2,1,0:T(8,128)(2,1)S(1)}, bf16[8,64,256]{2,1,0:T(8,128)(2,1)S(1)}, u32[]{:S(2)}, u32[]{:S(2)}) collective-permute-start(bf16[8,64,256]{2,1,0:T(8,128)(2,1)S(1)} %add_convert_fusion.1), channel_id=1, source_target_pairs={{0,1},{1,0},{2,3},{3,2},{4,5},{5,4},{6,7},{7,6},{8,9},{9,8},{10,11... | collective-permute-start | bytes 786440 | tf_op jit(solution)/shard_map/ppermute | solution.py:34
  24.4 13.4 %collective-permute-start.5 = (bf16[8,64,256]{2,1,0:T(8,128)(2,1)S(1)}, bf16[8,64,256]{2,1,0:T(8,128)(2,1)}, u32[]{:S(2)}, u32[]{:S(2)}) collective-permute-start(bf16[8,64,256]{2,1,0:T(8,128)(2,1)S(1)} %add_convert_fusion.3), channel_id=1, source_target_pairs={{0,3},{1,2},{2,1},{3,0},{4,7},{5,6},{6,5},{7,4},{8,11},{9,10},{10,... | collective-permute-start | bytes 786440 | tf_op jit(solution)/shard_map/ppermute | solution.py:34
  27.4 16.9 %all-to-all-start = ((bf16[8,176,128]{2,1,0:T(8,128)(2,1)}), bf16[8,176,128]{2,1,0:T(8,128)(2,1)S(1)}, u32[]{:S(2)}, u32[]{:S(2)}) async-start(bf16[8,176,128]{2,1,0:T(8,128)(2,1)} %pad_maximum_fusion.2), calls=%async_computation | async-start | bytes 720896 | tf_op jit(solution)/shard_map/all_to_all | solution.py:233
  45.0 26.2 %all-to-all-start.1 = ((bf16[8,128,256]{2,1,0:T(8,128)(2,1)}), bf16[8,128,256]{2,1,0:T(8,128)(2,1)S(1)}, u32[]{:S(2)}, u32[]{:S(2)}) async-start(bf16[8,128,256]{2,1,0:T(8,128)(2,1)} %pad_maximum_fusion), calls=%async_computation.1 | async-start | bytes 1048576 | tf_op jit(solution)/shard_map/all_to_all | solution.py:64
  72.1 13.3 %all-to-all-start.2 = ((bf16[8,128,256]{2,1,0:T(8,128)(2,1)}), bf16[8,128,256]{2,1,0:T(8,128)(2,1)S(1)}, u32[]{:S(2)}, u32[]{:S(2)}) async-start(bf16[8,128,256]{2,1,0:T(8,128)(2,1)} %broadcast_in_dim.12), calls=%async_computation.2 | async-start | bytes 1048576 | tf_op jit(solution)/shard_map/all_to_all | solution.py:252
  89.6 7.6 %collective-permute-start.9 = (bf16[8,32,512]{2,1,0:T(8,128)(2,1)S(1)}, bf16[8,32,512]{2,1,0:T(8,128)(2,1)S(1)}, u32[]{:S(2)}, u32[]{:S(2)}) collective-permute-start(bf16[8,32,512]{2,1,0:T(8,128)(2,1)S(1)} %bitcast.65), channel_id=1, source_target_pairs={{0,1},{1,0},{2,3},{3,2},{4,5},{5,4},{6,7},{7,6},{8,9},{9,8},{10,11... | collective-permute-start | bytes 786440 | tf_op jit(solution)/shard_map/ppermute | solution.py:34
  90.9 12.0 %collective-permute-start.8 = (bf16[8,32,512]{2,1,0:T(8,128)(2,1)S(1)}, bf16[8,32,512]{2,1,0:T(8,128)(2,1)S(1)}, u32[]{:S(2)}, u32[]{:S(2)}) collective-permute-start(bf16[8,32,512]{2,1,0:T(8,128)(2,1)S(1)} %bitcast.63), channel_id=1, source_target_pairs={{0,1},{1,0},{2,3},{3,2},{4,5},{5,4},{6,7},{7,6},{8,9},{9,8},{10,11... | collective-permute-start | bytes 786440 | tf_op jit(solution)/shard_map/ppermute | solution.py:34
  91.2 8.9 %collective-permute-start.12 = (bf16[8,32,512]{2,1,0:T(8,128)(2,1)S(1)}, bf16[8,32,512]{2,1,0:T(8,128)(2,1)S(1)}, u32[]{:S(2)}, u32[]{:S(2)}) collective-permute-start(bf16[8,32,512]{2,1,0:T(8,128)(2,1)S(1)} %bitcast.64), channel_id=1, source_target_pairs={{0,3},{1,2},{2,1},{3,0},{4,7},{5,6},{6,5},{7,4},{8,11},{9,10},{10,... | collective-permute-start | bytes 786440 | tf_op jit(solution)/shard_map/ppermute | solution.py:34
  97.3 7.1 %collective-permute-start.10 = (bf16[8,32,512]{2,1,0:T(8,128)(2,1)S(1)}, bf16[8,32,512]{2,1,0:T(8,128)(2,1)S(1)}, u32[]{:S(2)}, u32[]{:S(2)}) collective-permute-start(bf16[8,32,512]{2,1,0:T(8,128)(2,1)S(1)} %fusion.3), channel_id=1, source_target_pairs={{0,3},{1,2},{2,1},{3,0},{4,7},{5,6},{6,5},{7,4},{8,11},{9,10},{10,... | collective-permute-start | bytes 786440 | tf_op jit(solution)/shard_map/ppermute | solution.py:34
  97.8 12.1 %collective-permute-start.11 = (bf16[8,32,512]{2,1,0:T(8,128)(2,1)S(1)}, bf16[8,32,512]{2,1,0:T(8,128)(2,1)S(1)}, u32[]{:S(2)}, u32[]{:S(2)}) collective-permute-start(bf16[8,32,512]{2,1,0:T(8,128)(2,1)S(1)} %bitcast.62), channel_id=1, source_target_pairs={{0,3},{1,2},{2,1},{3,0},{4,7},{5,6},{6,5},{7,4},{8,11},{9,10},{10,... | collective-permute-start | bytes 786440 | tf_op jit(solution)/shard_map/ppermute | solution.py:34
  100.1 9.8 %collective-permute-start.13 = (bf16[8,32,512]{2,1,0:T(8,128)(2,1)S(1)}, bf16[8,32,512]{2,1,0:T(8,128)(2,1)S(1)}, u32[]{:S(2)}, u32[]{:S(2)}) collective-permute-start(bf16[8,32,512]{2,1,0:T(8,128)(2,1)S(1)} %fusion), channel_id=1, source_target_pairs={{0,1},{1,0},{2,3},{3,2},{4,5},{5,4},{6,7},{7,6},{8,9},{9,8},{10,11... | collective-permute-start | bytes 786440 | tf_op jit(solution)/shard_map/ppermute | solution.py:34
  110.9 17.9 %all-to-all-start.3 = ((bf16[8,64,512]{2,1,0:T(8,128)(2,1)}), bf16[8,64,512]{2,1,0:T(8,128)(2,1)S(1)}, u32[]{:S(2)}, u32[]{:S(2)}) async-start(bf16[8,64,512]{2,1,0:T(8,128)(2,1)} %pad_maximum_fusion.1), calls=%async_computation.3 | async-start | bytes 1048576 | tf_op jit(solution)/shard_map/all_to_all | solution.py:64
  144.3 6.5 %collective-permute-start.15 = (bf16[256,512]{1,0:T(8,128)(2,1)S(1)}, bf16[256,512]{1,0:T(8,128)(2,1)S(1)}, u32[]{:S(2)}, u32[]{:S(2)}) collective-permute-start(bf16[256,512]{1,0:T(8,128)(2,1)S(1)} %bitcast.53), channel_id=1, source_target_pairs={{0,3},{1,2},{2,1},{3,0},{4,7},{5,6},{6,5},{7,4},{8,11},{9,10},{10,... | collective-permute-start | bytes 786440 | tf_op jit(solution)/shard_map/ppermute | solution.py:34
  145.9 7.1 %collective-permute-start.14 = (bf16[256,512]{1,0:T(8,128)(2,1)S(1)}, bf16[256,512]{1,0:T(8,128)(2,1)S(1)}, u32[]{:S(2)}, u32[]{:S(2)}) collective-permute-start(bf16[256,512]{1,0:T(8,128)(2,1)S(1)} %bitcast.54), channel_id=1, source_target_pairs={{0,1},{1,0},{2,3},{3,2},{4,5},{5,4},{6,7},{7,6},{8,9},{9,8},{10,11... | collective-permute-start | bytes 786440 | tf_op jit(solution)/shard_map/ppermute | solution.py:34
  146.4 7.2 %collective-permute-start.19 = (bf16[256,512]{1,0:T(8,128)(2,1)S(1)}, bf16[256,512]{1,0:T(8,128)(2,1)S(1)}, u32[]{:S(2)}, u32[]{:S(2)}) collective-permute-start(bf16[256,512]{1,0:T(8,128)(2,1)S(1)} %bitcast.50), channel_id=1, source_target_pairs={{0,3},{1,2},{2,1},{3,0},{4,7},{5,6},{6,5},{7,4},{8,11},{9,10},{10,... | collective-permute-start | bytes 786440 | tf_op jit(solution)/shard_map/ppermute | solution.py:34
  150.8 8.1 %collective-permute-start.16 = (bf16[256,512]{1,0:T(8,128)(2,1)S(1)}, bf16[256,512]{1,0:T(8,128)(2,1)S(1)}, u32[]{:S(2)}, u32[]{:S(2)}) collective-permute-start(bf16[256,512]{1,0:T(8,128)(2,1)S(1)} %collective-permute-done.15.refs_3_), channel_id=1, source_target_pairs={{0,1},{1,0},{2,3},{3,2},{4,5},{5,4},{6,7},{7,6},{8,9},{9,8},{10,11... | collective-permute-start | bytes 786440 | tf_op jit(solution)/shard_map/ppermute | solution.py:34
  150.8 9.5 %collective-permute-start.18 = (bf16[256,512]{1,0:T(8,128)(2,1)S(1)}, bf16[256,512]{1,0:T(8,128)(2,1)S(1)}, u32[]{:S(2)}, u32[]{:S(2)}) collective-permute-start(bf16[256,512]{1,0:T(8,128)(2,1)S(1)} %collective-permute-done.17.refs_5_), channel_id=1, source_target_pairs={{0,3},{1,2},{2,1},{3,0},{4,7},{5,6},{6,5},{7,4},{8,11},{9,10},{10,... | collective-permute-start | bytes 786440 | tf_op jit(solution)/shard_map/ppermute | solution.py:34
  162.5 18.5 %all-to-all-start.5 = ((bf16[8,144,128]{2,1,0:T(8,128)(2,1)}), bf16[8,144,128]{2,1,0:T(8,128)(2,1)S(1)}, u32[]{:S(2)}, u32[]{:S(2)}) async-start(bf16[8,144,128]{2,1,0:T(8,128)(2,1)} %copy.46), calls=%async_computation.5 | async-start | bytes 589824 | tf_op jit(solution)/shard_map/all_to_all | solution.py:272
  (19 other events, 138.3 us)

commit v5 on v4

v5 whole, which is shorter than its diff:
```python
import jax
import jax.numpy as jnp
from jax import lax
from jax.experimental import pallas as pl
from jax.experimental.pallas import tpu as pltpu
from jax.sharding import Mesh, PartitionSpec as P

B16 = jnp.bfloat16
F32 = jnp.float32
NY, NZ, NX = 8, 8, 4
GROUP = ("ylo", "core")
COLUMN = ("ylo", "core", "seq")
PLANE = ("z", "x")
ROWS = 1024
COLS = 1024
PARAMS = pltpu.CompilerParams(vmem_limit_bytes=32 * 1024 * 1024)


def dot(a, b, dims):
    return lax.dot_general(a, b, (dims, ((), ())), preferred_element_type=F32)


def add(*terms):
    total = terms[0].astype(F32)
    for term in terms[1:]:
        total += term.astype(F32)
    return total.astype(B16)


def across(block, flip):
    return lax.ppermute(block, "x", [(i, i ^ flip) for i in range(NX)])


def reduce_x(first, second, tie=()):
    first_far = across(first[2], 1)
    second_far = across(second[2], 3)
    first_near = across(first[1], 1)
    second_near = across(second[3], 3)
    if tie:
        first_far, second_far, *tie = lax.optimization_barrier((first_far, second_far, *tie))
    first_last = across(add(first[3], first_far), 3)
    second_last = across(add(second[1], second_far), 1)
    return (
        add(first[0], first_near, first_last),
        add(second[0], second_near, second_last),
        *tie,
    )


def gather_x(first, second):
    first_three = across(first, 3)
    second_one = across(second, 1)
    first_one = across(first, 1)
    second_three = across(second, 3)
    first_two = across(first_three, 1)
    second_two = across(second_one, 3)
    return first, first_one, first_two, first_three, second, second_one, second_two, second_three


def whole(*shape):
    return pl.BlockSpec(shape, lambda i, m: (0,) * len(shape))


def call(kernel, in_specs, outs, flops, scratch=()):
    return pl.pallas_call(
        kernel,
        grid_spec=pltpu.PrefetchScalarGridSpec(
            num_scalar_prefetch=1,
            grid=(1,),
            in_specs=in_specs,
            out_specs=[whole(*out.shape) for out in outs],
            scratch_shapes=scratch,
        ),
        out_shape=outs,
        compiler_params=PARAMS,
        cost_estimate=pl.CostEstimate(flops=flops, bytes_accessed=5 << 20, transcendentals=0),
    )


def teacher_kernel(place_ref, rows_ref, out_ref, *refs):
    x = place_ref[2]
    parts, held, sems = refs[:NX], refs[NX], refs[NX + 1]
    copies = [
        pltpu.make_async_copy(out_ref.at[:, pl.ds(z * 1024, 1024)], held.at[z], sems.at[z]) for z in range(NZ)
    ]
    for copy in copies:
        copy.start()
    rows = rows_ref[...]
    for z in range(NZ):
        copies[z].wait()
        for k in range(NX):
            columns = pl.ds(pl.multiple_of((k ^ x) * 256, 256), 256)
            parts[k][z] = dot(rows, held[z, :, columns], ((1,), (0,))).astype(B16)


def teacher_parts(place, rows, teacher_out):
    outs = [jax.ShapeDtypeStruct((NZ, 64, 256), B16)] * NX
    scratch = [pltpu.VMEM((NZ, 256, 1024), B16), pltpu.SemaphoreType.DMA((NZ,))]
    specs = [whole(64, 256), pl.BlockSpec(memory_space=pl.ANY)]
    return call(teacher_kernel, specs, outs, 2 * 64 * 256 * 8192, scratch)(place, rows, teacher_out)


def student_kernel(place_ref, heads_ref, resid_ref, out_ref, parts_ref):
    plane = place_ref[3]
    row = lax.broadcasted_iota(jnp.int32, (256, 32), 0)
    line = lax.broadcasted_iota(jnp.int32, (256, 32), 1)
    spot = (line // 4) * 128 + plane * 4 + line % 4
    for w in range(NX):
        put = (row + w * 256 == spot).astype(F32).astype(B16)
        heads = jnp.concatenate([heads_ref[2 * w], heads_ref[2 * w + 1]], axis=0)
        total = dot(heads, out_ref[...], ((1,), (0,))) + dot(put, resid_ref[...], ((1,), (0,)))
        total = total.astype(B16)
        for z in range(NZ):
            parts_ref[w, z] = total[:, z * 128 : (z + 1) * 128]


def student_parts(place, heads, resid, out_cols):
    outs = [jax.ShapeDtypeStruct((NX, NZ, 256, 128), B16)]
    specs = [whole(NY, 128, 128), whole(32, COLS), whole(128, COLS)]
    return call(student_kernel, specs, outs, 2 * 1024 * 1024 * 160)(place, heads, resid, out_cols)[0]


def gather_hidden(place_ref, got_ref, hidden_ref):
    seq = place_ref[1]
    for g in range(4):
        near = pl.ds(pl.multiple_of(seq * 64, 64), 64)
        far = pl.ds(pl.multiple_of(64 - seq * 64, 64), 64)
        hidden_ref[g, near, 0:256] = got_ref[2 * g + seq, 0:64, :]
        hidden_ref[g, far, 0:256] = got_ref[2 * g + seq, 64:128, :]
        hidden_ref[g, far, 256:512] = got_ref[2 * g + 1 - seq, 0:64, :]
        hidden_ref[g, near, 256:512] = got_ref[2 * g + 1 - seq, 64:128, :]


def project_kernel(place_ref, got_ref, home_ref, other_ref, *refs):
    x = place_ref[2]
    parts, hidden_ref = refs[:-1], refs[-1]
    gather_hidden(place_ref, got_ref, hidden_ref)
    for k in (2, 1, 3, 0):
        rows = hidden_ref[k ^ x]
        total = dot(rows[:, :256], home_ref[...], ((1,), (0,))) + dot(rows[:, 256:], other_ref[...], ((1,), (0,)))
        total = total.astype(B16)
        for z in range(NZ):
            parts[k][z] = total[:64, z * 128 : (z + 1) * 128]
            parts[NX + k][z] = total[64:, z * 128 : (z + 1) * 128]


def projected_parts(place, got, home, other):
    specs = [whole(NY, 128, 256), whole(256, COLS), whole(256, COLS)]
    outs = [jax.ShapeDtypeStruct((NZ, 64, 128), B16)] * 8
    parts = call(project_kernel, specs, outs, 2 * 512 * 512 * 1024, [pltpu.VMEM((4, 128, 512), B16)])(
        place, got, home, other
    )
    return parts[:NX], parts[NX:]


def gradient_kernel(place_ref, moved_ref, sum_ref, matches_ref, grad_ref):
    projected = moved_ref[0].astype(F32)
    for z in range(1, NZ):
        projected += moved_ref[z].astype(F32)
    high = projected.astype(B16)
    low = (projected - high.astype(F32)).astype(B16)
    row = lax.broadcasted_iota(jnp.int32, (128, 256), 0)
    choose = (row == matches_ref[...]).astype(F32).astype(B16)
    selected = dot(choose, high, ((0,), (0,))) + dot(choose, low, ((0,), (0,)))
    grad = ((sum_ref[...].astype(F32) - selected) * 0.125).astype(B16)
    for z in range(NZ):
        grad_ref[z] = grad


def gradient_piece(place, moved, student_sum, picked):
    specs = [whole(NZ, 128, 128), whole(256, 128), whole(1, 256)]
    outs = [jax.ShapeDtypeStruct((NZ, 256, 128), B16)]
    return call(gradient_kernel, specs, outs, 2 * 256 * 256 * 128)(place, moved, student_sum, picked)[0]


def wide_rows(ref):
    return jnp.concatenate([ref[z] for z in range(NZ)], axis=1)


def heads_kernel(place_ref, *refs):
    x = place_ref[2]
    halves, out_ref, part_ref, sums_ref = (refs[:4], refs[4:8]), *refs[8:]
    for k in range(NX):
        line = jnp.zeros((1, 128), F32)
        for h in range(2):
            rows = wide_rows(halves[h][k])
            part_ref[2 * (k ^ x) + h, 0:128, :] = dot(rows, out_ref[...], ((1,), (1,))).astype(B16)
            for z in range(NZ):
                block = halves[h][k][z].astype(F32)
                line += jnp.sum(block * block, axis=0, keepdims=True)
        sums_ref[k ^ x] = line
    total = sums_ref[0] + sums_ref[1] + sums_ref[2] + sums_ref[3]
    top = total.astype(B16).astype(F32)
    middle = (total - top).astype(B16).astype(F32)
    bottom = total - top - middle
    row = lax.broadcasted_iota(jnp.int32, (16, 128), 0)
    lines = jnp.where(row == 0, top, jnp.where(row == 1, middle, jnp.where(row == 2, bottom, 0.0)))
    squares = lines.astype(B16)
    for gs in range(NY):
        part_ref[gs, 128:144, :] = squares


def weight_kernel(place_ref, *refs):
    x = place_ref[2]
    halves, heads_ref, weight_ref = (refs[:4], refs[4:8]), *refs[8:]
    total = jnp.zeros((128, COLS), F32)
    for k in range(NX):
        for h in range(2):
            total += dot(heads_ref[2 * (k ^ x) + h], wide_rows(halves[h][k]), ((0,), (0,)))
    weight_ref[...] = total.astype(B16)


def heads_parts(place, gathered, out_cols):
    specs = [whole(NZ, 128, 128)] * 8 + [whole(128, COLS)]
    outs = [jax.ShapeDtypeStruct((NY, 144, 128), B16)]
    return call(heads_kernel, specs, outs, 2 * 1024 * 1024 * 128, [pltpu.VMEM((NX, 1, 128), F32)])(
        place, *gathered, out_cols
    )[0]


def weight_grad(place, gathered, heads):
    specs = [whole(NZ, 128, 128)] * 8 + [whole(NY, 128, 128)]
    outs = [jax.ShapeDtypeStruct((128, COLS), B16)]
    return call(weight_kernel, specs, outs, 2 * 1024 * 1024 * 128)(place, *gathered, heads)[0]


def local(
    teacher_heads,
    teacher_out,
    teacher_resid,
    matches,
    projector,
    student_heads,
    student_out,
    student_resid,
):
    seq = lax.axis_index("seq")
    x = lax.axis_index("x")
    member = lax.axis_index(COLUMN)
    place = jnp.stack([member, seq, x, lax.axis_index(PLANE)]).astype(jnp.int32)
    swap = [(0, 1), (1, 0)]

    there = lax.ppermute(teacher_heads, "seq", swap)
    first = teacher_parts(place, teacher_heads, teacher_out)
    second = teacher_parts(place, there, teacher_out)

    *first, later = lax.optimization_barrier((*first, member))
    away = lax.dynamic_slice(projector, (0, (later + 1 - 2 * seq) * COLS), (256, COLS))
    other = lax.ppermute(away, "seq", swap)
    home = lax.dynamic_slice(projector, (0, later * COLS), (256, COLS))
    out_cols = lax.dynamic_slice(student_out, (0, later * COLS), (128, COLS))

    own_matches = lax.dynamic_slice(matches, (seq * 128,), (128,)).astype(B16)
    shared = jnp.concatenate([student_heads, jnp.broadcast_to(own_matches[None], (16, 128))], axis=0)
    resid_parts = jnp.transpose(student_resid.reshape(4, NY, 8, 128), (1, 0, 2, 3)).reshape(NY, 32, 128)
    early = jnp.concatenate([jnp.broadcast_to(shared[None], (NY,) + shared.shape), resid_parts], axis=1)
    early = lax.all_to_all(early, COLUMN, 0, 0)

    first, second, other, early = reduce_x(first, second, (other, early))

    heads = early[:, :128]
    picked = lax.dynamic_slice(early[:, 128], (2 * x, 0), (2, 128)).astype(jnp.int32).reshape(1, 256)
    partial = student_parts(place, heads, early[:, 144:].reshape(32, COLS), out_cols)
    first, partial, home = lax.optimization_barrier((first, partial, home))
    student_sum = lax.psum_scatter(partial, "x", scatter_dimension=0)
    student_sum = lax.psum_scatter(student_sum, "z", scatter_dimension=0)

    near = lax.dynamic_slice(teacher_resid, (seq * 64, 0), (64, 256))
    far = lax.dynamic_slice(teacher_resid, (64 - seq * 64, 0), (64, 256))
    moved = lax.all_to_all(jnp.concatenate([first, second], axis=1), "z", 0, 0)
    summed = jnp.sum(moved.astype(F32), axis=0)
    hidden = (jnp.concatenate([near, far], axis=0).astype(F32) + summed).astype(B16)

    got = lax.all_to_all(jnp.broadcast_to(hidden[None], (NY, 128, 256)), COLUMN, 0, 0)
    first, second = reduce_x(*projected_parts(place, got, home, other))
    moved = lax.all_to_all(jnp.concatenate([first, second], axis=1), "z", 0, 0)
    grad = gradient_piece(place, moved, student_sum, picked)

    tall = lax.all_to_all(grad, "z", 0, 0)
    gathered = gather_x(tall[:, :128], tall[:, 128:])

    sent = heads_parts(place, gathered, out_cols)
    back = lax.all_to_all(sent, COLUMN, 0, 0).astype(F32)
    grad_weight = weight_grad(place, gathered, heads)
    grad_heads = jnp.sum(back[:, :128], axis=0).astype(B16)
    total = jnp.sum(back[:, 128:])
    loss = (total * (64.0 / (ROWS * 8192))).reshape(1)
    return (loss, grad_heads, grad_weight)


def solution(mesh):
    cut = Mesh(mesh.devices.reshape(2, 2, 2, NZ, NX), COLUMN + PLANE)
    every = COLUMN + PLANE
    return jax.shard_map(
        local,
        mesh=cut,
        in_specs=(
            P(COLUMN, PLANE),
            P(PLANE, "seq"),
            P(GROUP, ("seq",) + PLANE),
            P(GROUP),
            P(("seq",) + PLANE, None),
            P(COLUMN, PLANE),
            P(PLANE, None),
            P(every, None),
        ),
        out_specs=(P(), P(COLUMN, PLANE), P(PLANE, COLUMN)),
        check_vma=False,
    )
```

time: 185 us -> 223 us (1.21)
  blocking collectives: 15.4 us -> 33.3 us
  between operations: 2.73 us -> 16.1 us
  other arithmetic: 6.96 us -> 14.7 us
  starting transfers between devices: 59.2 us -> 52.6 us
  Pallas kernels: 10.5 us -> 15.9 us
  waiting for transfers between devices: 69.5 us -> 66.6 us
  local copies, waits for them, and re-layouts: 19.8 us -> 22.5 us
    all_to_all x1 -> x2, blocking collectives: 15.4 us -> 33.3 us  [the longest x1 17.5 us: local(): lax.all_to_all(jnp.broadcast_to(hidden[None], (NY, 128, 256)), COLUMN, 0, 0)]
    all_to_all x3 -> x2, waiting for transfers between devices: 36.6 us -> 23.4 us  [local(): moved = lax.all_to_all(jnp.concatenate([first, second], axis=1), 'z', 0, 0)]
    reduce_scatter x0 -> x2, waiting for transfers between devices: none -> 12 us  [the longest x1 12 us: local(): student_sum = lax.psum_scatter(student_sum, 'z', scatter_dimension=0)]
    unnamed x35 -> x46, local copies, waits for them, and re-layouts: 11.9 us -> 17.7 us
    convert_element_type x8, other arithmetic: 2.81 us -> 7.8 us  [add(): return total.astype(B16)]
    all_to_all x1, waiting for transfers between devices: 4.39 us -> 0.01 us  [local(): early = lax.all_to_all(early, COLUMN, 0, 0)]
    pallas_call x4 -> x5, Pallas kernels: 7.5 us -> 11.5 us  [the longest x2 6.15 us: teacher_parts(): call(teacher_kernel, specs, outs, 2 * 64 * 256 * 8192, scratch)]
    all_to_all x3 -> x2, starting transfers between devices: 15.6 us -> 11.6 us  [local(): moved = lax.all_to_all(jnp.concatenate([first, second], axis=1), 'z', 0, 0)]
  transfers between devices with their start and end apart: 25 -> 26, of which waited for: 16 -> 16; matrix products, arithmetic and copies ran while one was open for 6% -> 7% of each run, Pallas kernels for 4% -> 6%
where the time goes in v5:
time: 223 us; the launch traced here: 222 us
  waiting for transfers between devices  66.6 us (30%)
  starting transfers between devices  52.6 us (24%)
  blocking collectives  33.3 us (15%)
  local copies, waits for them, and re-layouts  22.5 us (10%)
  between operations  16.1 us (7%)
  Pallas kernels  15.9 us (7%)
  other arithmetic  14.7 us (7%)
    ppermute x18, waiting for transfers between devices, across(): return lax.ppermute(block, 'x', [(i, i ^ flip) for i in range(NX)])  30.9 us
    all_to_all x2, waiting for transfers between devices, local(): moved = lax.all_to_all(jnp.concatenate([first, second], axis=1), 'z', 0, 0)  23.4 us
    ppermute x18, starting transfers between devices, across(): return lax.ppermute(block, 'x', [(i, i ^ flip) for i in range(NX)])  19.3 us
    unnamed x46, local copies, waits for them, and re-layouts  17.7 us
    all_to_all x1, blocking collectives, local(): lax.all_to_all(jnp.broadcast_to(hidden[None], (NY, 128, 256)), COLUMN, 0, 0)  17.5 us
    all_to_all x1, blocking collectives, local(): tall = lax.all_to_all(grad, 'z', 0, 0)  15.8 us
    reduce_scatter x1, waiting for transfers between devices, local(): student_sum = lax.psum_scatter(student_sum, 'z', scatter_dimension=0)  12 us
    all_to_all x2, starting transfers between devices, local(): moved = lax.all_to_all(jnp.concatenate([first, second], axis=1), 'z', 0, 0)  11.6 us
  transfers between devices with their start and end apart: 26, of which 16 were waited for; matrix products, arithmetic and copies ran while one was open for 7% of the time, Pallas kernels for 6%

profile of v5, /device:TPU:1, one launch (start us, length us, event | category | flops | bytes accessed | tf_op | source)
XLA Modules:
  0.0 221.6 jit_solution(17551538250036168043)
XLA Ops:
  7.2 3.8 %collective-permute-start.2 = (bf16[64,256]{1,0:T(8,128)(2,1)}, bf16[64,256]{1,0:T(8,128)(2,1)S(1)}, u32[]{:S(2)}, u32[]{:S(2)}) collective-permute-start(bf16[64,256]{1,0:T(8,128)(2,1)} %rows_ref.1), channel_id=1, source_target_pairs={{0,32},{32,0},{1,33},{33,1},{2,34},{34,2},{3,35},{35,3},{4,36},{36... | collective-permute-start | bytes 98312 | tf_op jit(solution)/shard_map/ppermute | solution.py:243
  11.1 2.2 copy-done.1
  14.1 3.5 %shard_map.103 = (bf16[8,64,256]{2,1,0:T(8,128)(2,1)S(1)}, bf16[8,64,256]{2,1,0:T(8,128)(2,1)}, bf16[8,64,256]{2,1,0:T(8,128)(2,1)}, bf16[8,64,256]{2,1,0:T(8,128)(2,1)S(1)}) custom-call(s32[4]{0:T(128)S(1)} %pad_add_fusion.place_ref, bf16[64,256]{1,0:T(8,128)(2,1)S(1)} %copy-done.17, bf16[256,8192]{1,0:T(8,128)(2,1)S(1)} %copy-done.1), custom_call_target="tpu_custom_call" | custom-call | flops 268435456 | bytes 5242880 | tf_op jit(solution)/shard_map/pallas_call | solution.py:100
  21.3 7.0 %all-to-all-start = ((bf16[8,176,128]{2,1,0:T(8,128)(2,1)}), bf16[8,176,128]{2,1,0:T(8,128)(2,1)}, u32[]{:S(2)}, u32[]{:S(2)}) async-start(bf16[8,176,128]{2,1,0:T(8,128)(2,1)} %pad_maximum_fusion.1), calls=%async_computation | async-start | bytes 720896 | tf_op jit(solution)/shard_map/all_to_all | solution.py:257
  28.3 2.2 copy-done.2
  30.4 2.7 %shard_map.104 = (bf16[8,64,256]{2,1,0:T(8,128)(2,1)S(1)}, bf16[8,64,256]{2,1,0:T(8,128)(2,1)S(1)}, bf16[8,64,256]{2,1,0:T(8,128)(2,1)S(1)}, bf16[8,64,256]{2,1,0:T(8,128)(2,1)S(1)}) custom-call(s32[4]{0:T(128)S(1)} %pad_add_fusion.place_ref, bf16[64,256]{1,0:T(8,128)(2,1)S(1)} %collective-permute-done.2.rows_ref, bf16[256,8192]{1,0:T(8,128)(2,1)S(1)} %copy-done.2), custom_call_target="tpu_custom_call" | custom-call | flops 268435456 | bytes 5242880 | tf_op jit(solution)/shard_map/pallas_call | solution.py:100
  36.6 6.7 %collective-permute-done.3 = bf16[8,64,256]{2,1,0:T(8,128)(2,1)} collective-permute-done((bf16[8,64,256]{2,1,0:T(8,128)(2,1)S(1)}, bf16[8,64,256]{2,1,0:T(8,128)(2,1)}, u32[]{:S(2)}, u32[]{:S(2)}) %collective-permute-start.3) | collective-permute-done | bytes 262176 | tf_op jit(solution)/shard_map/ppermute | solution.py:31
  58.0 4.3 %collective-permute-done.6 = bf16[8,64,256]{2,1,0:T(8,128)(2,1)S(1)} collective-permute-done((bf16[8,64,256]{2,1,0:T(8,128)(2,1)}, bf16[8,64,256]{2,1,0:T(8,128)(2,1)S(1)}, u32[]{:S(2)}, u32[]{:S(2)}) %collective-permute-start.6) | collective-permute-done | bytes 262176 | tf_op jit(solution)/shard_map/ppermute | solution.py:31
  66.4 8.2 %all-to-all-start.1 = ((bf16[8,128,256]{2,1,0:T(8,128)(2,1)}), bf16[8,128,256]{2,1,0:T(8,128)(2,1)}, u32[]{:S(2)}, u32[]{:S(2)}) async-start(bf16[8,128,256]{2,1,0:T(8,128)(2,1)} %pad_maximum_fusion), calls=%async_computation.1 | async-start | bytes 1048576 | tf_op jit(solution)/shard_map/all_to_all | solution.py:270
  74.7 14.1 %all-to-all-done.1 = bf16[8,128,256]{2,1,0:T(8,128)(2,1)} async-done(((bf16[8,128,256]{2,1,0:T(8,128)(2,1)}), bf16[8,128,256]{2,1,0:T(8,128)(2,1)}, u32[]{:S(2)}, u32[]{:S(2)}) %all-to-all-start.1) | async-done | bytes 524320 | tf_op jit(solution)/shard_map/all_to_all | solution.py:270
  90.0 17.5 %all_to_all.30.got_ref = bf16[8,128,256]{2,1,0:T(8,128)(2,1)S(1)} all-to-all(bf16[8,128,256]{2,1,0:T(8,128)(2,1)S(1)} %broadcast_in_dim.8), channel_id=1, replica_groups=mesh['ylo'=2,'core'=2,'seq'=2,'z'=8,'x'=4] {'ylo','core','seq'}, dimensions={0} | all-to-all | bytes 1048576 | tf_op jit(solution)/shard_map/all_to_all | solution.py:274
  107.5 2.9 %shard_map.106 = (bf16[8,64,128]{2,1,0:T(8,128)(2,1)S(1)}, bf16[8,64,128]{2,1,0:T(8,128)(2,1)}, bf16[8,64,128]{2,1,0:T(8,128)(2,1)S(1)}, bf16[8,64,128]{2,1,0:T(...) custom-call(s32[4]{0:T(128)S(1)} %pad_add_fusion.place_ref, ...), custom_call_target="tpu_custom_call" | custom-call | flops 536870912 | bytes 5242880 | tf_op jit(solution)/shard_map/pallas_call | solution.py:150
  116.4 3.9 %collective-permute-done.12 = bf16[8,64,128]{2,1,0:T(8,128)(2,1)S(1)} collective-permute-done((bf16[8,64,128]{2,1,0:T(8,128)(2,1)S(1)}, bf16[8,64,128]{2,1,0:T(8,128)(2,1)S(1)}, u32[]{:S(2)}, u32[]{:S(2)}) %collective-permute-start.12) | collective-permute-done | bytes 131104 | tf_op jit(solution)/shard_map/ppermute | solution.py:31
  120.5 2.7 %collective-permute-done.10 = bf16[8,64,128]{2,1,0:T(8,128)(2,1)} collective-permute-done((bf16[8,64,128]{2,1,0:T(8,128)(2,1)S(1)}, bf16[8,64,128]{2,1,0:T(8,128)(2,1)}, u32[]{:S(2)}, u32[]{:S(2)}) %collective-permute-start.10) | collective-permute-done | bytes 131104 | tf_op jit(solution)/shard_map/ppermute | solution.py:31
  126.0 3.4 %all-to-all-start.3 = ((bf16[8,128,128]{2,1,0:T(8,128)(2,1)}), bf16[8,128,128]{2,1,0:T(8,128)(2,1)S(1)}, u32[]{:S(2)}, u32[]{:S(2)}) async-start(bf16[8,128,128]{2,1,0:T(8,128)(2,1)} %pad_maximum_fusion.2), calls=%async_computation.3 | async-start | bytes 524288 | tf_op jit(solution)/shard_map/all_to_all | solution.py:276
  130.1 9.3 %all-to-all-done.3.moved_ref = bf16[8,128,128]{2,1,0:T(8,128)(2,1)S(1)} async-done(((bf16[8,128,128]{2,1,0:T(8,128)(2,1)}), bf16[8,128,128]{2,1,0:T(8,128)(2,1)S(1)}, u32[]{:S(2)}, u32[]{:S(2)}) %all-to-all-start.3) | async-done | bytes 262176 | tf_op jit(solution)/shard_map/all_to_all | solution.py:276
  139.4 12.0 %reduce-scatter.5.cloned.1.call-done = bf16[1,256,128]{2,1,0:T(8,128)(2,1)} async-done(((bf16[8,256,128]{2,1,0:T(8,128)(2,1)}), bf16[1,256,128]{2,1,0:T(8,128)(2,1)}) %reduce-scatter.5.cloned.1.call-update) | async-done | bytes 65552 | tf_op jit(solution)/shard_map/reduce_scatter | solution.py:266
  153.0 15.8 %all_to_all.31 = bf16[8,256,128]{2,1,0:T(8,128)(2,1)S(1)} all-to-all(bf16[8,256,128]{2,1,0:T(8,128)(2,1)S(1)} %shard_map.107), channel_id=1, replica_groups=mesh['ylo'=2,'core'=2,'seq'=2,'z'=8,'x'=4] {'z'}, dimensions={0} | all-to-all | bytes 1048576 | tf_op jit(solution)/shard_map/all_to_all | solution.py:279
  168.9 3.1 %collective-permute-start.17 = (bf16[8,128,128]{2,1,0:T(8,128)(2,1)S(1)}, bf16[8,128,128]{2,1,0:T(8,128)(2,1)S(1)}, u32[]{:S(2)}, u32[]{:S(2)}) collective-permute-start(bf16[8,128,128]{2,1,0:T(8,128)(2,1)S(1)} %get-tuple-element.61.refs_4_), channel_id=1, source_target_pairs={{0,1},{1,0},{2,3},{3,2},{4,5},{5,4},{6,7},{7,6},{8,9},{9,8},{10,11... | collective-permute-start | bytes 786440 | tf_op jit(solution)/shard_map/ppermute | solution.py:31
  175.7 2.7 %collective-permute-start.18 = (bf16[8,128,128]{2,1,0:T(8,128)(2,1)S(1)}, bf16[8,128,128]{2,1,0:T(8,128)(2,1)S(1)}, u32[]{:S(2)}, u32[]{:S(2)}) collective-permute-start(bf16[8,128,128]{2,1,0:T(8,128)(2,1)S(1)} %collective-permute-done.17.refs_5_), channel_id=1, source_target_pairs={{0,3},{1,2},{2,1},{3,0},{4,7},{5,6},{6,5},{7,4},{8,11},{9,10},{10,... | collective-permute-start | bytes 786440 | tf_op jit(solution)/shard_map/ppermute | solution.py:31
  178.4 2.8 %collective-permute-done.19.refs_7_ = bf16[8,128,128]{2,1,0:T(8,128)(2,1)S(1)} collective-permute-done((bf16[8,128,128]{2,1,0:T(8,128)(2,1)S(1)}, bf16[8,128,128]{2,1,0:T(8,128)(2,1)S(1)}, u32[]{:S(2)}, u32[]{:S(2)}) %collective-permute-start.19) | collective-permute-done | bytes 262176 | tf_op jit(solution)/shard_map/ppermute | solution.py:31
  181.4 5.1 %collective-permute-done.18.refs_6_ = bf16[8,128,128]{2,1,0:T(8,128)(2,1)S(1)} collective-permute-done((bf16[8,128,128]{2,1,0:T(8,128)(2,1)S(1)}, bf16[8,128,128]{2,1,0:T(8,128)(2,1)S(1)}, u32[]{:S(2)}, u32[]{:S(2)}) %collective-permute-start.18) | collective-permute-done | bytes 262176 | tf_op jit(solution)/shard_map/ppermute | solution.py:31
  187.1 2.4 %shard_map.108 = bf16[8,144,128]{2,1,0:T(8,128)(2,1)} custom-call(s32[4]{0:T(128)S(1)} %pad_add_fusion.place_ref, bf16[8,128,128]{2,1,0:T(8,128)(2,1)S(1)} %get-tuple-element.62.refs_0_, bf16[8,128,128]{2,1,0:T(8,128)(2,1)S(1)} %collective-permute-done.14.refs_1_, bf16[8,128,128]{2,1,0:T(8,128)(2,1)S(1)} %collective-permute-done.16.refs_2_, ...), custom_call_target="tpu_custom_call" | custom-call | flops 268435456 | bytes 5242880 | tf_op jit(solution)/shard_map/pallas_call | solution.py:216
  192.9 10.8 %all-to-all-start.5 = ((bf16[8,144,128]{2,1,0:T(8,128)(2,1)}), bf16[8,144,128]{2,1,0:T(8,128)(2,1)}, u32[]{:S(2)}, u32[]{:S(2)}) async-start(bf16[8,144,128]{2,1,0:T(8,128)(2,1)} %shard_map.108), calls=%async_computation.7 | async-start | bytes 589824 | tf_op jit(solution)/shard_map/all_to_all | solution.py:283
  (117 shorter events, 56.8 us)
Async XLA Ops:
  7.2 21.0 %collective-permute-start.2 = (bf16[64,256]{1,0:T(8,128)(2,1)}, bf16[64,256]{1,0:T(8,128)(2,1)S(1)}, u32[]{:S(2)}, u32[]{:S(2)}) collective-permute-start(bf16[64,256]{1,0:T(8,128)(2,1)} %rows_ref.1), channel_id=1, source_target_pairs={{0,32},{32,0},{1,33},{33,1},{2,34},{34,2},{3,35},{35,3},{4,36},{36... | collective-permute-start | bytes 98312 | tf_op jit(solution)/shard_map/ppermute | solution.py:243
  20.3 23.1 %collective-permute-start.4 = (bf16[256,1024]{1,0:T(8,128)(2,1)}, bf16[256,1024]{1,0:T(8,128)(2,1)}, u32[]{:S(2)}, u32[]{:S(2)}) collective-permute-start(bf16[256,1024]{1,0:T(8,128)(2,1)} %get-tuple-element.60), channel_id=1, source_target_pairs={{0,32},{32,0},{1,33},{33,1},{2,34},{34,2},{3,35},{35,3},{4,36},{36... | collective-permute-start | bytes 1572872 | tf_op jit(solution)/shard_map/ppermute | solution.py:249
  21.3 22.1 %all-to-all-start = ((bf16[8,176,128]{2,1,0:T(8,128)(2,1)}), bf16[8,176,128]{2,1,0:T(8,128)(2,1)}, u32[]{:S(2)}, u32[]{:S(2)}) async-start(bf16[8,176,128]{2,1,0:T(8,128)(2,1)} %pad_maximum_fusion.1), calls=%async_computation | async-start | bytes 720896 | tf_op jit(solution)/shard_map/all_to_all | solution.py:257
  28.2 92.2 %reduce-scatter.3.cloned.1.call-start = ((), (), s32[]{:S(2)}) async-start(), calls=%async_computation.8 | async-start | bytes 2621440 | tf_op jit(solution)/shard_map/reduce_scatter | solution.py:265
  28.2 8.4 %collective-permute-start.1 = (bf16[8,64,256]{2,1,0:T(8,128)(2,1)}, bf16[8,64,256]{2,1,0:T(8,128)(2,1)}, u32[]{:S(2)}, u32[]{:S(2)}) collective-permute-start(bf16[8,64,256]{2,1,0:T(8,128)(2,1)} %get-tuple-element.38), channel_id=1, source_target_pairs={{0,1},{1,0},{2,3},{3,2},{4,5},{5,4},{6,7},{7,6},{8,9},{9,8},{10,11... | collective-permute-start | bytes 786440 | tf_op jit(solution)/shard_map/ppermute | solution.py:31
  34.6 8.8 %collective-permute-start.3 = (bf16[8,64,256]{2,1,0:T(8,128)(2,1)S(1)}, bf16[8,64,256]{2,1,0:T(8,128)(2,1)}, u32[]{:S(2)}, u32[]{:S(2)}) collective-permute-start(bf16[8,64,256]{2,1,0:T(8,128)(2,1)S(1)} %get-tuple-element.39), channel_id=1, source_target_pairs={{0,3},{1,2},{2,1},{3,0},{4,7},{5,6},{6,5},{7,4},{8,11},{9,10},{10,... | collective-permute-start | bytes 786440 | tf_op jit(solution)/shard_map/ppermute | solution.py:31
  36.3 15.5 %collective-permute-start = (bf16[8,64,256]{2,1,0:T(8,128)(2,1)}, bf16[8,64,256]{2,1,0:T(8,128)(2,1)}, u32[]{:S(2)}, u32[]{:S(2)}) collective-permute-start(bf16[8,64,256]{2,1,0:T(8,128)(2,1)} %get-tuple-element.36), channel_id=1, source_target_pairs={{0,1},{1,0},{2,3},{3,2},{4,5},{5,4},{6,7},{7,6},{8,9},{9,8},{10,11... | collective-permute-start | bytes 786440 | tf_op jit(solution)/shard_map/ppermute | solution.py:31
  45.1 8.1 %collective-permute-start.5 = (bf16[8,64,256]{2,1,0:T(8,128)(2,1)}, bf16[8,64,256]{2,1,0:T(8,128)(2,1)}, u32[]{:S(2)}, u32[]{:S(2)}) collective-permute-start(bf16[8,64,256]{2,1,0:T(8,128)(2,1)} %add_convert_fusion.3), channel_id=1, source_target_pairs={{0,3},{1,2},{2,1},{3,0},{4,7},{5,6},{6,5},{7,4},{8,11},{9,10},{10,... | collective-permute-start | bytes 786440 | tf_op jit(solution)/shard_map/ppermute | solution.py:31
  55.1 7.2 %collective-permute-start.6 = (bf16[8,64,256]{2,1,0:T(8,128)(2,1)}, bf16[8,64,256]{2,1,0:T(8,128)(2,1)S(1)}, u32[]{:S(2)}, u32[]{:S(2)}) collective-permute-start(bf16[8,64,256]{2,1,0:T(8,128)(2,1)} %copy-done.18), channel_id=1, source_target_pairs={{0,3},{1,2},{2,1},{3,0},{4,7},{5,6},{6,5},{7,4},{8,11},{9,10},{10,... | collective-permute-start | bytes 786440 | tf_op jit(solution)/shard_map/ppermute | solution.py:31
  57.9 5.6 %collective-permute-start.7 = (bf16[8,64,256]{2,1,0:T(8,128)(2,1)S(1)}, bf16[8,64,256]{2,1,0:T(8,128)(2,1)S(1)}, u32[]{:S(2)}, u32[]{:S(2)}) collective-permute-start(bf16[8,64,256]{2,1,0:T(8,128)(2,1)S(1)} %add_convert_fusion.1), channel_id=1, source_target_pairs={{0,1},{1,0},{2,3},{3,2},{4,5},{5,4},{6,7},{7,6},{8,9},{9,8},{10,11... | collective-permute-start | bytes 786440 | tf_op jit(solution)/shard_map/ppermute | solution.py:31
  66.4 22.4 %all-to-all-start.1 = ((bf16[8,128,256]{2,1,0:T(8,128)(2,1)}), bf16[8,128,256]{2,1,0:T(8,128)(2,1)}, u32[]{:S(2)}, u32[]{:S(2)}) async-start(bf16[8,128,256]{2,1,0:T(8,128)(2,1)} %pad_maximum_fusion), calls=%async_computation.1 | async-start | bytes 1048576 | tf_op jit(solution)/shard_map/all_to_all | solution.py:270
  74.6 76.8 %reduce-scatter.5.cloned.1.call-start = ((), (), s32[]{:S(2)}) async-start(), calls=%async_computation.9 | async-start | bytes 589824 | tf_op jit(solution)/shard_map/reduce_scatter | solution.py:266
  110.3 10.2 %collective-permute-start.8 = (bf16[8,64,128]{2,1,0:T(8,128)(2,1)}, bf16[8,64,128]{2,1,0:T(8,128)(2,1)}, u32[]{:S(2)}, u32[]{:S(2)}) collective-permute-start(bf16[8,64,128]{2,1,0:T(8,128)(2,1)} %get-tuple-element.51), channel_id=1, source_target_pairs={{0,1},{1,0},{2,3},{3,2},{4,5},{5,4},{6,7},{7,6},{8,9},{9,8},{10,11... | collective-permute-start | bytes 393224 | tf_op jit(solution)/shard_map/ppermute | solution.py:31
  111.8 12.5 %collective-permute-start.11 = (bf16[8,64,128]{2,1,0:T(8,128)(2,1)S(1)}, bf16[8,64,128]{2,1,0:T(8,128)(2,1)}, u32[]{:S(2)}, u32[]{:S(2)}) collective-permute-start(bf16[8,64,128]{2,1,0:T(8,128)(2,1)S(1)} %get-tuple-element.55), channel_id=1, source_target_pairs={{0,3},{1,2},{2,1},{3,0},{4,7},{5,6},{6,5},{7,4},{8,11},{9,10},{10,... | collective-permute-start | bytes 393224 | tf_op jit(solution)/shard_map/ppermute | solution.py:31
  112.6 7.6 %collective-permute-start.12 = (bf16[8,64,128]{2,1,0:T(8,128)(2,1)S(1)}, bf16[8,64,128]{2,1,0:T(8,128)(2,1)S(1)}, u32[]{:S(2)}, u32[]{:S(2)}) collective-permute-start(bf16[8,64,128]{2,1,0:T(8,128)(2,1)S(1)} %get-tuple-element.57), channel_id=1, source_target_pairs={{0,3},{1,2},{2,1},{3,0},{4,7},{5,6},{6,5},{7,4},{8,11},{9,10},{10,... | collective-permute-start | bytes 393224 | tf_op jit(solution)/shard_map/ppermute | solution.py:31
  115.5 7.7 %collective-permute-start.10 = (bf16[8,64,128]{2,1,0:T(8,128)(2,1)S(1)}, bf16[8,64,128]{2,1,0:T(8,128)(2,1)}, u32[]{:S(2)}, u32[]{:S(2)}) collective-permute-start(bf16[8,64,128]{2,1,0:T(8,128)(2,1)S(1)} %add_convert_fusion.7), channel_id=1, source_target_pairs={{0,3},{1,2},{2,1},{3,0},{4,7},{5,6},{6,5},{7,4},{8,11},{9,10},{10,... | collective-permute-start | bytes 393224 | tf_op jit(solution)/shard_map/ppermute | solution.py:31
  126.0 13.4 %all-to-all-start.3 = ((bf16[8,128,128]{2,1,0:T(8,128)(2,1)}), bf16[8,128,128]{2,1,0:T(8,128)(2,1)S(1)}, u32[]{:S(2)}, u32[]{:S(2)}) async-start(bf16[8,128,128]{2,1,0:T(8,128)(2,1)} %pad_maximum_fusion.2), calls=%async_computation.3 | async-start | bytes 524288 | tf_op jit(solution)/shard_map/all_to_all | solution.py:276
  168.9 6.8 %collective-permute-start.17 = (bf16[8,128,128]{2,1,0:T(8,128)(2,1)S(1)}, bf16[8,128,128]{2,1,0:T(8,128)(2,1)S(1)}, u32[]{:S(2)}, u32[]{:S(2)}) collective-permute-start(bf16[8,128,128]{2,1,0:T(8,128)(2,1)S(1)} %get-tuple-element.61.refs_4_), channel_id=1, source_target_pairs={{0,1},{1,0},{2,3},{3,2},{4,5},{5,4},{6,7},{7,6},{8,9},{9,8},{10,11... | collective-permute-start | bytes 786440 | tf_op jit(solution)/shard_map/ppermute | solution.py:31
  171.9 6.5 %collective-permute-start.15 = (bf16[8,128,128]{2,1,0:T(8,128)(2,1)S(1)}, bf16[8,128,128]{2,1,0:T(8,128)(2,1)S(1)}, u32[]{:S(2)}, u32[]{:S(2)}) collective-permute-start(bf16[8,128,128]{2,1,0:T(8,128)(2,1)S(1)} %get-tuple-element.62.refs_0_), channel_id=1, source_target_pairs={{0,3},{1,2},{2,1},{3,0},{4,7},{5,6},{6,5},{7,4},{8,11},{9,10},{10,... | collective-permute-start | bytes 786440 | tf_op jit(solution)/shard_map/ppermute | solution.py:31
  173.3 7.9 %collective-permute-start.19 = (bf16[8,128,128]{2,1,0:T(8,128)(2,1)S(1)}, bf16[8,128,128]{2,1,0:T(8,128)(2,1)S(1)}, u32[]{:S(2)}, u32[]{:S(2)}) collective-permute-start(bf16[8,128,128]{2,1,0:T(8,128)(2,1)S(1)} %get-tuple-element.61.refs_4_), channel_id=1, source_target_pairs={{0,3},{1,2},{2,1},{3,0},{4,7},{5,6},{6,5},{7,4},{8,11},{9,10},{10,... | collective-permute-start | bytes 786440 | tf_op jit(solution)/shard_map/ppermute | solution.py:31
  174.6 6.8 %collective-permute-start.14 = (bf16[8,128,128]{2,1,0:T(8,128)(2,1)S(1)}, bf16[8,128,128]{2,1,0:T(8,128)(2,1)S(1)}, u32[]{:S(2)}, u32[]{:S(2)}) collective-permute-start(bf16[8,128,128]{2,1,0:T(8,128)(2,1)S(1)} %get-tuple-element.62.refs_0_), channel_id=1, source_target_pairs={{0,1},{1,0},{2,3},{3,2},{4,5},{5,4},{6,7},{7,6},{8,9},{9,8},{10,11... | collective-permute-start | bytes 786440 | tf_op jit(solution)/shard_map/ppermute | solution.py:31
  175.7 10.8 %collective-permute-start.18 = (bf16[8,128,128]{2,1,0:T(8,128)(2,1)S(1)}, bf16[8,128,128]{2,1,0:T(8,128)(2,1)S(1)}, u32[]{:S(2)}, u32[]{:S(2)}) collective-permute-start(bf16[8,128,128]{2,1,0:T(8,128)(2,1)S(1)} %collective-permute-done.17.refs_5_), channel_id=1, source_target_pairs={{0,3},{1,2},{2,1},{3,0},{4,7},{5,6},{6,5},{7,4},{8,11},{9,10},{10,... | collective-permute-start | bytes 786440 | tf_op jit(solution)/shard_map/ppermute | solution.py:31
  178.4 8.7 %collective-permute-start.16 = (bf16[8,128,128]{2,1,0:T(8,128)(2,1)S(1)}, bf16[8,128,128]{2,1,0:T(8,128)(2,1)S(1)}, u32[]{:S(2)}, u32[]{:S(2)}) collective-permute-start(bf16[8,128,128]{2,1,0:T(8,128)(2,1)S(1)} %collective-permute-done.15.refs_3_), channel_id=1, source_target_pairs={{0,1},{1,0},{2,3},{3,2},{4,5},{5,4},{6,7},{7,6},{8,9},{9,8},{10,11... | collective-permute-start | bytes 786440 | tf_op jit(solution)/shard_map/ppermute | solution.py:31
  192.9 17.8 %all-to-all-start.5 = ((bf16[8,144,128]{2,1,0:T(8,128)(2,1)}), bf16[8,144,128]{2,1,0:T(8,128)(2,1)}, u32[]{:S(2)}, u32[]{:S(2)}) async-start(bf16[8,144,128]{2,1,0:T(8,128)(2,1)} %shard_map.108), calls=%async_computation.7 | async-start | bytes 589824 | tf_op jit(solution)/shard_map/all_to_all | solution.py:283
  (25 other events, 122.0 us)
Sparse Core Ops, SparseCore 0:
  55.3 35.4 reduce-scatter.2
  120.6 30.7 reduce-scatter.4

commit v6 on v4

--- a/solution.py
+++ b/solution.py
@@ -97,20 +97,27 @@
     )
 
 
-def teacher_kernel(place_ref, rows_ref, out_ref, *parts):
+def teacher_kernel(place_ref, rows_ref, out_ref, *refs):
     x = place_ref[2]
+    parts, held, sems = refs[:NX], refs[NX], refs[NX + 1]
+    copies = [
+        pltpu.make_async_copy(out_ref.at[:, pl.ds(z * 1024, 1024)], held.at[z], sems.at[z]) for z in range(NZ)
+    ]
+    for copy in copies:
+        copy.start()
     rows = rows_ref[...]
     for z in range(NZ):
+        copies[z].wait()
         for k in range(NX):
-            columns = pl.ds(pl.multiple_of(z * 1024 + (k ^ x) * 256, 256), 256)
-            parts[k][z] = dot(rows, out_ref[:, columns], ((1,), (0,))).astype(B16)
+            columns = pl.ds(pl.multiple_of((k ^ x) * 256, 256), 256)
+            parts[k][z] = dot(rows, held[z, :, columns], ((1,), (0,))).astype(B16)
 
 
 def teacher_parts(place, rows, teacher_out):
     outs = [jax.ShapeDtypeStruct((NZ, 64, 256), B16)] * NX
-    return call(teacher_kernel, [whole(64, 256), whole(256, 8192)], outs, 2 * 64 * 256 * 8192)(
-        place, rows, teacher_out
-    )
+    scratch = [pltpu.VMEM((NZ, 256, 1024), B16), pltpu.SemaphoreType.DMA((NZ,))]
+    specs = [whole(64, 256), pl.BlockSpec(memory_space=pltpu.HBM)]
+    return call(teacher_kernel, specs, outs, 2 * 64 * 256 * 8192, scratch)(place, rows, teacher_out)
 
 
 def gather_hidden(place_ref, got_ref, hidden_ref):
@@ -145,32 +152,39 @@
 KEPT = ((3, ((0, 1),)), (1, ((1, 3),)), (0, ((0, 0), (1, 2))))
 
 
-def combined_parts(jobs, place, picked, got, heads, student_out, projector, other):
+def combined_parts(jobs, place, picked, got, heads, out_cols, home, other):
     specs = [
         whole(NX, 1, 256),
         whole(NY, 128, 256),
         whole(NX, 256, 128),
-        pl.BlockSpec((128, COLS), lambda i, m: (0, m[0])),
-        pl.BlockSpec((256, COLS), lambda i, m: (0, m[0])),
+        whole(128, COLS),
+        whole(256, COLS),
         whole(256, COLS),
     ]
     outs = [jax.ShapeDtypeStruct((256, HALF), B16)] * 4
     return call(
         functools.partial(combine_kernel, jobs), specs, outs, 2 * 512 * 1024 * 900, [pltpu.VMEM((512, 512), B16)]
-    )(place, picked, got, heads, student_out, projector, other)
-
-
-def heads_kernel(place_ref, *refs):
+    )(place, picked, got, heads, out_cols, home, other)
+
+
+def final_kernel(place_ref, *refs):
     x = place_ref[2]
     first, second = refs[:4], refs[4:8]
-    out_ref, part_ref, squares_ref, sums_ref = refs[8:]
+    out_ref, heads_ref, part_ref, squares_ref, weight_ref, sums_ref = refs[8:]
+    left = jnp.zeros((128, HALF), F32)
+    right = jnp.zeros((128, HALF), F32)
     for k in range(NX):
         near, far = first[k][...], second[k][...]
         part = dot(near, out_ref[:, :HALF], ((1,), (1,))) + dot(far, out_ref[:, HALF:], ((1,), (1,)))
         part_ref[k ^ x] = part.astype(B16)
+        heads = heads_ref[k ^ x]
+        left += dot(heads, near, ((0,), (0,)))
+        right += dot(heads, far, ((0,), (0,)))
         near, far = near.astype(F32), far.astype(F32)
         line = jnp.sum(near * near + far * far, axis=0, keepdims=True)
         sums_ref[k ^ x] = line[:, :128] + line[:, 128:256] + line[:, 256:384] + line[:, 384:]
+    weight_ref[:, :HALF] = left.astype(B16)
+    weight_ref[:, HALF:] = right.astype(B16)
     total = sums_ref[0] + sums_ref[1] + sums_ref[2] + sums_ref[3]
     top = total.astype(B16).astype(F32)
     middle = (total - top).astype(B16).astype(F32)
@@ -180,32 +194,16 @@
     squares_ref[...] = lines.astype(B16)
 
 
-def weight_kernel(place_ref, *refs):
-    x = place_ref[2]
-    first, second = refs[:4], refs[4:8]
-    heads_ref, weight_ref = refs[8:]
-    left = jnp.zeros((128, HALF), F32)
-    right = jnp.zeros((128, HALF), F32)
-    for k in range(NX):
-        heads = heads_ref[k ^ x]
-        left += dot(heads, first[k][...], ((0,), (0,)))
-        right += dot(heads, second[k][...], ((0,), (0,)))
-    weight_ref[:, :HALF] = left.astype(B16)
-    weight_ref[:, HALF:] = right.astype(B16)
-
-
-def heads_parts(place, gathered, student_out):
-    specs = [whole(256, HALF)] * 8 + [pl.BlockSpec((128, COLS), lambda i, m: (0, m[0]))]
-    outs = [jax.ShapeDtypeStruct((NX, 256, 128), B16), jax.ShapeDtypeStruct((16, 128), B16)]
-    return call(heads_kernel, specs, outs, 2 * 1024 * 1024 * 128, [pltpu.VMEM((NX, 1, 128), F32)])(
-        place, *gathered, student_out
-    )
-
-
-def weight_grad(place, gathered, heads):
-    specs = [whole(256, HALF)] * 8 + [whole(NX, 256, 128)]
-    outs = [jax.ShapeDtypeStruct((128, COLS), B16)]
-    return call(weight_kernel, specs, outs, 2 * 1024 * 1024 * 128)(place, *gathered, heads)[0]
+def final_parts(place, gathered, out_cols, heads):
+    specs = [whole(256, HALF)] * 8 + [whole(128, COLS), whole(NX, 256, 128)]
+    outs = [
+        jax.ShapeDtypeStruct((NX, 256, 128), B16),
+        jax.ShapeDtypeStruct((16, 128), B16),
+        jax.ShapeDtypeStruct((128, COLS), B16),
+    ]
+    return call(final_kernel, specs, outs, 2 * 1024 * 1024 * 256, [pltpu.VMEM((NX, 1, 128), F32)])(
+        place, *gathered, out_cols, heads
+    )
 
 
 def local(
@@ -223,23 +221,25 @@
     place = jnp.stack([member, seq, lax.axis_index("x")]).astype(jnp.int32)
     swap = [(0, 1), (1, 0)]
 
-    away = lax.dynamic_slice(projector, (0, (member + 1 - 2 * seq) * COLS), (256, COLS))
-    other = lax.ppermute(away, "seq", swap)
-
-    own_matches = lax.dynamic_slice(matches, (seq * 128,), (128,)).astype(B16)
+    there = lax.ppermute(teacher_heads, "seq", swap)
+    first = teacher_parts(place, teacher_heads, teacher_out)
+    second = teacher_parts(place, there, teacher_out)
+    *second, later = lax.optimization_barrier((*second, member))
+
+    own_matches = lax.dynamic_slice(matches, (later % 2 * 128,), (128,)).astype(B16)
     shared = jnp.concatenate([student_heads, jnp.broadcast_to(own_matches[None], (16, 128))], axis=0)
     resid_parts = jnp.transpose(student_resid.reshape(4, NY, 8, 128), (1, 0, 2, 3)).reshape(NY, 32, 128)
     early = jnp.concatenate([jnp.broadcast_to(shared[None], (NY,) + shared.shape), resid_parts], axis=1)
     early = lax.all_to_all(early, COLUMN, 0, 0)
 
-    there = lax.ppermute(teacher_heads, "seq", swap)
-    first, second, other = reduce_x(
-        teacher_parts(place, teacher_heads, teacher_out),
-        teacher_parts(place, there, teacher_out),
-        (other,),
-    )
-    summed = jnp.concatenate([first, second], axis=1)
-    summed, early = lax.optimization_barrier((summed, early))
+    away = lax.dynamic_slice(projector, (0, (later + 1 - 2 * seq) * COLS), (256, COLS))
+    other = lax.ppermute(away, "seq", swap)
+    home = lax.dynamic_slice(projector, (0, later * COLS), (256, COLS))
+    out_cols = lax.dynamic_slice(student_out, (0, later * COLS), (128, COLS))
+
+    first, second, early = reduce_x(first, second, (early,))
+    moved = lax.all_to_all(jnp.concatenate([first, second], axis=1), "z", 0, 0)
+    moved, other = lax.optimization_barrier((moved, other))
     heads = own_order(early[:, :128]).reshape(NX, 256, 128)
     base = (jnp.arange(NY, dtype=jnp.int32) // 2 * 128)[:, None]
     picked = own_order(early[:, 128].astype(jnp.int32) + base).reshape(NX, 1, 256)
@@ -247,10 +247,10 @@
     resid = jnp.concatenate([resid[:, 0], resid[:, 1]], axis=0)
     near = lax.dynamic_slice(teacher_resid, (seq * 64, 0), (64, 256))
     far = lax.dynamic_slice(teacher_resid, (64 - seq * 64, 0), (64, 256))
-    hidden = (jnp.concatenate([near, far], axis=0).astype(F32) + reduce_z(summed)).astype(B16)
+    hidden = (jnp.concatenate([near, far], axis=0).astype(F32) + jnp.sum(moved.astype(F32), axis=0)).astype(B16)
 
     got = lax.all_to_all(jnp.broadcast_to(hidden[None], (NY, 128, 256)), COLUMN, 0, 0)
-    operands = (place, picked, got, heads, student_out, projector, other)
+    operands = (place, picked, got, heads, out_cols, home, other)
     sent = combined_parts(SENT, *operands)
     kept = combined_parts(KEPT, *operands)
     sent = [part.reshape(NZ, 32, HALF) for part in sent]
@@ -265,12 +265,11 @@
     tall = lax.all_to_all(jnp.broadcast_to(grad[None], (NZ, 64, HALF)), "z", 0, 0)
     gathered = gather_x(tall[:, :32].reshape(256, HALF), tall[:, 32:].reshape(256, HALF))
 
-    heads_part, squares = heads_parts(place, gathered, student_out)
+    heads_part, squares, grad_weight = final_parts(place, gathered, out_cols, heads)
     sent = jnp.concatenate(
         [block_order(heads_part.reshape(ROWS, 128)), jnp.broadcast_to(squares[None], (NY, 16, 128))], axis=1
     )
     back = lax.all_to_all(sent, COLUMN, 0, 0).astype(F32)
-    grad_weight = weight_grad(place, gathered, heads)
     grad_heads = jnp.sum(back[:, :128], axis=0).astype(B16)
     total = jnp.sum(back[:, 128:])
     loss = (total * (64.0 / (ROWS * 8192))).reshape(1)

time: 185 us -> 192 us (1.038)
  blocking collectives: 15.4 us -> 34.6 us
  starting transfers between devices: 59.2 us -> 52.4 us
  local copies, waits for them, and re-layouts: 19.8 us -> 15.9 us
  waiting for transfers between devices: 69.5 us -> 66.1 us
    all_to_all x0 -> x1, blocking collectives: none -> 19 us  [local(): back = lax.all_to_all(sent, COLUMN, 0, 0).astype(F32)]
    all_to_all x2 -> x1, waiting for transfers between devices: 31.4 us -> 13.2 us  [reduce_z(): moved = lax.all_to_all(parts, 'z', 0, 0)]
    ppermute x1, waiting for transfers between devices: 0.01 us -> 10.4 us  [local(): other = lax.ppermute(away, 'seq', swap)]
    ppermute x18, waiting for transfers between devices: 27.1 us -> 35 us  [across(): return lax.ppermute(block, 'x', [(i, i ^ flip) for i in range(NX)])]
    all_to_all x2 -> x1, starting transfers between devices: 11.7 us -> 6.59 us  [reduce_z(): moved = lax.all_to_all(parts, 'z', 0, 0)]
    all_to_all x1, waiting for transfers between devices: 4.39 us -> 0.01 us  [local(): early = lax.all_to_all(early, COLUMN, 0, 0)]
    all_to_all x1, starting transfers between devices: 11.5 us -> 7.7 us  [local(): moved = lax.all_to_all(jnp.concatenate([first, second], axis=1), 'z', 0, 0)]
    unnamed x35 -> x29, local copies, waits for them, and re-layouts: 11.9 us -> 8.27 us
  transfers between devices with their start and end apart: 25 -> 24, of which waited for: 16 -> 18; matrix products, arithmetic and copies ran while one was open for 6% -> 5% of each run, Pallas kernels for 4% -> 2%
where the time goes in v6:
time: 192 us; the launch traced here: 191 us
  waiting for transfers between devices  66.1 us (34%)
  starting transfers between devices  52.4 us (27%)
  blocking collectives  34.6 us (18%)
  local copies, waits for them, and re-layouts  15.9 us (8%)
  Pallas kernels  11.7 us (6%)
  other arithmetic  7.69 us (4%)
  between operations  2.75 us (1%)
    ppermute x18, waiting for transfers between devices, across(): return lax.ppermute(block, 'x', [(i, i ^ flip) for i in range(NX)])  35 us
    all_to_all x1, blocking collectives, local(): back = lax.all_to_all(sent, COLUMN, 0, 0).astype(F32)  19 us
    ppermute x18, starting transfers between devices, across(): return lax.ppermute(block, 'x', [(i, i ^ flip) for i in range(NX)])  17.7 us
    all_to_all x1, blocking collectives, local(): lax.all_to_all(jnp.broadcast_to(grad[None], (NZ, 64, HALF)), 'z', 0, 0)  15.6 us
    all_to_all x1, waiting for transfers between devices, reduce_z(): moved = lax.all_to_all(parts, 'z', 0, 0)  13.2 us
    ppermute x1, waiting for transfers between devices, local(): other = lax.ppermute(away, 'seq', swap)  10.4 us
    unnamed x29, local copies, waits for them, and re-layouts  8.27 us
    all_to_all x1, starting transfers between devices, local(): moved = lax.all_to_all(jnp.concatenate([first, second], axis=1), 'z', 0, 0)  7.7 us
  transfers between devices with their start and end apart: 24, of which 18 were waited for; matrix products, arithmetic and copies ran while one was open for 5% of the time, Pallas kernels for 2%

profile of v6, /device:TPU:1, one launch (start us, length us, event | category | flops | bytes accessed | tf_op | source)
XLA Modules:
  0.0 191.2 jit_solution(13844864638821453570)
XLA Ops:
  0.7 3.8 %collective-permute-start.1 = (bf16[64,256]{1,0:T(8,128)(2,1)}, bf16[64,256]{1,0:T(8,128)(2,1)S(1)}, u32[]{:S(2)}, u32[]{:S(2)}) collective-permute-start(bf16[64,256]{1,0:T(8,128)(2,1)} %rows_ref.1), channel_id=1, source_target_pairs={{0,32},{32,0},{1,33},{33,1},{2,34},{34,2},{3,35},{35,3},{4,36},{36... | collective-permute-start | bytes 98312 | tf_op jit(solution)/shard_map/ppermute | solution.py:224
  6.0 2.2 %copy-done.1 = bf16[256,8192]{1,0:T(8,128)(2,1)S(1)} copy-done((bf16[256,8192]{1,0:T(8,128)(2,1)S(1)}, bf16[256,8192]{1,0:T(8,128)(2,1)}, u32[]{:S(2)}) %copy-start.1) | copy-done | bytes 4194328
  8.2 2.7 %shard_map.104 = (bf16[8,64,256]{2,1,0:T(8,128)(2,1)S(1)}, bf16[8,64,256]{2,1,0:T(8,128)(2,1)S(1)}, bf16[8,64,256]{2,1,0:T(8,128)(2,1)S(1)}, bf16[8,64,256]{2,1,0:T(8,128)(2,1)S(1)}) custom-call(s32[3]{0:T(128)S(1)} %pad_add_fusion.place_ref, bf16[64,256]{1,0:T(8,128)(2,1)S(1)} %collective-permute-done.1.rows_ref, bf16[256,8192]{1,0:T(8,128)(2,1)S(1)} %copy-done.1), custom_call_target="tpu_custom_call" | custom-call | flops 268435456 | bytes 5242880 | tf_op jit(solution)/shard_map/pallas_call | solution.py:120
  11.9 7.6 %all-to-all-start = ((bf16[8,176,128]{2,1,0:T(8,128)(2,1)}), bf16[8,176,128]{2,1,0:T(8,128)(2,1)}, u32[]{:S(2)}, u32[]{:S(2)}) async-start(bf16[8,176,128]{2,1,0:T(8,128)(2,1)} %pad_maximum_fusion.2), calls=%async_computation | async-start | bytes 720896 | tf_op jit(solution)/shard_map/all_to_all | solution.py:233
  19.4 2.2 %copy-done.2 = bf16[256,8192]{1,0:T(8,128)(2,1)S(1)} copy-done((bf16[256,8192]{1,0:T(8,128)(2,1)S(1)}, bf16[256,8192]{1,0:T(8,128)(2,1)}, u32[]{:S(2)}) %copy-start.2) | copy-done | bytes 4194328
  21.6 2.7 %shard_map.103 = (bf16[8,64,256]{2,1,0:T(8,128)(2,1)S(1)}, bf16[8,64,256]{2,1,0:T(8,128)(2,1)S(1)}, bf16[8,64,256]{2,1,0:T(8,128)(2,1)S(1)}, bf16[8,64,256]{2,1,0:T(8,128)(2,1)S(1)}) custom-call(s32[3]{0:T(128)S(1)} %pad_add_fusion.place_ref, bf16[64,256]{1,0:T(8,128)(2,1)S(1)} %copy-done.4, bf16[256,8192]{1,0:T(8,128)(2,1)S(1)} %copy-done.2), custom_call_target="tpu_custom_call" | custom-call | flops 268435456 | bytes 5242880 | tf_op jit(solution)/shard_map/pallas_call | solution.py:120
  27.8 5.1 %collective-permute-done = bf16[8,64,256]{2,1,0:T(8,128)(2,1)} collective-permute-done((bf16[8,64,256]{2,1,0:T(8,128)(2,1)S(1)}, bf16[8,64,256]{2,1,0:T(8,128)(2,1)}, u32[]{:S(2)}, u32[]{:S(2)}) %collective-permute-start) | collective-permute-done | bytes 262176 | tf_op jit(solution)/shard_map/ppermute | solution.py:34
  42.6 4.6 %collective-permute-done.3 = bf16[8,64,256]{2,1,0:T(8,128)(2,1)S(1)} collective-permute-done((bf16[8,64,256]{2,1,0:T(8,128)(2,1)}, bf16[8,64,256]{2,1,0:T(8,128)(2,1)S(1)}, u32[]{:S(2)}, u32[]{:S(2)}) %collective-permute-start.3) | collective-permute-done | bytes 262176 | tf_op jit(solution)/shard_map/ppermute | solution.py:34
  48.1 7.7 %all-to-all-start.1 = ((bf16[8,128,256]{2,1,0:T(8,128)(2,1)}), bf16[8,128,256]{2,1,0:T(8,128)(2,1)S(1)}, u32[]{:S(2)}, u32[]{:S(2)}) async-start(bf16[8,128,256]{2,1,0:T(8,128)(2,1)} %pad_maximum_fusion), calls=%async_computation.1 | async-start | bytes 1048576 | tf_op jit(solution)/shard_map/all_to_all | solution.py:241
  55.8 2.3 %constant_dynamic-slice_fusion = (bf16[256,1024]{1,0:T(8,128)(2,1)}, bf16[256,1024]{1,0:T(8,128)(2,1)}) fusion(bf16[256,8192]{1,0:T(8,128)(2,1)} %param.12, s32[]{:T(128)S(6)} %select_n.38, s32[]{:T(128)S(6)} %select_n.37), kind=kLoop, calls=%fused_computation.32 | loop fusion | bytes 2097160 | tf_op jit(solution)/shard_map/dynamic_slice | solution.py:237
  59.8 10.4 %collective-permute-done.7.other_ref = bf16[256,1024]{1,0:T(8,128)(2,1)S(1)} collective-permute-done((bf16[256,1024]{1,0:T(8,128)(2,1)}, bf16[256,1024]{1,0:T(8,128)(2,1)S(1)}, u32[]{:S(2)}, u32[]{:S(2)}) %collective-permute-start.7) | collective-permute-done | bytes 524320 | tf_op jit(solution)/shard_map/ppermute | solution.py:236
  71.2 7.4 %all-to-all-start.2 = ((bf16[8,128,256]{2,1,0:T(8,128)(2,1)}), bf16[8,128,256]{2,1,0:T(8,128)(2,1)S(1)}, u32[]{:S(2)}, u32[]{:S(2)}) async-start(bf16[8,128,256]{2,1,0:T(8,128)(2,1)} %broadcast_in_dim.12), calls=%async_computation.2 | async-start | bytes 1048576 | tf_op jit(solution)/shard_map/all_to_all | solution.py:252
  81.1 6.9 %all-to-all-done.2.got_ref = bf16[8,128,256]{2,1,0:T(8,128)(2,1)S(1)} async-done(((bf16[8,128,256]{2,1,0:T(8,128)(2,1)}), bf16[8,128,256]{2,1,0:T(8,128)(2,1)S(1)}, u32[]{:S(2)}, u32[]{:S(2)}) %all-to-all-start.2) | async-done | bytes 524320 | tf_op jit(solution)/shard_map/all_to_all | solution.py:252
  90.1 2.0 %shard_map.106 = (bf16[256,512]{1,0:T(8,128)(2,1)S(1)}, bf16[256,512]{1,0:T(8,128)(2,1)S(1)}, bf16[256,512]{1,0:T(8,128)(2,1)S(1)}, bf16[256,512]{1,0:T(8,128)(2,1)S(1)}) custom-call(s32[3]{0:T(128)S(1)} %pad_add_fusion.place_ref, s32[4,1,256]{2,1,0:T(1,128)S(1)} %reshape_reshape.12.picked_ref, bf16[8,128,256]{2,1,0:T(8,128)(2,1)S(1)} %all-to-all-done.2.got_ref, ...), custom_call_target="tpu_custom_call" | custom-call | flops 943718400 | bytes 5242880 | tf_op jit(solution)/shard_map/pallas_call | solution.py:165
  96.5 2.0 %shard_map.105 = (bf16[256,512]{1,0:T(8,128)(2,1)S(1)}, bf16[256,512]{1,0:T(8,128)(2,1)S(1)}, bf16[256,512]{1,0:T(8,128)(2,1)S(1)}, bf16[256,512]{1,0:T(8,128)(2,1)S(1)}) custom-call(s32[3]{0:T(128)S(1)} %pad_add_fusion.place_ref, s32[4,1,256]{2,1,0:T(1,128)S(1)} %reshape_reshape.12.picked_ref, bf16[8,128,256]{2,1,0:T(8,128)(2,1)S(1)} %all-to-all-done.2.got_ref, ...), custom_call_target="tpu_custom_call" | custom-call | flops 943718400 | bytes 5242880 | tf_op jit(solution)/shard_map/pallas_call | solution.py:165
  102.7 2.6 %collective-permute-done.8 = bf16[8,32,512]{2,1,0:T(8,128)(2,1)S(1)} collective-permute-done((bf16[8,32,512]{2,1,0:T(8,128)(2,1)S(1)}, bf16[8,32,512]{2,1,0:T(8,128)(2,1)S(1)}, u32[]{:S(2)}, u32[]{:S(2)}) %collective-permute-start.8) | collective-permute-done | bytes 262176 | tf_op jit(solution)/shard_map/ppermute | solution.py:34
  106.9 5.5 %collective-permute-done.11 = bf16[8,32,512]{2,1,0:T(8,128)(2,1)S(1)} collective-permute-done((bf16[8,32,512]{2,1,0:T(8,128)(2,1)S(1)}, bf16[8,32,512]{2,1,0:T(8,128)(2,1)S(1)}, u32[]{:S(2)}, u32[]{:S(2)}) %collective-permute-start.11) | collective-permute-done | bytes 262176 | tf_op jit(solution)/shard_map/ppermute | solution.py:34
  113.4 6.6 %all-to-all-start.3 = ((bf16[8,64,512]{2,1,0:T(8,128)(2,1)}), bf16[8,64,512]{2,1,0:T(8,128)(2,1)S(1)}, u32[]{:S(2)}, u32[]{:S(2)}) async-start(bf16[8,64,512]{2,1,0:T(8,128)(2,1)} %pad_maximum_fusion.1), calls=%async_computation.3 | async-start | bytes 1048576 | tf_op jit(solution)/shard_map/all_to_all | solution.py:64
  121.0 13.2 %all-to-all-done.3 = bf16[8,64,512]{2,1,0:T(8,128)(2,1)S(1)} async-done(((bf16[8,64,512]{2,1,0:T(8,128)(2,1)}), bf16[8,64,512]{2,1,0:T(8,128)(2,1)S(1)}, u32[]{:S(2)}, u32[]{:S(2)}) %all-to-all-start.3) | async-done | bytes 524320 | tf_op jit(solution)/shard_map/all_to_all | solution.py:64
  134.3 15.6 %all_to_all.30 = bf16[8,64,512]{2,1,0:T(8,128)(2,1)S(1)} all-to-all(bf16[8,64,512]{2,1,0:T(8,128)(2,1)S(1)} %broadcast_in_dim.13), channel_id=1, replica_groups=mesh['ylo'=2,'core'=2,'seq'=2,'z'=8,'x'=4] {'z'}, dimensions={0} | all-to-all | bytes 1048576 | tf_op jit(solution)/shard_map/all_to_all | solution.py:265
  154.2 2.3 %collective-permute-done.15.refs_3_ = bf16[256,512]{1,0:T(8,128)(2,1)S(1)} collective-permute-done((bf16[256,512]{1,0:T(8,128)(2,1)S(1)}, bf16[256,512]{1,0:T(8,128)(2,1)S(1)}, u32[]{:S(2)}, u32[]{:S(2)}) %collective-permute-start.15) | collective-permute-done | bytes 262176 | tf_op jit(solution)/shard_map/ppermute | solution.py:34
  160.2 5.0 %collective-permute-done.16.refs_2_ = bf16[256,512]{1,0:T(8,128)(2,1)S(1)} collective-permute-done((bf16[256,512]{1,0:T(8,128)(2,1)S(1)}, bf16[256,512]{1,0:T(8,128)(2,1)S(1)}, u32[]{:S(2)}, u32[]{:S(2)}) %collective-permute-start.16) | collective-permute-done | bytes 262176 | tf_op jit(solution)/shard_map/ppermute | solution.py:34
  166.6 2.3 %shard_map.107 = (bf16[4,256,128]{2,1,0:T(8,128)(2,1)S(1)}, bf16[16,128]{1,0:T(8,128)(2,1)S(1)}, bf16[128,1024]{1,0:T(8,128)(2,1)}) custom-call(s32[3]{0:T(128)S(1)} %pad_add_fusion.place_ref, bf16[256,512]{1,0:T(8,128)(2,1)S(1)} %bitcast.54, bf16[256,512]{1,0:T(8,128)(2,1)S(1)} %collective-permute-done.14.refs_1_, ...), custom_call_target="tpu_custom_call" | custom-call | flops 536870912 | bytes 5242880 | tf_op jit(solution)/shard_map/pallas_call | solution.py:204
  169.1 19.0 %all_to_all.31 = bf16[8,144,128]{2,1,0:T(8,128)(2,1)S(1)} all-to-all(bf16[8,144,128]{2,1,0:T(8,128)(2,1)S(1)} %copy.46), channel_id=1, replica_groups=mesh['ylo'=2,'core'=2,'seq'=2,'z'=8,'x'=4] {'ylo','core','seq'}, dimensions={0} | all-to-all | bytes 589824 | tf_op jit(solution)/shard_map/all_to_all | solution.py:272
  (106 shorter events, 46.8 us)
Async XLA Ops:
  0.7 5.3 %collective-permute-start.1 = (bf16[64,256]{1,0:T(8,128)(2,1)}, bf16[64,256]{1,0:T(8,128)(2,1)S(1)}, u32[]{:S(2)}, u32[]{:S(2)}) collective-permute-start(bf16[64,256]{1,0:T(8,128)(2,1)} %rows_ref.1), channel_id=1, source_target_pairs={{0,32},{32,0},{1,33},{33,1},{2,34},{34,2},{3,35},{35,3},{4,36},{36... | collective-permute-start | bytes 98312 | tf_op jit(solution)/shard_map/ppermute | solution.py:224
  11.9 22.3 %all-to-all-start = ((bf16[8,176,128]{2,1,0:T(8,128)(2,1)}), bf16[8,176,128]{2,1,0:T(8,128)(2,1)}, u32[]{:S(2)}, u32[]{:S(2)}) async-start(bf16[8,176,128]{2,1,0:T(8,128)(2,1)} %pad_maximum_fusion.2), calls=%async_computation | async-start | bytes 720896 | tf_op jit(solution)/shard_map/all_to_all | solution.py:233
  25.1 7.9 %collective-permute-start = (bf16[8,64,256]{2,1,0:T(8,128)(2,1)S(1)}, bf16[8,64,256]{2,1,0:T(8,128)(2,1)}, u32[]{:S(2)}, u32[]{:S(2)}) collective-permute-start(bf16[8,64,256]{2,1,0:T(8,128)(2,1)S(1)} %get-tuple-element.32), channel_id=1, source_target_pairs={{0,1},{1,0},{2,3},{3,2},{4,5},{5,4},{6,7},{7,6},{8,9},{9,8},{10,11... | collective-permute-start | bytes 786440 | tf_op jit(solution)/shard_map/ppermute | solution.py:34
  25.1 9.1 %collective-permute-start.2 = (bf16[8,64,256]{2,1,0:T(8,128)(2,1)S(1)}, bf16[8,64,256]{2,1,0:T(8,128)(2,1)}, u32[]{:S(2)}, u32[]{:S(2)}) collective-permute-start(bf16[8,64,256]{2,1,0:T(8,128)(2,1)S(1)} %copy-done.9), channel_id=1, source_target_pairs={{0,3},{1,2},{2,1},{3,0},{4,7},{5,6},{6,5},{7,4},{8,11},{9,10},{10,... | collective-permute-start | bytes 786440 | tf_op jit(solution)/shard_map/ppermute | solution.py:34
  26.9 13.0 %collective-permute-start.5 = (bf16[8,64,256]{2,1,0:T(8,128)(2,1)S(1)}, bf16[8,64,256]{2,1,0:T(8,128)(2,1)}, u32[]{:S(2)}, u32[]{:S(2)}) collective-permute-start(bf16[8,64,256]{2,1,0:T(8,128)(2,1)S(1)} %get-tuple-element.45), channel_id=1, source_target_pairs={{0,3},{1,2},{2,1},{3,0},{4,7},{5,6},{6,5},{7,4},{8,11},{9,10},{10,... | collective-permute-start | bytes 786440 | tf_op jit(solution)/shard_map/ppermute | solution.py:34
  35.2 6.3 %collective-permute-start.6 = (bf16[8,64,256]{2,1,0:T(8,128)(2,1)S(1)}, bf16[8,64,256]{2,1,0:T(8,128)(2,1)S(1)}, u32[]{:S(2)}, u32[]{:S(2)}) collective-permute-start(bf16[8,64,256]{2,1,0:T(8,128)(2,1)S(1)} %add_convert_fusion.1), channel_id=1, source_target_pairs={{0,1},{1,0},{2,3},{3,2},{4,5},{5,4},{6,7},{7,6},{8,9},{9,8},{10,11... | collective-permute-start | bytes 786440 | tf_op jit(solution)/shard_map/ppermute | solution.py:34
  35.3 11.8 %collective-permute-start.3 = (bf16[8,64,256]{2,1,0:T(8,128)(2,1)}, bf16[8,64,256]{2,1,0:T(8,128)(2,1)S(1)}, u32[]{:S(2)}, u32[]{:S(2)}) collective-permute-start(bf16[8,64,256]{2,1,0:T(8,128)(2,1)} %copy-done.10), channel_id=1, source_target_pairs={{0,1},{1,0},{2,3},{3,2},{4,5},{5,4},{6,7},{7,6},{8,9},{9,8},{10,11... | collective-permute-start | bytes 786440 | tf_op jit(solution)/shard_map/ppermute | solution.py:34
  37.8 9.4 %collective-permute-start.4 = (bf16[8,64,256]{2,1,0:T(8,128)(2,1)S(1)}, bf16[8,64,256]{2,1,0:T(8,128)(2,1)S(1)}, u32[]{:S(2)}, u32[]{:S(2)}) collective-permute-start(bf16[8,64,256]{2,1,0:T(8,128)(2,1)S(1)} %add_convert_fusion.3), channel_id=1, source_target_pairs={{0,3},{1,2},{2,1},{3,0},{4,7},{5,6},{6,5},{7,4},{8,11},{9,10},{10,... | collective-permute-start | bytes 786440 | tf_op jit(solution)/shard_map/ppermute | solution.py:34
  48.1 22.1 %all-to-all-start.1 = ((bf16[8,128,256]{2,1,0:T(8,128)(2,1)}), bf16[8,128,256]{2,1,0:T(8,128)(2,1)S(1)}, u32[]{:S(2)}, u32[]{:S(2)}) async-start(bf16[8,128,256]{2,1,0:T(8,128)(2,1)} %pad_maximum_fusion), calls=%async_computation.1 | async-start | bytes 1048576 | tf_op jit(solution)/shard_map/all_to_all | solution.py:241
  58.1 12.1 %collective-permute-start.7 = (bf16[256,1024]{1,0:T(8,128)(2,1)}, bf16[256,1024]{1,0:T(8,128)(2,1)S(1)}, u32[]{:S(2)}, u32[]{:S(2)}) collective-permute-start(bf16[256,1024]{1,0:T(8,128)(2,1)} %get-tuple-element.62), channel_id=1, source_target_pairs={{0,32},{32,0},{1,33},{33,1},{2,34},{34,2},{3,35},{35,3},{4,36},{36... | collective-permute-start | bytes 1572872 | tf_op jit(solution)/shard_map/ppermute | solution.py:236
  71.2 16.8 %all-to-all-start.2 = ((bf16[8,128,256]{2,1,0:T(8,128)(2,1)}), bf16[8,128,256]{2,1,0:T(8,128)(2,1)S(1)}, u32[]{:S(2)}, u32[]{:S(2)}) async-start(bf16[8,128,256]{2,1,0:T(8,128)(2,1)} %broadcast_in_dim.12), calls=%async_computation.2 | async-start | bytes 1048576 | tf_op jit(solution)/shard_map/all_to_all | solution.py:252
  92.1 7.6 %collective-permute-start.9 = (bf16[8,32,512]{2,1,0:T(8,128)(2,1)S(1)}, bf16[8,32,512]{2,1,0:T(8,128)(2,1)S(1)}, u32[]{:S(2)}, u32[]{:S(2)}) collective-permute-start(bf16[8,32,512]{2,1,0:T(8,128)(2,1)S(1)} %bitcast.63), channel_id=1, source_target_pairs={{0,1},{1,0},{2,3},{3,2},{4,5},{5,4},{6,7},{7,6},{8,9},{9,8},{10,11... | collective-permute-start | bytes 786440 | tf_op jit(solution)/shard_map/ppermute | solution.py:34
  92.5 12.8 %collective-permute-start.8 = (bf16[8,32,512]{2,1,0:T(8,128)(2,1)S(1)}, bf16[8,32,512]{2,1,0:T(8,128)(2,1)S(1)}, u32[]{:S(2)}, u32[]{:S(2)}) collective-permute-start(bf16[8,32,512]{2,1,0:T(8,128)(2,1)S(1)} %bitcast.61), channel_id=1, source_target_pairs={{0,1},{1,0},{2,3},{3,2},{4,5},{5,4},{6,7},{7,6},{8,9},{9,8},{10,11... | collective-permute-start | bytes 786440 | tf_op jit(solution)/shard_map/ppermute | solution.py:34
  93.7 8.9 %collective-permute-start.12 = (bf16[8,32,512]{2,1,0:T(8,128)(2,1)S(1)}, bf16[8,32,512]{2,1,0:T(8,128)(2,1)S(1)}, u32[]{:S(2)}, u32[]{:S(2)}) collective-permute-start(bf16[8,32,512]{2,1,0:T(8,128)(2,1)S(1)} %bitcast.62), channel_id=1, source_target_pairs={{0,3},{1,2},{2,1},{3,0},{4,7},{5,6},{6,5},{7,4},{8,11},{9,10},{10,... | collective-permute-start | bytes 786440 | tf_op jit(solution)/shard_map/ppermute | solution.py:34
  99.8 7.1 %collective-permute-start.10 = (bf16[8,32,512]{2,1,0:T(8,128)(2,1)S(1)}, bf16[8,32,512]{2,1,0:T(8,128)(2,1)S(1)}, u32[]{:S(2)}, u32[]{:S(2)}) collective-permute-start(bf16[8,32,512]{2,1,0:T(8,128)(2,1)S(1)} %fusion.3), channel_id=1, source_target_pairs={{0,3},{1,2},{2,1},{3,0},{4,7},{5,6},{6,5},{7,4},{8,11},{9,10},{10,... | collective-permute-start | bytes 786440 | tf_op jit(solution)/shard_map/ppermute | solution.py:34
  101.7 10.8 %collective-permute-start.11 = (bf16[8,32,512]{2,1,0:T(8,128)(2,1)S(1)}, bf16[8,32,512]{2,1,0:T(8,128)(2,1)S(1)}, u32[]{:S(2)}, u32[]{:S(2)}) collective-permute-start(bf16[8,32,512]{2,1,0:T(8,128)(2,1)S(1)} %bitcast.60), channel_id=1, source_target_pairs={{0,3},{1,2},{2,1},{3,0},{4,7},{5,6},{6,5},{7,4},{8,11},{9,10},{10,... | collective-permute-start | bytes 786440 | tf_op jit(solution)/shard_map/ppermute | solution.py:34
  102.6 9.8 %collective-permute-start.13 = (bf16[8,32,512]{2,1,0:T(8,128)(2,1)S(1)}, bf16[8,32,512]{2,1,0:T(8,128)(2,1)S(1)}, u32[]{:S(2)}, u32[]{:S(2)}) collective-permute-start(bf16[8,32,512]{2,1,0:T(8,128)(2,1)S(1)} %fusion), channel_id=1, source_target_pairs={{0,1},{1,0},{2,3},{3,2},{4,5},{5,4},{6,7},{7,6},{8,9},{9,8},{10,11... | collective-permute-start | bytes 786440 | tf_op jit(solution)/shard_map/ppermute | solution.py:34
  113.4 20.8 %all-to-all-start.3 = ((bf16[8,64,512]{2,1,0:T(8,128)(2,1)}), bf16[8,64,512]{2,1,0:T(8,128)(2,1)S(1)}, u32[]{:S(2)}, u32[]{:S(2)}) async-start(bf16[8,64,512]{2,1,0:T(8,128)(2,1)} %pad_maximum_fusion.1), calls=%async_computation.3 | async-start | bytes 1048576 | tf_op jit(solution)/shard_map/all_to_all | solution.py:64
  150.0 6.5 %collective-permute-start.15 = (bf16[256,512]{1,0:T(8,128)(2,1)S(1)}, bf16[256,512]{1,0:T(8,128)(2,1)S(1)}, u32[]{:S(2)}, u32[]{:S(2)}) collective-permute-start(bf16[256,512]{1,0:T(8,128)(2,1)S(1)} %bitcast.52), channel_id=1, source_target_pairs={{0,3},{1,2},{2,1},{3,0},{4,7},{5,6},{6,5},{7,4},{8,11},{9,10},{10,... | collective-permute-start | bytes 786440 | tf_op jit(solution)/shard_map/ppermute | solution.py:34
  151.9 5.2 %collective-permute-start.17 = (bf16[256,512]{1,0:T(8,128)(2,1)S(1)}, bf16[256,512]{1,0:T(8,128)(2,1)S(1)}, u32[]{:S(2)}, u32[]{:S(2)}) collective-permute-start(bf16[256,512]{1,0:T(8,128)(2,1)S(1)} %bitcast.49), channel_id=1, source_target_pairs={{0,1},{1,0},{2,3},{3,2},{4,5},{5,4},{6,7},{7,6},{8,9},{9,8},{10,11... | collective-permute-start | bytes 786440 | tf_op jit(solution)/shard_map/ppermute | solution.py:34
  151.9 8.3 %collective-permute-start.14 = (bf16[256,512]{1,0:T(8,128)(2,1)S(1)}, bf16[256,512]{1,0:T(8,128)(2,1)S(1)}, u32[]{:S(2)}, u32[]{:S(2)}) collective-permute-start(bf16[256,512]{1,0:T(8,128)(2,1)S(1)} %bitcast.53), channel_id=1, source_target_pairs={{0,1},{1,0},{2,3},{3,2},{4,5},{5,4},{6,7},{7,6},{8,9},{9,8},{10,11... | collective-permute-start | bytes 786440 | tf_op jit(solution)/shard_map/ppermute | solution.py:34
  153.3 6.9 %collective-permute-start.19 = (bf16[256,512]{1,0:T(8,128)(2,1)S(1)}, bf16[256,512]{1,0:T(8,128)(2,1)S(1)}, u32[]{:S(2)}, u32[]{:S(2)}) collective-permute-start(bf16[256,512]{1,0:T(8,128)(2,1)S(1)} %bitcast.50), channel_id=1, source_target_pairs={{0,3},{1,2},{2,1},{3,0},{4,7},{5,6},{6,5},{7,4},{8,11},{9,10},{10,... | collective-permute-start | bytes 786440 | tf_op jit(solution)/shard_map/ppermute | solution.py:34
  156.5 8.7 %collective-permute-start.16 = (bf16[256,512]{1,0:T(8,128)(2,1)S(1)}, bf16[256,512]{1,0:T(8,128)(2,1)S(1)}, u32[]{:S(2)}, u32[]{:S(2)}) collective-permute-start(bf16[256,512]{1,0:T(8,128)(2,1)S(1)} %collective-permute-done.15.refs_3_), channel_id=1, source_target_pairs={{0,1},{1,0},{2,3},{3,2},{4,5},{5,4},{6,7},{7,6},{8,9},{9,8},{10,11... | collective-permute-start | bytes 786440 | tf_op jit(solution)/shard_map/ppermute | solution.py:34
  157.1 9.5 %collective-permute-start.18 = (bf16[256,512]{1,0:T(8,128)(2,1)S(1)}, bf16[256,512]{1,0:T(8,128)(2,1)S(1)}, u32[]{:S(2)}, u32[]{:S(2)}) collective-permute-start(bf16[256,512]{1,0:T(8,128)(2,1)S(1)} %collective-permute-done.17.refs_5_), channel_id=1, source_target_pairs={{0,3},{1,2},{2,1},{3,0},{4,7},{5,6},{6,5},{7,4},{8,11},{9,10},{10,... | collective-permute-start | bytes 786440 | tf_op jit(solution)/shard_map/ppermute | solution.py:34
  (14 other events, 173.2 us)

commit v7 on v6

--- a/solution.py
+++ b/solution.py
@@ -16,7 +16,6 @@
 ROWS = 1024
 COLS = 1024
 HALF = COLS // 2
-PARAMS = pltpu.CompilerParams(vmem_limit_bytes=32 * 1024 * 1024)
 
 
 def dot(a, b, dims):
@@ -39,10 +38,10 @@
     second_far = across(second[2], 3)
     first_near = across(first[1], 1)
     second_near = across(second[3], 3)
-    if tie:
-        first_far, second_far, *tie = lax.optimization_barrier((first_far, second_far, *tie))
     first_last = across(add(first[3], first_far), 3)
     second_last = across(add(second[1], second_far), 1)
+    if tie:
+        second_last, *tie = lax.optimization_barrier((second_last, *tie))
     return (
         add(first[0], first_near, first_last),
         add(second[0], second_near, second_last),
@@ -81,7 +80,7 @@
     return pl.BlockSpec(shape, lambda i, m: (0,) * len(shape))
 
 
-def call(kernel, in_specs, outs, flops, scratch=()):
+def call(kernel, in_specs, outs, flops, scratch=(), limit=32):
     return pl.pallas_call(
         kernel,
         grid_spec=pltpu.PrefetchScalarGridSpec(
@@ -92,7 +91,7 @@
             scratch_shapes=scratch,
         ),
         out_shape=outs,
-        compiler_params=PARAMS,
+        compiler_params=pltpu.CompilerParams(vmem_limit_bytes=limit << 20),
         cost_estimate=pl.CostEstimate(flops=flops, bytes_accessed=5 << 20, transcendentals=0),
     )
 
@@ -117,7 +116,7 @@
     outs = [jax.ShapeDtypeStruct((NZ, 64, 256), B16)] * NX
     scratch = [pltpu.VMEM((NZ, 256, 1024), B16), pltpu.SemaphoreType.DMA((NZ,))]
     specs = [whole(64, 256), pl.BlockSpec(memory_space=pltpu.HBM)]
-    return call(teacher_kernel, specs, outs, 2 * 64 * 256 * 8192, scratch)(place, rows, teacher_out)
+    return call(teacher_kernel, specs, outs, 2 * 64 * 256 * 8192, scratch, 57)(place, rows, teacher_out)
 
 
 def gather_hidden(place_ref, got_ref, hidden_ref):
@@ -125,10 +124,12 @@
     for g in range(4):
         near = pl.ds(pl.multiple_of(g * 128 + seq * 64, 64), 64)
         far = pl.ds(pl.multiple_of(g * 128 + 64 - seq * 64, 64), 64)
-        hidden_ref[near, 0:256] = got_ref[2 * g + seq, 0:64, :]
-        hidden_ref[far, 0:256] = got_ref[2 * g + seq, 64:128, :]
-        hidden_ref[far, 256:512] = got_ref[2 * g + 1 - seq, 0:64, :]
-        hidden_ref[near, 256:512] = got_ref[2 * g + 1 - seq, 64:128, :]
+        for c in range(2):
+            at, home, other = c * 128, slice(c * 128, c * 128 + 128), slice(256 + c * 128, 384 + c * 128)
+            hidden_ref[near, home] = got_ref[2 * g + seq, at : at + 64, :]
+            hidden_ref[far, home] = got_ref[2 * g + seq, at + 64 : at + 128, :]
+            hidden_ref[far, other] = got_ref[2 * g + 1 - seq, at : at + 64, :]
+            hidden_ref[near, other] = got_ref[2 * g + 1 - seq, at + 64 : at + 128, :]
 
 
 def combine_kernel(jobs, place_ref, picked_ref, got_ref, heads_ref, out_ref, home_ref, other_ref, *refs):
@@ -152,19 +153,19 @@
 KEPT = ((3, ((0, 1),)), (1, ((1, 3),)), (0, ((0, 0), (1, 2))))
 
 
-def combined_parts(jobs, place, picked, got, heads, out_cols, home, other):
+def combined_parts(jobs, place, picked, got, heads, student_out, projector, other):
     specs = [
         whole(NX, 1, 256),
-        whole(NY, 128, 256),
+        whole(NY, 432, 128),
         whole(NX, 256, 128),
-        whole(128, COLS),
-        whole(256, COLS),
+        pl.BlockSpec((128, COLS), lambda i, m: (0, m[0])),
+        pl.BlockSpec((256, COLS), lambda i, m: (0, m[0])),
         whole(256, COLS),
     ]
     outs = [jax.ShapeDtypeStruct((256, HALF), B16)] * 4
     return call(
-        functools.partial(combine_kernel, jobs), specs, outs, 2 * 512 * 1024 * 900, [pltpu.VMEM((512, 512), B16)]
-    )(place, picked, got, heads, out_cols, home, other)
+        functools.partial(combine_kernel, jobs), specs, outs, 2 * 512 * 1024 * 900, [pltpu.VMEM((512, 512), B16)], 57
+    )(place, picked, got, heads, student_out, projector, other)
 
 
 def final_kernel(place_ref, *refs):
@@ -194,15 +195,15 @@
     squares_ref[...] = lines.astype(B16)
 
 
-def final_parts(place, gathered, out_cols, heads):
-    specs = [whole(256, HALF)] * 8 + [whole(128, COLS), whole(NX, 256, 128)]
+def final_parts(place, gathered, student_out, heads):
+    specs = [whole(256, HALF)] * 8 + [pl.BlockSpec((128, COLS), lambda i, m: (0, m[0])), whole(NX, 256, 128)]
     outs = [
         jax.ShapeDtypeStruct((NX, 256, 128), B16),
         jax.ShapeDtypeStruct((16, 128), B16),
         jax.ShapeDtypeStruct((128, COLS), B16),
     ]
     return call(final_kernel, specs, outs, 2 * 1024 * 1024 * 256, [pltpu.VMEM((NX, 1, 128), F32)])(
-        place, *gathered, out_cols, heads
+        place, *gathered, student_out, heads
     )
 
 
@@ -222,39 +223,37 @@
     swap = [(0, 1), (1, 0)]
 
     there = lax.ppermute(teacher_heads, "seq", swap)
-    first = teacher_parts(place, teacher_heads, teacher_out)
-    second = teacher_parts(place, there, teacher_out)
-    *second, later = lax.optimization_barrier((*second, member))
-
-    own_matches = lax.dynamic_slice(matches, (later % 2 * 128,), (128,)).astype(B16)
-    shared = jnp.concatenate([student_heads, jnp.broadcast_to(own_matches[None], (16, 128))], axis=0)
-    resid_parts = jnp.transpose(student_resid.reshape(4, NY, 8, 128), (1, 0, 2, 3)).reshape(NY, 32, 128)
-    early = jnp.concatenate([jnp.broadcast_to(shared[None], (NY,) + shared.shape), resid_parts], axis=1)
-    early = lax.all_to_all(early, COLUMN, 0, 0)
-
+    first = list(teacher_parts(place, teacher_heads, teacher_out))
+    first[2], there = lax.optimization_barrier((first[2], there))
+    second = list(teacher_parts(place, there, teacher_out))
+
+    second[2], later = lax.optimization_barrier((second[2], member))
     away = lax.dynamic_slice(projector, (0, (later + 1 - 2 * seq) * COLS), (256, COLS))
     other = lax.ppermute(away, "seq", swap)
-    home = lax.dynamic_slice(projector, (0, later * COLS), (256, COLS))
-    out_cols = lax.dynamic_slice(student_out, (0, later * COLS), (128, COLS))
-
-    first, second, early = reduce_x(first, second, (early,))
+
+    first, second, other = reduce_x(first, second, (other,))
     moved = lax.all_to_all(jnp.concatenate([first, second], axis=1), "z", 0, 0)
-    moved, other = lax.optimization_barrier((moved, other))
-    heads = own_order(early[:, :128]).reshape(NX, 256, 128)
-    base = (jnp.arange(NY, dtype=jnp.int32) // 2 * 128)[:, None]
-    picked = own_order(early[:, 128].astype(jnp.int32) + base).reshape(NX, 1, 256)
-    resid = early[:, 144:].reshape(32, 2, HALF)
-    resid = jnp.concatenate([resid[:, 0], resid[:, 1]], axis=0)
     near = lax.dynamic_slice(teacher_resid, (seq * 64, 0), (64, 256))
     far = lax.dynamic_slice(teacher_resid, (64 - seq * 64, 0), (64, 256))
     hidden = (jnp.concatenate([near, far], axis=0).astype(F32) + jnp.sum(moved.astype(F32), axis=0)).astype(B16)
 
-    got = lax.all_to_all(jnp.broadcast_to(hidden[None], (NY, 128, 256)), COLUMN, 0, 0)
-    operands = (place, picked, got, heads, out_cols, home, other)
+    own_matches = lax.dynamic_slice(matches, (seq * 128,), (128,)).astype(B16)
+    shared = jnp.concatenate(
+        [hidden[:, :128], hidden[:, 128:], student_heads, jnp.broadcast_to(own_matches[None], (16, 128))], axis=0
+    )
+    resid_parts = jnp.transpose(student_resid.reshape(4, NY, 8, 128), (1, 0, 2, 3)).reshape(NY, 32, 128)
+    sent = jnp.concatenate([jnp.broadcast_to(shared[None], (NY,) + shared.shape), resid_parts], axis=1)
+    got = lax.all_to_all(sent, COLUMN, 0, 0)
+    heads = own_order(got[:, 256:384]).reshape(NX, 256, 128)
+    base = (jnp.arange(NY, dtype=jnp.int32) // 2 * 128)[:, None]
+    picked = own_order(got[:, 384].astype(jnp.int32) + base).reshape(NX, 1, 256)
+    operands = (place, picked, got, heads, student_out, projector, other)
     sent = combined_parts(SENT, *operands)
     kept = combined_parts(KEPT, *operands)
     sent = [part.reshape(NZ, 32, HALF) for part in sent]
     kept = [part.reshape(NZ, 32, HALF) for part in kept]
+    resid = got[:, 400:].reshape(32, 2, HALF)
+    resid = jnp.concatenate([resid[:, 0], resid[:, 1]], axis=0)
     first, second = reduce_x(
         (kept[0], sent[0], sent[1], kept[1]), (kept[2], kept[3], sent[2], sent[3])
     )
@@ -265,7 +264,7 @@
     tall = lax.all_to_all(jnp.broadcast_to(grad[None], (NZ, 64, HALF)), "z", 0, 0)
     gathered = gather_x(tall[:, :32].reshape(256, HALF), tall[:, 32:].reshape(256, HALF))
 
-    heads_part, squares, grad_weight = final_parts(place, gathered, out_cols, heads)
+    heads_part, squares, grad_weight = final_parts(place, gathered, student_out, heads)
     sent = jnp.concatenate(
         [block_order(heads_part.reshape(ROWS, 128)), jnp.broadcast_to(squares[None], (NY, 16, 128))], axis=1
     )

time: 192 us -> 185 us (0.964)
  local copies, waits for them, and re-layouts: 15.9 us -> 3.49 us
  Pallas kernels: 11.7 us -> 22 us
  starting transfers between devices: 52.4 us -> 44.2 us
  waiting for transfers between devices: 66.1 us -> 69.3 us
    all_to_all x1, waiting for transfers between devices: 0.01 us -> 14.1 us  [local(): moved = lax.all_to_all(jnp.concatenate([first, second], axis=1), 'z', 0, 0)]
    ppermute x18, waiting for transfers between devices: 35 us -> 25.4 us  [across(): return lax.ppermute(block, 'x', [(i, i ^ flip) for i in range(NX)])]
    unnamed x29 -> x32, local copies, waits for them, and re-layouts: 8.27 us -> 0.07 us
    ppermute x1, waiting for transfers between devices: 10.4 us -> 2.44 us  [local(): other = lax.ppermute(away, 'seq', swap)]
    all_to_all x2 -> x1, starting transfers between devices: 15 us -> 7.73 us  [local(): got = lax.all_to_all(sent, COLUMN, 0, 0)]
    all_to_all x2 -> x1, waiting for transfers between devices: 6.86 us -> 13.2 us  [local(): got = lax.all_to_all(sent, COLUMN, 0, 0)]
    pallas_call x2, Pallas kernels: 4.06 us -> 9.25 us  [combined_parts(): call(functools.partial(combine_kernel, jobs), specs, outs, 2 * 512 * 1024...]
    pallas_call x2, Pallas kernels: 5.37 us -> 10.5 us  [teacher_parts(): call(teacher_kernel, specs, outs, 2 * 64 * 256 * 8192, scratch, 57)]
  transfers between devices with their start and end apart: 24 -> 23, of which waited for: 18 -> 17; matrix products, arithmetic and copies ran while one was open for 5% -> 3% of each run, Pallas kernels for 2% -> 8%
where the time goes in v7:
time: 185 us; the launch traced here: 184 us
  waiting for transfers between devices  69.3 us (37%)
  starting transfers between devices  44.2 us (24%)
  blocking collectives  33.2 us (18%)
  Pallas kernels  22 us (12%)
  other arithmetic  9.39 us (5%)
  local copies, waits for them, and re-layouts  3.49 us (2%)
  between operations  2.78 us (2%)
    ppermute x18, waiting for transfers between devices, across(): return lax.ppermute(block, 'x', [(i, i ^ flip) for i in range(NX)])  25.4 us
    ppermute x18, starting transfers between devices, across(): return lax.ppermute(block, 'x', [(i, i ^ flip) for i in range(NX)])  20.8 us
    all_to_all x1, blocking collectives, local(): back = lax.all_to_all(sent, COLUMN, 0, 0).astype(F32)  17.8 us
    all_to_all x1, blocking collectives, local(): lax.all_to_all(jnp.broadcast_to(grad[None], (NZ, 64, HALF)), 'z', 0, 0)  15.4 us
    all_to_all x1, waiting for transfers between devices, reduce_z(): moved = lax.all_to_all(parts, 'z', 0, 0)  14.1 us
    all_to_all x1, waiting for transfers between devices, local(): moved = lax.all_to_all(jnp.concatenate([first, second], axis=1), 'z', 0, 0)  14.1 us
    all_to_all x1, waiting for transfers between devices, local(): got = lax.all_to_all(sent, COLUMN, 0, 0)  13.2 us
    pallas_call x2, Pallas kernels, teacher_parts(): call(teacher_kernel, specs, outs, 2 * 64 * 256 * 8192, scratch, 57)  10.5 us
  transfers between devices with their start and end apart: 23, of which 17 were waited for; matrix products, arithmetic and copies ran while one was open for 3% of the time, Pallas kernels for 8%

profile of v7, /device:TPU:1, one launch (start us, length us, event | category | flops | bytes accessed | tf_op | source)
XLA Modules:
  0.0 184.3 jit_solution(2353131310524652829)
XLA Ops:
  0.6 3.8 %collective-permute-start.1 = (bf16[64,256]{1,0:T(8,128)(2,1)}, bf16[64,256]{1,0:T(8,128)(2,1)S(1)}, u32[]{:S(2)}, u32[]{:S(2)}) collective-permute-start(bf16[64,256]{1,0:T(8,128)(2,1)} %rows_ref.1), channel_id=1, source_target_pairs={{0,32},{32,0},{1,33},{33,1},{2,34},{34,2},{3,35},{35,3},{4,36},{36... | collective-permute-start | bytes 98312 | tf_op jit(solution)/shard_map/ppermute | solution.py:225
  5.1 5.2 %shard_map.103 = (bf16[8,64,256]{2,1,0:T(8,128)(2,1)}, bf16[8,64,256]{2,1,0:T(8,128)(2,1)}, bf16[8,64,256]{2,1,0:T(8,128)(2,1)}, bf16[8,64,256]{2,1,0:T(8,128)(2,1)}) custom-call(s32[3]{0:T(128)} %pad_add_fusion.place_ref, bf16[64,256]{1,0:T(8,128)(2,1)} %rows_ref.1, bf16[256,8192]{1,0:T(8,128)(2,1)} %out_ref.5), custom_call_target="tpu_custom_call" | custom-call | flops 268435456 | bytes 5242880 | tf_op jit(solution)/shard_map/pallas_call | solution.py:119
  11.9 5.3 %shard_map.104 = (bf16[8,64,256]{2,1,0:T(8,128)(2,1)}, bf16[8,64,256]{2,1,0:T(8,128)(2,1)}, bf16[8,64,256]{2,1,0:T(8,128)(2,1)}, bf16[8,64,256]{2,1,0:T(8,128)(2,1)}) custom-call(s32[3]{0:T(128)} %pad_add_fusion.place_ref, bf16[64,256]{1,0:T(8,128)(2,1)} %copy-done.11, bf16[256,8192]{1,0:T(8,128)(2,1)} %out_ref.5), custom_call_target="tpu_custom_call" | custom-call | flops 268435456 | bytes 5242880 | tf_op jit(solution)/shard_map/pallas_call | solution.py:119
  17.2 2.6 %collective-permute-start.5 = (bf16[8,64,256]{2,1,0:T(8,128)(2,1)}, bf16[8,64,256]{2,1,0:T(8,128)(2,1)S(1)}, u32[]{:S(2)}, u32[]{:S(2)}) collective-permute-start(bf16[8,64,256]{2,1,0:T(8,128)(2,1)} %get-tuple-element.38), channel_id=1, source_target_pairs={{0,3},{1,2},{2,1},{3,0},{4,7},{5,6},{6,5},{7,4},{8,11},{9,10},{10,... | collective-permute-start | bytes 786440 | tf_op jit(solution)/shard_map/ppermute | solution.py:33
  21.3 3.7 %collective-permute-done.5 = bf16[8,64,256]{2,1,0:T(8,128)(2,1)S(1)} collective-permute-done((bf16[8,64,256]{2,1,0:T(8,128)(2,1)}, bf16[8,64,256]{2,1,0:T(8,128)(2,1)S(1)}, u32[]{:S(2)}, u32[]{:S(2)}) %collective-permute-start.5) | collective-permute-done | bytes 262176 | tf_op jit(solution)/shard_map/ppermute | solution.py:33
  26.1 2.6 %collective-permute-start.4 = (bf16[8,64,256]{2,1,0:T(8,128)(2,1)S(1)}, bf16[8,64,256]{2,1,0:T(8,128)(2,1)S(1)}, u32[]{:S(2)}, u32[]{:S(2)}) collective-permute-start(bf16[8,64,256]{2,1,0:T(8,128)(2,1)S(1)} %copy-done.13), channel_id=1, source_target_pairs={{0,3},{1,2},{2,1},{3,0},{4,7},{5,6},{6,5},{7,4},{8,11},{9,10},{10,... | collective-permute-start | bytes 786440 | tf_op jit(solution)/shard_map/ppermute | solution.py:33
  31.6 2.4 %collective-permute-done.7.other_ref = bf16[256,1024]{1,0:T(8,128)(2,1)S(1)} collective-permute-done((bf16[256,1024]{1,0:T(8,128)(2,1)S(1)}, bf16[256,1024]{1,0:T(8,128)(2,1)S(1)}, u32[]{:S(2)}, u32[]{:S(2)}) %collective-permute-start.7) | collective-permute-done | bytes 524320 | tf_op jit(solution)/shard_map/ppermute | solution.py:232
  36.5 8.2 %all-to-all-start = ((bf16[8,128,256]{2,1,0:T(8,128)(2,1)}), bf16[8,128,256]{2,1,0:T(8,128)(2,1)S(1)}, u32[]{:S(2)}, u32[]{:S(2)}) async-start(bf16[8,128,256]{2,1,0:T(8,128)(2,1)} %pad_maximum_fusion.1), calls=%async_computation | async-start | bytes 1048576 | tf_op jit(solution)/shard_map/all_to_all | solution.py:235
  44.8 14.1 %all-to-all-done = bf16[8,128,256]{2,1,0:T(8,128)(2,1)S(1)} async-done(((bf16[8,128,256]{2,1,0:T(8,128)(2,1)}), bf16[8,128,256]{2,1,0:T(8,128)(2,1)S(1)}, u32[]{:S(2)}, u32[]{:S(2)}) %all-to-all-start) | async-done | bytes 524320 | tf_op jit(solution)/shard_map/all_to_all | solution.py:235
  60.2 7.7 %all-to-all-start.1 = ((bf16[8,432,128]{2,1,0:T(8,128)(2,1)}), bf16[8,432,128]{2,1,0:T(8,128)(2,1)S(1)}, u32[]{:S(2)}, u32[]{:S(2)}) async-start(bf16[8,432,128]{2,1,0:T(8,128)(2,1)} %pad_maximum_fusion), calls=%async_computation.1 | async-start | bytes 1769472 | tf_op jit(solution)/shard_map/all_to_all | solution.py:246
  67.9 13.2 %all-to-all-done.1.got_ref = bf16[8,432,128]{2,1,0:T(8,128)(2,1)S(1)} async-done(((bf16[8,432,128]{2,1,0:T(8,128)(2,1)}), bf16[8,432,128]{2,1,0:T(8,128)(2,1)S(1)}, u32[]{:S(2)}, u32[]{:S(2)}) %all-to-all-start.1) | async-done | bytes 884768 | tf_op jit(solution)/shard_map/all_to_all | solution.py:246
  83.1 4.6 %shard_map.106 = (bf16[256,512]{1,0:T(8,128)(2,1)}, bf16[256,512]{1,0:T(8,128)(2,1)}, bf16[256,512]{1,0:T(8,128)(2,1)}, bf16[256,512]{1,0:T(8,128)(2,1)}) custom-call(s32[3]{0:T(128)} %pad_add_fusion.place_ref, s32[4,1,256]{2,1,0:T(1,128)} %reshape_reshape.12.picked_ref, bf16[8,432,128]{2,1,0:T(8,128)(2,1)} %copy-done.3, bf16[4,256,128]{2,1,0:T(8,128)(2,1)} %bitcast.44, ...), custom_call_target="tpu_custom_call" | custom-call | flops 943718400 | bytes 5242880 | tf_op jit(solution)/shard_map/pallas_call | solution.py:166
  87.7 2.6 %collective-permute-start.12 = (bf16[8,32,512]{2,1,0:T(8,128)(2,1)}, bf16[8,32,512]{2,1,0:T(8,128)(2,1)S(1)}, u32[]{:S(2)}, u32[]{:S(2)}) collective-permute-start(bf16[8,32,512]{2,1,0:T(8,128)(2,1)} %bitcast.65), channel_id=1, source_target_pairs={{0,3},{1,2},{2,1},{3,0},{4,7},{5,6},{6,5},{7,4},{8,11},{9,10},{10,... | collective-permute-start | bytes 786440 | tf_op jit(solution)/shard_map/ppermute | solution.py:33
  90.4 4.7 %shard_map.105 = (bf16[256,512]{1,0:T(8,128)(2,1)}, bf16[256,512]{1,0:T(8,128)(2,1)}, bf16[256,512]{1,0:T(8,128)(2,1)}, bf16[256,512]{1,0:T(8,128)(2,1)}) custom-call(s32[3]{0:T(128)} %pad_add_fusion.place_ref, s32[4,1,256]{2,1,0:T(1,128)} %reshape_reshape.12.picked_ref, bf16[8,432,128]{2,1,0:T(8,128)(2,1)} %copy-done.3, bf16[4,256,128]{2,1,0:T(8,128)(2,1)} %bitcast.45, ...), custom_call_target="tpu_custom_call" | custom-call | flops 943718400 | bytes 5242880 | tf_op jit(solution)/shard_map/pallas_call | solution.py:166
  100.2 2.7 %collective-permute-start.10 = (bf16[8,32,512]{2,1,0:T(8,128)(2,1)S(1)}, bf16[8,32,512]{2,1,0:T(8,128)(2,1)S(1)}, u32[]{:S(2)}, u32[]{:S(2)}) collective-permute-start(bf16[8,32,512]{2,1,0:T(8,128)(2,1)S(1)} %fusion.3), channel_id=1, source_target_pairs={{0,3},{1,2},{2,1},{3,0},{4,7},{5,6},{6,5},{7,4},{8,11},{9,10},{10,... | collective-permute-start | bytes 786440 | tf_op jit(solution)/shard_map/ppermute | solution.py:33
  104.5 4.5 %collective-permute-done.8 = bf16[8,32,512]{2,1,0:T(8,128)(2,1)S(1)} collective-permute-done((bf16[8,32,512]{2,1,0:T(8,128)(2,1)S(1)}, bf16[8,32,512]{2,1,0:T(8,128)(2,1)S(1)}, u32[]{:S(2)}, u32[]{:S(2)}) %collective-permute-start.8) | collective-permute-done | bytes 262176 | tf_op jit(solution)/shard_map/ppermute | solution.py:33
  110.0 3.5 %all-to-all-start.2 = ((bf16[8,64,512]{2,1,0:T(8,128)(2,1)}), bf16[8,64,512]{2,1,0:T(8,128)(2,1)S(1)}, u32[]{:S(2)}, u32[]{:S(2)}) async-start(bf16[8,64,512]{2,1,0:T(8,128)(2,1)} %pad_maximum_fusion.2), calls=%async_computation.2 | async-start | bytes 1048576 | tf_op jit(solution)/shard_map/all_to_all | solution.py:63
  113.7 14.1 %all-to-all-done.2 = bf16[8,64,512]{2,1,0:T(8,128)(2,1)S(1)} async-done(((bf16[8,64,512]{2,1,0:T(8,128)(2,1)}), bf16[8,64,512]{2,1,0:T(8,128)(2,1)S(1)}, u32[]{:S(2)}, u32[]{:S(2)}) %all-to-all-start.2) | async-done | bytes 524320 | tf_op jit(solution)/shard_map/all_to_all | solution.py:63
  128.0 15.4 %all_to_all.25 = bf16[8,64,512]{2,1,0:T(8,128)(2,1)S(1)} all-to-all(bf16[8,64,512]{2,1,0:T(8,128)(2,1)S(1)} %broadcast_in_dim.10), channel_id=1, replica_groups=mesh['ylo'=2,'core'=2,'seq'=2,'z'=8,'x'=4] {'z'}, dimensions={0} | all-to-all | bytes 1048576 | tf_op jit(solution)/shard_map/all_to_all | solution.py:264
  143.4 2.7 %collective-permute-start.15 = (bf16[256,512]{1,0:T(8,128)(2,1)S(1)}, bf16[256,512]{1,0:T(8,128)(2,1)S(1)}, u32[]{:S(2)}, u32[]{:S(2)}) collective-permute-start(bf16[256,512]{1,0:T(8,128)(2,1)S(1)} %bitcast.50), channel_id=1, source_target_pairs={{0,3},{1,2},{2,1},{3,0},{4,7},{5,6},{6,5},{7,4},{8,11},{9,10},{10,... | collective-permute-start | bytes 786440 | tf_op jit(solution)/shard_map/ppermute | solution.py:33
  147.9 2.1 %collective-permute-done.15.refs_3_ = bf16[256,512]{1,0:T(8,128)(2,1)S(1)} collective-permute-done((bf16[256,512]{1,0:T(8,128)(2,1)S(1)}, bf16[256,512]{1,0:T(8,128)(2,1)S(1)}, u32[]{:S(2)}, u32[]{:S(2)}) %collective-permute-start.15) | collective-permute-done | bytes 262176 | tf_op jit(solution)/shard_map/ppermute | solution.py:33
  155.2 4.2 %collective-permute-done.16.refs_2_ = bf16[256,512]{1,0:T(8,128)(2,1)S(1)} collective-permute-done((bf16[256,512]{1,0:T(8,128)(2,1)S(1)}, bf16[256,512]{1,0:T(8,128)(2,1)S(1)}, u32[]{:S(2)}, u32[]{:S(2)}) %collective-permute-start.16) | collective-permute-done | bytes 262176 | tf_op jit(solution)/shard_map/ppermute | solution.py:33
  161.0 2.3 %shard_map.107 = (bf16[4,256,128]{2,1,0:T(8,128)(2,1)S(1)}, bf16[16,128]{1,0:T(8,128)(2,1)S(1)}, bf16[128,1024]{1,0:T(8,128)(2,1)}) custom-call(s32[3]{0:T(128)S(1)} %copy-done.2, bf16[256,512]{1,0:T(8,128)(2,1)S(1)} %bitcast.52, bf16[256,512]{1,0:T(8,128)(2,1)S(1)} %collective-permute-done.14.refs_1_, bf16[256,512]{1,0:T(8,128)(2,1)S(1)} %collective-permute-done.16.refs_2_, ...), custom_call_target="tpu_custom_call" | custom-call | flops 536870912 | bytes 5242880 | tf_op jit(solution)/shard_map/pallas_call | solution.py:205
  163.4 17.8 %all_to_all.26 = bf16[8,144,128]{2,1,0:T(8,128)(2,1)S(1)} all-to-all(bf16[8,144,128]{2,1,0:T(8,128)(2,1)S(1)} %copy.43), channel_id=1, replica_groups=mesh['ylo'=2,'core'=2,'seq'=2,'z'=8,'x'=4] {'ylo','core','seq'}, dimensions={0} | all-to-all | bytes 589824 | tf_op jit(solution)/shard_map/all_to_all | solution.py:271
  (107 shorter events, 31.5 us)
Async XLA Ops:
  0.6 9.7 %collective-permute-start.1 = (bf16[64,256]{1,0:T(8,128)(2,1)}, bf16[64,256]{1,0:T(8,128)(2,1)S(1)}, u32[]{:S(2)}, u32[]{:S(2)}) collective-permute-start(bf16[64,256]{1,0:T(8,128)(2,1)} %rows_ref.1), channel_id=1, source_target_pairs={{0,32},{32,0},{1,33},{33,1},{2,34},{34,2},{3,35},{35,3},{4,36},{36... | collective-permute-start | bytes 98312 | tf_op jit(solution)/shard_map/ppermute | solution.py:225
  10.3 10.7 %collective-permute-start.2 = (bf16[8,64,256]{2,1,0:T(8,128)(2,1)}, bf16[8,64,256]{2,1,0:T(8,128)(2,1)S(1)}, u32[]{:S(2)}, u32[]{:S(2)}) collective-permute-start(bf16[8,64,256]{2,1,0:T(8,128)(2,1)} %get-tuple-element.32), channel_id=1, source_target_pairs={{0,1},{1,0},{2,3},{3,2},{4,5},{5,4},{6,7},{7,6},{8,9},{9,8},{10,11... | collective-permute-start | bytes 786440 | tf_op jit(solution)/shard_map/ppermute | solution.py:33
  11.6 17.1 %collective-permute-start = (bf16[8,64,256]{2,1,0:T(8,128)(2,1)}, bf16[8,64,256]{2,1,0:T(8,128)(2,1)S(1)}, u32[]{:S(2)}, u32[]{:S(2)}) collective-permute-start(bf16[8,64,256]{2,1,0:T(8,128)(2,1)} %get-tuple-element.29), channel_id=1, source_target_pairs={{0,1},{1,0},{2,3},{3,2},{4,5},{5,4},{6,7},{7,6},{8,9},{9,8},{10,11... | collective-permute-start | bytes 786440 | tf_op jit(solution)/shard_map/ppermute | solution.py:33
  17.2 7.8 %collective-permute-start.5 = (bf16[8,64,256]{2,1,0:T(8,128)(2,1)}, bf16[8,64,256]{2,1,0:T(8,128)(2,1)S(1)}, u32[]{:S(2)}, u32[]{:S(2)}) collective-permute-start(bf16[8,64,256]{2,1,0:T(8,128)(2,1)} %get-tuple-element.38), channel_id=1, source_target_pairs={{0,3},{1,2},{2,1},{3,0},{4,7},{5,6},{6,5},{7,4},{8,11},{9,10},{10,... | collective-permute-start | bytes 786440 | tf_op jit(solution)/shard_map/ppermute | solution.py:33
  20.8 13.2 %collective-permute-start.7 = (bf16[256,1024]{1,0:T(8,128)(2,1)S(1)}, bf16[256,1024]{1,0:T(8,128)(2,1)S(1)}, u32[]{:S(2)}, u32[]{:S(2)}) collective-permute-start(bf16[256,1024]{1,0:T(8,128)(2,1)S(1)} %constant_dynamic-slice_fusion), channel_id=1, source_target_pairs={{0,32},{32,0},{1,33},{33,1},{2,34},{34,2},{3,35},{35,3},{4,36},{36... | collective-permute-start | bytes 1572872 | tf_op jit(solution)/shard_map/ppermute | solution.py:232
  21.0 9.7 %collective-permute-start.3 = (bf16[8,64,256]{2,1,0:T(8,128)(2,1)S(1)}, bf16[8,64,256]{2,1,0:T(8,128)(2,1)S(1)}, u32[]{:S(2)}, u32[]{:S(2)}) collective-permute-start(bf16[8,64,256]{2,1,0:T(8,128)(2,1)S(1)} %add_convert_fusion.3), channel_id=1, source_target_pairs={{0,3},{1,2},{2,1},{3,0},{4,7},{5,6},{6,5},{7,4},{8,11},{9,10},{10,... | collective-permute-start | bytes 786440 | tf_op jit(solution)/shard_map/ppermute | solution.py:33
  26.0 5.6 %collective-permute-start.6 = (bf16[8,64,256]{2,1,0:T(8,128)(2,1)S(1)}, bf16[8,64,256]{2,1,0:T(8,128)(2,1)S(1)}, u32[]{:S(2)}, u32[]{:S(2)}) collective-permute-start(bf16[8,64,256]{2,1,0:T(8,128)(2,1)S(1)} %add_convert_fusion.1), channel_id=1, source_target_pairs={{0,1},{1,0},{2,3},{3,2},{4,5},{5,4},{6,7},{7,6},{8,9},{9,8},{10,11... | collective-permute-start | bytes 786440 | tf_op jit(solution)/shard_map/ppermute | solution.py:33
  26.1 9.5 %collective-permute-start.4 = (bf16[8,64,256]{2,1,0:T(8,128)(2,1)S(1)}, bf16[8,64,256]{2,1,0:T(8,128)(2,1)S(1)}, u32[]{:S(2)}, u32[]{:S(2)}) collective-permute-start(bf16[8,64,256]{2,1,0:T(8,128)(2,1)S(1)} %copy-done.13), channel_id=1, source_target_pairs={{0,3},{1,2},{2,1},{3,0},{4,7},{5,6},{6,5},{7,4},{8,11},{9,10},{10,... | collective-permute-start | bytes 786440 | tf_op jit(solution)/shard_map/ppermute | solution.py:33
  36.5 22.4 %all-to-all-start = ((bf16[8,128,256]{2,1,0:T(8,128)(2,1)}), bf16[8,128,256]{2,1,0:T(8,128)(2,1)S(1)}, u32[]{:S(2)}, u32[]{:S(2)}) async-start(bf16[8,128,256]{2,1,0:T(8,128)(2,1)} %pad_maximum_fusion.1), calls=%async_computation | async-start | bytes 1048576 | tf_op jit(solution)/shard_map/all_to_all | solution.py:235
  60.2 21.0 %all-to-all-start.1 = ((bf16[8,432,128]{2,1,0:T(8,128)(2,1)}), bf16[8,432,128]{2,1,0:T(8,128)(2,1)S(1)}, u32[]{:S(2)}, u32[]{:S(2)}) async-start(bf16[8,432,128]{2,1,0:T(8,128)(2,1)} %pad_maximum_fusion), calls=%async_computation.1 | async-start | bytes 1769472 | tf_op jit(solution)/shard_map/all_to_all | solution.py:246
  87.7 8.9 %collective-permute-start.12 = (bf16[8,32,512]{2,1,0:T(8,128)(2,1)}, bf16[8,32,512]{2,1,0:T(8,128)(2,1)S(1)}, u32[]{:S(2)}, u32[]{:S(2)}) collective-permute-start(bf16[8,32,512]{2,1,0:T(8,128)(2,1)} %bitcast.65), channel_id=1, source_target_pairs={{0,3},{1,2},{2,1},{3,0},{4,7},{5,6},{6,5},{7,4},{8,11},{9,10},{10,... | collective-permute-start | bytes 786440 | tf_op jit(solution)/shard_map/ppermute | solution.py:33
  90.3 12.6 %collective-permute-start.11 = (bf16[8,32,512]{2,1,0:T(8,128)(2,1)}, bf16[8,32,512]{2,1,0:T(8,128)(2,1)S(1)}, u32[]{:S(2)}, u32[]{:S(2)}) collective-permute-start(bf16[8,32,512]{2,1,0:T(8,128)(2,1)} %bitcast.63), channel_id=1, source_target_pairs={{0,3},{1,2},{2,1},{3,0},{4,7},{5,6},{6,5},{7,4},{8,11},{9,10},{10,... | collective-permute-start | bytes 786440 | tf_op jit(solution)/shard_map/ppermute | solution.py:33
  90.4 8.8 %collective-permute-start.9 = (bf16[8,32,512]{2,1,0:T(8,128)(2,1)}, bf16[8,32,512]{2,1,0:T(8,128)(2,1)S(1)}, u32[]{:S(2)}, u32[]{:S(2)}) collective-permute-start(bf16[8,32,512]{2,1,0:T(8,128)(2,1)} %bitcast.64), channel_id=1, source_target_pairs={{0,1},{1,0},{2,3},{3,2},{4,5},{5,4},{6,7},{7,6},{8,9},{9,8},{10,11... | collective-permute-start | bytes 786440 | tf_op jit(solution)/shard_map/ppermute | solution.py:33
  97.6 5.8 %collective-permute-start.13 = (bf16[8,32,512]{2,1,0:T(8,128)(2,1)S(1)}, bf16[8,32,512]{2,1,0:T(8,128)(2,1)S(1)}, u32[]{:S(2)}, u32[]{:S(2)}) collective-permute-start(bf16[8,32,512]{2,1,0:T(8,128)(2,1)S(1)} %fusion), channel_id=1, source_target_pairs={{0,1},{1,0},{2,3},{3,2},{4,5},{5,4},{6,7},{7,6},{8,9},{9,8},{10,11... | collective-permute-start | bytes 786440 | tf_op jit(solution)/shard_map/ppermute | solution.py:33
  97.7 11.3 %collective-permute-start.8 = (bf16[8,32,512]{2,1,0:T(8,128)(2,1)S(1)}, bf16[8,32,512]{2,1,0:T(8,128)(2,1)S(1)}, u32[]{:S(2)}, u32[]{:S(2)}) collective-permute-start(bf16[8,32,512]{2,1,0:T(8,128)(2,1)S(1)} %bitcast.62), channel_id=1, source_target_pairs={{0,1},{1,0},{2,3},{3,2},{4,5},{5,4},{6,7},{7,6},{8,9},{9,8},{10,11... | collective-permute-start | bytes 786440 | tf_op jit(solution)/shard_map/ppermute | solution.py:33
  100.2 8.9 %collective-permute-start.10 = (bf16[8,32,512]{2,1,0:T(8,128)(2,1)S(1)}, bf16[8,32,512]{2,1,0:T(8,128)(2,1)S(1)}, u32[]{:S(2)}, u32[]{:S(2)}) collective-permute-start(bf16[8,32,512]{2,1,0:T(8,128)(2,1)S(1)} %fusion.3), channel_id=1, source_target_pairs={{0,3},{1,2},{2,1},{3,0},{4,7},{5,6},{6,5},{7,4},{8,11},{9,10},{10,... | collective-permute-start | bytes 786440 | tf_op jit(solution)/shard_map/ppermute | solution.py:33
  110.0 17.9 %all-to-all-start.2 = ((bf16[8,64,512]{2,1,0:T(8,128)(2,1)}), bf16[8,64,512]{2,1,0:T(8,128)(2,1)S(1)}, u32[]{:S(2)}, u32[]{:S(2)}) async-start(bf16[8,64,512]{2,1,0:T(8,128)(2,1)} %pad_maximum_fusion.2), calls=%async_computation.2 | async-start | bytes 1048576 | tf_op jit(solution)/shard_map/all_to_all | solution.py:63
  113.5 47.4 %copy-start = (bf16[128,8192]{1,0:T(8,128)(2,1)S(1)}, bf16[128,8192]{1,0:T(8,128)(2,1)}, u32[]{:S(2)}) copy-start(bf16[128,8192]{1,0:T(8,128)(2,1)} %refs_8_.1) | copy-start | bytes 6291460
  143.4 6.5 %collective-permute-start.15 = (bf16[256,512]{1,0:T(8,128)(2,1)S(1)}, bf16[256,512]{1,0:T(8,128)(2,1)S(1)}, u32[]{:S(2)}, u32[]{:S(2)}) collective-permute-start(bf16[256,512]{1,0:T(8,128)(2,1)S(1)} %bitcast.50), channel_id=1, source_target_pairs={{0,3},{1,2},{2,1},{3,0},{4,7},{5,6},{6,5},{7,4},{8,11},{9,10},{10,... | collective-permute-start | bytes 786440 | tf_op jit(solution)/shard_map/ppermute | solution.py:33
  146.2 5.2 %collective-permute-start.17 = (bf16[256,512]{1,0:T(8,128)(2,1)S(1)}, bf16[256,512]{1,0:T(8,128)(2,1)S(1)}, u32[]{:S(2)}, u32[]{:S(2)}) collective-permute-start(bf16[256,512]{1,0:T(8,128)(2,1)S(1)} %bitcast.47), channel_id=1, source_target_pairs={{0,1},{1,0},{2,3},{3,2},{4,5},{5,4},{6,7},{7,6},{8,9},{9,8},{10,11... | collective-permute-start | bytes 786440 | tf_op jit(solution)/shard_map/ppermute | solution.py:33
  147.1 7.4 %collective-permute-start.14 = (bf16[256,512]{1,0:T(8,128)(2,1)S(1)}, bf16[256,512]{1,0:T(8,128)(2,1)S(1)}, u32[]{:S(2)}, u32[]{:S(2)}) collective-permute-start(bf16[256,512]{1,0:T(8,128)(2,1)S(1)} %bitcast.51), channel_id=1, source_target_pairs={{0,1},{1,0},{2,3},{3,2},{4,5},{5,4},{6,7},{7,6},{8,9},{9,8},{10,11... | collective-permute-start | bytes 786440 | tf_op jit(solution)/shard_map/ppermute | solution.py:33
  147.6 7.6 %collective-permute-start.19 = (bf16[256,512]{1,0:T(8,128)(2,1)S(1)}, bf16[256,512]{1,0:T(8,128)(2,1)S(1)}, u32[]{:S(2)}, u32[]{:S(2)}) collective-permute-start(bf16[256,512]{1,0:T(8,128)(2,1)S(1)} %bitcast.48), channel_id=1, source_target_pairs={{0,3},{1,2},{2,1},{3,0},{4,7},{5,6},{6,5},{7,4},{8,11},{9,10},{10,... | collective-permute-start | bytes 786440 | tf_op jit(solution)/shard_map/ppermute | solution.py:33
  149.9 9.5 %collective-permute-start.16 = (bf16[256,512]{1,0:T(8,128)(2,1)S(1)}, bf16[256,512]{1,0:T(8,128)(2,1)S(1)}, u32[]{:S(2)}, u32[]{:S(2)}) collective-permute-start(bf16[256,512]{1,0:T(8,128)(2,1)S(1)} %collective-permute-done.15.refs_3_), channel_id=1, source_target_pairs={{0,1},{1,0},{2,3},{3,2},{4,5},{5,4},{6,7},{7,6},{8,9},{9,8},{10,11... | collective-permute-start | bytes 786440 | tf_op jit(solution)/shard_map/ppermute | solution.py:33
  151.4 9.6 %collective-permute-start.18 = (bf16[256,512]{1,0:T(8,128)(2,1)S(1)}, bf16[256,512]{1,0:T(8,128)(2,1)S(1)}, u32[]{:S(2)}, u32[]{:S(2)}) collective-permute-start(bf16[256,512]{1,0:T(8,128)(2,1)S(1)} %collective-permute-done.17.refs_5_), channel_id=1, source_target_pairs={{0,3},{1,2},{2,1},{3,0},{4,7},{5,6},{6,5},{7,4},{8,11},{9,10},{10,... | collective-permute-start | bytes 786440 | tf_op jit(solution)/shard_map/ppermute | solution.py:33
  (16 other events, 270.4 us)

commit v8 on v7

--- a/solution.py
+++ b/solution.py
@@ -33,7 +33,7 @@
     return lax.ppermute(block, "x", [(i, i ^ flip) for i in range(NX)])
 
 
-def reduce_x(first, second, tie=()):
+def reduce_x(place, first, second, tie=()):
     first_far = across(first[2], 1)
     second_far = across(second[2], 3)
     first_near = across(first[1], 1)
@@ -42,11 +42,7 @@
     second_last = across(add(second[1], second_far), 1)
     if tie:
         second_last, *tie = lax.optimization_barrier((second_last, *tie))
-    return (
-        add(first[0], first_near, first_last),
-        add(second[0], second_near, second_last),
-        *tie,
-    )
+    return (merge(place, first[0], first_near, first_last, second[0], second_near, second_last), *tie)
 
 
 def gather_x(first, second):
@@ -96,8 +92,13 @@
     )
 
 
-def teacher_kernel(place_ref, rows_ref, out_ref, *refs):
-    x = place_ref[2]
+def multiply(rows, weights, z, x, parts):
+    for k in range(NX):
+        columns = pl.ds(pl.multiple_of((k ^ x) * 256, 256), 256)
+        parts[k][z] = dot(rows, weights[z, :, columns], ((1,), (0,))).astype(B16)
+
+
+def own_kernel(place_ref, rows_ref, out_ref, *refs):
     parts, held, sems = refs[:NX], refs[NX], refs[NX + 1]
     copies = [
         pltpu.make_async_copy(out_ref.at[:, pl.ds(z * 1024, 1024)], held.at[z], sems.at[z]) for z in range(NZ)
@@ -107,16 +108,60 @@
     rows = rows_ref[...]
     for z in range(NZ):
         copies[z].wait()
-        for k in range(NX):
-            columns = pl.ds(pl.multiple_of((k ^ x) * 256, 256), 256)
-            parts[k][z] = dot(rows, held[z, :, columns], ((1,), (0,))).astype(B16)
-
-
-def teacher_parts(place, rows, teacher_out):
-    outs = [jax.ShapeDtypeStruct((NZ, 64, 256), B16)] * NX
-    scratch = [pltpu.VMEM((NZ, 256, 1024), B16), pltpu.SemaphoreType.DMA((NZ,))]
+        multiply(rows, held, z, place_ref[2], parts)
+
+
+def there_kernel(place_ref, rows_ref, held_ref, *parts):
+    rows = rows_ref[...]
+    for z in range(NZ):
+        multiply(rows, held_ref, z, place_ref[2], parts)
+
+
+PARTS = [jax.ShapeDtypeStruct((NZ, 64, 256), B16)] * NX
+
+
+def own_parts(place, rows, teacher_out):
     specs = [whole(64, 256), pl.BlockSpec(memory_space=pltpu.HBM)]
-    return call(teacher_kernel, specs, outs, 2 * 64 * 256 * 8192, scratch, 57)(place, rows, teacher_out)
+    outs = PARTS + [jax.ShapeDtypeStruct((NZ, 256, 1024), B16)]
+    *parts, held = call(own_kernel, specs, outs, 2 * 64 * 256 * 8192, [pltpu.SemaphoreType.DMA((NZ,))], 24)(
+        place, rows, teacher_out
+    )
+    return parts, held
+
+
+def there_parts(place, rows, held):
+    specs = [whole(64, 256), whole(NZ, 256, 1024)]
+    return list(call(there_kernel, specs, PARTS, 2 * 64 * 256 * 8192, (), 24)(place, rows, held))
+
+
+def merge_kernel(place_ref, *refs):
+    rows = refs[0].shape[1]
+    for half in range(2):
+        terms = refs[3 * half : 3 * half + 3]
+        total = terms[0][...].astype(F32) + terms[1][...].astype(F32) + terms[2][...].astype(F32)
+        refs[6][:, half * rows : (half + 1) * rows, :] = total.astype(B16)
+
+
+def merge(place, *terms):
+    n, rows, columns = terms[0].shape
+    outs = [jax.ShapeDtypeStruct((n, 2 * rows, columns), B16)]
+    return call(merge_kernel, [whole(n, rows, columns)] * 6, outs, 1 << 21, (), 16)(place, *terms)[0]
+
+
+def layout_kernel(place_ref, home_in, other_in, out_in, weights_ref, out_ref):
+    weights_ref[0:256, :] = home_in[...]
+    weights_ref[256:512, :] = other_in[...]
+    out_ref[...] = out_in[...]
+
+
+def layout(place, projector, other, student_out):
+    specs = [
+        pl.BlockSpec((256, COLS), lambda i, m: (0, m[0])),
+        whole(256, COLS),
+        pl.BlockSpec((128, COLS), lambda i, m: (0, m[0])),
+    ]
+    outs = [jax.ShapeDtypeStruct((512, COLS), B16), jax.ShapeDtypeStruct((128, COLS), B16)]
+    return call(layout_kernel, specs, outs, 1 << 21, (), 16)(place, projector, other, student_out)
 
 
 def gather_hidden(place_ref, got_ref, hidden_ref):
@@ -132,7 +177,7 @@
             hidden_ref[near, other] = got_ref[2 * g + 1 - seq, at + 64 : at + 128, :]
 
 
-def combine_kernel(jobs, place_ref, picked_ref, got_ref, heads_ref, out_ref, home_ref, other_ref, *refs):
+def combine_kernel(jobs, place_ref, picked_ref, got_ref, heads_ref, out_ref, weights_ref, *refs):
     x = place_ref[2]
     parts, hidden_ref = refs[:-1], refs[-1]
     gather_hidden(place_ref, got_ref, hidden_ref)
@@ -144,8 +189,7 @@
         for half, to in halves:
             columns = slice(half * HALF, (half + 1) * HALF)
             total = dot(heads, out_ref[:, columns], ((1,), (0,)))
-            total -= dot(selected[:, :256], home_ref[:, columns], ((1,), (0,)))
-            total -= dot(selected[:, 256:], other_ref[:, columns], ((1,), (0,)))
+            total -= dot(selected, weights_ref[:, columns], ((1,), (0,)))
             parts[to][...] = total.astype(B16)
 
 
@@ -153,19 +197,12 @@
 KEPT = ((3, ((0, 1),)), (1, ((1, 3),)), (0, ((0, 0), (1, 2))))
 
 
-def combined_parts(jobs, place, picked, got, heads, student_out, projector, other):
-    specs = [
-        whole(NX, 1, 256),
-        whole(NY, 432, 128),
-        whole(NX, 256, 128),
-        pl.BlockSpec((128, COLS), lambda i, m: (0, m[0])),
-        pl.BlockSpec((256, COLS), lambda i, m: (0, m[0])),
-        whole(256, COLS),
-    ]
+def combined_parts(jobs, place, picked, got, heads, out_cols, weights):
+    specs = [whole(NX, 1, 256), whole(NY, 432, 128), whole(NX, 256, 128), whole(128, COLS), whole(512, COLS)]
     outs = [jax.ShapeDtypeStruct((256, HALF), B16)] * 4
     return call(
-        functools.partial(combine_kernel, jobs), specs, outs, 2 * 512 * 1024 * 900, [pltpu.VMEM((512, 512), B16)], 57
-    )(place, picked, got, heads, student_out, projector, other)
+        functools.partial(combine_kernel, jobs), specs, outs, 2 * 512 * 1024 * 900, [pltpu.VMEM((512, 512), B16)], 24
+    )(place, picked, got, heads, out_cols, weights)
 
 
 def final_kernel(place_ref, *refs):
@@ -223,19 +260,21 @@
     swap = [(0, 1), (1, 0)]
 
     there = lax.ppermute(teacher_heads, "seq", swap)
-    first = list(teacher_parts(place, teacher_heads, teacher_out))
-    first[2], there = lax.optimization_barrier((first[2], there))
-    second = list(teacher_parts(place, there, teacher_out))
+    first, held = own_parts(place, teacher_heads, teacher_out)
+    second = there_parts(place, there, held)
 
     second[2], later = lax.optimization_barrier((second[2], member))
     away = lax.dynamic_slice(projector, (0, (later + 1 - 2 * seq) * COLS), (256, COLS))
     other = lax.ppermute(away, "seq", swap)
 
-    first, second, other = reduce_x(first, second, (other,))
-    moved = lax.all_to_all(jnp.concatenate([first, second], axis=1), "z", 0, 0)
+    summed, other = reduce_x(place, first, second, (other,))
+    moved = lax.all_to_all(summed, "z", 0, 0)
     near = lax.dynamic_slice(teacher_resid, (seq * 64, 0), (64, 256))
     far = lax.dynamic_slice(teacher_resid, (64 - seq * 64, 0), (64, 256))
     hidden = (jnp.concatenate([near, far], axis=0).astype(F32) + jnp.sum(moved.astype(F32), axis=0)).astype(B16)
+
+    spot, hidden = lax.optimization_barrier((place, hidden))
+    weights, out_cols = layout(spot, projector, other, student_out)
 
     own_matches = lax.dynamic_slice(matches, (seq * 128,), (128,)).astype(B16)
     shared = jnp.concatenate(
@@ -247,17 +286,17 @@
     heads = own_order(got[:, 256:384]).reshape(NX, 256, 128)
     base = (jnp.arange(NY, dtype=jnp.int32) // 2 * 128)[:, None]
     picked = own_order(got[:, 384].astype(jnp.int32) + base).reshape(NX, 1, 256)
-    operands = (place, picked, got, heads, student_out, projector, other)
+    operands = (place, picked, got, heads, out_cols, weights)
     sent = combined_parts(SENT, *operands)
     kept = combined_parts(KEPT, *operands)
     sent = [part.reshape(NZ, 32, HALF) for part in sent]
     kept = [part.reshape(NZ, 32, HALF) for part in kept]
     resid = got[:, 400:].reshape(32, 2, HALF)
     resid = jnp.concatenate([resid[:, 0], resid[:, 1]], axis=0)
-    first, second = reduce_x(
-        (kept[0], sent[0], sent[1], kept[1]), (kept[2], kept[3], sent[2], sent[3])
-    )
-    summed = reduce_z(jnp.concatenate([first, second], axis=1))
+    (summed,) = reduce_x(
+        place, (kept[0], sent[0], sent[1], kept[1]), (kept[2], kept[3], sent[2], sent[3])
+    )
+    summed = reduce_z(summed)
     difference = resid.astype(F32) + summed
     grad = (difference * 0.125).astype(B16)
 

time: 185 us -> 182 us (0.984)
  local copies, waits for them, and re-layouts: 3.49 us -> 14.4 us
  Pallas kernels: 22 us -> 14.1 us
  other arithmetic: 9.39 us -> 5.87 us
  starting transfers between devices: 44.2 us -> 41.2 us
    ppermute x18, waiting for transfers between devices: 25.4 us -> 37.8 us  [across(): return lax.ppermute(block, 'x', [(i, i ^ flip) for i in range(NX)])]
    unnamed x32 -> x26, local copies, waits for them, and re-layouts: 0.07 us -> 10.6 us
    ppermute x18, starting transfers between devices: 20.8 us -> 15 us  [across(): return lax.ppermute(block, 'x', [(i, i ^ flip) for i in range(NX)])]
    pallas_call x2, Pallas kernels: 9.25 us -> 4.08 us  [combined_parts(): call(functools.partial(combine_kernel, jobs), specs, outs, 2 * 512 * 1024...]
    all_to_all x1, waiting for transfers between devices: 13.2 us -> 8.75 us  [local(): got = lax.all_to_all(sent, COLUMN, 0, 0)]
    all_to_all x1, waiting for transfers between devices: 14.1 us -> 10.5 us  [local(): moved = lax.all_to_all(summed, 'z', 0, 0)]
    pallas_call x2 -> x5, Pallas kernels: 10.5 us -> 7.77 us  [the longest x2 3.05 us: merge(): call(merge_kernel, [whole(n, rows, columns)] * 6, outs, 1 << 21, (), 16)]
    ppermute x1, waiting for transfers between devices: 2.44 us -> 0.01 us  [local(): other = lax.ppermute(away, 'seq', swap)]
  transfers between devices with their start and end apart: 23 -> 23, of which waited for: 17 -> 16; matrix products, arithmetic and copies ran while one was open for 3% -> 3% of each run, Pallas kernels for 8% -> 3%
where the time goes in v8:
time: 182 us; the launch traced here: 181 us
  waiting for transfers between devices  69.8 us (38%)
  starting transfers between devices  41.2 us (23%)
  blocking collectives  33.1 us (18%)
  local copies, waits for them, and re-layouts  14.4 us (8%)
  Pallas kernels  14.1 us (8%)
  other arithmetic  5.87 us (3%)
  between operations  2.78 us (2%)
    ppermute x18, waiting for transfers between devices, across(): return lax.ppermute(block, 'x', [(i, i ^ flip) for i in range(NX)])  37.8 us
    all_to_all x1, blocking collectives, local(): back = lax.all_to_all(sent, COLUMN, 0, 0).astype(F32)  18.1 us
    ppermute x18, starting transfers between devices, across(): return lax.ppermute(block, 'x', [(i, i ^ flip) for i in range(NX)])  15 us
    all_to_all x1, blocking collectives, local(): lax.all_to_all(jnp.broadcast_to(grad[None], (NZ, 64, HALF)), 'z', 0, 0)  15 us
    all_to_all x1, waiting for transfers between devices, reduce_z(): moved = lax.all_to_all(parts, 'z', 0, 0)  12.6 us
    unnamed x26, local copies, waits for them, and re-layouts  10.6 us
    all_to_all x1, waiting for transfers between devices, local(): moved = lax.all_to_all(summed, 'z', 0, 0)  10.5 us
    all_to_all x1, starting transfers between devices, local(): got = lax.all_to_all(sent, COLUMN, 0, 0)  9.86 us
  transfers between devices with their start and end apart: 23, of which 16 were waited for; matrix products, arithmetic and copies ran while one was open for 3% of the time, Pallas kernels for 3%

profile of v8, /device:TPU:1, one launch (start us, length us, event | category | flops | bytes accessed | tf_op | source)
XLA Modules:
  0.0 181.1 jit_solution(7541001128596016849)
XLA Ops:
  0.6 3.8 %collective-permute-start.3 = (bf16[64,256]{1,0:T(8,128)(2,1)}, bf16[64,256]{1,0:T(8,128)(2,1)S(1)}, u32[]{:S(2)}, u32[]{:S(2)}) collective-permute-start(bf16[64,256]{1,0:T(8,128)(2,1)} %rows_ref.1), channel_id=1, source_target_pairs={{0,32},{32,0},{1,33},{33,1},{2,34},{34,2},{3,35},{35,3},{4,36},{36... | collective-permute-start | bytes 98312 | tf_op jit(solution)/shard_map/ppermute | solution.py:262
  4.5 2.2 %copy-done.2 = bf16[256,8192]{1,0:T(8,128)(2,1)S(1)} copy-done((bf16[256,8192]{1,0:T(8,128)(2,1)S(1)}, bf16[256,8192]{1,0:T(8,128)(2,1)}, u32[]{:S(2)}) %copy-start.2) | copy-done | bytes 4194328
  7.5 2.7 %shard_map.103 = (bf16[8,64,256]{2,1,0:T(8,128)(2,1)S(1)}, bf16[8,64,256]{2,1,0:T(8,128)(2,1)S(1)}, bf16[8,64,256]{2,1,0:T(8,128)(2,1)S(1)}, bf16[8,64,256]{2,1,0:T(8,128)(2,1)S(1)}, bf16[8,256,1024]{2,1,0:T(8,128)(2,1)S(1)}) custom-call(s32[3]{0:T(128)S(1)} %pad_add_fusion.place_ref, bf16[64,256]{1,0:T(8,128)(2,1)S(1)} %copy-done.5, ...), custom_call_target="tpu_custom_call" | custom-call | flops 268435456 | bytes 5242880 | tf_op jit(solution)/shard_map/pallas_call | solution.py:126
  11.6 2.6 %collective-permute-start.5 = (bf16[8,64,256]{2,1,0:T(8,128)(2,1)S(1)}, bf16[8,64,256]{2,1,0:T(8,128)(2,1)}, u32[]{:S(2)}, u32[]{:S(2)}) collective-permute-start(bf16[8,64,256]{2,1,0:T(8,128)(2,1)S(1)} %get-tuple-element.40), channel_id=1, source_target_pairs={{0,3},{1,2},{2,1},{3,0},{4,7},{5,6},{6,5},{7,4},{8,11},{9,10},{10,... | collective-permute-start | bytes 786440 | tf_op jit(solution)/shard_map/ppermute | solution.py:33
  17.1 2.8 %collective-permute-done.5 = bf16[8,64,256]{2,1,0:T(8,128)(2,1)} collective-permute-done((bf16[8,64,256]{2,1,0:T(8,128)(2,1)S(1)}, bf16[8,64,256]{2,1,0:T(8,128)(2,1)}, u32[]{:S(2)}, u32[]{:S(2)}) %collective-permute-start.5) | collective-permute-done | bytes 262176 | tf_op jit(solution)/shard_map/ppermute | solution.py:33
  21.0 5.5 %collective-permute-done.1 = bf16[8,64,256]{2,1,0:T(8,128)(2,1)} collective-permute-done((bf16[8,64,256]{2,1,0:T(8,128)(2,1)S(1)}, bf16[8,64,256]{2,1,0:T(8,128)(2,1)}, u32[]{:S(2)}, u32[]{:S(2)}) %collective-permute-start.1) | collective-permute-done | bytes 262176 | tf_op jit(solution)/shard_map/ppermute | solution.py:33
  27.8 4.2 %collective-permute-done.6.refs_5_ = bf16[8,64,256]{2,1,0:T(8,128)(2,1)S(1)} collective-permute-done((bf16[8,64,256]{2,1,0:T(8,128)(2,1)S(1)}, bf16[8,64,256]{2,1,0:T(8,128)(2,1)S(1)}, u32[]{:S(2)}, u32[]{:S(2)}) %collective-permute-start.6) | collective-permute-done | bytes 262176 | tf_op jit(solution)/shard_map/ppermute | solution.py:33
  36.5 8.2 %all-to-all-start = ((bf16[8,128,256]{2,1,0:T(8,128)(2,1)}), bf16[8,128,256]{2,1,0:T(8,128)(2,1)S(1)}, u32[]{:S(2)}, u32[]{:S(2)}) async-start(bf16[8,128,256]{2,1,0:T(8,128)(2,1)} %shard_map.105), calls=%async_computation | async-start | bytes 1048576 | tf_op jit(solution)/shard_map/all_to_all | solution.py:271
  46.4 10.5 %all-to-all-done = bf16[8,128,256]{2,1,0:T(8,128)(2,1)S(1)} async-done(((bf16[8,128,256]{2,1,0:T(8,128)(2,1)}), bf16[8,128,256]{2,1,0:T(8,128)(2,1)S(1)}, u32[]{:S(2)}, u32[]{:S(2)}) %all-to-all-start) | async-done | bytes 524320 | tf_op jit(solution)/shard_map/all_to_all | solution.py:271
  58.2 9.9 %all-to-all-start.1 = ((bf16[8,432,128]{2,1,0:T(8,128)(2,1)}), bf16[8,432,128]{2,1,0:T(8,128)(2,1)S(1)}, u32[]{:S(2)}, u32[]{:S(2)}) async-start(bf16[8,432,128]{2,1,0:T(8,128)(2,1)} %pad_maximum_fusion), calls=%async_computation.1 | async-start | bytes 1769472 | tf_op jit(solution)/shard_map/all_to_all | solution.py:285
  68.0 2.2 %copy-done.1 = bf16[256,8192]{1,0:T(8,128)(2,1)S(1)} copy-done((bf16[256,8192]{1,0:T(8,128)(2,1)S(1)}, bf16[256,8192]{1,0:T(8,128)(2,1)}, u32[]{:S(2)}) %copy-start.1) | copy-done | bytes 4194328
  72.5 8.7 %all-to-all-done.1.got_ref = bf16[8,432,128]{2,1,0:T(8,128)(2,1)S(1)} async-done(((bf16[8,432,128]{2,1,0:T(8,128)(2,1)}), bf16[8,432,128]{2,1,0:T(8,128)(2,1)S(1)}, u32[]{:S(2)}, u32[]{:S(2)}) %all-to-all-start.1) | async-done | bytes 884768 | tf_op jit(solution)/shard_map/all_to_all | solution.py:285
  84.1 2.0 %shard_map.108 = (bf16[256,512]{1,0:T(8,128)(2,1)S(1)}, bf16[256,512]{1,0:T(8,128)(2,1)S(1)}, bf16[256,512]{1,0:T(8,128)(2,1)S(1)}, bf16[256,512]{1,0:T(8,128)(2,1)S(1)}) custom-call(s32[3]{0:T(128)S(1)} %pad_add_fusion.place_ref, s32[4,1,256]{2,1,0:T(1,128)S(1)} %reshape_reshape.12.picked_ref, bf16[8,432,128]{2,1,0:T(8,128)(2,1)S(1)} %all-to-all-done.1.got_ref, ...), custom_call_target="tpu_custom_call" | custom-call | flops 943718400 | bytes 5242880 | tf_op jit(solution)/shard_map/pallas_call | solution.py:203
  88.0 2.4 %collective-permute-start.12 = (bf16[8,32,512]{2,1,0:T(8,128)(2,1)S(1)}, bf16[8,32,512]{2,1,0:T(8,128)(2,1)S(1)}, u32[]{:S(2)}, u32[]{:S(2)}) collective-permute-start(bf16[8,32,512]{2,1,0:T(8,128)(2,1)S(1)} %bitcast.58), channel_id=1, source_target_pairs={{0,3},{1,2},{2,1},{3,0},{4,7},{5,6},{6,5},{7,4},{8,11},{9,10},{10,... | collective-permute-start | bytes 786440 | tf_op jit(solution)/shard_map/ppermute | solution.py:33
  94.2 7.2 %collective-permute-done.12 = bf16[8,32,512]{2,1,0:T(8,128)(2,1)S(1)} collective-permute-done((bf16[8,32,512]{2,1,0:T(8,128)(2,1)S(1)}, bf16[8,32,512]{2,1,0:T(8,128)(2,1)S(1)}, u32[]{:S(2)}, u32[]{:S(2)}) %collective-permute-start.12) | collective-permute-done | bytes 262176 | tf_op jit(solution)/shard_map/ppermute | solution.py:33
  101.6 5.4 %collective-permute-done.10.refs_2_ = bf16[8,32,512]{2,1,0:T(8,128)(2,1)S(1)} collective-permute-done((bf16[8,32,512]{2,1,0:T(8,128)(2,1)S(1)}, bf16[8,32,512]{2,1,0:T(8,128)(2,1)S(1)}, u32[]{:S(2)}, u32[]{:S(2)}) %collective-permute-start.10) | collective-permute-done | bytes 262176 | tf_op jit(solution)/shard_map/ppermute | solution.py:33
  108.6 4.1 %all-to-all-start.2 = ((bf16[8,64,512]{2,1,0:T(8,128)(2,1)}), bf16[8,64,512]{2,1,0:T(8,128)(2,1)}, u32[]{:S(2)}, u32[]{:S(2)}) async-start(bf16[8,64,512]{2,1,0:T(8,128)(2,1)} %shard_map.109), calls=%async_computation.2 | async-start | bytes 1048576 | tf_op jit(solution)/shard_map/all_to_all | solution.py:59
  112.9 12.6 %all-to-all-done.2 = bf16[8,64,512]{2,1,0:T(8,128)(2,1)} async-done(((bf16[8,64,512]{2,1,0:T(8,128)(2,1)}), bf16[8,64,512]{2,1,0:T(8,128)(2,1)}, u32[]{:S(2)}, u32[]{:S(2)}) %all-to-all-start.2) | async-done | bytes 524320 | tf_op jit(solution)/shard_map/all_to_all | solution.py:59
  126.8 15.0 %all_to_all.25 = bf16[8,64,512]{2,1,0:T(8,128)(2,1)S(1)} all-to-all(bf16[8,64,512]{2,1,0:T(8,128)(2,1)S(1)} %broadcast_in_dim.10), channel_id=1, replica_groups=mesh['ylo'=2,'core'=2,'seq'=2,'z'=8,'x'=4] {'z'}, dimensions={0} | all-to-all | bytes 1048576 | tf_op jit(solution)/shard_map/all_to_all | solution.py:303
  143.7 2.4 %collective-permute-start.19 = (bf16[256,512]{1,0:T(8,128)(2,1)S(1)}, bf16[256,512]{1,0:T(8,128)(2,1)S(1)}, u32[]{:S(2)}, u32[]{:S(2)}) collective-permute-start(bf16[256,512]{1,0:T(8,128)(2,1)S(1)} %bitcast.46), channel_id=1, source_target_pairs={{0,3},{1,2},{2,1},{3,0},{4,7},{5,6},{6,5},{7,4},{8,11},{9,10},{10,... | collective-permute-start | bytes 786440 | tf_op jit(solution)/shard_map/ppermute | solution.py:33
  146.0 2.3 %collective-permute-done.15.refs_3_ = bf16[256,512]{1,0:T(8,128)(2,1)S(1)} collective-permute-done((bf16[256,512]{1,0:T(8,128)(2,1)S(1)}, bf16[256,512]{1,0:T(8,128)(2,1)S(1)}, u32[]{:S(2)}, u32[]{:S(2)}) %collective-permute-start.15) | collective-permute-done | bytes 262176 | tf_op jit(solution)/shard_map/ppermute | solution.py:33
  151.1 4.5 %collective-permute-done.16.refs_2_ = bf16[256,512]{1,0:T(8,128)(2,1)S(1)} collective-permute-done((bf16[256,512]{1,0:T(8,128)(2,1)S(1)}, bf16[256,512]{1,0:T(8,128)(2,1)S(1)}, u32[]{:S(2)}, u32[]{:S(2)}) %collective-permute-start.16) | collective-permute-done | bytes 262176 | tf_op jit(solution)/shard_map/ppermute | solution.py:33
  157.5 2.2 %shard_map.110 = (bf16[4,256,128]{2,1,0:T(8,128)(2,1)S(1)}, bf16[16,128]{1,0:T(8,128)(2,1)S(1)}, bf16[128,1024]{1,0:T(8,128)(2,1)}) custom-call(s32[3]{0:T(128)S(1)} %pad_add_fusion.place_ref, bf16[256,512]{1,0:T(8,128)(2,1)S(1)} %bitcast.50, bf16[256,512]{1,0:T(8,128)(2,1)S(1)} %collective-permute-done.14.refs_1_, ...), custom_call_target="tpu_custom_call" | custom-call | flops 536870912 | bytes 5242880 | tf_op jit(solution)/shard_map/pallas_call | solution.py:242
  159.9 18.1 %all_to_all.26 = bf16[8,144,128]{2,1,0:T(8,128)(2,1)S(1)} all-to-all(bf16[8,144,128]{2,1,0:T(8,128)(2,1)S(1)} %copy.43), channel_id=1, replica_groups=mesh['ylo'=2,'core'=2,'seq'=2,'z'=8,'x'=4] {'ylo','core','seq'}, dimensions={0} | all-to-all | bytes 589824 | tf_op jit(solution)/shard_map/all_to_all | solution.py:310
  (97 shorter events, 36.8 us)
Async XLA Ops:
  0.6 9.6 %collective-permute-start.3 = (bf16[64,256]{1,0:T(8,128)(2,1)}, bf16[64,256]{1,0:T(8,128)(2,1)S(1)}, u32[]{:S(2)}, u32[]{:S(2)}) collective-permute-start(bf16[64,256]{1,0:T(8,128)(2,1)} %rows_ref.1), channel_id=1, source_target_pairs={{0,32},{32,0},{1,33},{33,1},{2,34},{34,2},{3,35},{35,3},{4,36},{36... | collective-permute-start | bytes 98312 | tf_op jit(solution)/shard_map/ppermute | solution.py:262
  11.6 45.4 %copy-start.11 = (bf16[128,128]{1,0:T(8,128)(2,1)S(1)}, bf16[128,128]{1,0:T(8,128)(2,1)}, u32[]{:S(2)}) copy-start(bf16[128,128]{1,0:T(8,128)(2,1)} %param.13) | copy-start | bytes 98308
  11.6 8.3 %collective-permute-start.5 = (bf16[8,64,256]{2,1,0:T(8,128)(2,1)S(1)}, bf16[8,64,256]{2,1,0:T(8,128)(2,1)}, u32[]{:S(2)}, u32[]{:S(2)}) collective-permute-start(bf16[8,64,256]{2,1,0:T(8,128)(2,1)S(1)} %get-tuple-element.40), channel_id=1, source_target_pairs={{0,3},{1,2},{2,1},{3,0},{4,7},{5,6},{6,5},{7,4},{8,11},{9,10},{10,... | collective-permute-start | bytes 786440 | tf_op jit(solution)/shard_map/ppermute | solution.py:33
  14.2 17.8 %collective-permute-start = (bf16[8,64,256]{2,1,0:T(8,128)(2,1)S(1)}, bf16[8,64,256]{2,1,0:T(8,128)(2,1)S(1)}, u32[]{:S(2)}, u32[]{:S(2)}) collective-permute-start(bf16[8,64,256]{2,1,0:T(8,128)(2,1)S(1)} %get-tuple-element.32), channel_id=1, source_target_pairs={{0,1},{1,0},{2,3},{3,2},{4,5},{5,4},{6,7},{7,6},{8,9},{9,8},{10,11... | collective-permute-start | bytes 786440 | tf_op jit(solution)/shard_map/ppermute | solution.py:33
  14.2 12.3 %collective-permute-start.1 = (bf16[8,64,256]{2,1,0:T(8,128)(2,1)S(1)}, bf16[8,64,256]{2,1,0:T(8,128)(2,1)}, u32[]{:S(2)}, u32[]{:S(2)}) collective-permute-start(bf16[8,64,256]{2,1,0:T(8,128)(2,1)S(1)} %get-tuple-element.34), channel_id=1, source_target_pairs={{0,1},{1,0},{2,3},{3,2},{4,5},{5,4},{6,7},{7,6},{8,9},{9,8},{10,11... | collective-permute-start | bytes 786440 | tf_op jit(solution)/shard_map/ppermute | solution.py:33
  15.7 16.3 %collective-permute-start.4 = (bf16[8,64,256]{2,1,0:T(8,128)(2,1)S(1)}, bf16[8,64,256]{2,1,0:T(8,128)(2,1)S(1)}, u32[]{:S(2)}, u32[]{:S(2)}) collective-permute-start(bf16[8,64,256]{2,1,0:T(8,128)(2,1)S(1)} %get-tuple-element.37), channel_id=1, source_target_pairs={{0,3},{1,2},{2,1},{3,0},{4,7},{5,6},{6,5},{7,4},{8,11},{9,10},{10,... | collective-permute-start | bytes 786440 | tf_op jit(solution)/shard_map/ppermute | solution.py:33
  16.9 15.1 %collective-permute-start.7 = (bf16[256,1024]{1,0:T(8,128)(2,1)S(1)}, bf16[256,1024]{1,0:T(8,128)(2,1)S(1)}, u32[]{:S(2)}, u32[]{:S(2)}) collective-permute-start(bf16[256,1024]{1,0:T(8,128)(2,1)S(1)} %constant_dynamic-slice_fusion), channel_id=1, source_target_pairs={{0,32},{32,0},{1,33},{33,1},{2,34},{34,2},{3,35},{35,3},{4,36},{36... | collective-permute-start | bytes 1572872 | tf_op jit(solution)/shard_map/ppermute | solution.py:268
  20.9 11.1 %collective-permute-start.6 = (bf16[8,64,256]{2,1,0:T(8,128)(2,1)S(1)}, bf16[8,64,256]{2,1,0:T(8,128)(2,1)S(1)}, u32[]{:S(2)}, u32[]{:S(2)}) collective-permute-start(bf16[8,64,256]{2,1,0:T(8,128)(2,1)S(1)} %add_convert_fusion), channel_id=1, source_target_pairs={{0,1},{1,0},{2,3},{3,2},{4,5},{5,4},{6,7},{7,6},{8,9},{9,8},{10,11... | collective-permute-start | bytes 786440 | tf_op jit(solution)/shard_map/ppermute | solution.py:33
  27.5 6.5 %collective-permute-start.2 = (bf16[8,64,256]{2,1,0:T(8,128)(2,1)S(1)}, bf16[8,64,256]{2,1,0:T(8,128)(2,1)S(1)}, u32[]{:S(2)}, u32[]{:S(2)}) collective-permute-start(bf16[8,64,256]{2,1,0:T(8,128)(2,1)S(1)} %add_convert_fusion.1), channel_id=1, source_target_pairs={{0,3},{1,2},{2,1},{3,0},{4,7},{5,6},{6,5},{7,4},{8,11},{9,10},{10,... | collective-permute-start | bytes 786440 | tf_op jit(solution)/shard_map/ppermute | solution.py:33
  36.5 20.4 %all-to-all-start = ((bf16[8,128,256]{2,1,0:T(8,128)(2,1)}), bf16[8,128,256]{2,1,0:T(8,128)(2,1)S(1)}, u32[]{:S(2)}, u32[]{:S(2)}) async-start(bf16[8,128,256]{2,1,0:T(8,128)(2,1)} %shard_map.105), calls=%async_computation | async-start | bytes 1048576 | tf_op jit(solution)/shard_map/all_to_all | solution.py:271
  58.2 23.1 %all-to-all-start.1 = ((bf16[8,432,128]{2,1,0:T(8,128)(2,1)}), bf16[8,432,128]{2,1,0:T(8,128)(2,1)S(1)}, u32[]{:S(2)}, u32[]{:S(2)}) async-start(bf16[8,432,128]{2,1,0:T(8,128)(2,1)} %pad_maximum_fusion), calls=%async_computation.1 | async-start | bytes 1769472 | tf_op jit(solution)/shard_map/all_to_all | solution.py:285
  86.1 7.6 %collective-permute-start.9 = (bf16[8,32,512]{2,1,0:T(8,128)(2,1)S(1)}, bf16[8,32,512]{2,1,0:T(8,128)(2,1)S(1)}, u32[]{:S(2)}, u32[]{:S(2)}) collective-permute-start(bf16[8,32,512]{2,1,0:T(8,128)(2,1)S(1)} %bitcast.59), channel_id=1, source_target_pairs={{0,1},{1,0},{2,3},{3,2},{4,5},{5,4},{6,7},{7,6},{8,9},{9,8},{10,11... | collective-permute-start | bytes 786440 | tf_op jit(solution)/shard_map/ppermute | solution.py:33
  86.2 15.3 %collective-permute-start.8 = (bf16[8,32,512]{2,1,0:T(8,128)(2,1)S(1)}, bf16[8,32,512]{2,1,0:T(8,128)(2,1)S(1)}, u32[]{:S(2)}, u32[]{:S(2)}) collective-permute-start(bf16[8,32,512]{2,1,0:T(8,128)(2,1)S(1)} %bitcast.57), channel_id=1, source_target_pairs={{0,1},{1,0},{2,3},{3,2},{4,5},{5,4},{6,7},{7,6},{8,9},{9,8},{10,11... | collective-permute-start | bytes 786440 | tf_op jit(solution)/shard_map/ppermute | solution.py:33
  87.7 13.9 %collective-permute-start.11 = (bf16[8,32,512]{2,1,0:T(8,128)(2,1)S(1)}, bf16[8,32,512]{2,1,0:T(8,128)(2,1)S(1)}, u32[]{:S(2)}, u32[]{:S(2)}) collective-permute-start(bf16[8,32,512]{2,1,0:T(8,128)(2,1)S(1)} %bitcast.56), channel_id=1, source_target_pairs={{0,3},{1,2},{2,1},{3,0},{4,7},{5,6},{6,5},{7,4},{8,11},{9,10},{10,... | collective-permute-start | bytes 786440 | tf_op jit(solution)/shard_map/ppermute | solution.py:33
  88.0 13.4 %collective-permute-start.12 = (bf16[8,32,512]{2,1,0:T(8,128)(2,1)S(1)}, bf16[8,32,512]{2,1,0:T(8,128)(2,1)S(1)}, u32[]{:S(2)}, u32[]{:S(2)}) collective-permute-start(bf16[8,32,512]{2,1,0:T(8,128)(2,1)S(1)} %bitcast.58), channel_id=1, source_target_pairs={{0,3},{1,2},{2,1},{3,0},{4,7},{5,6},{6,5},{7,4},{8,11},{9,10},{10,... | collective-permute-start | bytes 786440 | tf_op jit(solution)/shard_map/ppermute | solution.py:33
  93.8 13.2 %collective-permute-start.10 = (bf16[8,32,512]{2,1,0:T(8,128)(2,1)S(1)}, bf16[8,32,512]{2,1,0:T(8,128)(2,1)S(1)}, u32[]{:S(2)}, u32[]{:S(2)}) collective-permute-start(bf16[8,32,512]{2,1,0:T(8,128)(2,1)S(1)} %fusion.1), channel_id=1, source_target_pairs={{0,3},{1,2},{2,1},{3,0},{4,7},{5,6},{6,5},{7,4},{8,11},{9,10},{10,... | collective-permute-start | bytes 786440 | tf_op jit(solution)/shard_map/ppermute | solution.py:33
  101.5 5.6 %collective-permute-start.13 = (bf16[8,32,512]{2,1,0:T(8,128)(2,1)S(1)}, bf16[8,32,512]{2,1,0:T(8,128)(2,1)S(1)}, u32[]{:S(2)}, u32[]{:S(2)}) collective-permute-start(bf16[8,32,512]{2,1,0:T(8,128)(2,1)S(1)} %fusion), channel_id=1, source_target_pairs={{0,1},{1,0},{2,3},{3,2},{4,5},{5,4},{6,7},{7,6},{8,9},{9,8},{10,11... | collective-permute-start | bytes 786440 | tf_op jit(solution)/shard_map/ppermute | solution.py:33
  108.6 17.0 %all-to-all-start.2 = ((bf16[8,64,512]{2,1,0:T(8,128)(2,1)}), bf16[8,64,512]{2,1,0:T(8,128)(2,1)}, u32[]{:S(2)}, u32[]{:S(2)}) async-start(bf16[8,64,512]{2,1,0:T(8,128)(2,1)} %shard_map.109), calls=%async_computation.2 | async-start | bytes 1048576 | tf_op jit(solution)/shard_map/all_to_all | solution.py:59
  141.8 6.5 %collective-permute-start.15 = (bf16[256,512]{1,0:T(8,128)(2,1)S(1)}, bf16[256,512]{1,0:T(8,128)(2,1)S(1)}, u32[]{:S(2)}, u32[]{:S(2)}) collective-permute-start(bf16[256,512]{1,0:T(8,128)(2,1)S(1)} %bitcast.48), channel_id=1, source_target_pairs={{0,3},{1,2},{2,1},{3,0},{4,7},{5,6},{6,5},{7,4},{8,11},{9,10},{10,... | collective-permute-start | bytes 786440 | tf_op jit(solution)/shard_map/ppermute | solution.py:33
  142.2 6.1 %collective-permute-start.17 = (bf16[256,512]{1,0:T(8,128)(2,1)S(1)}, bf16[256,512]{1,0:T(8,128)(2,1)S(1)}, u32[]{:S(2)}, u32[]{:S(2)}) collective-permute-start(bf16[256,512]{1,0:T(8,128)(2,1)S(1)} %bitcast.45), channel_id=1, source_target_pairs={{0,1},{1,0},{2,3},{3,2},{4,5},{5,4},{6,7},{7,6},{8,9},{9,8},{10,11... | collective-permute-start | bytes 786440 | tf_op jit(solution)/shard_map/ppermute | solution.py:33
  142.2 8.0 %collective-permute-start.14 = (bf16[256,512]{1,0:T(8,128)(2,1)S(1)}, bf16[256,512]{1,0:T(8,128)(2,1)S(1)}, u32[]{:S(2)}, u32[]{:S(2)}) collective-permute-start(bf16[256,512]{1,0:T(8,128)(2,1)S(1)} %bitcast.49), channel_id=1, source_target_pairs={{0,1},{1,0},{2,3},{3,2},{4,5},{5,4},{6,7},{7,6},{8,9},{9,8},{10,11... | collective-permute-start | bytes 786440 | tf_op jit(solution)/shard_map/ppermute | solution.py:33
  143.7 7.5 %collective-permute-start.19 = (bf16[256,512]{1,0:T(8,128)(2,1)S(1)}, bf16[256,512]{1,0:T(8,128)(2,1)S(1)}, u32[]{:S(2)}, u32[]{:S(2)}) collective-permute-start(bf16[256,512]{1,0:T(8,128)(2,1)S(1)} %bitcast.46), channel_id=1, source_target_pairs={{0,3},{1,2},{2,1},{3,0},{4,7},{5,6},{6,5},{7,4},{8,11},{9,10},{10,... | collective-permute-start | bytes 786440 | tf_op jit(solution)/shard_map/ppermute | solution.py:33
  148.3 7.3 %collective-permute-start.16 = (bf16[256,512]{1,0:T(8,128)(2,1)S(1)}, bf16[256,512]{1,0:T(8,128)(2,1)S(1)}, u32[]{:S(2)}, u32[]{:S(2)}) collective-permute-start(bf16[256,512]{1,0:T(8,128)(2,1)S(1)} %collective-permute-done.15.refs_3_), channel_id=1, source_target_pairs={{0,1},{1,0},{2,3},{3,2},{4,5},{5,4},{6,7},{7,6},{8,9},{9,8},{10,11... | collective-permute-start | bytes 786440 | tf_op jit(solution)/shard_map/ppermute | solution.py:33
  148.3 9.2 %collective-permute-start.18 = (bf16[256,512]{1,0:T(8,128)(2,1)S(1)}, bf16[256,512]{1,0:T(8,128)(2,1)S(1)}, u32[]{:S(2)}, u32[]{:S(2)}) collective-permute-start(bf16[256,512]{1,0:T(8,128)(2,1)S(1)} %collective-permute-done.17.refs_5_), channel_id=1, source_target_pairs={{0,3},{1,2},{2,1},{3,0},{4,7},{5,6},{6,5},{7,4},{8,11},{9,10},{10,... | collective-permute-start | bytes 786440 | tf_op jit(solution)/shard_map/ppermute | solution.py:33
  (12 other events, 86.8 us)

commit v9 on v8

--- a/solution.py
+++ b/solution.py
@@ -33,16 +33,22 @@
     return lax.ppermute(block, "x", [(i, i ^ flip) for i in range(NX)])
 
 
-def reduce_x(place, first, second, tie=()):
+def reduce_x(first, second, before, tie=()):
     first_far = across(first[2], 1)
     second_far = across(second[2], 3)
-    first_near = across(first[1], 1)
-    second_near = across(second[3], 3)
+    first_near, second_near, *before = lax.optimization_barrier((first[1], second[3], *before))
+    first_near = across(first_near, 1)
+    second_near = across(second_near, 3)
     first_last = across(add(first[3], first_far), 3)
     second_last = across(add(second[1], second_far), 1)
     if tie:
         second_last, *tie = lax.optimization_barrier((second_last, *tie))
-    return (merge(place, first[0], first_near, first_last, second[0], second_near, second_last), *tie)
+    return (
+        jnp.concatenate(
+            [add(first[0], first_near, first_last), add(second[0], second_near, second_last)], axis=1
+        ),
+        *tie,
+    )
 
 
 def gather_x(first, second):
@@ -132,20 +138,6 @@
 def there_parts(place, rows, held):
     specs = [whole(64, 256), whole(NZ, 256, 1024)]
     return list(call(there_kernel, specs, PARTS, 2 * 64 * 256 * 8192, (), 24)(place, rows, held))
-
-
-def merge_kernel(place_ref, *refs):
-    rows = refs[0].shape[1]
-    for half in range(2):
-        terms = refs[3 * half : 3 * half + 3]
-        total = terms[0][...].astype(F32) + terms[1][...].astype(F32) + terms[2][...].astype(F32)
-        refs[6][:, half * rows : (half + 1) * rows, :] = total.astype(B16)
-
-
-def merge(place, *terms):
-    n, rows, columns = terms[0].shape
-    outs = [jax.ShapeDtypeStruct((n, 2 * rows, columns), B16)]
-    return call(merge_kernel, [whole(n, rows, columns)] * 6, outs, 1 << 21, (), 16)(place, *terms)[0]
 
 
 def layout_kernel(place_ref, home_in, other_in, out_in, weights_ref, out_ref):
@@ -193,15 +185,16 @@
             parts[to][...] = total.astype(B16)
 
 
-SENT = ((2, ((0, 1), (1, 2))), (1, ((0, 0),)), (3, ((1, 3),)))
-KEPT = ((3, ((0, 1),)), (1, ((1, 3),)), (0, ((0, 0), (1, 2))))
+FAR = ((2, ((0, 0), (1, 1))),)
+REST = ((1, ((0, 0), (1, 3))), (3, ((1, 4), (0, 1))), (0, ((0, 2), (1, 5))))
 
 
 def combined_parts(jobs, place, picked, got, heads, out_cols, weights):
     specs = [whole(NX, 1, 256), whole(NY, 432, 128), whole(NX, 256, 128), whole(128, COLS), whole(512, COLS)]
-    outs = [jax.ShapeDtypeStruct((256, HALF), B16)] * 4
+    count = sum(len(halves) for _, halves in jobs)
+    outs = [jax.ShapeDtypeStruct((256, HALF), B16)] * count
     return call(
-        functools.partial(combine_kernel, jobs), specs, outs, 2 * 512 * 1024 * 900, [pltpu.VMEM((512, 512), B16)], 24
+        functools.partial(combine_kernel, jobs), specs, outs, count * 2 * 256 * 512 * 900, [pltpu.VMEM((512, 512), B16)], 24
     )(place, picked, got, heads, out_cols, weights)
 
 
@@ -267,7 +260,7 @@
     away = lax.dynamic_slice(projector, (0, (later + 1 - 2 * seq) * COLS), (256, COLS))
     other = lax.ppermute(away, "seq", swap)
 
-    summed, other = reduce_x(place, first, second, (other,))
+    summed, other = reduce_x(first, second, (away,), (other,))
     moved = lax.all_to_all(summed, "z", 0, 0)
     near = lax.dynamic_slice(teacher_resid, (seq * 64, 0), (64, 256))
     far = lax.dynamic_slice(teacher_resid, (64 - seq * 64, 0), (64, 256))
@@ -287,15 +280,11 @@
     base = (jnp.arange(NY, dtype=jnp.int32) // 2 * 128)[:, None]
     picked = own_order(got[:, 384].astype(jnp.int32) + base).reshape(NX, 1, 256)
     operands = (place, picked, got, heads, out_cols, weights)
-    sent = combined_parts(SENT, *operands)
-    kept = combined_parts(KEPT, *operands)
-    sent = [part.reshape(NZ, 32, HALF) for part in sent]
-    kept = [part.reshape(NZ, 32, HALF) for part in kept]
+    far = [part.reshape(NZ, 32, HALF) for part in combined_parts(FAR, *operands)]
+    rest = [part.reshape(NZ, 32, HALF) for part in combined_parts(REST, *operands)]
     resid = got[:, 400:].reshape(32, 2, HALF)
     resid = jnp.concatenate([resid[:, 0], resid[:, 1]], axis=0)
-    (summed,) = reduce_x(
-        place, (kept[0], sent[0], sent[1], kept[1]), (kept[2], kept[3], sent[2], sent[3])
-    )
+    (summed,) = reduce_x((rest[2], rest[0], far[0], rest[1]), (rest[5], rest[3], far[1], rest[4]), ())
     summed = reduce_z(summed)
     difference = resid.astype(F32) + summed
     grad = (difference * 0.125).astype(B16)

time: 182 us -> 185 us (1.016)
  starting transfers between devices: 41.2 us -> 48.1 us
  Pallas kernels: 14.1 us -> 10.9 us
  waiting for transfers between devices: 69.8 us -> 67.7 us
    ppermute x18, waiting for transfers between devices: 37.8 us -> 30.5 us  [across(): return lax.ppermute(block, 'x', [(i, i ^ flip) for i in range(NX)])]
    ppermute x18, starting transfers between devices: 15 us -> 19.2 us  [across(): return lax.ppermute(block, 'x', [(i, i ^ flip) for i in range(NX)])]
    pallas_call x4 -> x2, Pallas kernels: 7.13 us -> 3.84 us  [combined_parts(): call(functools.partial(combine_kernel, jobs), specs, outs, count * 2 * 25...]
    ppermute x1, starting transfers between devices: 0.11 us -> 3 us  [local(): other = lax.ppermute(away, 'seq', swap)]
    unnamed x26 -> x28, local copies, waits for them, and re-layouts: 10.6 us -> 13.2 us
    all_to_all x1, waiting for transfers between devices: 10.5 us -> 12.8 us  [local(): moved = lax.all_to_all(summed, 'z', 0, 0)]
  transfers between devices with their start and end apart: 23 -> 23, of which waited for: 16 -> 16; matrix products, arithmetic and copies ran while one was open for 3% -> 1% of each run, Pallas kernels for 3% -> 2%
where the time goes in v9:
time: 185 us; the launch traced here: 184 us
  waiting for transfers between devices  67.7 us (37%)
  starting transfers between devices  48.1 us (26%)
  blocking collectives  33.1 us (18%)
  local copies, waits for them, and re-layouts  15.3 us (8%)
  Pallas kernels  10.9 us (6%)
  other arithmetic  6.08 us (3%)
  between operations  2.8 us (2%)
    ppermute x18, waiting for transfers between devices, across(): return lax.ppermute(block, 'x', [(i, i ^ flip) for i in range(NX)])  30.5 us
    ppermute x18, starting transfers between devices, across(): return lax.ppermute(block, 'x', [(i, i ^ flip) for i in range(NX)])  19.2 us
    all_to_all x1, blocking collectives, local(): back = lax.all_to_all(sent, COLUMN, 0, 0).astype(F32)  17.6 us
    all_to_all x1, blocking collectives, local(): lax.all_to_all(jnp.broadcast_to(grad[None], (NZ, 64, HALF)), 'z', 0, 0)  15.4 us
    all_to_all x1, waiting for transfers between devices, reduce_z(): moved = lax.all_to_all(parts, 'z', 0, 0)  14.3 us
    unnamed x28, local copies, waits for them, and re-layouts  13.2 us
    all_to_all x1, waiting for transfers between devices, local(): moved = lax.all_to_all(summed, 'z', 0, 0)  12.8 us
    all_to_all x1, starting transfers between devices, local(): got = lax.all_to_all(sent, COLUMN, 0, 0)  10.7 us
  transfers between devices with their start and end apart: 23, of which 16 were waited for; matrix products, arithmetic and copies ran while one was open for 1% of the time, Pallas kernels for 2%

profile of v9, /device:TPU:1, one launch (start us, length us, event | category | flops | bytes accessed | tf_op | source)
XLA Modules:
  0.0 183.9 jit_solution(8888938715287260562)
XLA Ops:
  0.7 2.2 %copy-done.2 = bf16[256,8192]{1,0:T(8,128)(2,1)S(1)} copy-done((bf16[256,8192]{1,0:T(8,128)(2,1)S(1)}, bf16[256,8192]{1,0:T(8,128)(2,1)}, u32[]{:S(2)}) %copy-start.2) | copy-done | bytes 4194328
  3.7 2.7 %shard_map.103 = (bf16[8,64,256]{2,1,0:T(8,128)(2,1)S(1)}, bf16[8,64,256]{2,1,0:T(8,128)(2,1)S(1)}, bf16[8,64,256]{2,1,0:T(8,128)(2,1)S(1)}, bf16[8,64,256]{2,1,0:T(8,128)(2,1)S(1)}, bf16[8,256,1024]{2,1,0:T(8,128)(2,1)S(1)}) custom-call(s32[3]{0:T(128)S(1)} %pad_add_fusion.place_ref, bf16[64,256]{1,0:T(8,128)(2,1)S(1)} %copy-done.9, ...), custom_call_target="tpu_custom_call" | custom-call | flops 268435456 | bytes 5242880 | tf_op jit(solution)/shard_map/pallas_call | solution.py:132
  6.4 2.0 %copy-done.3 = bf16[8,256,1024]{2,1,0:T(8,128)(2,1)} copy-done((bf16[8,256,1024]{2,1,0:T(8,128)(2,1)}, bf16[8,256,1024]{2,1,0:T(8,128)(2,1)S(1)}, u32[]{:S(2)}) %copy-start.3) | copy-done | bytes 4194328
  8.4 2.0 %collective-permute-start.2 = (bf16[8,64,256]{2,1,0:T(8,128)(2,1)S(1)}, bf16[8,64,256]{2,1,0:T(8,128)(2,1)S(1)}, u32[]{:S(2)}, u32[]{:S(2)}) collective-permute-start(bf16[8,64,256]{2,1,0:T(8,128)(2,1)S(1)} %get-tuple-element.43), channel_id=1, source_target_pairs={{0,1},{1,0},{2,3},{3,2},{4,5},{5,4},{6,7},{7,6},{8,9},{9,8},{10,11... | collective-permute-start | bytes 786440 | tf_op jit(solution)/shard_map/ppermute | solution.py:33
  10.4 2.9 %collective-permute-start = (bf16[64,256]{1,0:T(8,128)(2,1)S(1)}, bf16[64,256]{1,0:T(8,128)(2,1)S(1)}, u32[]{:S(2)}, u32[]{:S(2)}) collective-permute-start(bf16[64,256]{1,0:T(8,128)(2,1)S(1)} %copy-done.9), channel_id=1, source_target_pairs={{0,32},{32,0},{1,33},{33,1},{2,34},{34,2},{3,35},{35,3},{4,36},{36... | collective-permute-start | bytes 98312 | tf_op jit(solution)/shard_map/ppermute | solution.py:255
  14.7 2.2 %copy-done.4 = bf16[8,256,1024]{2,1,0:T(8,128)(2,1)S(1)} copy-done((bf16[8,256,1024]{2,1,0:T(8,128)(2,1)S(1)}, bf16[8,256,1024]{2,1,0:T(8,128)(2,1)}, u32[]{:S(2)}) %copy-start.4) | copy-done | bytes 4194328
  21.3 3.0 %collective-permute-start.7 = (bf16[256,1024]{1,0:T(8,128)(2,1)S(1)}, bf16[256,1024]{1,0:T(8,128)(2,1)S(1)}, u32[]{:S(2)}, u32[]{:S(2)}) collective-permute-start(bf16[256,1024]{1,0:T(8,128)(2,1)S(1)} %constant_dynamic-slice_fusion), channel_id=1, source_target_pairs={{0,32},{32,0},{1,33},{33,1},{2,34},{34,2},{3,35},{35,3},{4,36},{36... | collective-permute-start | bytes 1572872 | tf_op jit(solution)/shard_map/ppermute | solution.py:261
  31.6 3.4 %collective-permute-done.6 = bf16[8,64,256]{2,1,0:T(8,128)(2,1)S(1)} collective-permute-done((bf16[8,64,256]{2,1,0:T(8,128)(2,1)S(1)}, bf16[8,64,256]{2,1,0:T(8,128)(2,1)S(1)}, u32[]{:S(2)}, u32[]{:S(2)}) %collective-permute-start.6) | collective-permute-done | bytes 262176 | tf_op jit(solution)/shard_map/ppermute | solution.py:33
  37.4 8.2 %all-to-all-start = ((bf16[8,128,256]{2,1,0:T(8,128)(2,1)}), bf16[8,128,256]{2,1,0:T(8,128)(2,1)S(1)}, u32[]{:S(2)}, u32[]{:S(2)}) async-start(bf16[8,128,256]{2,1,0:T(8,128)(2,1)} %pad_maximum_fusion.1), calls=%async_computation | async-start | bytes 1048576 | tf_op jit(solution)/shard_map/all_to_all | solution.py:264
  45.7 12.8 %all-to-all-done = bf16[8,128,256]{2,1,0:T(8,128)(2,1)S(1)} async-done(((bf16[8,128,256]{2,1,0:T(8,128)(2,1)}), bf16[8,128,256]{2,1,0:T(8,128)(2,1)S(1)}, u32[]{:S(2)}, u32[]{:S(2)}) %all-to-all-start) | async-done | bytes 524320 | tf_op jit(solution)/shard_map/all_to_all | solution.py:264
  59.7 10.7 %all-to-all-start.1 = ((bf16[8,432,128]{2,1,0:T(8,128)(2,1)}), bf16[8,432,128]{2,1,0:T(8,128)(2,1)S(1)}, u32[]{:S(2)}, u32[]{:S(2)}) async-start(bf16[8,432,128]{2,1,0:T(8,128)(2,1)} %pad_maximum_fusion), calls=%async_computation.1 | async-start | bytes 1769472 | tf_op jit(solution)/shard_map/all_to_all | solution.py:278
  70.4 2.2 %copy-done.1 = bf16[256,8192]{1,0:T(8,128)(2,1)S(1)} copy-done((bf16[256,8192]{1,0:T(8,128)(2,1)S(1)}, bf16[256,8192]{1,0:T(8,128)(2,1)}, u32[]{:S(2)}) %copy-start.1) | copy-done | bytes 4194328
  74.9 8.7 %all-to-all-done.1.got_ref = bf16[8,432,128]{2,1,0:T(8,128)(2,1)S(1)} async-done(((bf16[8,432,128]{2,1,0:T(8,128)(2,1)}), bf16[8,432,128]{2,1,0:T(8,128)(2,1)S(1)}, u32[]{:S(2)}, u32[]{:S(2)}) %all-to-all-start.1) | async-done | bytes 884768 | tf_op jit(solution)/shard_map/all_to_all | solution.py:278
  89.1 2.5 %shard_map.106 = (bf16[256,512]{1,0:T(8,128)(2,1)S(1)}, bf16[256,512]{1,0:T(8,128)(2,1)S(1)}, bf16[256,512]{1,0:T(8,128)(2,1)S(1)}, bf16[256,512]{1,0:T(8,128)(2...) custom-call(s32[3]{0:T(128)S(1)} %pad_add_fusion.place_ref, ...), custom_call_target="tpu_custom_call" | custom-call | flops 1415577600 | bytes 5242880 | tf_op jit(solution)/shard_map/pallas_call | solution.py:196
  93.1 3.5 %collective-permute-done.12 = bf16[8,32,512]{2,1,0:T(8,128)(2,1)S(1)} collective-permute-done((bf16[8,32,512]{2,1,0:T(8,128)(2,1)S(1)}, bf16[8,32,512]{2,1,0:T(8,128)(2,1)S(1)}, u32[]{:S(2)}, u32[]{:S(2)}) %collective-permute-start.12) | collective-permute-done | bytes 262176 | tf_op jit(solution)/shard_map/ppermute | solution.py:33
  99.9 2.4 %collective-permute-done.11 = bf16[8,32,512]{2,1,0:T(8,128)(2,1)S(1)} collective-permute-done((bf16[8,32,512]{2,1,0:T(8,128)(2,1)S(1)}, bf16[8,32,512]{2,1,0:T(8,128)(2,1)S(1)}, u32[]{:S(2)}, u32[]{:S(2)}) %collective-permute-start.11) | collective-permute-done | bytes 262176 | tf_op jit(solution)/shard_map/ppermute | solution.py:33
  102.9 5.5 %collective-permute-done.8 = bf16[8,32,512]{2,1,0:T(8,128)(2,1)S(1)} collective-permute-done((bf16[8,32,512]{2,1,0:T(8,128)(2,1)S(1)}, bf16[8,32,512]{2,1,0:T(8,128)(2,1)S(1)}, u32[]{:S(2)}, u32[]{:S(2)}) %collective-permute-start.8) | collective-permute-done | bytes 262176 | tf_op jit(solution)/shard_map/ppermute | solution.py:33
  109.4 4.1 %all-to-all-start.2 = ((bf16[8,64,512]{2,1,0:T(8,128)(2,1)}), bf16[8,64,512]{2,1,0:T(8,128)(2,1)}, u32[]{:S(2)}, u32[]{:S(2)}) async-start(bf16[8,64,512]{2,1,0:T(8,128)(2,1)} %pad_maximum_fusion.2), calls=%async_computation.2 | async-start | bytes 1048576 | tf_op jit(solution)/shard_map/all_to_all | solution.py:65
  113.7 14.3 %all-to-all-done.2 = bf16[8,64,512]{2,1,0:T(8,128)(2,1)} async-done(((bf16[8,64,512]{2,1,0:T(8,128)(2,1)}), bf16[8,64,512]{2,1,0:T(8,128)(2,1)}, u32[]{:S(2)}, u32[]{:S(2)}) %all-to-all-start.2) | async-done | bytes 524320 | tf_op jit(solution)/shard_map/all_to_all | solution.py:65
  129.2 15.4 %all_to_all.25 = bf16[8,64,512]{2,1,0:T(8,128)(2,1)S(1)} all-to-all(bf16[8,64,512]{2,1,0:T(8,128)(2,1)S(1)} %broadcast_in_dim.10), channel_id=1, replica_groups=mesh['ylo'=2,'core'=2,'seq'=2,'z'=8,'x'=4] {'z'}, dimensions={0} | all-to-all | bytes 1048576 | tf_op jit(solution)/shard_map/all_to_all | solution.py:292
  148.9 2.3 %collective-permute-done.15.refs_3_ = bf16[256,512]{1,0:T(8,128)(2,1)S(1)} collective-permute-done((bf16[256,512]{1,0:T(8,128)(2,1)S(1)}, bf16[256,512]{1,0:T(8,128)(2,1)S(1)}, u32[]{:S(2)}, u32[]{:S(2)}) %collective-permute-start.15) | collective-permute-done | bytes 262176 | tf_op jit(solution)/shard_map/ppermute | solution.py:33
  154.1 5.3 %collective-permute-done.16.refs_2_ = bf16[256,512]{1,0:T(8,128)(2,1)S(1)} collective-permute-done((bf16[256,512]{1,0:T(8,128)(2,1)S(1)}, bf16[256,512]{1,0:T(8,128)(2,1)S(1)}, u32[]{:S(2)}, u32[]{:S(2)}) %collective-permute-start.16) | collective-permute-done | bytes 262176 | tf_op jit(solution)/shard_map/ppermute | solution.py:33
  160.7 2.3 %shard_map.108 = (bf16[4,256,128]{2,1,0:T(8,128)(2,1)S(1)}, bf16[16,128]{1,0:T(8,128)(2,1)S(1)}, bf16[128,1024]{1,0:T(8,128)(2,1)}) custom-call(s32[3]{0:T(128)S(1)} %pad_add_fusion.place_ref, bf16[256,512]{1,0:T(8,128)(2,1)S(1)} %bitcast.52, bf16[256,512]{1,0:T(8,128)(2,1)S(1)} %collective-permute-done.14.refs_1_, ...), custom_call_target="tpu_custom_call" | custom-call | flops 536870912 | bytes 5242880 | tf_op jit(solution)/shard_map/pallas_call | solution.py:235
  163.2 17.6 %all_to_all.26 = bf16[8,144,128]{2,1,0:T(8,128)(2,1)S(1)} all-to-all(bf16[8,144,128]{2,1,0:T(8,128)(2,1)S(1)} %copy.43), channel_id=1, replica_groups=mesh['ylo'=2,'core'=2,'seq'=2,'z'=8,'x'=4] {'ylo','core','seq'}, dimensions={0} | all-to-all | bytes 589824 | tf_op jit(solution)/shard_map/all_to_all | solution.py:299
  (103 shorter events, 42.8 us)
Async XLA Ops:
  8.4 16.3 %collective-permute-start.2 = (bf16[8,64,256]{2,1,0:T(8,128)(2,1)S(1)}, bf16[8,64,256]{2,1,0:T(8,128)(2,1)S(1)}, u32[]{:S(2)}, u32[]{:S(2)}) collective-permute-start(bf16[8,64,256]{2,1,0:T(8,128)(2,1)S(1)} %get-tuple-element.43), channel_id=1, source_target_pairs={{0,1},{1,0},{2,3},{3,2},{4,5},{5,4},{6,7},{7,6},{8,9},{9,8},{10,11... | collective-permute-start | bytes 786440 | tf_op jit(solution)/shard_map/ppermute | solution.py:33
  10.4 4.3 %collective-permute-start = (bf16[64,256]{1,0:T(8,128)(2,1)S(1)}, bf16[64,256]{1,0:T(8,128)(2,1)S(1)}, u32[]{:S(2)}, u32[]{:S(2)}) collective-permute-start(bf16[64,256]{1,0:T(8,128)(2,1)S(1)} %copy-done.9), channel_id=1, source_target_pairs={{0,32},{32,0},{1,33},{33,1},{2,34},{34,2},{3,35},{35,3},{4,36},{36... | collective-permute-start | bytes 98312 | tf_op jit(solution)/shard_map/ppermute | solution.py:255
  18.3 40.3 %copy-start.12 = (bf16[128,128]{1,0:T(8,128)(2,1)S(1)}, bf16[128,128]{1,0:T(8,128)(2,1)}, u32[]{:S(2)}) copy-start(bf16[128,128]{1,0:T(8,128)(2,1)} %param.13) | copy-start | bytes 98308
  18.3 7.1 %collective-permute-start.5 = (bf16[8,64,256]{2,1,0:T(8,128)(2,1)S(1)}, bf16[8,64,256]{2,1,0:T(8,128)(2,1)S(1)}, u32[]{:S(2)}, u32[]{:S(2)}) collective-permute-start(bf16[8,64,256]{2,1,0:T(8,128)(2,1)S(1)} %get-tuple-element.47), channel_id=1, source_target_pairs={{0,3},{1,2},{2,1},{3,0},{4,7},{5,6},{6,5},{7,4},{8,11},{9,10},{10,... | collective-permute-start | bytes 786440 | tf_op jit(solution)/shard_map/ppermute | solution.py:33
  21.3 13.8 %collective-permute-start.7 = (bf16[256,1024]{1,0:T(8,128)(2,1)S(1)}, bf16[256,1024]{1,0:T(8,128)(2,1)S(1)}, u32[]{:S(2)}, u32[]{:S(2)}) collective-permute-start(bf16[256,1024]{1,0:T(8,128)(2,1)S(1)} %constant_dynamic-slice_fusion), channel_id=1, source_target_pairs={{0,32},{32,0},{1,33},{33,1},{2,34},{34,2},{3,35},{35,3},{4,36},{36... | collective-permute-start | bytes 1572872 | tf_op jit(solution)/shard_map/ppermute | solution.py:261
  24.3 5.5 %collective-permute-start.1 = (bf16[8,64,256]{2,1,0:T(8,128)(2,1)S(1)}, bf16[8,64,256]{2,1,0:T(8,128)(2,1)S(1)}, u32[]{:S(2)}, u32[]{:S(2)}) collective-permute-start(bf16[8,64,256]{2,1,0:T(8,128)(2,1)S(1)} %get-tuple-element.41), channel_id=1, source_target_pairs={{0,1},{1,0},{2,3},{3,2},{4,5},{5,4},{6,7},{7,6},{8,9},{9,8},{10,11... | collective-permute-start | bytes 786440 | tf_op jit(solution)/shard_map/ppermute | solution.py:33
  24.7 6.8 %collective-permute-start.3 = (bf16[8,64,256]{2,1,0:T(8,128)(2,1)S(1)}, bf16[8,64,256]{2,1,0:T(8,128)(2,1)S(1)}, u32[]{:S(2)}, u32[]{:S(2)}) collective-permute-start(bf16[8,64,256]{2,1,0:T(8,128)(2,1)S(1)} %add_convert_fusion.3), channel_id=1, source_target_pairs={{0,3},{1,2},{2,1},{3,0},{4,7},{5,6},{6,5},{7,4},{8,11},{9,10},{10,... | collective-permute-start | bytes 786440 | tf_op jit(solution)/shard_map/ppermute | solution.py:33
  25.5 9.6 %collective-permute-start.6 = (bf16[8,64,256]{2,1,0:T(8,128)(2,1)S(1)}, bf16[8,64,256]{2,1,0:T(8,128)(2,1)S(1)}, u32[]{:S(2)}, u32[]{:S(2)}) collective-permute-start(bf16[8,64,256]{2,1,0:T(8,128)(2,1)S(1)} %add_convert_fusion.1), channel_id=1, source_target_pairs={{0,1},{1,0},{2,3},{3,2},{4,5},{5,4},{6,7},{7,6},{8,9},{9,8},{10,11... | collective-permute-start | bytes 786440 | tf_op jit(solution)/shard_map/ppermute | solution.py:33
  26.3 10.1 %collective-permute-start.4 = (bf16[8,64,256]{2,1,0:T(8,128)(2,1)S(1)}, bf16[8,64,256]{2,1,0:T(8,128)(2,1)S(1)}, u32[]{:S(2)}, u32[]{:S(2)}) collective-permute-start(bf16[8,64,256]{2,1,0:T(8,128)(2,1)S(1)} %get-tuple-element.45), channel_id=1, source_target_pairs={{0,3},{1,2},{2,1},{3,0},{4,7},{5,6},{6,5},{7,4},{8,11},{9,10},{10,... | collective-permute-start | bytes 786440 | tf_op jit(solution)/shard_map/ppermute | solution.py:33
  37.4 21.1 %all-to-all-start = ((bf16[8,128,256]{2,1,0:T(8,128)(2,1)}), bf16[8,128,256]{2,1,0:T(8,128)(2,1)S(1)}, u32[]{:S(2)}, u32[]{:S(2)}) async-start(bf16[8,128,256]{2,1,0:T(8,128)(2,1)} %pad_maximum_fusion.1), calls=%async_computation | async-start | bytes 1048576 | tf_op jit(solution)/shard_map/all_to_all | solution.py:264
  59.7 23.9 %all-to-all-start.1 = ((bf16[8,432,128]{2,1,0:T(8,128)(2,1)}), bf16[8,432,128]{2,1,0:T(8,128)(2,1)S(1)}, u32[]{:S(2)}, u32[]{:S(2)}) async-start(bf16[8,432,128]{2,1,0:T(8,128)(2,1)} %pad_maximum_fusion), calls=%async_computation.1 | async-start | bytes 1769472 | tf_op jit(solution)/shard_map/all_to_all | solution.py:278
  87.8 8.8 %collective-permute-start.12 = (bf16[8,32,512]{2,1,0:T(8,128)(2,1)S(1)}, bf16[8,32,512]{2,1,0:T(8,128)(2,1)S(1)}, u32[]{:S(2)}, u32[]{:S(2)}) collective-permute-start(bf16[8,32,512]{2,1,0:T(8,128)(2,1)S(1)} %bitcast.61), channel_id=1, source_target_pairs={{0,3},{1,2},{2,1},{3,0},{4,7},{5,6},{6,5},{7,4},{8,11},{9,10},{10,... | collective-permute-start | bytes 786440 | tf_op jit(solution)/shard_map/ppermute | solution.py:33
  89.1 9.3 %collective-permute-start.9 = (bf16[8,32,512]{2,1,0:T(8,128)(2,1)S(1)}, bf16[8,32,512]{2,1,0:T(8,128)(2,1)S(1)}, u32[]{:S(2)}, u32[]{:S(2)}) collective-permute-start(bf16[8,32,512]{2,1,0:T(8,128)(2,1)S(1)} %bitcast.59), channel_id=1, source_target_pairs={{0,1},{1,0},{2,3},{3,2},{4,5},{5,4},{6,7},{7,6},{8,9},{9,8},{10,11... | collective-permute-start | bytes 786440 | tf_op jit(solution)/shard_map/ppermute | solution.py:33
  91.6 10.6 %collective-permute-start.11 = (bf16[8,32,512]{2,1,0:T(8,128)(2,1)S(1)}, bf16[8,32,512]{2,1,0:T(8,128)(2,1)S(1)}, u32[]{:S(2)}, u32[]{:S(2)}) collective-permute-start(bf16[8,32,512]{2,1,0:T(8,128)(2,1)S(1)} %bitcast.60), channel_id=1, source_target_pairs={{0,3},{1,2},{2,1},{3,0},{4,7},{5,6},{6,5},{7,4},{8,11},{9,10},{10,... | collective-permute-start | bytes 786440 | tf_op jit(solution)/shard_map/ppermute | solution.py:33
  96.7 6.1 %collective-permute-start.13 = (bf16[8,32,512]{2,1,0:T(8,128)(2,1)S(1)}, bf16[8,32,512]{2,1,0:T(8,128)(2,1)S(1)}, u32[]{:S(2)}, u32[]{:S(2)}) collective-permute-start(bf16[8,32,512]{2,1,0:T(8,128)(2,1)S(1)} %fusion), channel_id=1, source_target_pairs={{0,1},{1,0},{2,3},{3,2},{4,5},{5,4},{6,7},{7,6},{8,9},{9,8},{10,11... | collective-permute-start | bytes 786440 | tf_op jit(solution)/shard_map/ppermute | solution.py:33
  97.0 11.4 %collective-permute-start.8 = (bf16[8,32,512]{2,1,0:T(8,128)(2,1)S(1)}, bf16[8,32,512]{2,1,0:T(8,128)(2,1)S(1)}, u32[]{:S(2)}, u32[]{:S(2)}) collective-permute-start(bf16[8,32,512]{2,1,0:T(8,128)(2,1)S(1)} %bitcast.58), channel_id=1, source_target_pairs={{0,1},{1,0},{2,3},{3,2},{4,5},{5,4},{6,7},{7,6},{8,9},{9,8},{10,11... | collective-permute-start | bytes 786440 | tf_op jit(solution)/shard_map/ppermute | solution.py:33
  98.5 9.9 %collective-permute-start.10 = (bf16[8,32,512]{2,1,0:T(8,128)(2,1)S(1)}, bf16[8,32,512]{2,1,0:T(8,128)(2,1)S(1)}, u32[]{:S(2)}, u32[]{:S(2)}) collective-permute-start(bf16[8,32,512]{2,1,0:T(8,128)(2,1)S(1)} %fusion.3), channel_id=1, source_target_pairs={{0,3},{1,2},{2,1},{3,0},{4,7},{5,6},{6,5},{7,4},{8,11},{9,10},{10,... | collective-permute-start | bytes 786440 | tf_op jit(solution)/shard_map/ppermute | solution.py:33
  109.4 18.7 %all-to-all-start.2 = ((bf16[8,64,512]{2,1,0:T(8,128)(2,1)}), bf16[8,64,512]{2,1,0:T(8,128)(2,1)}, u32[]{:S(2)}, u32[]{:S(2)}) async-start(bf16[8,64,512]{2,1,0:T(8,128)(2,1)} %pad_maximum_fusion.2), calls=%async_computation.2 | async-start | bytes 1048576 | tf_op jit(solution)/shard_map/all_to_all | solution.py:65
  144.7 6.5 %collective-permute-start.15 = (bf16[256,512]{1,0:T(8,128)(2,1)S(1)}, bf16[256,512]{1,0:T(8,128)(2,1)S(1)}, u32[]{:S(2)}, u32[]{:S(2)}) collective-permute-start(bf16[256,512]{1,0:T(8,128)(2,1)S(1)} %bitcast.50), channel_id=1, source_target_pairs={{0,3},{1,2},{2,1},{3,0},{4,7},{5,6},{6,5},{7,4},{8,11},{9,10},{10,... | collective-permute-start | bytes 786440 | tf_op jit(solution)/shard_map/ppermute | solution.py:33
  146.0 5.2 %collective-permute-start.17 = (bf16[256,512]{1,0:T(8,128)(2,1)S(1)}, bf16[256,512]{1,0:T(8,128)(2,1)S(1)}, u32[]{:S(2)}, u32[]{:S(2)}) collective-permute-start(bf16[256,512]{1,0:T(8,128)(2,1)S(1)} %bitcast.47), channel_id=1, source_target_pairs={{0,1},{1,0},{2,3},{3,2},{4,5},{5,4},{6,7},{7,6},{8,9},{9,8},{10,11... | collective-permute-start | bytes 786440 | tf_op jit(solution)/shard_map/ppermute | solution.py:33
  146.3 7.7 %collective-permute-start.14 = (bf16[256,512]{1,0:T(8,128)(2,1)S(1)}, bf16[256,512]{1,0:T(8,128)(2,1)S(1)}, u32[]{:S(2)}, u32[]{:S(2)}) collective-permute-start(bf16[256,512]{1,0:T(8,128)(2,1)S(1)} %bitcast.51), channel_id=1, source_target_pairs={{0,1},{1,0},{2,3},{3,2},{4,5},{5,4},{6,7},{7,6},{8,9},{9,8},{10,11... | collective-permute-start | bytes 786440 | tf_op jit(solution)/shard_map/ppermute | solution.py:33
  147.5 6.6 %collective-permute-start.19 = (bf16[256,512]{1,0:T(8,128)(2,1)S(1)}, bf16[256,512]{1,0:T(8,128)(2,1)S(1)}, u32[]{:S(2)}, u32[]{:S(2)}) collective-permute-start(bf16[256,512]{1,0:T(8,128)(2,1)S(1)} %bitcast.48), channel_id=1, source_target_pairs={{0,3},{1,2},{2,1},{3,0},{4,7},{5,6},{6,5},{7,4},{8,11},{9,10},{10,... | collective-permute-start | bytes 786440 | tf_op jit(solution)/shard_map/ppermute | solution.py:33
  151.2 8.2 %collective-permute-start.16 = (bf16[256,512]{1,0:T(8,128)(2,1)S(1)}, bf16[256,512]{1,0:T(8,128)(2,1)S(1)}, u32[]{:S(2)}, u32[]{:S(2)}) collective-permute-start(bf16[256,512]{1,0:T(8,128)(2,1)S(1)} %collective-permute-done.15.refs_3_), channel_id=1, source_target_pairs={{0,1},{1,0},{2,3},{3,2},{4,5},{5,4},{6,7},{7,6},{8,9},{9,8},{10,11... | collective-permute-start | bytes 786440 | tf_op jit(solution)/shard_map/ppermute | solution.py:33
  151.3 9.5 %collective-permute-start.18 = (bf16[256,512]{1,0:T(8,128)(2,1)S(1)}, bf16[256,512]{1,0:T(8,128)(2,1)S(1)}, u32[]{:S(2)}, u32[]{:S(2)}) collective-permute-start(bf16[256,512]{1,0:T(8,128)(2,1)S(1)} %collective-permute-done.17.refs_5_), channel_id=1, source_target_pairs={{0,3},{1,2},{2,1},{3,0},{4,7},{5,6},{6,5},{7,4},{8,11},{9,10},{10,... | collective-permute-start | bytes 786440 | tf_op jit(solution)/shard_map/ppermute | solution.py:33
  (13 other events, 129.1 us)

commit v10 on v9

--- a/solution.py
+++ b/solution.py
@@ -82,7 +82,7 @@
     return pl.BlockSpec(shape, lambda i, m: (0,) * len(shape))
 
 
-def call(kernel, in_specs, outs, flops, scratch=(), limit=32):
+def call(kernel, in_specs, outs, flops, scratch=(), limit=16):
     return pl.pallas_call(
         kernel,
         grid_spec=pltpu.PrefetchScalarGridSpec(
@@ -98,46 +98,38 @@
     )
 
 
-def multiply(rows, weights, z, x, parts):
-    for k in range(NX):
-        columns = pl.ds(pl.multiple_of((k ^ x) * 256, 256), 256)
-        parts[k][z] = dot(rows, weights[z, :, columns], ((1,), (0,))).astype(B16)
-
-
-def own_kernel(place_ref, rows_ref, out_ref, *refs):
-    parts, held, sems = refs[:NX], refs[NX], refs[NX + 1]
+def load_kernel(place_ref, out_ref, held_ref, sems):
     copies = [
-        pltpu.make_async_copy(out_ref.at[:, pl.ds(z * 1024, 1024)], held.at[z], sems.at[z]) for z in range(NZ)
+        pltpu.make_async_copy(out_ref.at[:, pl.ds(z * 1024, 1024)], held_ref.at[z], sems.at[z]) for z in range(NZ)
     ]
     for copy in copies:
         copy.start()
-    rows = rows_ref[...]
-    for z in range(NZ):
-        copies[z].wait()
-        multiply(rows, held, z, place_ref[2], parts)
-
-
-def there_kernel(place_ref, rows_ref, held_ref, *parts):
-    rows = rows_ref[...]
-    for z in range(NZ):
-        multiply(rows, held_ref, z, place_ref[2], parts)
-
-
-PARTS = [jax.ShapeDtypeStruct((NZ, 64, 256), B16)] * NX
-
-
-def own_parts(place, rows, teacher_out):
-    specs = [whole(64, 256), pl.BlockSpec(memory_space=pltpu.HBM)]
-    outs = PARTS + [jax.ShapeDtypeStruct((NZ, 256, 1024), B16)]
-    *parts, held = call(own_kernel, specs, outs, 2 * 64 * 256 * 8192, [pltpu.SemaphoreType.DMA((NZ,))], 24)(
-        place, rows, teacher_out
-    )
-    return parts, held
-
-
-def there_parts(place, rows, held):
-    specs = [whole(64, 256), whole(NZ, 256, 1024)]
-    return list(call(there_kernel, specs, PARTS, 2 * 64 * 256 * 8192, (), 24)(place, rows, held))
+    for copy in copies:
+        copy.wait()
+
+
+def load(place, teacher_out):
+    outs = [jax.ShapeDtypeStruct((NZ, 256, 1024), B16)]
+    specs = [pl.BlockSpec(memory_space=pltpu.HBM)]
+    return call(load_kernel, specs, outs, 1 << 21, [pltpu.SemaphoreType.DMA((NZ,))], 16)(place, teacher_out)[0]
+
+
+def teacher_kernel(jobs, place_ref, own_ref, there_ref, held_ref, *parts):
+    x = place_ref[2]
+    rows = jnp.concatenate([own_ref[...], there_ref[...]], axis=0)
+    for k, first, second in jobs:
+        columns = pl.ds(pl.multiple_of((k ^ x) * 256, 256), 256)
+        for z in range(NZ):
+            product = dot(rows, held_ref[z, :, columns], ((1,), (0,))).astype(B16)
+            parts[first][z] = product[:64]
+            parts[second][z] = product[64:]
+
+
+def teacher_parts(jobs, place, own, there, held):
+    specs = [whole(64, 256), whole(64, 256), whole(NZ, 256, 1024)]
+    outs = [jax.ShapeDtypeStruct((NZ, 64, 256), B16)] * (2 * len(jobs))
+    flops = 2 * 128 * 256 * 2048 * len(jobs)
+    return call(functools.partial(teacher_kernel, jobs), specs, outs, flops, (), 20)(place, own, there, held)
 
 
 def layout_kernel(place_ref, home_in, other_in, out_in, weights_ref, out_ref):
@@ -153,7 +145,7 @@
         pl.BlockSpec((128, COLS), lambda i, m: (0, m[0])),
     ]
     outs = [jax.ShapeDtypeStruct((512, COLS), B16), jax.ShapeDtypeStruct((128, COLS), B16)]
-    return call(layout_kernel, specs, outs, 1 << 21, (), 16)(place, projector, other, student_out)
+    return call(layout_kernel, specs, outs, 1 << 21, (), 8)(place, projector, other, student_out)
 
 
 def gather_hidden(place_ref, got_ref, hidden_ref):
@@ -194,7 +186,7 @@
     count = sum(len(halves) for _, halves in jobs)
     outs = [jax.ShapeDtypeStruct((256, HALF), B16)] * count
     return call(
-        functools.partial(combine_kernel, jobs), specs, outs, count * 2 * 256 * 512 * 900, [pltpu.VMEM((512, 512), B16)], 24
+        functools.partial(combine_kernel, jobs), specs, outs, count * 2 * 256 * 512 * 900, [pltpu.VMEM((512, 512), B16)], 16
     )(place, picked, got, heads, out_cols, weights)
 
 
@@ -253,14 +245,17 @@
     swap = [(0, 1), (1, 0)]
 
     there = lax.ppermute(teacher_heads, "seq", swap)
-    first, held = own_parts(place, teacher_heads, teacher_out)
-    second = there_parts(place, there, held)
+    held = load(place, teacher_out)
+    far = teacher_parts(((2, 0, 1),), place, teacher_heads, there, held)
+    rest = teacher_parts(((1, 0, 3), (3, 1, 4), (0, 2, 5)), place, teacher_heads, there, held)
+    first = (rest[2], rest[0], far[0], rest[1])
+    second = [rest[5], rest[3], far[1], rest[4]]
 
     second[2], later = lax.optimization_barrier((second[2], member))
     away = lax.dynamic_slice(projector, (0, (later + 1 - 2 * seq) * COLS), (256, COLS))
     other = lax.ppermute(away, "seq", swap)
 
-    summed, other = reduce_x(first, second, (away,), (other,))
+    summed, other = reduce_x(first, second, (), (other,))
     moved = lax.all_to_all(summed, "z", 0, 0)
     near = lax.dynamic_slice(teacher_resid, (seq * 64, 0), (64, 256))
     far = lax.dynamic_slice(teacher_resid, (64 - seq * 64, 0), (64, 256))

time: 185 us -> 183 us (0.989)
    ppermute x18, waiting for transfers between devices: 30.5 us -> 26.3 us  [across(): return lax.ppermute(block, 'x', [(i, i ^ flip) for i in range(NX)])]
    ppermute x1, waiting for transfers between devices: 0.01 us -> 3.33 us  [local(): other = lax.ppermute(away, 'seq', swap)]
    all_to_all x1, starting transfers between devices: 10.7 us -> 7.61 us  [local(): got = lax.all_to_all(sent, COLUMN, 0, 0)]
    ppermute x18, starting transfers between devices: 19.2 us -> 21.7 us  [across(): return lax.ppermute(block, 'x', [(i, i ^ flip) for i in range(NX)])]
    pallas_call x3 -> x4, Pallas kernels: 4.72 us -> 3.65 us  [the longest x2 2.03 us: teacher_parts(): call(functools.partial(teacher_kernel, jobs), specs, outs, flops, (), 20)]
    unnamed x28 -> x26, local copies, waits for them, and re-layouts: 13.2 us -> 12.4 us
  transfers between devices with their start and end apart: 23 -> 23, of which waited for: 16 -> 15; matrix products, arithmetic and copies ran while one was open for 1% -> 2% of each run, Pallas kernels for 2% -> 3%
where the time goes in v10:
time: 183 us; the launch traced here: 182 us
  waiting for transfers between devices  67.1 us (37%)
  starting transfers between devices  46.6 us (25%)
  blocking collectives  33.3 us (18%)
  local copies, waits for them, and re-layouts  14.5 us (8%)
  Pallas kernels  9.73 us (5%)
  other arithmetic  7.78 us (4%)
  between operations  2.78 us (2%)
    ppermute x18, waiting for transfers between devices, across(): return lax.ppermute(block, 'x', [(i, i ^ flip) for i in range(NX)])  26.3 us
    ppermute x18, starting transfers between devices, across(): return lax.ppermute(block, 'x', [(i, i ^ flip) for i in range(NX)])  21.7 us
    all_to_all x1, blocking collectives, local(): back = lax.all_to_all(sent, COLUMN, 0, 0).astype(F32)  17 us
    all_to_all x1, blocking collectives, local(): lax.all_to_all(jnp.broadcast_to(grad[None], (NZ, 64, HALF)), 'z', 0, 0)  16.2 us
    all_to_all x1, waiting for transfers between devices, reduce_z(): moved = lax.all_to_all(parts, 'z', 0, 0)  14.5 us
    all_to_all x1, waiting for transfers between devices, local(): moved = lax.all_to_all(summed, 'z', 0, 0)  14.2 us
    unnamed x26, local copies, waits for them, and re-layouts  12.4 us
    all_to_all x1, waiting for transfers between devices, local(): got = lax.all_to_all(sent, COLUMN, 0, 0)  8.75 us
  transfers between devices with their start and end apart: 23, of which 15 were waited for; matrix products, arithmetic and copies ran while one was open for 2% of the time, Pallas kernels for 3%

profile of v10, /device:TPU:1, one launch (start us, length us, event | category | flops | bytes accessed | tf_op | source)
XLA Modules:
  0.0 181.8 jit_solution(9127318077336011622)
XLA Ops:
  0.6 3.8 %collective-permute-start = (bf16[64,256]{1,0:T(8,128)(2,1)}, bf16[64,256]{1,0:T(8,128)(2,1)S(1)}, u32[]{:S(2)}, u32[]{:S(2)}) collective-permute-start(bf16[64,256]{1,0:T(8,128)(2,1)} %own_ref.3), channel_id=1, source_target_pairs={{0,32},{32,0},{1,33},{33,1},{2,34},{34,2},{3,35},{35,3},{4,36},{36... | collective-permute-start | bytes 98312 | tf_op jit(solution)/shard_map/ppermute | solution.py:247
  4.5 2.2 %copy-done.4 = bf16[256,8192]{1,0:T(8,128)(2,1)S(1)} copy-done((bf16[256,8192]{1,0:T(8,128)(2,1)S(1)}, bf16[256,8192]{1,0:T(8,128)(2,1)}, u32[]{:S(2)}) %copy-start.4) | copy-done | bytes 4194328
  11.8 2.2 %copy-done.1 = bf16[8,256,1024]{2,1,0:T(8,128)(2,1)S(1)} copy-done((bf16[8,256,1024]{2,1,0:T(8,128)(2,1)S(1)}, bf16[8,256,1024]{2,1,0:T(8,128)(2,1)}, u32[]{:S(2)}) %copy-start.1) | copy-done | bytes 4194328
  15.5 2.5 %collective-permute-start.5 = (bf16[8,64,256]{2,1,0:T(8,128)(2,1)S(1)}, bf16[8,64,256]{2,1,0:T(8,128)(2,1)S(1)}, u32[]{:S(2)}, u32[]{:S(2)}) collective-permute-start(bf16[8,64,256]{2,1,0:T(8,128)(2,1)S(1)} %get-tuple-element.44), channel_id=1, source_target_pairs={{0,3},{1,2},{2,1},{3,0},{4,7},{5,6},{6,5},{7,4},{8,11},{9,10},{10,... | collective-permute-start | bytes 786440 | tf_op jit(solution)/shard_map/ppermute | solution.py:33
  23.3 2.5 %collective-permute-start.4 = (bf16[8,64,256]{2,1,0:T(8,128)(2,1)S(1)}, bf16[8,64,256]{2,1,0:T(8,128)(2,1)S(1)}, u32[]{:S(2)}, u32[]{:S(2)}) collective-permute-start(bf16[8,64,256]{2,1,0:T(8,128)(2,1)S(1)} %get-tuple-element.41), channel_id=1, source_target_pairs={{0,3},{1,2},{2,1},{3,0},{4,7},{5,6},{6,5},{7,4},{8,11},{9,10},{10,... | collective-permute-start | bytes 786440 | tf_op jit(solution)/shard_map/ppermute | solution.py:33
  29.0 3.3 %collective-permute-done.7.other_in = bf16[256,1024]{1,0:T(8,128)(2,1)S(1)} collective-permute-done((bf16[256,1024]{1,0:T(8,128)(2,1)S(1)}, bf16[256,1024]{1,0:T(8,128)(2,1)S(1)}, u32[]{:S(2)}, u32[]{:S(2)}) %collective-permute-start.7) | collective-permute-done | bytes 524320 | tf_op jit(solution)/shard_map/ppermute | solution.py:256
  34.5 8.1 %all-to-all-start = ((bf16[8,128,256]{2,1,0:T(8,128)(2,1)}), bf16[8,128,256]{2,1,0:T(8,128)(2,1)S(1)}, u32[]{:S(2)}, u32[]{:S(2)}) async-start(bf16[8,128,256]{2,1,0:T(8,128)(2,1)} %pad_maximum_fusion.1), calls=%async_computation | async-start | bytes 1048576 | tf_op jit(solution)/shard_map/all_to_all | solution.py:259
  42.7 14.2 %all-to-all-done = bf16[8,128,256]{2,1,0:T(8,128)(2,1)S(1)} async-done(((bf16[8,128,256]{2,1,0:T(8,128)(2,1)}), bf16[8,128,256]{2,1,0:T(8,128)(2,1)S(1)}, u32[]{:S(2)}, u32[]{:S(2)}) %all-to-all-start) | async-done | bytes 524320 | tf_op jit(solution)/shard_map/all_to_all | solution.py:259
  58.9 7.6 %all-to-all-start.1 = ((bf16[8,432,128]{2,1,0:T(8,128)(2,1)}), bf16[8,432,128]{2,1,0:T(8,128)(2,1)S(1)}, u32[]{:S(2)}, u32[]{:S(2)}) async-start(bf16[8,432,128]{2,1,0:T(8,128)(2,1)} %pad_maximum_fusion), calls=%async_computation.1 | async-start | bytes 1769472 | tf_op jit(solution)/shard_map/all_to_all | solution.py:273
  66.5 2.2 %copy-done.3 = bf16[256,8192]{1,0:T(8,128)(2,1)S(1)} copy-done((bf16[256,8192]{1,0:T(8,128)(2,1)S(1)}, bf16[256,8192]{1,0:T(8,128)(2,1)}, u32[]{:S(2)}) %copy-start.3) | copy-done | bytes 4194328
  71.0 8.7 %all-to-all-done.1.got_ref = bf16[8,432,128]{2,1,0:T(8,128)(2,1)S(1)} async-done(((bf16[8,432,128]{2,1,0:T(8,128)(2,1)}), bf16[8,432,128]{2,1,0:T(8,128)(2,1)S(1)}, u32[]{:S(2)}, u32[]{:S(2)}) %all-to-all-start.1) | async-done | bytes 884768 | tf_op jit(solution)/shard_map/all_to_all | solution.py:273
  84.8 2.6 %collective-permute-start.12 = (bf16[8,32,512]{2,1,0:T(8,128)(2,1)S(1)}, bf16[8,32,512]{2,1,0:T(8,128)(2,1)S(1)}, u32[]{:S(2)}, u32[]{:S(2)}) collective-permute-start(bf16[8,32,512]{2,1,0:T(8,128)(2,1)S(1)} %bitcast.59), channel_id=1, source_target_pairs={{0,3},{1,2},{2,1},{3,0},{4,7},{5,6},{6,5},{7,4},{8,11},{9,10},{10,... | collective-permute-start | bytes 786440 | tf_op jit(solution)/shard_map/ppermute | solution.py:33
  87.4 2.5 %shard_map.107 = (bf16[256,512]{1,0:T(8,128)(2,1)S(1)}, bf16[256,512]{1,0:T(8,128)(2,1)S(1)}, bf16[256,512]{1,0:T(8,128)(2,1)S(1)}, bf16[256,512]{1,0:T(8,128)(2...) custom-call(s32[3]{0:T(128)S(1)} %pad_add_fusion.place_ref, ...), custom_call_target="tpu_custom_call" | custom-call | flops 1415577600 | bytes 5242880 | tf_op jit(solution)/shard_map/pallas_call | solution.py:188
  91.6 3.4 %collective-permute-start.10 = (bf16[8,32,512]{2,1,0:T(8,128)(2,1)S(1)}, bf16[8,32,512]{2,1,0:T(8,128)(2,1)S(1)}, u32[]{:S(2)}, u32[]{:S(2)}) collective-permute-start(bf16[8,32,512]{2,1,0:T(8,128)(2,1)S(1)} %fusion.3), channel_id=1, source_target_pairs={{0,3},{1,2},{2,1},{3,0},{4,7},{5,6},{6,5},{7,4},{8,11},{9,10},{10,... | collective-permute-start | bytes 786440 | tf_op jit(solution)/shard_map/ppermute | solution.py:33
  97.1 2.4 %collective-permute-done.10 = bf16[8,32,512]{2,1,0:T(8,128)(2,1)S(1)} collective-permute-done((bf16[8,32,512]{2,1,0:T(8,128)(2,1)S(1)}, bf16[8,32,512]{2,1,0:T(8,128)(2,1)S(1)}, u32[]{:S(2)}, u32[]{:S(2)}) %collective-permute-start.10) | collective-permute-done | bytes 262176 | tf_op jit(solution)/shard_map/ppermute | solution.py:33
  99.6 5.5 %collective-permute-done.11 = bf16[8,32,512]{2,1,0:T(8,128)(2,1)S(1)} collective-permute-done((bf16[8,32,512]{2,1,0:T(8,128)(2,1)S(1)}, bf16[8,32,512]{2,1,0:T(8,128)(2,1)S(1)}, u32[]{:S(2)}, u32[]{:S(2)}) %collective-permute-start.11) | collective-permute-done | bytes 262176 | tf_op jit(solution)/shard_map/ppermute | solution.py:33
  106.1 4.1 %all-to-all-start.2 = ((bf16[8,64,512]{2,1,0:T(8,128)(2,1)}), bf16[8,64,512]{2,1,0:T(8,128)(2,1)}, u32[]{:S(2)}, u32[]{:S(2)}) async-start(bf16[8,64,512]{2,1,0:T(8,128)(2,1)} %pad_maximum_fusion.2), calls=%async_computation.2 | async-start | bytes 1048576 | tf_op jit(solution)/shard_map/all_to_all | solution.py:65
  110.4 14.5 %all-to-all-done.2 = bf16[8,64,512]{2,1,0:T(8,128)(2,1)} async-done(((bf16[8,64,512]{2,1,0:T(8,128)(2,1)}), bf16[8,64,512]{2,1,0:T(8,128)(2,1)}, u32[]{:S(2)}, u32[]{:S(2)}) %all-to-all-start.2) | async-done | bytes 524320 | tf_op jit(solution)/shard_map/all_to_all | solution.py:65
  126.2 16.2 %all_to_all.25 = bf16[8,64,512]{2,1,0:T(8,128)(2,1)S(1)} all-to-all(bf16[8,64,512]{2,1,0:T(8,128)(2,1)S(1)} %broadcast_in_dim.10), channel_id=1, replica_groups=mesh['ylo'=2,'core'=2,'seq'=2,'z'=8,'x'=4] {'z'}, dimensions={0} | all-to-all | bytes 1048576 | tf_op jit(solution)/shard_map/all_to_all | solution.py:287
  146.7 2.3 %collective-permute-done.15.refs_3_ = bf16[256,512]{1,0:T(8,128)(2,1)S(1)} collective-permute-done((bf16[256,512]{1,0:T(8,128)(2,1)S(1)}, bf16[256,512]{1,0:T(8,128)(2,1)S(1)}, u32[]{:S(2)}, u32[]{:S(2)}) %collective-permute-start.15) | collective-permute-done | bytes 262176 | tf_op jit(solution)/shard_map/ppermute | solution.py:33
  152.1 4.9 %collective-permute-done.16.refs_2_ = bf16[256,512]{1,0:T(8,128)(2,1)S(1)} collective-permute-done((bf16[256,512]{1,0:T(8,128)(2,1)S(1)}, bf16[256,512]{1,0:T(8,128)(2,1)S(1)}, u32[]{:S(2)}, u32[]{:S(2)}) %collective-permute-start.16) | collective-permute-done | bytes 262176 | tf_op jit(solution)/shard_map/ppermute | solution.py:33
  157.0 2.2 %collective-permute-done.18.refs_6_ = bf16[256,512]{1,0:T(8,128)(2,1)S(1)} collective-permute-done((bf16[256,512]{1,0:T(8,128)(2,1)S(1)}, bf16[256,512]{1,0:T(8,128)(2,1)S(1)}, u32[]{:S(2)}, u32[]{:S(2)}) %collective-permute-start.18) | collective-permute-done | bytes 262176 | tf_op jit(solution)/shard_map/ppermute | solution.py:33
  159.3 2.3 %shard_map.109 = (bf16[4,256,128]{2,1,0:T(8,128)(2,1)S(1)}, bf16[16,128]{1,0:T(8,128)(2,1)S(1)}, bf16[128,1024]{1,0:T(8,128)(2,1)}) custom-call(s32[3]{0:T(128)S(1)} %pad_add_fusion.place_ref, bf16[256,512]{1,0:T(8,128)(2,1)S(1)} %bitcast.52, bf16[256,512]{1,0:T(8,128)(2,1)S(1)} %collective-permute-done.14.refs_1_, ...), custom_call_target="tpu_custom_call" | custom-call | flops 536870912 | bytes 5242880 | tf_op jit(solution)/shard_map/pallas_call | solution.py:227
  161.7 17.0 %all_to_all.26 = bf16[8,144,128]{2,1,0:T(8,128)(2,1)S(1)} all-to-all(bf16[8,144,128]{2,1,0:T(8,128)(2,1)S(1)} %copy.43), channel_id=1, replica_groups=mesh['ylo'=2,'core'=2,'seq'=2,'z'=8,'x'=4] {'ylo','core','seq'}, dimensions={0} | all-to-all | bytes 589824 | tf_op jit(solution)/shard_map/all_to_all | solution.py:294
  (102 shorter events, 41.7 us)
Async XLA Ops:
  0.6 7.1 %collective-permute-start = (bf16[64,256]{1,0:T(8,128)(2,1)}, bf16[64,256]{1,0:T(8,128)(2,1)S(1)}, u32[]{:S(2)}, u32[]{:S(2)}) collective-permute-start(bf16[64,256]{1,0:T(8,128)(2,1)} %own_ref.3), channel_id=1, source_target_pairs={{0,32},{32,0},{1,33},{33,1},{2,34},{34,2},{3,35},{35,3},{4,36},{36... | collective-permute-start | bytes 98312 | tf_op jit(solution)/shard_map/ppermute | solution.py:247
  10.6 9.8 %collective-permute-start.2 = (bf16[8,64,256]{2,1,0:T(8,128)(2,1)S(1)}, bf16[8,64,256]{2,1,0:T(8,128)(2,1)S(1)}, u32[]{:S(2)}, u32[]{:S(2)}) collective-permute-start(bf16[8,64,256]{2,1,0:T(8,128)(2,1)S(1)} %get-tuple-element.39), channel_id=1, source_target_pairs={{0,1},{1,0},{2,3},{3,2},{4,5},{5,4},{6,7},{7,6},{8,9},{9,8},{10,11... | collective-permute-start | bytes 786440 | tf_op jit(solution)/shard_map/ppermute | solution.py:33
  15.2 10.6 %collective-permute-start.1 = (bf16[8,64,256]{2,1,0:T(8,128)(2,1)S(1)}, bf16[8,64,256]{2,1,0:T(8,128)(2,1)}, u32[]{:S(2)}, u32[]{:S(2)}) collective-permute-start(bf16[8,64,256]{2,1,0:T(8,128)(2,1)S(1)} %get-tuple-element.37), channel_id=1, source_target_pairs={{0,1},{1,0},{2,3},{3,2},{4,5},{5,4},{6,7},{7,6},{8,9},{9,8},{10,11... | collective-permute-start | bytes 786440 | tf_op jit(solution)/shard_map/ppermute | solution.py:33
  15.5 6.6 %collective-permute-start.5 = (bf16[8,64,256]{2,1,0:T(8,128)(2,1)S(1)}, bf16[8,64,256]{2,1,0:T(8,128)(2,1)S(1)}, u32[]{:S(2)}, u32[]{:S(2)}) collective-permute-start(bf16[8,64,256]{2,1,0:T(8,128)(2,1)S(1)} %get-tuple-element.44), channel_id=1, source_target_pairs={{0,3},{1,2},{2,1},{3,0},{4,7},{5,6},{6,5},{7,4},{8,11},{9,10},{10,... | collective-permute-start | bytes 786440 | tf_op jit(solution)/shard_map/ppermute | solution.py:33
  19.1 13.2 %collective-permute-start.7 = (bf16[256,1024]{1,0:T(8,128)(2,1)S(1)}, bf16[256,1024]{1,0:T(8,128)(2,1)S(1)}, u32[]{:S(2)}, u32[]{:S(2)}) collective-permute-start(bf16[256,1024]{1,0:T(8,128)(2,1)S(1)} %constant_dynamic-slice_fusion), channel_id=1, source_target_pairs={{0,32},{32,0},{1,33},{33,1},{2,34},{34,2},{3,35},{35,3},{4,36},{36... | collective-permute-start | bytes 1572872 | tf_op jit(solution)/shard_map/ppermute | solution.py:256
  20.4 7.5 %collective-permute-start.3 = (bf16[8,64,256]{2,1,0:T(8,128)(2,1)S(1)}, bf16[8,64,256]{2,1,0:T(8,128)(2,1)S(1)}, u32[]{:S(2)}, u32[]{:S(2)}) collective-permute-start(bf16[8,64,256]{2,1,0:T(8,128)(2,1)S(1)} %add_convert_fusion.3), channel_id=1, source_target_pairs={{0,3},{1,2},{2,1},{3,0},{4,7},{5,6},{6,5},{7,4},{8,11},{9,10},{10,... | collective-permute-start | bytes 786440 | tf_op jit(solution)/shard_map/ppermute | solution.py:33
  22.2 6.8 %collective-permute-start.6 = (bf16[8,64,256]{2,1,0:T(8,128)(2,1)S(1)}, bf16[8,64,256]{2,1,0:T(8,128)(2,1)S(1)}, u32[]{:S(2)}, u32[]{:S(2)}) collective-permute-start(bf16[8,64,256]{2,1,0:T(8,128)(2,1)S(1)} %add_convert_fusion.1), channel_id=1, source_target_pairs={{0,1},{1,0},{2,3},{3,2},{4,5},{5,4},{6,7},{7,6},{8,9},{9,8},{10,11... | collective-permute-start | bytes 786440 | tf_op jit(solution)/shard_map/ppermute | solution.py:33
  23.3 10.2 %collective-permute-start.4 = (bf16[8,64,256]{2,1,0:T(8,128)(2,1)S(1)}, bf16[8,64,256]{2,1,0:T(8,128)(2,1)S(1)}, u32[]{:S(2)}, u32[]{:S(2)}) collective-permute-start(bf16[8,64,256]{2,1,0:T(8,128)(2,1)S(1)} %get-tuple-element.41), channel_id=1, source_target_pairs={{0,3},{1,2},{2,1},{3,0},{4,7},{5,6},{6,5},{7,4},{8,11},{9,10},{10,... | collective-permute-start | bytes 786440 | tf_op jit(solution)/shard_map/ppermute | solution.py:33
  33.6 32.9 %copy-start.2 = (bf16[128,8192]{1,0:T(8,128)(2,1)S(1)}, bf16[128,8192]{1,0:T(8,128)(2,1)}, u32[]{:S(2)}) copy-start(bf16[128,8192]{1,0:T(8,128)(2,1)} %refs_8_.1) | copy-start | bytes 6291460
  34.5 22.4 %all-to-all-start = ((bf16[8,128,256]{2,1,0:T(8,128)(2,1)}), bf16[8,128,256]{2,1,0:T(8,128)(2,1)S(1)}, u32[]{:S(2)}, u32[]{:S(2)}) async-start(bf16[8,128,256]{2,1,0:T(8,128)(2,1)} %pad_maximum_fusion.1), calls=%async_computation | async-start | bytes 1048576 | tf_op jit(solution)/shard_map/all_to_all | solution.py:259
  58.9 20.9 %all-to-all-start.1 = ((bf16[8,432,128]{2,1,0:T(8,128)(2,1)}), bf16[8,432,128]{2,1,0:T(8,128)(2,1)S(1)}, u32[]{:S(2)}, u32[]{:S(2)}) async-start(bf16[8,432,128]{2,1,0:T(8,128)(2,1)} %pad_maximum_fusion), calls=%async_computation.1 | async-start | bytes 1769472 | tf_op jit(solution)/shard_map/all_to_all | solution.py:273
  83.9 7.6 %collective-permute-start.9 = (bf16[8,32,512]{2,1,0:T(8,128)(2,1)S(1)}, bf16[8,32,512]{2,1,0:T(8,128)(2,1)S(1)}, u32[]{:S(2)}, u32[]{:S(2)}) collective-permute-start(bf16[8,32,512]{2,1,0:T(8,128)(2,1)S(1)} %bitcast.61), channel_id=1, source_target_pairs={{0,1},{1,0},{2,3},{3,2},{4,5},{5,4},{6,7},{7,6},{8,9},{9,8},{10,11... | collective-permute-start | bytes 786440 | tf_op jit(solution)/shard_map/ppermute | solution.py:33
  84.8 10.4 %collective-permute-start.12 = (bf16[8,32,512]{2,1,0:T(8,128)(2,1)S(1)}, bf16[8,32,512]{2,1,0:T(8,128)(2,1)S(1)}, u32[]{:S(2)}, u32[]{:S(2)}) collective-permute-start(bf16[8,32,512]{2,1,0:T(8,128)(2,1)S(1)} %bitcast.59), channel_id=1, source_target_pairs={{0,3},{1,2},{2,1},{3,0},{4,7},{5,6},{6,5},{7,4},{8,11},{9,10},{10,... | collective-permute-start | bytes 786440 | tf_op jit(solution)/shard_map/ppermute | solution.py:33
  89.8 7.3 %collective-permute-start.8 = (bf16[8,32,512]{2,1,0:T(8,128)(2,1)S(1)}, bf16[8,32,512]{2,1,0:T(8,128)(2,1)S(1)}, u32[]{:S(2)}, u32[]{:S(2)}) collective-permute-start(bf16[8,32,512]{2,1,0:T(8,128)(2,1)S(1)} %bitcast.60), channel_id=1, source_target_pairs={{0,1},{1,0},{2,3},{3,2},{4,5},{5,4},{6,7},{7,6},{8,9},{9,8},{10,11... | collective-permute-start | bytes 786440 | tf_op jit(solution)/shard_map/ppermute | solution.py:33
  91.6 7.9 %collective-permute-start.10 = (bf16[8,32,512]{2,1,0:T(8,128)(2,1)S(1)}, bf16[8,32,512]{2,1,0:T(8,128)(2,1)S(1)}, u32[]{:S(2)}, u32[]{:S(2)}) collective-permute-start(bf16[8,32,512]{2,1,0:T(8,128)(2,1)S(1)} %fusion.3), channel_id=1, source_target_pairs={{0,3},{1,2},{2,1},{3,0},{4,7},{5,6},{6,5},{7,4},{8,11},{9,10},{10,... | collective-permute-start | bytes 786440 | tf_op jit(solution)/shard_map/ppermute | solution.py:33
  94.9 10.2 %collective-permute-start.11 = (bf16[8,32,512]{2,1,0:T(8,128)(2,1)S(1)}, bf16[8,32,512]{2,1,0:T(8,128)(2,1)S(1)}, u32[]{:S(2)}, u32[]{:S(2)}) collective-permute-start(bf16[8,32,512]{2,1,0:T(8,128)(2,1)S(1)} %bitcast.58), channel_id=1, source_target_pairs={{0,3},{1,2},{2,1},{3,0},{4,7},{5,6},{6,5},{7,4},{8,11},{9,10},{10,... | collective-permute-start | bytes 786440 | tf_op jit(solution)/shard_map/ppermute | solution.py:33
  95.3 9.8 %collective-permute-start.13 = (bf16[8,32,512]{2,1,0:T(8,128)(2,1)S(1)}, bf16[8,32,512]{2,1,0:T(8,128)(2,1)S(1)}, u32[]{:S(2)}, u32[]{:S(2)}) collective-permute-start(bf16[8,32,512]{2,1,0:T(8,128)(2,1)S(1)} %fusion), channel_id=1, source_target_pairs={{0,1},{1,0},{2,3},{3,2},{4,5},{5,4},{6,7},{7,6},{8,9},{9,8},{10,11... | collective-permute-start | bytes 786440 | tf_op jit(solution)/shard_map/ppermute | solution.py:33
  106.1 18.9 %all-to-all-start.2 = ((bf16[8,64,512]{2,1,0:T(8,128)(2,1)}), bf16[8,64,512]{2,1,0:T(8,128)(2,1)}, u32[]{:S(2)}, u32[]{:S(2)}) async-start(bf16[8,64,512]{2,1,0:T(8,128)(2,1)} %pad_maximum_fusion.2), calls=%async_computation.2 | async-start | bytes 1048576 | tf_op jit(solution)/shard_map/all_to_all | solution.py:65
  142.4 6.5 %collective-permute-start.15 = (bf16[256,512]{1,0:T(8,128)(2,1)S(1)}, bf16[256,512]{1,0:T(8,128)(2,1)S(1)}, u32[]{:S(2)}, u32[]{:S(2)}) collective-permute-start(bf16[256,512]{1,0:T(8,128)(2,1)S(1)} %bitcast.50), channel_id=1, source_target_pairs={{0,3},{1,2},{2,1},{3,0},{4,7},{5,6},{6,5},{7,4},{8,11},{9,10},{10,... | collective-permute-start | bytes 786440 | tf_op jit(solution)/shard_map/ppermute | solution.py:33
  143.8 5.9 %collective-permute-start.17 = (bf16[256,512]{1,0:T(8,128)(2,1)S(1)}, bf16[256,512]{1,0:T(8,128)(2,1)S(1)}, u32[]{:S(2)}, u32[]{:S(2)}) collective-permute-start(bf16[256,512]{1,0:T(8,128)(2,1)S(1)} %bitcast.47), channel_id=1, source_target_pairs={{0,1},{1,0},{2,3},{3,2},{4,5},{5,4},{6,7},{7,6},{8,9},{9,8},{10,11... | collective-permute-start | bytes 786440 | tf_op jit(solution)/shard_map/ppermute | solution.py:33
  144.5 7.6 %collective-permute-start.14 = (bf16[256,512]{1,0:T(8,128)(2,1)S(1)}, bf16[256,512]{1,0:T(8,128)(2,1)S(1)}, u32[]{:S(2)}, u32[]{:S(2)}) collective-permute-start(bf16[256,512]{1,0:T(8,128)(2,1)S(1)} %bitcast.51), channel_id=1, source_target_pairs={{0,1},{1,0},{2,3},{3,2},{4,5},{5,4},{6,7},{7,6},{8,9},{9,8},{10,11... | collective-permute-start | bytes 786440 | tf_op jit(solution)/shard_map/ppermute | solution.py:33
  145.2 6.9 %collective-permute-start.19 = (bf16[256,512]{1,0:T(8,128)(2,1)S(1)}, bf16[256,512]{1,0:T(8,128)(2,1)S(1)}, u32[]{:S(2)}, u32[]{:S(2)}) collective-permute-start(bf16[256,512]{1,0:T(8,128)(2,1)S(1)} %bitcast.48), channel_id=1, source_target_pairs={{0,3},{1,2},{2,1},{3,0},{4,7},{5,6},{6,5},{7,4},{8,11},{9,10},{10,... | collective-permute-start | bytes 786440 | tf_op jit(solution)/shard_map/ppermute | solution.py:33
  148.9 8.1 %collective-permute-start.16 = (bf16[256,512]{1,0:T(8,128)(2,1)S(1)}, bf16[256,512]{1,0:T(8,128)(2,1)S(1)}, u32[]{:S(2)}, u32[]{:S(2)}) collective-permute-start(bf16[256,512]{1,0:T(8,128)(2,1)S(1)} %collective-permute-done.15.refs_3_), channel_id=1, source_target_pairs={{0,1},{1,0},{2,3},{3,2},{4,5},{5,4},{6,7},{7,6},{8,9},{9,8},{10,11... | collective-permute-start | bytes 786440 | tf_op jit(solution)/shard_map/ppermute | solution.py:33
  149.7 9.6 %collective-permute-start.18 = (bf16[256,512]{1,0:T(8,128)(2,1)S(1)}, bf16[256,512]{1,0:T(8,128)(2,1)S(1)}, u32[]{:S(2)}, u32[]{:S(2)}) collective-permute-start(bf16[256,512]{1,0:T(8,128)(2,1)S(1)} %collective-permute-done.17.refs_5_), channel_id=1, source_target_pairs={{0,3},{1,2},{2,1},{3,0},{4,7},{5,6},{6,5},{7,4},{8,11},{9,10},{10,... | collective-permute-start | bytes 786440 | tf_op jit(solution)/shard_map/ppermute | solution.py:33
  (12 other events, 95.8 us)

commit v11 on v10

--- a/solution.py
+++ b/solution.py
@@ -130,6 +130,45 @@
     outs = [jax.ShapeDtypeStruct((NZ, 64, 256), B16)] * (2 * len(jobs))
     flops = 2 * 128 * 256 * 2048 * len(jobs)
     return call(functools.partial(teacher_kernel, jobs), specs, outs, flops, (), 20)(place, own, there, held)
+
+
+def payload_kernel(place_ref, moved_ref, resid_ref, heads_ref, matches_ref, parts_ref, sent_ref):
+    seq = place_ref[1]
+    summed = moved_ref[0].astype(F32)
+    for z in range(1, NZ):
+        summed += moved_ref[z].astype(F32)
+    near = resid_ref[pl.ds(pl.multiple_of(seq * 64, 64), 64), :]
+    far = resid_ref[pl.ds(pl.multiple_of(64 - seq * 64, 64), 64), :]
+    hidden = (jnp.concatenate([near, far], axis=0).astype(F32) + summed).astype(B16)
+    matched = jnp.broadcast_to(matches_ref[...].astype(F32), (16, 128)).astype(B16)
+    for gs in range(NY):
+        sent_ref[gs, 0:128, :] = hidden[:, :128]
+        sent_ref[gs, 128:256, :] = hidden[:, 128:]
+        sent_ref[gs, 256:384, :] = heads_ref[...]
+        sent_ref[gs, 384:400, :] = matched
+        sent_ref[gs, 400:432, :] = parts_ref[gs]
+
+
+def payload(place, moved, resid, heads, matches, parts):
+    specs = [whole(NZ, 128, 256), whole(128, 256), whole(128, 128), whole(1, 128), whole(NY, 32, 128)]
+    outs = [jax.ShapeDtypeStruct((NY, 432, 128), B16)]
+    return call(payload_kernel, specs, outs, 1 << 20)(place, moved, resid, heads, matches, parts)[0]
+
+
+def last_kernel(place_ref, back_ref, grad_ref, lines_ref):
+    grad = back_ref[0, 0:128, :].astype(F32)
+    lines = back_ref[0, 128:144, :].astype(F32)
+    for gs in range(1, NY):
+        grad += back_ref[gs, 0:128, :].astype(F32)
+        lines += back_ref[gs, 128:144, :].astype(F32)
+    grad_ref[...] = grad.astype(B16)
+    total = jnp.sum(jnp.sum(lines, axis=1, keepdims=True), axis=0, keepdims=True)
+    lines_ref[...] = jnp.broadcast_to(total * (64.0 / (ROWS * 8192)), (1, 128))
+
+
+def last_sums(place, back):
+    outs = [jax.ShapeDtypeStruct((128, 128), B16), jax.ShapeDtypeStruct((1, 128), F32)]
+    return call(last_kernel, [whole(NY, 144, 128)], outs, 1 << 18)(place, back)
 
 
 def layout_kernel(place_ref, home_in, other_in, out_in, weights_ref, out_ref):
@@ -246,30 +285,21 @@
 
     there = lax.ppermute(teacher_heads, "seq", swap)
     held = load(place, teacher_out)
-    far = teacher_parts(((2, 0, 1),), place, teacher_heads, there, held)
-    rest = teacher_parts(((1, 0, 3), (3, 1, 4), (0, 2, 5)), place, teacher_heads, there, held)
-    first = (rest[2], rest[0], far[0], rest[1])
-    second = [rest[5], rest[3], far[1], rest[4]]
-
-    second[2], later = lax.optimization_barrier((second[2], member))
+    jobs = ((2, 2, 6), (1, 1, 5), (3, 3, 7), (0, 0, 4))
+    parts = list(teacher_parts(jobs, place, teacher_heads, there, held))
+    first, second = parts[:NX], parts[NX:]
+
+    second[0], later = lax.optimization_barrier((second[0], member))
     away = lax.dynamic_slice(projector, (0, (later + 1 - 2 * seq) * COLS), (256, COLS))
     other = lax.ppermute(away, "seq", swap)
 
-    summed, other = reduce_x(first, second, (), (other,))
+    summed, other = reduce_x(first, second, (away,), (other,))
     moved = lax.all_to_all(summed, "z", 0, 0)
-    near = lax.dynamic_slice(teacher_resid, (seq * 64, 0), (64, 256))
-    far = lax.dynamic_slice(teacher_resid, (64 - seq * 64, 0), (64, 256))
-    hidden = (jnp.concatenate([near, far], axis=0).astype(F32) + jnp.sum(moved.astype(F32), axis=0)).astype(B16)
-
-    spot, hidden = lax.optimization_barrier((place, hidden))
+    own_matches = lax.dynamic_slice(matches, (seq * 128,), (128,)).astype(B16)
+    resid_parts = jnp.transpose(student_resid.reshape(4, NY, 8, 128), (1, 0, 2, 3)).reshape(NY, 32, 128)
+    sent = payload(place, moved, teacher_resid, student_heads, own_matches.reshape(1, 128), resid_parts)
+    spot, sent = lax.optimization_barrier((place, sent))
     weights, out_cols = layout(spot, projector, other, student_out)
-
-    own_matches = lax.dynamic_slice(matches, (seq * 128,), (128,)).astype(B16)
-    shared = jnp.concatenate(
-        [hidden[:, :128], hidden[:, 128:], student_heads, jnp.broadcast_to(own_matches[None], (16, 128))], axis=0
-    )
-    resid_parts = jnp.transpose(student_resid.reshape(4, NY, 8, 128), (1, 0, 2, 3)).reshape(NY, 32, 128)
-    sent = jnp.concatenate([jnp.broadcast_to(shared[None], (NY,) + shared.shape), resid_parts], axis=1)
     got = lax.all_to_all(sent, COLUMN, 0, 0)
     heads = own_order(got[:, 256:384]).reshape(NX, 256, 128)
     base = (jnp.arange(NY, dtype=jnp.int32) // 2 * 128)[:, None]
@@ -291,10 +321,9 @@
     sent = jnp.concatenate(
         [block_order(heads_part.reshape(ROWS, 128)), jnp.broadcast_to(squares[None], (NY, 16, 128))], axis=1
     )
-    back = lax.all_to_all(sent, COLUMN, 0, 0).astype(F32)
-    grad_heads = jnp.sum(back[:, :128], axis=0).astype(B16)
-    total = jnp.sum(back[:, 128:])
-    loss = (total * (64.0 / (ROWS * 8192))).reshape(1)
+    back = lax.all_to_all(sent, COLUMN, 0, 0)
+    grad_heads, loss = last_sums(place, back)
+    loss = loss[0, :1]
     return (loss, grad_heads, grad_weight)
 
 

time: 183 us -> 176 us (0.962)
  other arithmetic: 7.78 us -> 4.85 us
  waiting for transfers between devices: 67.1 us -> 64.5 us
  between operations: 2.78 us -> 0.92 us
    ppermute x1, waiting for transfers between devices: 3.33 us -> 0.56 us  [local(): other = lax.ppermute(away, 'seq', swap)]
    unnamed x26 -> x28, local copies, waits for them, and re-layouts: 12.4 us -> 9.89 us
    pallas_call x0 -> x2, Pallas kernels: none -> 1.84 us  [the longest x1 1.19 us: last_sums(): return call(last_kernel, [whole(NY, 144, 128)], outs, 1 << 18)(place, back)]
  transfers between devices with their start and end apart: 23 -> 23, of which waited for: 15 -> 16; matrix products, arithmetic and copies ran while one was open for 2% -> 2% of each run, Pallas kernels for 3% -> 2%
where the time goes in v11:
time: 176 us; the launch traced here: 175 us
  waiting for transfers between devices  64.5 us (37%)
  starting transfers between devices  46.5 us (26%)
  blocking collectives  34 us (19%)
  local copies, waits for them, and re-layouts  12.7 us (7%)
  Pallas kernels  11.4 us (6%)
  other arithmetic  4.85 us (3%)
    ppermute x18, waiting for transfers between devices, across(): return lax.ppermute(block, 'x', [(i, i ^ flip) for i in range(NX)])  27.7 us
    ppermute x18, starting transfers between devices, across(): return lax.ppermute(block, 'x', [(i, i ^ flip) for i in range(NX)])  21.1 us
    all_to_all x1, blocking collectives, local(): back = lax.all_to_all(sent, COLUMN, 0, 0)  17.8 us
    all_to_all x1, blocking collectives, local(): lax.all_to_all(jnp.broadcast_to(grad[None], (NZ, 64, HALF)), 'z', 0, 0)  16.2 us
    all_to_all x1, waiting for transfers between devices, reduce_z(): moved = lax.all_to_all(parts, 'z', 0, 0)  14.5 us
    all_to_all x1, waiting for transfers between devices, local(): moved = lax.all_to_all(summed, 'z', 0, 0)  13 us
    unnamed x28, local copies, waits for them, and re-layouts  9.89 us
    all_to_all x1, waiting for transfers between devices, local(): got = lax.all_to_all(sent, COLUMN, 0, 0)  8.7 us
  transfers between devices with their start and end apart: 23, of which 16 were waited for; matrix products, arithmetic and copies ran while one was open for 2% of the time, Pallas kernels for 2%

profile of v11, /device:TPU:1, one launch (start us, length us, event | category | flops | bytes accessed | tf_op | source)
XLA Modules:
  0.0 174.9 jit_solution(5889264676259104874)
XLA Ops:
  0.6 3.8 %collective-permute-start = (bf16[64,256]{1,0:T(8,128)(2,1)}, bf16[64,256]{1,0:T(8,128)(2,1)S(1)}, u32[]{:S(2)}, u32[]{:S(2)}) collective-permute-start(bf16[64,256]{1,0:T(8,128)(2,1)} %own_ref.1), channel_id=1, source_target_pairs={{0,32},{32,0},{1,33},{33,1},{2,34},{34,2},{3,35},{35,3},{4,36},{36... | collective-permute-start | bytes 98312 | tf_op jit(solution)/shard_map/ppermute | solution.py:286
  4.5 2.2 %copy-done.2 = bf16[256,8192]{1,0:T(8,128)(2,1)S(1)} copy-done((bf16[256,8192]{1,0:T(8,128)(2,1)S(1)}, bf16[256,8192]{1,0:T(8,128)(2,1)}, u32[]{:S(2)}) %copy-start.2) | copy-done | bytes 4194328
  7.8 1.9 %shard_map.104 = (bf16[8,64,256]{2,1,0:T(8,128)(2,1)S(1)}, bf16[8,64,256]{2,1,0:T(8,128)(2,1)}, bf16[8,64,256]{2,1,0:T(8,128)(2,1)S(1)}, bf16[8,64,256]{2,1,0:T(...) custom-call(s32[3]{0:T(128)S(1)} %pad_add_fusion.place_ref, ...), custom_call_target="tpu_custom_call" | custom-call | flops 536870912 | bytes 5242880 | tf_op jit(solution)/shard_map/pallas_call | solution.py:132
  10.9 1.8 %collective-permute-start.5 = (bf16[8,64,256]{2,1,0:T(8,128)(2,1)S(1)}, bf16[8,64,256]{2,1,0:T(8,128)(2,1)S(1)}, u32[]{:S(2)}, u32[]{:S(2)}) collective-permute-start(bf16[8,64,256]{2,1,0:T(8,128)(2,1)S(1)} %get-tuple-element.47), channel_id=1, source_target_pairs={{0,3},{1,2},{2,1},{3,0},{4,7},{5,6},{6,5},{7,4},{8,11},{9,10},{10,... | collective-permute-start | bytes 786440 | tf_op jit(solution)/shard_map/ppermute | solution.py:33
  15.8 3.5 %collective-permute-start.3 = (bf16[8,64,256]{2,1,0:T(8,128)(2,1)S(1)}, bf16[8,64,256]{2,1,0:T(8,128)(2,1)S(1)}, u32[]{:S(2)}, u32[]{:S(2)}) collective-permute-start(bf16[8,64,256]{2,1,0:T(8,128)(2,1)S(1)} %add_convert_fusion.3), channel_id=1, source_target_pairs={{0,3},{1,2},{2,1},{3,0},{4,7},{5,6},{6,5},{7,4},{8,11},{9,10},{10,... | collective-permute-start | bytes 786440 | tf_op jit(solution)/shard_map/ppermute | solution.py:33
  23.4 3.4 %collective-permute-done.6 = bf16[8,64,256]{2,1,0:T(8,128)(2,1)S(1)} collective-permute-done((bf16[8,64,256]{2,1,0:T(8,128)(2,1)S(1)}, bf16[8,64,256]{2,1,0:T(8,128)(2,1)S(1)}, u32[]{:S(2)}, u32[]{:S(2)}) %collective-permute-start.6) | collective-permute-done | bytes 262176 | tf_op jit(solution)/shard_map/ppermute | solution.py:33
  27.3 2.0 %collective-permute-done.4 = bf16[8,64,256]{2,1,0:T(8,128)(2,1)S(1)} collective-permute-done((bf16[8,64,256]{2,1,0:T(8,128)(2,1)}, bf16[8,64,256]{2,1,0:T(8,128)(2,1)S(1)}, u32[]{:S(2)}, u32[]{:S(2)}) %collective-permute-start.4) | collective-permute-done | bytes 262176 | tf_op jit(solution)/shard_map/ppermute | solution.py:33
  30.3 8.2 %all-to-all-start = ((bf16[8,128,256]{2,1,0:T(8,128)(2,1)}), bf16[8,128,256]{2,1,0:T(8,128)(2,1)S(1)}, u32[]{:S(2)}, u32[]{:S(2)}) async-start(bf16[8,128,256]{2,1,0:T(8,128)(2,1)} %pad_maximum_fusion), calls=%async_computation | async-start | bytes 1048576 | tf_op jit(solution)/shard_map/all_to_all | solution.py:297
  39.5 13.0 %all-to-all-done.moved_ref = bf16[8,128,256]{2,1,0:T(8,128)(2,1)S(1)} async-done(((bf16[8,128,256]{2,1,0:T(8,128)(2,1)}), bf16[8,128,256]{2,1,0:T(8,128)(2,1)S(1)}, u32[]{:S(2)}, u32[]{:S(2)}) %all-to-all-start) | async-done | bytes 524320 | tf_op jit(solution)/shard_map/all_to_all | solution.py:297
  54.0 8.0 %all-to-all-start.1 = ((bf16[8,432,128]{2,1,0:T(8,128)(2,1)}), bf16[8,432,128]{2,1,0:T(8,128)(2,1)S(1)}, u32[]{:S(2)}, u32[]{:S(2)}) async-start(bf16[8,432,128]{2,1,0:T(8,128)(2,1)} %copy-done.3), calls=%async_computation.1 | async-start | bytes 1769472 | tf_op jit(solution)/shard_map/all_to_all | solution.py:303
  62.0 2.2 %copy-done.1 = bf16[256,8192]{1,0:T(8,128)(2,1)S(1)} copy-done((bf16[256,8192]{1,0:T(8,128)(2,1)S(1)}, bf16[256,8192]{1,0:T(8,128)(2,1)}, u32[]{:S(2)}) %copy-start.1) | copy-done | bytes 4194328
  66.5 8.7 %all-to-all-done.1.got_ref = bf16[8,432,128]{2,1,0:T(8,128)(2,1)S(1)} async-done(((bf16[8,432,128]{2,1,0:T(8,128)(2,1)}), bf16[8,432,128]{2,1,0:T(8,128)(2,1)S(1)}, u32[]{:S(2)}, u32[]{:S(2)}) %all-to-all-start.1) | async-done | bytes 884768 | tf_op jit(solution)/shard_map/all_to_all | solution.py:303
  79.9 2.7 %collective-permute-start.12 = (bf16[8,32,512]{2,1,0:T(8,128)(2,1)S(1)}, bf16[8,32,512]{2,1,0:T(8,128)(2,1)S(1)}, u32[]{:S(2)}, u32[]{:S(2)}) collective-permute-start(bf16[8,32,512]{2,1,0:T(8,128)(2,1)S(1)} %bitcast.62), channel_id=1, source_target_pairs={{0,3},{1,2},{2,1},{3,0},{4,7},{5,6},{6,5},{7,4},{8,11},{9,10},{10,... | collective-permute-start | bytes 786440 | tf_op jit(solution)/shard_map/ppermute | solution.py:33
  82.6 2.5 %shard_map.107 = (bf16[256,512]{1,0:T(8,128)(2,1)S(1)}, bf16[256,512]{1,0:T(8,128)(2,1)S(1)}, bf16[256,512]{1,0:T(8,128)(2,1)S(1)}, bf16[256,512]{1,0:T(8,128)(2...) custom-call(s32[3]{0:T(128)S(1)} %pad_add_fusion.place_ref, ...), custom_call_target="tpu_custom_call" | custom-call | flops 1415577600 | bytes 5242880 | tf_op jit(solution)/shard_map/pallas_call | solution.py:227
  87.1 2.9 %collective-permute-start.10 = (bf16[8,32,512]{2,1,0:T(8,128)(2,1)S(1)}, bf16[8,32,512]{2,1,0:T(8,128)(2,1)S(1)}, u32[]{:S(2)}, u32[]{:S(2)}) collective-permute-start(bf16[8,32,512]{2,1,0:T(8,128)(2,1)S(1)} %fusion.3), channel_id=1, source_target_pairs={{0,3},{1,2},{2,1},{3,0},{4,7},{5,6},{6,5},{7,4},{8,11},{9,10},{10,... | collective-permute-start | bytes 786440 | tf_op jit(solution)/shard_map/ppermute | solution.py:33
  92.0 2.5 %collective-permute-done.10 = bf16[8,32,512]{2,1,0:T(8,128)(2,1)S(1)} collective-permute-done((bf16[8,32,512]{2,1,0:T(8,128)(2,1)S(1)}, bf16[8,32,512]{2,1,0:T(8,128)(2,1)S(1)}, u32[]{:S(2)}, u32[]{:S(2)}) %collective-permute-start.10) | collective-permute-done | bytes 262176 | tf_op jit(solution)/shard_map/ppermute | solution.py:33
  94.6 5.5 %collective-permute-done.11 = bf16[8,32,512]{2,1,0:T(8,128)(2,1)S(1)} collective-permute-done((bf16[8,32,512]{2,1,0:T(8,128)(2,1)S(1)}, bf16[8,32,512]{2,1,0:T(8,128)(2,1)S(1)}, u32[]{:S(2)}, u32[]{:S(2)}) %collective-permute-start.11) | collective-permute-done | bytes 262176 | tf_op jit(solution)/shard_map/ppermute | solution.py:33
  101.1 4.1 %all-to-all-start.2 = ((bf16[8,64,512]{2,1,0:T(8,128)(2,1)}), bf16[8,64,512]{2,1,0:T(8,128)(2,1)}, u32[]{:S(2)}, u32[]{:S(2)}) async-start(bf16[8,64,512]{2,1,0:T(8,128)(2,1)} %pad_maximum_fusion.1), calls=%async_computation.2 | async-start | bytes 1048576 | tf_op jit(solution)/shard_map/all_to_all | solution.py:65
  105.5 14.5 %all-to-all-done.2 = bf16[8,64,512]{2,1,0:T(8,128)(2,1)} async-done(((bf16[8,64,512]{2,1,0:T(8,128)(2,1)}), bf16[8,64,512]{2,1,0:T(8,128)(2,1)}, u32[]{:S(2)}, u32[]{:S(2)}) %all-to-all-start.2) | async-done | bytes 524320 | tf_op jit(solution)/shard_map/all_to_all | solution.py:65
  121.2 16.2 %all_to_all.25 = bf16[8,64,512]{2,1,0:T(8,128)(2,1)S(1)} all-to-all(bf16[8,64,512]{2,1,0:T(8,128)(2,1)S(1)} %broadcast_in_dim.4), channel_id=1, replica_groups=mesh['ylo'=2,'core'=2,'seq'=2,'z'=8,'x'=4] {'z'}, dimensions={0} | all-to-all | bytes 1048576 | tf_op jit(solution)/shard_map/all_to_all | solution.py:317
  141.7 2.3 %collective-permute-done.15.refs_3_ = bf16[256,512]{1,0:T(8,128)(2,1)S(1)} collective-permute-done((bf16[256,512]{1,0:T(8,128)(2,1)S(1)}, bf16[256,512]{1,0:T(8,128)(2,1)S(1)}, u32[]{:S(2)}, u32[]{:S(2)}) %collective-permute-start.15) | collective-permute-done | bytes 262176 | tf_op jit(solution)/shard_map/ppermute | solution.py:33
  147.1 4.9 %collective-permute-done.16.refs_2_ = bf16[256,512]{1,0:T(8,128)(2,1)S(1)} collective-permute-done((bf16[256,512]{1,0:T(8,128)(2,1)S(1)}, bf16[256,512]{1,0:T(8,128)(2,1)S(1)}, u32[]{:S(2)}, u32[]{:S(2)}) %collective-permute-start.16) | collective-permute-done | bytes 262176 | tf_op jit(solution)/shard_map/ppermute | solution.py:33
  153.6 2.2 %shard_map.109 = (bf16[4,256,128]{2,1,0:T(8,128)(2,1)S(1)}, bf16[16,128]{1,0:T(8,128)(2,1)S(1)}, bf16[128,1024]{1,0:T(8,128)(2,1)}) custom-call(s32[3]{0:T(128)S(1)} %pad_add_fusion.place_ref, bf16[256,512]{1,0:T(8,128)(2,1)S(1)} %bitcast.55, bf16[256,512]{1,0:T(8,128)(2,1)S(1)} %collective-permute-done.14.refs_1_, ...), custom_call_target="tpu_custom_call" | custom-call | flops 536870912 | bytes 5242880 | tf_op jit(solution)/shard_map/pallas_call | solution.py:266
  155.9 17.8 %all_to_all.26.back_ref = bf16[8,144,128]{2,1,0:T(8,128)(2,1)S(1)} all-to-all(bf16[8,144,128]{2,1,0:T(8,128)(2,1)S(1)} %pad_maximum_fusion.2), channel_id=1, replica_groups=mesh['ylo'=2,'core'=2,'seq'=2,'z'=8,'x'=4] {'ylo','core','seq'}, dimensions={0} | all-to-all | bytes 589824 | tf_op jit(solution)/shard_map/all_to_all | solution.py:324
  (93 shorter events, 37.2 us)
Async XLA Ops:
  0.6 7.1 %collective-permute-start = (bf16[64,256]{1,0:T(8,128)(2,1)}, bf16[64,256]{1,0:T(8,128)(2,1)S(1)}, u32[]{:S(2)}, u32[]{:S(2)}) collective-permute-start(bf16[64,256]{1,0:T(8,128)(2,1)} %own_ref.1), channel_id=1, source_target_pairs={{0,32},{32,0},{1,33},{33,1},{2,34},{34,2},{3,35},{35,3},{4,36},{36... | collective-permute-start | bytes 98312 | tf_op jit(solution)/shard_map/ppermute | solution.py:286
  9.6 42.8 %copy-start.10 = (bf16[128,128]{1,0:T(8,128)(2,1)S(1)}, bf16[128,128]{1,0:T(8,128)(2,1)}, u32[]{:S(2)}) copy-start(bf16[128,128]{1,0:T(8,128)(2,1)} %heads_ref.1) | copy-start | bytes 98308
  9.6 6.1 %collective-permute-start.2 = (bf16[8,64,256]{2,1,0:T(8,128)(2,1)S(1)}, bf16[8,64,256]{2,1,0:T(8,128)(2,1)S(1)}, u32[]{:S(2)}, u32[]{:S(2)}) collective-permute-start(bf16[8,64,256]{2,1,0:T(8,128)(2,1)S(1)} %get-tuple-element.43), channel_id=1, source_target_pairs={{0,1},{1,0},{2,3},{3,2},{4,5},{5,4},{6,7},{7,6},{8,9},{9,8},{10,11... | collective-permute-start | bytes 786440 | tf_op jit(solution)/shard_map/ppermute | solution.py:33
  10.9 8.3 %collective-permute-start.5 = (bf16[8,64,256]{2,1,0:T(8,128)(2,1)S(1)}, bf16[8,64,256]{2,1,0:T(8,128)(2,1)S(1)}, u32[]{:S(2)}, u32[]{:S(2)}) collective-permute-start(bf16[8,64,256]{2,1,0:T(8,128)(2,1)S(1)} %get-tuple-element.47), channel_id=1, source_target_pairs={{0,3},{1,2},{2,1},{3,0},{4,7},{5,6},{6,5},{7,4},{8,11},{9,10},{10,... | collective-permute-start | bytes 786440 | tf_op jit(solution)/shard_map/ppermute | solution.py:33
  13.8 13.5 %collective-permute-start.7 = (bf16[256,1024]{1,0:T(8,128)(2,1)S(1)}, bf16[256,1024]{1,0:T(8,128)(2,1)S(1)}, u32[]{:S(2)}, u32[]{:S(2)}) collective-permute-start(bf16[256,1024]{1,0:T(8,128)(2,1)S(1)} %constant_dynamic-slice_fusion), channel_id=1, source_target_pairs={{0,32},{32,0},{1,33},{33,1},{2,34},{34,2},{3,35},{35,3},{4,36},{36... | collective-permute-start | bytes 1572872 | tf_op jit(solution)/shard_map/ppermute | solution.py:294
  15.1 7.5 %collective-permute-start.1 = (bf16[8,64,256]{2,1,0:T(8,128)(2,1)}, bf16[8,64,256]{2,1,0:T(8,128)(2,1)S(1)}, u32[]{:S(2)}, u32[]{:S(2)}) collective-permute-start(bf16[8,64,256]{2,1,0:T(8,128)(2,1)} %get-tuple-element.41), channel_id=1, source_target_pairs={{0,1},{1,0},{2,3},{3,2},{4,5},{5,4},{6,7},{7,6},{8,9},{9,8},{10,11... | collective-permute-start | bytes 786440 | tf_op jit(solution)/shard_map/ppermute | solution.py:33
  15.8 7.6 %collective-permute-start.3 = (bf16[8,64,256]{2,1,0:T(8,128)(2,1)S(1)}, bf16[8,64,256]{2,1,0:T(8,128)(2,1)S(1)}, u32[]{:S(2)}, u32[]{:S(2)}) collective-permute-start(bf16[8,64,256]{2,1,0:T(8,128)(2,1)S(1)} %add_convert_fusion.3), channel_id=1, source_target_pairs={{0,3},{1,2},{2,1},{3,0},{4,7},{5,6},{6,5},{7,4},{8,11},{9,10},{10,... | collective-permute-start | bytes 786440 | tf_op jit(solution)/shard_map/ppermute | solution.py:33
  21.1 5.6 %collective-permute-start.6 = (bf16[8,64,256]{2,1,0:T(8,128)(2,1)S(1)}, bf16[8,64,256]{2,1,0:T(8,128)(2,1)S(1)}, u32[]{:S(2)}, u32[]{:S(2)}) collective-permute-start(bf16[8,64,256]{2,1,0:T(8,128)(2,1)S(1)} %add_convert_fusion.1), channel_id=1, source_target_pairs={{0,1},{1,0},{2,3},{3,2},{4,5},{5,4},{6,7},{7,6},{8,9},{9,8},{10,11... | collective-permute-start | bytes 786440 | tf_op jit(solution)/shard_map/ppermute | solution.py:33
  21.2 8.1 %collective-permute-start.4 = (bf16[8,64,256]{2,1,0:T(8,128)(2,1)}, bf16[8,64,256]{2,1,0:T(8,128)(2,1)S(1)}, u32[]{:S(2)}, u32[]{:S(2)}) collective-permute-start(bf16[8,64,256]{2,1,0:T(8,128)(2,1)} %copy-done.11), channel_id=1, source_target_pairs={{0,3},{1,2},{2,1},{3,0},{4,7},{5,6},{6,5},{7,4},{8,11},{9,10},{10,... | collective-permute-start | bytes 786440 | tf_op jit(solution)/shard_map/ppermute | solution.py:33
  30.3 22.1 %all-to-all-start = ((bf16[8,128,256]{2,1,0:T(8,128)(2,1)}), bf16[8,128,256]{2,1,0:T(8,128)(2,1)S(1)}, u32[]{:S(2)}, u32[]{:S(2)}) async-start(bf16[8,128,256]{2,1,0:T(8,128)(2,1)} %pad_maximum_fusion), calls=%async_computation | async-start | bytes 1048576 | tf_op jit(solution)/shard_map/all_to_all | solution.py:297
  54.0 21.2 %all-to-all-start.1 = ((bf16[8,432,128]{2,1,0:T(8,128)(2,1)}), bf16[8,432,128]{2,1,0:T(8,128)(2,1)S(1)}, u32[]{:S(2)}, u32[]{:S(2)}) async-start(bf16[8,432,128]{2,1,0:T(8,128)(2,1)} %copy-done.3), calls=%async_computation.1 | async-start | bytes 1769472 | tf_op jit(solution)/shard_map/all_to_all | solution.py:303
  79.4 7.6 %collective-permute-start.9 = (bf16[8,32,512]{2,1,0:T(8,128)(2,1)S(1)}, bf16[8,32,512]{2,1,0:T(8,128)(2,1)S(1)}, u32[]{:S(2)}, u32[]{:S(2)}) collective-permute-start(bf16[8,32,512]{2,1,0:T(8,128)(2,1)S(1)} %bitcast.64), channel_id=1, source_target_pairs={{0,1},{1,0},{2,3},{3,2},{4,5},{5,4},{6,7},{7,6},{8,9},{9,8},{10,11... | collective-permute-start | bytes 786440 | tf_op jit(solution)/shard_map/ppermute | solution.py:33
  79.9 10.3 %collective-permute-start.12 = (bf16[8,32,512]{2,1,0:T(8,128)(2,1)S(1)}, bf16[8,32,512]{2,1,0:T(8,128)(2,1)S(1)}, u32[]{:S(2)}, u32[]{:S(2)}) collective-permute-start(bf16[8,32,512]{2,1,0:T(8,128)(2,1)S(1)} %bitcast.62), channel_id=1, source_target_pairs={{0,3},{1,2},{2,1},{3,0},{4,7},{5,6},{6,5},{7,4},{8,11},{9,10},{10,... | collective-permute-start | bytes 786440 | tf_op jit(solution)/shard_map/ppermute | solution.py:33
  85.1 6.9 %collective-permute-start.8 = (bf16[8,32,512]{2,1,0:T(8,128)(2,1)S(1)}, bf16[8,32,512]{2,1,0:T(8,128)(2,1)S(1)}, u32[]{:S(2)}, u32[]{:S(2)}) collective-permute-start(bf16[8,32,512]{2,1,0:T(8,128)(2,1)S(1)} %bitcast.63), channel_id=1, source_target_pairs={{0,1},{1,0},{2,3},{3,2},{4,5},{5,4},{6,7},{7,6},{8,9},{9,8},{10,11... | collective-permute-start | bytes 786440 | tf_op jit(solution)/shard_map/ppermute | solution.py:33
  87.1 7.4 %collective-permute-start.10 = (bf16[8,32,512]{2,1,0:T(8,128)(2,1)S(1)}, bf16[8,32,512]{2,1,0:T(8,128)(2,1)S(1)}, u32[]{:S(2)}, u32[]{:S(2)}) collective-permute-start(bf16[8,32,512]{2,1,0:T(8,128)(2,1)S(1)} %fusion.3), channel_id=1, source_target_pairs={{0,3},{1,2},{2,1},{3,0},{4,7},{5,6},{6,5},{7,4},{8,11},{9,10},{10,... | collective-permute-start | bytes 786440 | tf_op jit(solution)/shard_map/ppermute | solution.py:33
  89.9 10.2 %collective-permute-start.11 = (bf16[8,32,512]{2,1,0:T(8,128)(2,1)S(1)}, bf16[8,32,512]{2,1,0:T(8,128)(2,1)S(1)}, u32[]{:S(2)}, u32[]{:S(2)}) collective-permute-start(bf16[8,32,512]{2,1,0:T(8,128)(2,1)S(1)} %bitcast.61), channel_id=1, source_target_pairs={{0,3},{1,2},{2,1},{3,0},{4,7},{5,6},{6,5},{7,4},{8,11},{9,10},{10,... | collective-permute-start | bytes 786440 | tf_op jit(solution)/shard_map/ppermute | solution.py:33
  90.3 9.8 %collective-permute-start.13 = (bf16[8,32,512]{2,1,0:T(8,128)(2,1)S(1)}, bf16[8,32,512]{2,1,0:T(8,128)(2,1)S(1)}, u32[]{:S(2)}, u32[]{:S(2)}) collective-permute-start(bf16[8,32,512]{2,1,0:T(8,128)(2,1)S(1)} %fusion), channel_id=1, source_target_pairs={{0,1},{1,0},{2,3},{3,2},{4,5},{5,4},{6,7},{7,6},{8,9},{9,8},{10,11... | collective-permute-start | bytes 786440 | tf_op jit(solution)/shard_map/ppermute | solution.py:33
  101.1 18.9 %all-to-all-start.2 = ((bf16[8,64,512]{2,1,0:T(8,128)(2,1)}), bf16[8,64,512]{2,1,0:T(8,128)(2,1)}, u32[]{:S(2)}, u32[]{:S(2)}) async-start(bf16[8,64,512]{2,1,0:T(8,128)(2,1)} %pad_maximum_fusion.1), calls=%async_computation.2 | async-start | bytes 1048576 | tf_op jit(solution)/shard_map/all_to_all | solution.py:65
  137.5 6.5 %collective-permute-start.15 = (bf16[256,512]{1,0:T(8,128)(2,1)S(1)}, bf16[256,512]{1,0:T(8,128)(2,1)S(1)}, u32[]{:S(2)}, u32[]{:S(2)}) collective-permute-start(bf16[256,512]{1,0:T(8,128)(2,1)S(1)} %bitcast.53), channel_id=1, source_target_pairs={{0,3},{1,2},{2,1},{3,0},{4,7},{5,6},{6,5},{7,4},{8,11},{9,10},{10,... | collective-permute-start | bytes 786440 | tf_op jit(solution)/shard_map/ppermute | solution.py:33
  138.8 5.2 %collective-permute-start.17 = (bf16[256,512]{1,0:T(8,128)(2,1)S(1)}, bf16[256,512]{1,0:T(8,128)(2,1)S(1)}, u32[]{:S(2)}, u32[]{:S(2)}) collective-permute-start(bf16[256,512]{1,0:T(8,128)(2,1)S(1)} %bitcast.50), channel_id=1, source_target_pairs={{0,1},{1,0},{2,3},{3,2},{4,5},{5,4},{6,7},{7,6},{8,9},{9,8},{10,11... | collective-permute-start | bytes 786440 | tf_op jit(solution)/shard_map/ppermute | solution.py:33
  138.8 8.3 %collective-permute-start.14 = (bf16[256,512]{1,0:T(8,128)(2,1)S(1)}, bf16[256,512]{1,0:T(8,128)(2,1)S(1)}, u32[]{:S(2)}, u32[]{:S(2)}) collective-permute-start(bf16[256,512]{1,0:T(8,128)(2,1)S(1)} %bitcast.54), channel_id=1, source_target_pairs={{0,1},{1,0},{2,3},{3,2},{4,5},{5,4},{6,7},{7,6},{8,9},{9,8},{10,11... | collective-permute-start | bytes 786440 | tf_op jit(solution)/shard_map/ppermute | solution.py:33
  140.3 6.9 %collective-permute-start.19 = (bf16[256,512]{1,0:T(8,128)(2,1)S(1)}, bf16[256,512]{1,0:T(8,128)(2,1)S(1)}, u32[]{:S(2)}, u32[]{:S(2)}) collective-permute-start(bf16[256,512]{1,0:T(8,128)(2,1)S(1)} %bitcast.51), channel_id=1, source_target_pairs={{0,3},{1,2},{2,1},{3,0},{4,7},{5,6},{6,5},{7,4},{8,11},{9,10},{10,... | collective-permute-start | bytes 786440 | tf_op jit(solution)/shard_map/ppermute | solution.py:33
  144.0 8.1 %collective-permute-start.16 = (bf16[256,512]{1,0:T(8,128)(2,1)S(1)}, bf16[256,512]{1,0:T(8,128)(2,1)S(1)}, u32[]{:S(2)}, u32[]{:S(2)}) collective-permute-start(bf16[256,512]{1,0:T(8,128)(2,1)S(1)} %collective-permute-done.15.refs_3_), channel_id=1, source_target_pairs={{0,1},{1,0},{2,3},{3,2},{4,5},{5,4},{6,7},{7,6},{8,9},{9,8},{10,11... | collective-permute-start | bytes 786440 | tf_op jit(solution)/shard_map/ppermute | solution.py:33
  144.0 9.5 %collective-permute-start.18 = (bf16[256,512]{1,0:T(8,128)(2,1)S(1)}, bf16[256,512]{1,0:T(8,128)(2,1)S(1)}, u32[]{:S(2)}, u32[]{:S(2)}) collective-permute-start(bf16[256,512]{1,0:T(8,128)(2,1)S(1)} %collective-permute-done.17.refs_5_), channel_id=1, source_target_pairs={{0,3},{1,2},{2,1},{3,0},{4,7},{5,6},{6,5},{7,4},{8,11},{9,10},{10,... | collective-permute-start | bytes 786440 | tf_op jit(solution)/shard_map/ppermute | solution.py:33
  (13 other events, 134.3 us)

commit v12 on v11

--- a/solution.py
+++ b/solution.py
@@ -61,11 +61,6 @@
     return first, first_one, first_two, first_three, second, second_one, second_two, second_three
 
 
-def reduce_z(parts):
-    moved = lax.all_to_all(parts, "z", 0, 0)
-    return jnp.sum(moved.astype(F32), axis=0)
-
-
 def own_order(rows):
     rest = rows.shape[2:]
     parts = rows.reshape((NY, NZ, NX, 4) + rest)
@@ -155,6 +150,21 @@
     return call(payload_kernel, specs, outs, 1 << 20)(place, moved, resid, heads, matches, parts)[0]
 
 
+def gradient_kernel(place_ref, moved_ref, resid_ref, grad_ref):
+    total = moved_ref[0].astype(F32)
+    for z in range(1, NZ):
+        total += moved_ref[z].astype(F32)
+    grad = ((resid_ref[...].astype(F32) + total) * 0.125).astype(B16)
+    for z in range(NZ):
+        grad_ref[z] = grad
+
+
+def gradient_piece(place, moved, resid):
+    outs = [jax.ShapeDtypeStruct((NZ, 64, HALF), B16)]
+    specs = [whole(NZ, 64, HALF), whole(64, HALF)]
+    return call(gradient_kernel, specs, outs, 1 << 19, (), 8)(place, moved, resid)[0]
+
+
 def last_kernel(place_ref, back_ref, grad_ref, lines_ref):
     grad = back_ref[0, 0:128, :].astype(F32)
     lines = back_ref[0, 128:144, :].astype(F32)
@@ -171,10 +181,10 @@
     return call(last_kernel, [whole(NY, 144, 128)], outs, 1 << 18)(place, back)
 
 
-def layout_kernel(place_ref, home_in, other_in, out_in, weights_ref, out_ref):
+def layout_kernel(place_ref, home_in, other_in, out_in, weights_ref):
     weights_ref[0:256, :] = home_in[...]
     weights_ref[256:512, :] = other_in[...]
-    out_ref[...] = out_in[...]
+    weights_ref[512:640, :] = out_in[...]
 
 
 def layout(place, projector, other, student_out):
@@ -183,8 +193,8 @@
         whole(256, COLS),
         pl.BlockSpec((128, COLS), lambda i, m: (0, m[0])),
     ]
-    outs = [jax.ShapeDtypeStruct((512, COLS), B16), jax.ShapeDtypeStruct((128, COLS), B16)]
-    return call(layout_kernel, specs, outs, 1 << 21, (), 8)(place, projector, other, student_out)
+    outs = [jax.ShapeDtypeStruct((640, COLS), B16)]
+    return call(layout_kernel, specs, outs, 1 << 21, (), 8)(place, projector, other, student_out)[0]
 
 
 def gather_hidden(place_ref, got_ref, hidden_ref):
@@ -200,7 +210,7 @@
             hidden_ref[near, other] = got_ref[2 * g + 1 - seq, at + 64 : at + 128, :]
 
 
-def combine_kernel(jobs, place_ref, picked_ref, got_ref, heads_ref, out_ref, weights_ref, *refs):
+def combine_kernel(jobs, place_ref, picked_ref, got_ref, heads_ref, weights_ref, *refs):
     x = place_ref[2]
     parts, hidden_ref = refs[:-1], refs[-1]
     gather_hidden(place_ref, got_ref, hidden_ref)
@@ -211,8 +221,8 @@
         heads = heads_ref[k ^ x]
         for half, to in halves:
             columns = slice(half * HALF, (half + 1) * HALF)
-            total = dot(heads, out_ref[:, columns], ((1,), (0,)))
-            total -= dot(selected, weights_ref[:, columns], ((1,), (0,)))
+            total = dot(heads, weights_ref[512:640, columns], ((1,), (0,)))
+            total -= dot(selected, weights_ref[0:512, columns], ((1,), (0,)))
             parts[to][...] = total.astype(B16)
 
 
@@ -220,13 +230,13 @@
 REST = ((1, ((0, 0), (1, 3))), (3, ((1, 4), (0, 1))), (0, ((0, 2), (1, 5))))
 
 
-def combined_parts(jobs, place, picked, got, heads, out_cols, weights):
-    specs = [whole(NX, 1, 256), whole(NY, 432, 128), whole(NX, 256, 128), whole(128, COLS), whole(512, COLS)]
+def combined_parts(jobs, place, picked, got, heads, weights):
+    specs = [whole(NX, 1, 256), whole(NY, 432, 128), whole(NX, 256, 128), whole(640, COLS)]
     count = sum(len(halves) for _, halves in jobs)
     outs = [jax.ShapeDtypeStruct((256, HALF), B16)] * count
     return call(
         functools.partial(combine_kernel, jobs), specs, outs, count * 2 * 256 * 512 * 900, [pltpu.VMEM((512, 512), B16)], 16
-    )(place, picked, got, heads, out_cols, weights)
+    )(place, picked, got, heads, weights)
 
 
 def final_kernel(place_ref, *refs):
@@ -299,22 +309,21 @@
     resid_parts = jnp.transpose(student_resid.reshape(4, NY, 8, 128), (1, 0, 2, 3)).reshape(NY, 32, 128)
     sent = payload(place, moved, teacher_resid, student_heads, own_matches.reshape(1, 128), resid_parts)
     spot, sent = lax.optimization_barrier((place, sent))
-    weights, out_cols = layout(spot, projector, other, student_out)
+    weights = layout(spot, projector, other, student_out)
     got = lax.all_to_all(sent, COLUMN, 0, 0)
     heads = own_order(got[:, 256:384]).reshape(NX, 256, 128)
     base = (jnp.arange(NY, dtype=jnp.int32) // 2 * 128)[:, None]
     picked = own_order(got[:, 384].astype(jnp.int32) + base).reshape(NX, 1, 256)
-    operands = (place, picked, got, heads, out_cols, weights)
+    operands = (place, picked, got, heads, weights)
     far = [part.reshape(NZ, 32, HALF) for part in combined_parts(FAR, *operands)]
     rest = [part.reshape(NZ, 32, HALF) for part in combined_parts(REST, *operands)]
     resid = got[:, 400:].reshape(32, 2, HALF)
     resid = jnp.concatenate([resid[:, 0], resid[:, 1]], axis=0)
     (summed,) = reduce_x((rest[2], rest[0], far[0], rest[1]), (rest[5], rest[3], far[1], rest[4]), ())
-    summed = reduce_z(summed)
-    difference = resid.astype(F32) + summed
-    grad = (difference * 0.125).astype(B16)
-
-    tall = lax.all_to_all(jnp.broadcast_to(grad[None], (NZ, 64, HALF)), "z", 0, 0)
+    moved = lax.all_to_all(summed, "z", 0, 0)
+    grad = gradient_piece(place, moved, resid)
+
+    tall = lax.all_to_all(grad, "z", 0, 0)
     gathered = gather_x(tall[:, :32].reshape(256, HALF), tall[:, 32:].reshape(256, HALF))
 
     heads_part, squares, grad_weight = final_parts(place, gathered, student_out, heads)

time: 176 us -> 178 us (1.011)
  Pallas kernels: 11.4 us -> 15.4 us
    all_to_all x1 -> x0, waiting for transfers between devices: 14.5 us -> none  [reduce_z(): moved = lax.all_to_all(parts, 'z', 0, 0)]
    all_to_all x1 -> x2, waiting for transfers between devices: 13 us -> 26 us  [local(): moved = lax.all_to_all(summed, 'z', 0, 0)]
    all_to_all x1 -> x0, starting transfers between devices: 4.14 us -> none  [reduce_z(): moved = lax.all_to_all(parts, 'z', 0, 0)]
    all_to_all x1 -> x2, starting transfers between devices: 8.19 us -> 11.7 us  [local(): moved = lax.all_to_all(summed, 'z', 0, 0)]
    unnamed x28 -> x22, local copies, waits for them, and re-layouts: 9.89 us -> 7.18 us
    pallas_call x2, Pallas kernels: 3.81 us -> 6.17 us  [combined_parts(): call(functools.partial(combine_kernel, jobs), specs, outs, count * 2 * 25...]
  transfers between devices with their start and end apart: 23 -> 23, of which waited for: 16 -> 17; matrix products, arithmetic and copies ran while one was open for 2% -> 2% of each run, Pallas kernels for 2% -> 3%
where the time goes in v12:
time: 178 us; the launch traced here: 177 us
  waiting for transfers between devices  63.4 us (36%)
  starting transfers between devices  46.7 us (26%)
  blocking collectives  33.4 us (19%)
  Pallas kernels  15.4 us (9%)
  local copies, waits for them, and re-layouts  13.3 us (7%)
  other arithmetic  3.92 us (2%)
    ppermute x18, waiting for transfers between devices, across(): return lax.ppermute(block, 'x', [(i, i ^ flip) for i in range(NX)])  28 us
    all_to_all x2, waiting for transfers between devices, local(): moved = lax.all_to_all(summed, 'z', 0, 0)  26 us
    ppermute x18, starting transfers between devices, across(): return lax.ppermute(block, 'x', [(i, i ^ flip) for i in range(NX)])  20.4 us
    all_to_all x1, blocking collectives, local(): back = lax.all_to_all(sent, COLUMN, 0, 0)  17.1 us
    all_to_all x1, blocking collectives, local(): tall = lax.all_to_all(grad, 'z', 0, 0)  16.3 us
    all_to_all x2, starting transfers between devices, local(): moved = lax.all_to_all(summed, 'z', 0, 0)  11.7 us
    all_to_all x1, starting transfers between devices, local(): got = lax.all_to_all(sent, COLUMN, 0, 0)  9.55 us
    all_to_all x1, waiting for transfers between devices, local(): got = lax.all_to_all(sent, COLUMN, 0, 0)  9.48 us
  transfers between devices with their start and end apart: 23, of which 17 were waited for; matrix products, arithmetic and copies ran while one was open for 2% of the time, Pallas kernels for 3%

profile of v12, /device:TPU:1, one launch (start us, length us, event | category | flops | bytes accessed | tf_op | source)
XLA Modules:
  0.0 177.0 jit_solution(14642479995660174028)
XLA Ops:
  0.6 3.8 %collective-permute-start = (bf16[64,256]{1,0:T(8,128)(2,1)}, bf16[64,256]{1,0:T(8,128)(2,1)S(1)}, u32[]{:S(2)}, u32[]{:S(2)}) collective-permute-start(bf16[64,256]{1,0:T(8,128)(2,1)} %own_ref.1), channel_id=1, source_target_pairs={{0,32},{32,0},{1,33},{33,1},{2,34},{34,2},{3,35},{35,3},{4,36},{36... | collective-permute-start | bytes 98312 | tf_op jit(solution)/shard_map/ppermute | solution.py:296
  4.5 2.2 %copy-done.2 = bf16[256,8192]{1,0:T(8,128)(2,1)S(1)} copy-done((bf16[256,8192]{1,0:T(8,128)(2,1)S(1)}, bf16[256,8192]{1,0:T(8,128)(2,1)}, u32[]{:S(2)}) %copy-start.2) | copy-done | bytes 4194328
  15.7 3.4 %collective-permute-start.3 = (bf16[8,64,256]{2,1,0:T(8,128)(2,1)S(1)}, bf16[8,64,256]{2,1,0:T(8,128)(2,1)S(1)}, u32[]{:S(2)}, u32[]{:S(2)}) collective-permute-start(bf16[8,64,256]{2,1,0:T(8,128)(2,1)S(1)} %add_convert_fusion.3), channel_id=1, source_target_pairs={{0,3},{1,2},{2,1},{3,0},{4,7},{5,6},{6,5},{7,4},{8,11},{9,10},{10,... | collective-permute-start | bytes 786440 | tf_op jit(solution)/shard_map/ppermute | solution.py:33
  20.8 2.4 %collective-permute-done.3 = bf16[8,64,256]{2,1,0:T(8,128)(2,1)S(1)} collective-permute-done((bf16[8,64,256]{2,1,0:T(8,128)(2,1)S(1)}, bf16[8,64,256]{2,1,0:T(8,128)(2,1)S(1)}, u32[]{:S(2)}, u32[]{:S(2)}) %collective-permute-start.3) | collective-permute-done | bytes 262176 | tf_op jit(solution)/shard_map/ppermute | solution.py:33
  23.3 3.9 %collective-permute-done.6 = bf16[8,64,256]{2,1,0:T(8,128)(2,1)S(1)} collective-permute-done((bf16[8,64,256]{2,1,0:T(8,128)(2,1)S(1)}, bf16[8,64,256]{2,1,0:T(8,128)(2,1)S(1)}, u32[]{:S(2)}, u32[]{:S(2)}) %collective-permute-start.6) | collective-permute-done | bytes 262176 | tf_op jit(solution)/shard_map/ppermute | solution.py:33
  29.4 8.2 %all-to-all-start = ((bf16[8,128,256]{2,1,0:T(8,128)(2,1)}), bf16[8,128,256]{2,1,0:T(8,128)(2,1)S(1)}, u32[]{:S(2)}, u32[]{:S(2)}) async-start(bf16[8,128,256]{2,1,0:T(8,128)(2,1)} %pad_maximum_fusion), calls=%async_computation | async-start | bytes 1048576 | tf_op jit(solution)/shard_map/all_to_all | solution.py:307
  38.5 12.1 %all-to-all-done.moved_ref = bf16[8,128,256]{2,1,0:T(8,128)(2,1)S(1)} async-done(((bf16[8,128,256]{2,1,0:T(8,128)(2,1)}), bf16[8,128,256]{2,1,0:T(8,128)(2,1)S(1)}, u32[]{:S(2)}, u32[]{:S(2)}) %all-to-all-start) | async-done | bytes 524320 | tf_op jit(solution)/shard_map/all_to_all | solution.py:307
  52.2 9.6 %all-to-all-start.1 = ((bf16[8,432,128]{2,1,0:T(8,128)(2,1)}), bf16[8,432,128]{2,1,0:T(8,128)(2,1)}, u32[]{:S(2)}, u32[]{:S(2)}) async-start(bf16[8,432,128]{2,1,0:T(8,128)(2,1)} %shard_map.105), calls=%async_computation.1 | async-start | bytes 1769472 | tf_op jit(solution)/shard_map/all_to_all | solution.py:313
  61.7 2.2 %copy-done.1 = bf16[256,8192]{1,0:T(8,128)(2,1)S(1)} copy-done((bf16[256,8192]{1,0:T(8,128)(2,1)S(1)}, bf16[256,8192]{1,0:T(8,128)(2,1)}, u32[]{:S(2)}) %copy-start.1) | copy-done | bytes 4194328
  65.6 9.5 %all-to-all-done.1.got_ref = bf16[8,432,128]{2,1,0:T(8,128)(2,1)} async-done(((bf16[8,432,128]{2,1,0:T(8,128)(2,1)}), bf16[8,432,128]{2,1,0:T(8,128)(2,1)}, u32[]{:S(2)}, u32[]{:S(2)}) %all-to-all-start.1) | async-done | bytes 884768 | tf_op jit(solution)/shard_map/all_to_all | solution.py:313
  80.5 2.5 %shard_map.108 = (bf16[256,512]{1,0:T(8,128)(2,1)S(1)}, bf16[256,512]{1,0:T(8,128)(2,1)S(1)}) custom-call(s32[3]{0:T(128)S(1)} %pad_add_fusion.place_ref, s32[4,1,256]{2,1,0:T(1,128)S(1)} %reshape_reshape.12.picked_ref, bf16[8,432,128]{2,1,0:T(8,128)(2,1)} %all-to-all-done.1.got_ref, bf16[4,256,128]{2,1,0:T(8,128)(2,1)S(1)} %bitcast.47, ...), custom_call_target="tpu_custom_call" | custom-call | flops 471859200 | bytes 5242880 | tf_op jit(solution)/shard_map/pallas_call | solution.py:237
  83.7 2.6 %collective-permute-start.12 = (bf16[8,32,512]{2,1,0:T(8,128)(2,1)S(1)}, bf16[8,32,512]{2,1,0:T(8,128)(2,1)S(1)}, u32[]{:S(2)}, u32[]{:S(2)}) collective-permute-start(bf16[8,32,512]{2,1,0:T(8,128)(2,1)S(1)} %bitcast.62), channel_id=1, source_target_pairs={{0,3},{1,2},{2,1},{3,0},{4,7},{5,6},{6,5},{7,4},{8,11},{9,10},{10,... | collective-permute-start | bytes 786440 | tf_op jit(solution)/shard_map/ppermute | solution.py:33
  86.3 3.6 %shard_map.107 = (bf16[256,512]{1,0:T(8,128)(2,1)S(1)}, bf16[256,512]{1,0:T(8,128)(2,1)S(1)}, bf16[256,512]{1,0:T(8,128)(2,1)S(1)}, bf16[256,512]{1,0:T(8,128)(2...) custom-call(s32[3]{0:T(128)S(1)} %pad_add_fusion.place_ref, ...), custom_call_target="tpu_custom_call" | custom-call | flops 1415577600 | bytes 5242880 | tf_op jit(solution)/shard_map/pallas_call | solution.py:237
  90.7 2.5 %collective-permute-start.10 = (bf16[8,32,512]{2,1,0:T(8,128)(2,1)S(1)}, bf16[8,32,512]{2,1,0:T(8,128)(2,1)S(1)}, u32[]{:S(2)}, u32[]{:S(2)}) collective-permute-start(bf16[8,32,512]{2,1,0:T(8,128)(2,1)S(1)} %fusion.3), channel_id=1, source_target_pairs={{0,3},{1,2},{2,1},{3,0},{4,7},{5,6},{6,5},{7,4},{8,11},{9,10},{10,... | collective-permute-start | bytes 786440 | tf_op jit(solution)/shard_map/ppermute | solution.py:33
  93.8 3.1 %collective-permute-done.8 = bf16[8,32,512]{2,1,0:T(8,128)(2,1)S(1)} collective-permute-done((bf16[8,32,512]{2,1,0:T(8,128)(2,1)S(1)}, bf16[8,32,512]{2,1,0:T(8,128)(2,1)S(1)}, u32[]{:S(2)}, u32[]{:S(2)}) %collective-permute-start.8) | collective-permute-done | bytes 262176 | tf_op jit(solution)/shard_map/ppermute | solution.py:33
  98.3 5.5 %collective-permute-done.11 = bf16[8,32,512]{2,1,0:T(8,128)(2,1)S(1)} collective-permute-done((bf16[8,32,512]{2,1,0:T(8,128)(2,1)S(1)}, bf16[8,32,512]{2,1,0:T(8,128)(2,1)S(1)}, u32[]{:S(2)}, u32[]{:S(2)}) %collective-permute-start.11) | collective-permute-done | bytes 262176 | tf_op jit(solution)/shard_map/ppermute | solution.py:33
  104.8 3.5 %all-to-all-start.2 = ((bf16[8,64,512]{2,1,0:T(8,128)(2,1)}), bf16[8,64,512]{2,1,0:T(8,128)(2,1)S(1)}, u32[]{:S(2)}, u32[]{:S(2)}) async-start(bf16[8,64,512]{2,1,0:T(8,128)(2,1)} %pad_maximum_fusion.1), calls=%async_computation.2 | async-start | bytes 1048576 | tf_op jit(solution)/shard_map/all_to_all | solution.py:323
  109.3 13.9 %all-to-all-done.2.moved_ref = bf16[8,64,512]{2,1,0:T(8,128)(2,1)S(1)} async-done(((bf16[8,64,512]{2,1,0:T(8,128)(2,1)}), bf16[8,64,512]{2,1,0:T(8,128)(2,1)S(1)}, u32[]{:S(2)}, u32[]{:S(2)}) %all-to-all-start.2) | async-done | bytes 524320 | tf_op jit(solution)/shard_map/all_to_all | solution.py:323
  123.8 16.3 %all_to_all.25 = bf16[8,64,512]{2,1,0:T(8,128)(2,1)S(1)} all-to-all(bf16[8,64,512]{2,1,0:T(8,128)(2,1)S(1)} %shard_map.109), channel_id=1, replica_groups=mesh['ylo'=2,'core'=2,'seq'=2,'z'=8,'x'=4] {'z'}, dimensions={0} | all-to-all | bytes 1048576 | tf_op jit(solution)/shard_map/all_to_all | solution.py:326
  142.2 2.2 %collective-permute-start.19 = (bf16[256,512]{1,0:T(8,128)(2,1)S(1)}, bf16[256,512]{1,0:T(8,128)(2,1)S(1)}, u32[]{:S(2)}, u32[]{:S(2)}) collective-permute-start(bf16[256,512]{1,0:T(8,128)(2,1)S(1)} %bitcast.51), channel_id=1, source_target_pairs={{0,3},{1,2},{2,1},{3,0},{4,7},{5,6},{6,5},{7,4},{8,11},{9,10},{10,... | collective-permute-start | bytes 786440 | tf_op jit(solution)/shard_map/ppermute | solution.py:33
  144.4 2.3 %collective-permute-done.15.refs_3_ = bf16[256,512]{1,0:T(8,128)(2,1)S(1)} collective-permute-done((bf16[256,512]{1,0:T(8,128)(2,1)S(1)}, bf16[256,512]{1,0:T(8,128)(2,1)S(1)}, u32[]{:S(2)}, u32[]{:S(2)}) %collective-permute-start.15) | collective-permute-done | bytes 262176 | tf_op jit(solution)/shard_map/ppermute | solution.py:33
  150.0 4.8 %collective-permute-done.16.refs_2_ = bf16[256,512]{1,0:T(8,128)(2,1)S(1)} collective-permute-done((bf16[256,512]{1,0:T(8,128)(2,1)S(1)}, bf16[256,512]{1,0:T(8,128)(2,1)S(1)}, u32[]{:S(2)}, u32[]{:S(2)}) %collective-permute-start.16) | collective-permute-done | bytes 262176 | tf_op jit(solution)/shard_map/ppermute | solution.py:33
  156.3 2.3 %shard_map.110 = (bf16[4,256,128]{2,1,0:T(8,128)(2,1)S(1)}, bf16[16,128]{1,0:T(8,128)(2,1)S(1)}, bf16[128,1024]{1,0:T(8,128)(2,1)}) custom-call(s32[3]{0:T(128)S(1)} %pad_add_fusion.place_ref, bf16[256,512]{1,0:T(8,128)(2,1)S(1)} %bitcast.55, bf16[256,512]{1,0:T(8,128)(2,1)S(1)} %collective-permute-done.14.refs_1_, ...), custom_call_target="tpu_custom_call" | custom-call | flops 536870912 | bytes 5242880 | tf_op jit(solution)/shard_map/pallas_call | solution.py:276
  158.7 17.1 %all_to_all.26.back_ref = bf16[8,144,128]{2,1,0:T(8,128)(2,1)S(1)} all-to-all(bf16[8,144,128]{2,1,0:T(8,128)(2,1)S(1)} %pad_maximum_fusion.2), channel_id=1, replica_groups=mesh['ylo'=2,'core'=2,'seq'=2,'z'=8,'x'=4] {'ylo','core','seq'}, dimensions={0} | all-to-all | bytes 589824 | tf_op jit(solution)/shard_map/all_to_all | solution.py:333
  (86 shorter events, 36.6 us)
Async XLA Ops:
  0.6 7.1 %collective-permute-start = (bf16[64,256]{1,0:T(8,128)(2,1)}, bf16[64,256]{1,0:T(8,128)(2,1)S(1)}, u32[]{:S(2)}, u32[]{:S(2)}) collective-permute-start(bf16[64,256]{1,0:T(8,128)(2,1)} %own_ref.1), channel_id=1, source_target_pairs={{0,32},{32,0},{1,33},{33,1},{2,34},{34,2},{3,35},{35,3},{4,36},{36... | collective-permute-start | bytes 98312 | tf_op jit(solution)/shard_map/ppermute | solution.py:296
  9.7 6.0 %collective-permute-start.2 = (bf16[8,64,256]{2,1,0:T(8,128)(2,1)S(1)}, bf16[8,64,256]{2,1,0:T(8,128)(2,1)S(1)}, u32[]{:S(2)}, u32[]{:S(2)}) collective-permute-start(bf16[8,64,256]{2,1,0:T(8,128)(2,1)S(1)} %get-tuple-element.41), channel_id=1, source_target_pairs={{0,1},{1,0},{2,3},{3,2},{4,5},{5,4},{6,7},{7,6},{8,9},{9,8},{10,11... | collective-permute-start | bytes 786440 | tf_op jit(solution)/shard_map/ppermute | solution.py:33
  10.9 8.3 %collective-permute-start.5 = (bf16[8,64,256]{2,1,0:T(8,128)(2,1)S(1)}, bf16[8,64,256]{2,1,0:T(8,128)(2,1)S(1)}, u32[]{:S(2)}, u32[]{:S(2)}) collective-permute-start(bf16[8,64,256]{2,1,0:T(8,128)(2,1)S(1)} %get-tuple-element.45), channel_id=1, source_target_pairs={{0,3},{1,2},{2,1},{3,0},{4,7},{5,6},{6,5},{7,4},{8,11},{9,10},{10,... | collective-permute-start | bytes 786440 | tf_op jit(solution)/shard_map/ppermute | solution.py:33
  13.7 13.5 %collective-permute-start.7 = (bf16[256,1024]{1,0:T(8,128)(2,1)S(1)}, bf16[256,1024]{1,0:T(8,128)(2,1)S(1)}, u32[]{:S(2)}, u32[]{:S(2)}) collective-permute-start(bf16[256,1024]{1,0:T(8,128)(2,1)S(1)} %constant_dynamic-slice_fusion), channel_id=1, source_target_pairs={{0,32},{32,0},{1,33},{33,1},{2,34},{34,2},{3,35},{35,3},{4,36},{36... | collective-permute-start | bytes 1572872 | tf_op jit(solution)/shard_map/ppermute | solution.py:304
  15.0 5.8 %collective-permute-start.1 = (bf16[8,64,256]{2,1,0:T(8,128)(2,1)}, bf16[8,64,256]{2,1,0:T(8,128)(2,1)S(1)}, u32[]{:S(2)}, u32[]{:S(2)}) collective-permute-start(bf16[8,64,256]{2,1,0:T(8,128)(2,1)} %get-tuple-element.39), channel_id=1, source_target_pairs={{0,1},{1,0},{2,3},{3,2},{4,5},{5,4},{6,7},{7,6},{8,9},{9,8},{10,11... | collective-permute-start | bytes 786440 | tf_op jit(solution)/shard_map/ppermute | solution.py:33
  15.7 7.5 %collective-permute-start.3 = (bf16[8,64,256]{2,1,0:T(8,128)(2,1)S(1)}, bf16[8,64,256]{2,1,0:T(8,128)(2,1)S(1)}, u32[]{:S(2)}, u32[]{:S(2)}) collective-permute-start(bf16[8,64,256]{2,1,0:T(8,128)(2,1)S(1)} %add_convert_fusion.3), channel_id=1, source_target_pairs={{0,3},{1,2},{2,1},{3,0},{4,7},{5,6},{6,5},{7,4},{8,11},{9,10},{10,... | collective-permute-start | bytes 786440 | tf_op jit(solution)/shard_map/ppermute | solution.py:33
  19.2 8.0 %collective-permute-start.6 = (bf16[8,64,256]{2,1,0:T(8,128)(2,1)S(1)}, bf16[8,64,256]{2,1,0:T(8,128)(2,1)S(1)}, u32[]{:S(2)}, u32[]{:S(2)}) collective-permute-start(bf16[8,64,256]{2,1,0:T(8,128)(2,1)S(1)} %add_convert_fusion.1), channel_id=1, source_target_pairs={{0,1},{1,0},{2,3},{3,2},{4,5},{5,4},{6,7},{7,6},{8,9},{9,8},{10,11... | collective-permute-start | bytes 786440 | tf_op jit(solution)/shard_map/ppermute | solution.py:33
  19.3 9.1 %collective-permute-start.4 = (bf16[8,64,256]{2,1,0:T(8,128)(2,1)S(1)}, bf16[8,64,256]{2,1,0:T(8,128)(2,1)S(1)}, u32[]{:S(2)}, u32[]{:S(2)}) collective-permute-start(bf16[8,64,256]{2,1,0:T(8,128)(2,1)S(1)} %get-tuple-element.43), channel_id=1, source_target_pairs={{0,3},{1,2},{2,1},{3,0},{4,7},{5,6},{6,5},{7,4},{8,11},{9,10},{10,... | collective-permute-start | bytes 786440 | tf_op jit(solution)/shard_map/ppermute | solution.py:33
  29.4 21.2 %all-to-all-start = ((bf16[8,128,256]{2,1,0:T(8,128)(2,1)}), bf16[8,128,256]{2,1,0:T(8,128)(2,1)S(1)}, u32[]{:S(2)}, u32[]{:S(2)}) async-start(bf16[8,128,256]{2,1,0:T(8,128)(2,1)} %pad_maximum_fusion), calls=%async_computation | async-start | bytes 1048576 | tf_op jit(solution)/shard_map/all_to_all | solution.py:307
  52.2 22.9 %all-to-all-start.1 = ((bf16[8,432,128]{2,1,0:T(8,128)(2,1)}), bf16[8,432,128]{2,1,0:T(8,128)(2,1)}, u32[]{:S(2)}, u32[]{:S(2)}) async-start(bf16[8,432,128]{2,1,0:T(8,128)(2,1)} %shard_map.105), calls=%async_computation.1 | async-start | bytes 1769472 | tf_op jit(solution)/shard_map/all_to_all | solution.py:313
  83.0 7.6 %collective-permute-start.9 = (bf16[8,32,512]{2,1,0:T(8,128)(2,1)S(1)}, bf16[8,32,512]{2,1,0:T(8,128)(2,1)S(1)}, u32[]{:S(2)}, u32[]{:S(2)}) collective-permute-start(bf16[8,32,512]{2,1,0:T(8,128)(2,1)S(1)} %bitcast.64), channel_id=1, source_target_pairs={{0,1},{1,0},{2,3},{3,2},{4,5},{5,4},{6,7},{7,6},{8,9},{9,8},{10,11... | collective-permute-start | bytes 786440 | tf_op jit(solution)/shard_map/ppermute | solution.py:33
  83.7 9.9 %collective-permute-start.12 = (bf16[8,32,512]{2,1,0:T(8,128)(2,1)S(1)}, bf16[8,32,512]{2,1,0:T(8,128)(2,1)S(1)}, u32[]{:S(2)}, u32[]{:S(2)}) collective-permute-start(bf16[8,32,512]{2,1,0:T(8,128)(2,1)S(1)} %bitcast.62), channel_id=1, source_target_pairs={{0,3},{1,2},{2,1},{3,0},{4,7},{5,6},{6,5},{7,4},{8,11},{9,10},{10,... | collective-permute-start | bytes 786440 | tf_op jit(solution)/shard_map/ppermute | solution.py:33
  89.9 6.9 %collective-permute-start.8 = (bf16[8,32,512]{2,1,0:T(8,128)(2,1)S(1)}, bf16[8,32,512]{2,1,0:T(8,128)(2,1)S(1)}, u32[]{:S(2)}, u32[]{:S(2)}) collective-permute-start(bf16[8,32,512]{2,1,0:T(8,128)(2,1)S(1)} %bitcast.63), channel_id=1, source_target_pairs={{0,1},{1,0},{2,3},{3,2},{4,5},{5,4},{6,7},{7,6},{8,9},{9,8},{10,11... | collective-permute-start | bytes 786440 | tf_op jit(solution)/shard_map/ppermute | solution.py:33
  90.7 7.5 %collective-permute-start.10 = (bf16[8,32,512]{2,1,0:T(8,128)(2,1)S(1)}, bf16[8,32,512]{2,1,0:T(8,128)(2,1)S(1)}, u32[]{:S(2)}, u32[]{:S(2)}) collective-permute-start(bf16[8,32,512]{2,1,0:T(8,128)(2,1)S(1)} %fusion.3), channel_id=1, source_target_pairs={{0,3},{1,2},{2,1},{3,0},{4,7},{5,6},{6,5},{7,4},{8,11},{9,10},{10,... | collective-permute-start | bytes 786440 | tf_op jit(solution)/shard_map/ppermute | solution.py:33
  93.2 10.6 %collective-permute-start.11 = (bf16[8,32,512]{2,1,0:T(8,128)(2,1)S(1)}, bf16[8,32,512]{2,1,0:T(8,128)(2,1)S(1)}, u32[]{:S(2)}, u32[]{:S(2)}) collective-permute-start(bf16[8,32,512]{2,1,0:T(8,128)(2,1)S(1)} %bitcast.61), channel_id=1, source_target_pairs={{0,3},{1,2},{2,1},{3,0},{4,7},{5,6},{6,5},{7,4},{8,11},{9,10},{10,... | collective-permute-start | bytes 786440 | tf_op jit(solution)/shard_map/ppermute | solution.py:33
  93.6 62.7 %copy-start.4 = (bf16[8,8,4,4,128]{4,3,0,1,2:T(4,128)(2,1)S(1)}, bf16[8,8,4,4,128]{4,3,0,1,2:T(4,128)(2,1)}, u32[]{:S(2)}) copy-start(bf16[8,8,4,4,128]{4,3,0,1,2:T(4,128)(2,1)} %copy.27) | copy-start | bytes 786436
  93.6 10.3 %collective-permute-start.13 = (bf16[8,32,512]{2,1,0:T(8,128)(2,1)S(1)}, bf16[8,32,512]{2,1,0:T(8,128)(2,1)S(1)}, u32[]{:S(2)}, u32[]{:S(2)}) collective-permute-start(bf16[8,32,512]{2,1,0:T(8,128)(2,1)S(1)} %fusion), channel_id=1, source_target_pairs={{0,1},{1,0},{2,3},{3,2},{4,5},{5,4},{6,7},{7,6},{8,9},{9,8},{10,11... | collective-permute-start | bytes 786440 | tf_op jit(solution)/shard_map/ppermute | solution.py:33
  104.8 18.4 %all-to-all-start.2 = ((bf16[8,64,512]{2,1,0:T(8,128)(2,1)}), bf16[8,64,512]{2,1,0:T(8,128)(2,1)S(1)}, u32[]{:S(2)}, u32[]{:S(2)}) async-start(bf16[8,64,512]{2,1,0:T(8,128)(2,1)} %pad_maximum_fusion.1), calls=%async_computation.2 | async-start | bytes 1048576 | tf_op jit(solution)/shard_map/all_to_all | solution.py:323
  140.2 6.5 %collective-permute-start.15 = (bf16[256,512]{1,0:T(8,128)(2,1)S(1)}, bf16[256,512]{1,0:T(8,128)(2,1)S(1)}, u32[]{:S(2)}, u32[]{:S(2)}) collective-permute-start(bf16[256,512]{1,0:T(8,128)(2,1)S(1)} %bitcast.53), channel_id=1, source_target_pairs={{0,3},{1,2},{2,1},{3,0},{4,7},{5,6},{6,5},{7,4},{8,11},{9,10},{10,... | collective-permute-start | bytes 786440 | tf_op jit(solution)/shard_map/ppermute | solution.py:33
  140.7 6.0 %collective-permute-start.17 = (bf16[256,512]{1,0:T(8,128)(2,1)S(1)}, bf16[256,512]{1,0:T(8,128)(2,1)S(1)}, u32[]{:S(2)}, u32[]{:S(2)}) collective-permute-start(bf16[256,512]{1,0:T(8,128)(2,1)S(1)} %bitcast.50), channel_id=1, source_target_pairs={{0,1},{1,0},{2,3},{3,2},{4,5},{5,4},{6,7},{7,6},{8,9},{9,8},{10,11... | collective-permute-start | bytes 786440 | tf_op jit(solution)/shard_map/ppermute | solution.py:33
  140.7 8.0 %collective-permute-start.14 = (bf16[256,512]{1,0:T(8,128)(2,1)S(1)}, bf16[256,512]{1,0:T(8,128)(2,1)S(1)}, u32[]{:S(2)}, u32[]{:S(2)}) collective-permute-start(bf16[256,512]{1,0:T(8,128)(2,1)S(1)} %bitcast.54), channel_id=1, source_target_pairs={{0,1},{1,0},{2,3},{3,2},{4,5},{5,4},{6,7},{7,6},{8,9},{9,8},{10,11... | collective-permute-start | bytes 786440 | tf_op jit(solution)/shard_map/ppermute | solution.py:33
  142.2 7.8 %collective-permute-start.19 = (bf16[256,512]{1,0:T(8,128)(2,1)S(1)}, bf16[256,512]{1,0:T(8,128)(2,1)S(1)}, u32[]{:S(2)}, u32[]{:S(2)}) collective-permute-start(bf16[256,512]{1,0:T(8,128)(2,1)S(1)} %bitcast.51), channel_id=1, source_target_pairs={{0,3},{1,2},{2,1},{3,0},{4,7},{5,6},{6,5},{7,4},{8,11},{9,10},{10,... | collective-permute-start | bytes 786440 | tf_op jit(solution)/shard_map/ppermute | solution.py:33
  146.7 8.1 %collective-permute-start.16 = (bf16[256,512]{1,0:T(8,128)(2,1)S(1)}, bf16[256,512]{1,0:T(8,128)(2,1)S(1)}, u32[]{:S(2)}, u32[]{:S(2)}) collective-permute-start(bf16[256,512]{1,0:T(8,128)(2,1)S(1)} %collective-permute-done.15.refs_3_), channel_id=1, source_target_pairs={{0,1},{1,0},{2,3},{3,2},{4,5},{5,4},{6,7},{7,6},{8,9},{9,8},{10,11... | collective-permute-start | bytes 786440 | tf_op jit(solution)/shard_map/ppermute | solution.py:33
  146.7 9.5 %collective-permute-start.18 = (bf16[256,512]{1,0:T(8,128)(2,1)S(1)}, bf16[256,512]{1,0:T(8,128)(2,1)S(1)}, u32[]{:S(2)}, u32[]{:S(2)}) collective-permute-start(bf16[256,512]{1,0:T(8,128)(2,1)S(1)} %collective-permute-done.17.refs_5_), channel_id=1, source_target_pairs={{0,3},{1,2},{2,1},{3,0},{4,7},{5,6},{6,5},{7,4},{8,11},{9,10},{10,... | collective-permute-start | bytes 786440 | tf_op jit(solution)/shard_map/ppermute | solution.py:33
  (10 other events, 160.7 us)

commit v13 on v12

--- a/solution.py
+++ b/solution.py
@@ -181,20 +181,15 @@
     return call(last_kernel, [whole(NY, 144, 128)], outs, 1 << 18)(place, back)
 
 
-def layout_kernel(place_ref, home_in, other_in, out_in, weights_ref):
+def layout_kernel(place_ref, home_in, other_in, weights_ref):
     weights_ref[0:256, :] = home_in[...]
     weights_ref[256:512, :] = other_in[...]
-    weights_ref[512:640, :] = out_in[...]
-
-
-def layout(place, projector, other, student_out):
-    specs = [
-        pl.BlockSpec((256, COLS), lambda i, m: (0, m[0])),
-        whole(256, COLS),
-        pl.BlockSpec((128, COLS), lambda i, m: (0, m[0])),
-    ]
-    outs = [jax.ShapeDtypeStruct((640, COLS), B16)]
-    return call(layout_kernel, specs, outs, 1 << 21, (), 8)(place, projector, other, student_out)[0]
+
+
+def layout(place, projector, other):
+    specs = [pl.BlockSpec((256, COLS), lambda i, m: (0, m[0])), whole(256, COLS)]
+    outs = [jax.ShapeDtypeStruct((512, COLS), B16)]
+    return call(layout_kernel, specs, outs, 1 << 21, (), 8)(place, projector, other)[0]
 
 
 def gather_hidden(place_ref, got_ref, hidden_ref):
@@ -210,7 +205,7 @@
             hidden_ref[near, other] = got_ref[2 * g + 1 - seq, at + 64 : at + 128, :]
 
 
-def combine_kernel(jobs, place_ref, picked_ref, got_ref, heads_ref, weights_ref, *refs):
+def combine_kernel(jobs, place_ref, picked_ref, got_ref, heads_ref, out_ref, weights_ref, *refs):
     x = place_ref[2]
     parts, hidden_ref = refs[:-1], refs[-1]
     gather_hidden(place_ref, got_ref, hidden_ref)
@@ -221,8 +216,8 @@
         heads = heads_ref[k ^ x]
         for half, to in halves:
             columns = slice(half * HALF, (half + 1) * HALF)
-            total = dot(heads, weights_ref[512:640, columns], ((1,), (0,)))
-            total -= dot(selected, weights_ref[0:512, columns], ((1,), (0,)))
+            total = dot(heads, out_ref[:, columns], ((1,), (0,)))
+            total -= dot(selected, weights_ref[:, columns], ((1,), (0,)))
             parts[to][...] = total.astype(B16)
 
 
@@ -230,13 +225,14 @@
 REST = ((1, ((0, 0), (1, 3))), (3, ((1, 4), (0, 1))), (0, ((0, 2), (1, 5))))
 
 
-def combined_parts(jobs, place, picked, got, heads, weights):
-    specs = [whole(NX, 1, 256), whole(NY, 432, 128), whole(NX, 256, 128), whole(640, COLS)]
+def combined_parts(jobs, place, picked, got, heads, student_out, weights):
+    block = pl.BlockSpec((128, COLS), lambda i, m: (0, m[0]))
+    specs = [whole(NX, 1, 256), whole(NY, 432, 128), whole(NX, 256, 128), block, whole(512, COLS)]
     count = sum(len(halves) for _, halves in jobs)
     outs = [jax.ShapeDtypeStruct((256, HALF), B16)] * count
     return call(
         functools.partial(combine_kernel, jobs), specs, outs, count * 2 * 256 * 512 * 900, [pltpu.VMEM((512, 512), B16)], 16
-    )(place, picked, got, heads, weights)
+    )(place, picked, got, heads, student_out, weights)
 
 
 def final_kernel(place_ref, *refs):
@@ -309,12 +305,12 @@
     resid_parts = jnp.transpose(student_resid.reshape(4, NY, 8, 128), (1, 0, 2, 3)).reshape(NY, 32, 128)
     sent = payload(place, moved, teacher_resid, student_heads, own_matches.reshape(1, 128), resid_parts)
     spot, sent = lax.optimization_barrier((place, sent))
-    weights = layout(spot, projector, other, student_out)
+    weights = layout(spot, projector, other)
     got = lax.all_to_all(sent, COLUMN, 0, 0)
     heads = own_order(got[:, 256:384]).reshape(NX, 256, 128)
     base = (jnp.arange(NY, dtype=jnp.int32) // 2 * 128)[:, None]
     picked = own_order(got[:, 384].astype(jnp.int32) + base).reshape(NX, 1, 256)
-    operands = (place, picked, got, heads, weights)
+    operands = (place, picked, got, heads, student_out, weights)
     far = [part.reshape(NZ, 32, HALF) for part in combined_parts(FAR, *operands)]
     rest = [part.reshape(NZ, 32, HALF) for part in combined_parts(REST, *operands)]
     resid = got[:, 400:].reshape(32, 2, HALF)

time: 178 us -> 173 us (0.972)
  waiting for transfers between devices: 63.4 us -> 68.5 us
  local copies, waits for them, and re-layouts: 13.3 us -> 10.3 us
  Pallas kernels: 15.4 us -> 12.5 us
  starting transfers between devices: 46.7 us -> 44.1 us
    ppermute x18, waiting for transfers between devices: 28 us -> 30.7 us  [across(): return lax.ppermute(block, 'x', [(i, i ^ flip) for i in range(NX)])]
    pallas_call x2, Pallas kernels: 6.17 us -> 3.81 us  [combined_parts(): call(functools.partial(combine_kernel, jobs), specs, outs, count * 2 * 25...]
    unnamed x22 -> x20, local copies, waits for them, and re-layouts: 7.18 us -> 7.52 us
  transfers between devices with their start and end apart: 23 -> 23, of which waited for: 17 -> 17; matrix products, arithmetic and copies ran while one was open for 2% -> 2% of each run, Pallas kernels for 3% -> 2%
where the time goes in v13:
time: 173 us
  waiting for transfers between devices  68.5 us (40%)
  starting transfers between devices  44.1 us (25%)
  blocking collectives  32.8 us (19%)
  Pallas kernels  12.5 us (7%)
  local copies, waits for them, and re-layouts  10.3 us (6%)
  other arithmetic  3.53 us (2%)
    ppermute x18, waiting for transfers between devices, across(): return lax.ppermute(block, 'x', [(i, i ^ flip) for i in range(NX)])  30.7 us
    all_to_all x2, waiting for transfers between devices, local(): moved = lax.all_to_all(summed, 'z', 0, 0)  27.6 us
    ppermute x18, starting transfers between devices, across(): return lax.ppermute(block, 'x', [(i, i ^ flip) for i in range(NX)])  18.9 us
    all_to_all x1, blocking collectives, local(): back = lax.all_to_all(sent, COLUMN, 0, 0)  17.4 us
    all_to_all x1, blocking collectives, local(): tall = lax.all_to_all(grad, 'z', 0, 0)  15.4 us
    all_to_all x2, starting transfers between devices, local(): moved = lax.all_to_all(summed, 'z', 0, 0)  12.3 us
    all_to_all x1, waiting for transfers between devices, local(): got = lax.all_to_all(sent, COLUMN, 0, 0)  9.45 us
    all_to_all x1, starting transfers between devices, local(): got = lax.all_to_all(sent, COLUMN, 0, 0)  7.79 us
  transfers between devices with their start and end apart: 23, of which 17 were waited for; matrix products, arithmetic and copies ran while one was open for 2% of the time, Pallas kernels for 2%

profile of v13, /device:TPU:1, one launch (start us, length us, event | category | flops | bytes accessed | tf_op | source)
XLA Modules:
  0.0 172.6 jit_solution(8823283212397236053)
XLA Ops:
  0.6 3.8 %collective-permute-start = (bf16[64,256]{1,0:T(8,128)(2,1)}, bf16[64,256]{1,0:T(8,128)(2,1)S(1)}, u32[]{:S(2)}, u32[]{:S(2)}) collective-permute-start(bf16[64,256]{1,0:T(8,128)(2,1)} %own_ref.1), channel_id=1, source_target_pairs={{0,32},{32,0},{1,33},{33,1},{2,34},{34,2},{3,35},{35,3},{4,36},{36... | collective-permute-start | bytes 98312 | tf_op jit(solution)/shard_map/ppermute | solution.py:292
  4.5 2.2 %copy-done.2 = bf16[256,8192]{1,0:T(8,128)(2,1)S(1)} copy-done((bf16[256,8192]{1,0:T(8,128)(2,1)S(1)}, bf16[256,8192]{1,0:T(8,128)(2,1)}, u32[]{:S(2)}) %copy-start.2) | copy-done | bytes 4194328
  10.4 1.8 %collective-permute-start.5 = (bf16[8,64,256]{2,1,0:T(8,128)(2,1)S(1)}, bf16[8,64,256]{2,1,0:T(8,128)(2,1)}, u32[]{:S(2)}, u32[]{:S(2)}) collective-permute-start(bf16[8,64,256]{2,1,0:T(8,128)(2,1)S(1)} %get-tuple-element.45), channel_id=1, source_target_pairs={{0,3},{1,2},{2,1},{3,0},{4,7},{5,6},{6,5},{7,4},{8,11},{9,10},{10,... | collective-permute-start | bytes 786440 | tf_op jit(solution)/shard_map/ppermute | solution.py:33
  15.2 3.6 %collective-permute-start.3 = (bf16[8,64,256]{2,1,0:T(8,128)(2,1)S(1)}, bf16[8,64,256]{2,1,0:T(8,128)(2,1)S(1)}, u32[]{:S(2)}, u32[]{:S(2)}) collective-permute-start(bf16[8,64,256]{2,1,0:T(8,128)(2,1)S(1)} %add_convert_fusion.3), channel_id=1, source_target_pairs={{0,3},{1,2},{2,1},{3,0},{4,7},{5,6},{6,5},{7,4},{8,11},{9,10},{10,... | collective-permute-start | bytes 786440 | tf_op jit(solution)/shard_map/ppermute | solution.py:33
  23.0 3.0 %collective-permute-done.6 = bf16[8,64,256]{2,1,0:T(8,128)(2,1)S(1)} collective-permute-done((bf16[8,64,256]{2,1,0:T(8,128)(2,1)S(1)}, bf16[8,64,256]{2,1,0:T(8,128)(2,1)S(1)}, u32[]{:S(2)}, u32[]{:S(2)}) %collective-permute-start.6) | collective-permute-done | bytes 262176 | tf_op jit(solution)/shard_map/ppermute | solution.py:33
  26.8 2.7 %collective-permute-done.4 = bf16[8,64,256]{2,1,0:T(8,128)(2,1)S(1)} collective-permute-done((bf16[8,64,256]{2,1,0:T(8,128)(2,1)S(1)}, bf16[8,64,256]{2,1,0:T(8,128)(2,1)S(1)}, u32[]{:S(2)}, u32[]{:S(2)}) %collective-permute-start.4) | collective-permute-done | bytes 262176 | tf_op jit(solution)/shard_map/ppermute | solution.py:33
  30.4 8.1 %all-to-all-start = ((bf16[8,128,256]{2,1,0:T(8,128)(2,1)}), bf16[8,128,256]{2,1,0:T(8,128)(2,1)S(1)}, u32[]{:S(2)}, u32[]{:S(2)}) async-start(bf16[8,128,256]{2,1,0:T(8,128)(2,1)} %pad_maximum_fusion), calls=%async_computation | async-start | bytes 1048576 | tf_op jit(solution)/shard_map/all_to_all | solution.py:303
  39.5 13.3 %all-to-all-done.moved_ref = bf16[8,128,256]{2,1,0:T(8,128)(2,1)S(1)} async-done(((bf16[8,128,256]{2,1,0:T(8,128)(2,1)}), bf16[8,128,256]{2,1,0:T(8,128)(2,1)S(1)}, u32[]{:S(2)}, u32[]{:S(2)}) %all-to-all-start) | async-done | bytes 524320 | tf_op jit(solution)/shard_map/all_to_all | solution.py:303
  54.4 7.8 %all-to-all-start.1 = ((bf16[8,432,128]{2,1,0:T(8,128)(2,1)}), bf16[8,432,128]{2,1,0:T(8,128)(2,1)S(1)}, u32[]{:S(2)}, u32[]{:S(2)}) async-start(bf16[8,432,128]{2,1,0:T(8,128)(2,1)} %copy-done.5), calls=%async_computation.1 | async-start | bytes 1769472 | tf_op jit(solution)/shard_map/all_to_all | solution.py:309
  62.2 2.2 %copy-done.1 = bf16[256,8192]{1,0:T(8,128)(2,1)S(1)} copy-done((bf16[256,8192]{1,0:T(8,128)(2,1)S(1)}, bf16[256,8192]{1,0:T(8,128)(2,1)}, u32[]{:S(2)}) %copy-start.1) | copy-done | bytes 4194328
  65.9 9.5 %all-to-all-done.1.got_ref = bf16[8,432,128]{2,1,0:T(8,128)(2,1)S(1)} async-done(((bf16[8,432,128]{2,1,0:T(8,128)(2,1)}), bf16[8,432,128]{2,1,0:T(8,128)(2,1)S(1)}, u32[]{:S(2)}, u32[]{:S(2)}) %all-to-all-start.1) | async-done | bytes 884768 | tf_op jit(solution)/shard_map/all_to_all | solution.py:309
  80.0 2.5 %shard_map.107 = (bf16[256,512]{1,0:T(8,128)(2,1)S(1)}, bf16[256,512]{1,0:T(8,128)(2,1)S(1)}, bf16[256,512]{1,0:T(8,128)(2,1)S(1)}, bf16[256,512]{1,0:T(8,128)(2...) custom-call(s32[3]{0:T(128)S(1)} %pad_add_fusion.place_ref, ...), custom_call_target="tpu_custom_call" | custom-call | flops 1415577600 | bytes 5242880 | tf_op jit(solution)/shard_map/pallas_call | solution.py:233
  82.8 3.4 %collective-permute-done.9 = bf16[8,32,512]{2,1,0:T(8,128)(2,1)S(1)} collective-permute-done((bf16[8,32,512]{2,1,0:T(8,128)(2,1)S(1)}, bf16[8,32,512]{2,1,0:T(8,128)(2,1)S(1)}, u32[]{:S(2)}, u32[]{:S(2)}) %collective-permute-start.9) | collective-permute-done | bytes 262176 | tf_op jit(solution)/shard_map/ppermute | solution.py:33
  87.1 2.0 %collective-permute-start.11 = (bf16[8,32,512]{2,1,0:T(8,128)(2,1)S(1)}, bf16[8,32,512]{2,1,0:T(8,128)(2,1)S(1)}, u32[]{:S(2)}, u32[]{:S(2)}) collective-permute-start(bf16[8,32,512]{2,1,0:T(8,128)(2,1)S(1)} %bitcast.61), channel_id=1, source_target_pairs={{0,3},{1,2},{2,1},{3,0},{4,7},{5,6},{6,5},{7,4},{8,11},{9,10},{10,... | collective-permute-start | bytes 786440 | tf_op jit(solution)/shard_map/ppermute | solution.py:33
  89.4 2.4 %collective-permute-done.8 = bf16[8,32,512]{2,1,0:T(8,128)(2,1)S(1)} collective-permute-done((bf16[8,32,512]{2,1,0:T(8,128)(2,1)S(1)}, bf16[8,32,512]{2,1,0:T(8,128)(2,1)S(1)}, u32[]{:S(2)}, u32[]{:S(2)}) %collective-permute-start.8) | collective-permute-done | bytes 262176 | tf_op jit(solution)/shard_map/ppermute | solution.py:33
  93.5 5.5 %collective-permute-done.11 = bf16[8,32,512]{2,1,0:T(8,128)(2,1)S(1)} collective-permute-done((bf16[8,32,512]{2,1,0:T(8,128)(2,1)S(1)}, bf16[8,32,512]{2,1,0:T(8,128)(2,1)S(1)}, u32[]{:S(2)}, u32[]{:S(2)}) %collective-permute-start.11) | collective-permute-done | bytes 262176 | tf_op jit(solution)/shard_map/ppermute | solution.py:33
  99.9 4.1 %all-to-all-start.2 = ((bf16[8,64,512]{2,1,0:T(8,128)(2,1)}), bf16[8,64,512]{2,1,0:T(8,128)(2,1)}, u32[]{:S(2)}, u32[]{:S(2)}) async-start(bf16[8,64,512]{2,1,0:T(8,128)(2,1)} %pad_maximum_fusion.1), calls=%async_computation.2 | async-start | bytes 1048576 | tf_op jit(solution)/shard_map/all_to_all | solution.py:319
  104.3 14.2 %all-to-all-done.2.moved_ref = bf16[8,64,512]{2,1,0:T(8,128)(2,1)} async-done(((bf16[8,64,512]{2,1,0:T(8,128)(2,1)}), bf16[8,64,512]{2,1,0:T(8,128)(2,1)}, u32[]{:S(2)}, u32[]{:S(2)}) %all-to-all-start.2) | async-done | bytes 524320 | tf_op jit(solution)/shard_map/all_to_all | solution.py:319
  120.2 15.4 %all_to_all.25 = bf16[8,64,512]{2,1,0:T(8,128)(2,1)S(1)} all-to-all(bf16[8,64,512]{2,1,0:T(8,128)(2,1)S(1)} %shard_map.109), channel_id=1, replica_groups=mesh['ylo'=2,'core'=2,'seq'=2,'z'=8,'x'=4] {'z'}, dimensions={0} | all-to-all | bytes 1048576 | tf_op jit(solution)/shard_map/all_to_all | solution.py:322
  137.9 2.0 %collective-permute-start.19 = (bf16[256,512]{1,0:T(8,128)(2,1)S(1)}, bf16[256,512]{1,0:T(8,128)(2,1)S(1)}, u32[]{:S(2)}, u32[]{:S(2)}) collective-permute-start(bf16[256,512]{1,0:T(8,128)(2,1)S(1)} %bitcast.51), channel_id=1, source_target_pairs={{0,3},{1,2},{2,1},{3,0},{4,7},{5,6},{6,5},{7,4},{8,11},{9,10},{10,... | collective-permute-start | bytes 786440 | tf_op jit(solution)/shard_map/ppermute | solution.py:33
  139.8 2.3 %collective-permute-done.15.refs_3_ = bf16[256,512]{1,0:T(8,128)(2,1)S(1)} collective-permute-done((bf16[256,512]{1,0:T(8,128)(2,1)S(1)}, bf16[256,512]{1,0:T(8,128)(2,1)S(1)}, u32[]{:S(2)}, u32[]{:S(2)}) %collective-permute-start.15) | collective-permute-done | bytes 262176 | tf_op jit(solution)/shard_map/ppermute | solution.py:33
  144.9 5.1 %collective-permute-done.16.refs_2_ = bf16[256,512]{1,0:T(8,128)(2,1)S(1)} collective-permute-done((bf16[256,512]{1,0:T(8,128)(2,1)S(1)}, bf16[256,512]{1,0:T(8,128)(2,1)S(1)}, u32[]{:S(2)}, u32[]{:S(2)}) %collective-permute-start.16) | collective-permute-done | bytes 262176 | tf_op jit(solution)/shard_map/ppermute | solution.py:33
  151.6 2.2 %shard_map.110 = (bf16[4,256,128]{2,1,0:T(8,128)(2,1)S(1)}, bf16[16,128]{1,0:T(8,128)(2,1)S(1)}, bf16[128,1024]{1,0:T(8,128)(2,1)}) custom-call(s32[3]{0:T(128)S(1)} %pad_add_fusion.place_ref, bf16[256,512]{1,0:T(8,128)(2,1)S(1)} %bitcast.55, bf16[256,512]{1,0:T(8,128)(2,1)S(1)} %collective-permute-done.14.refs_1_, ...), custom_call_target="tpu_custom_call" | custom-call | flops 536870912 | bytes 5242880 | tf_op jit(solution)/shard_map/pallas_call | solution.py:272
  154.0 17.4 %all_to_all.26.back_ref = bf16[8,144,128]{2,1,0:T(8,128)(2,1)S(1)} all-to-all(bf16[8,144,128]{2,1,0:T(8,128)(2,1)S(1)} %pad_maximum_fusion.2), channel_id=1, replica_groups=mesh['ylo'=2,'core'=2,'seq'=2,'z'=8,'x'=4] {'ylo','core','seq'}, dimensions={0} | all-to-all | bytes 589824 | tf_op jit(solution)/shard_map/all_to_all | solution.py:329
  (84 shorter events, 35.2 us)
Async XLA Ops:
  0.6 7.1 %collective-permute-start = (bf16[64,256]{1,0:T(8,128)(2,1)}, bf16[64,256]{1,0:T(8,128)(2,1)S(1)}, u32[]{:S(2)}, u32[]{:S(2)}) collective-permute-start(bf16[64,256]{1,0:T(8,128)(2,1)} %own_ref.1), channel_id=1, source_target_pairs={{0,32},{32,0},{1,33},{33,1},{2,34},{34,2},{3,35},{35,3},{4,36},{36... | collective-permute-start | bytes 98312 | tf_op jit(solution)/shard_map/ppermute | solution.py:292
  9.1 43.7 %copy-start.6 = (bf16[128,256]{1,0:T(8,128)(2,1)S(1)}, bf16[128,256]{1,0:T(8,128)(2,1)}, u32[]{:S(2)}) copy-start(bf16[128,256]{1,0:T(8,128)(2,1)} %resid_ref.1) | copy-start | bytes 196612
  9.1 6.1 %collective-permute-start.2 = (bf16[8,64,256]{2,1,0:T(8,128)(2,1)S(1)}, bf16[8,64,256]{2,1,0:T(8,128)(2,1)S(1)}, u32[]{:S(2)}, u32[]{:S(2)}) collective-permute-start(bf16[8,64,256]{2,1,0:T(8,128)(2,1)S(1)} %get-tuple-element.41), channel_id=1, source_target_pairs={{0,1},{1,0},{2,3},{3,2},{4,5},{5,4},{6,7},{7,6},{8,9},{9,8},{10,11... | collective-permute-start | bytes 786440 | tf_op jit(solution)/shard_map/ppermute | solution.py:33
  10.4 8.4 %collective-permute-start.5 = (bf16[8,64,256]{2,1,0:T(8,128)(2,1)S(1)}, bf16[8,64,256]{2,1,0:T(8,128)(2,1)}, u32[]{:S(2)}, u32[]{:S(2)}) collective-permute-start(bf16[8,64,256]{2,1,0:T(8,128)(2,1)S(1)} %get-tuple-element.45), channel_id=1, source_target_pairs={{0,3},{1,2},{2,1},{3,0},{4,7},{5,6},{6,5},{7,4},{8,11},{9,10},{10,... | collective-permute-start | bytes 786440 | tf_op jit(solution)/shard_map/ppermute | solution.py:33
  13.3 13.5 %collective-permute-start.7 = (bf16[256,1024]{1,0:T(8,128)(2,1)S(1)}, bf16[256,1024]{1,0:T(8,128)(2,1)S(1)}, u32[]{:S(2)}, u32[]{:S(2)}) collective-permute-start(bf16[256,1024]{1,0:T(8,128)(2,1)S(1)} %constant_dynamic-slice_fusion), channel_id=1, source_target_pairs={{0,32},{32,0},{1,33},{33,1},{2,34},{34,2},{3,35},{35,3},{4,36},{36... | collective-permute-start | bytes 1572872 | tf_op jit(solution)/shard_map/ppermute | solution.py:300
  14.6 6.7 %collective-permute-start.1 = (bf16[8,64,256]{2,1,0:T(8,128)(2,1)S(1)}, bf16[8,64,256]{2,1,0:T(8,128)(2,1)S(1)}, u32[]{:S(2)}, u32[]{:S(2)}) collective-permute-start(bf16[8,64,256]{2,1,0:T(8,128)(2,1)S(1)} %get-tuple-element.39), channel_id=1, source_target_pairs={{0,1},{1,0},{2,3},{3,2},{4,5},{5,4},{6,7},{7,6},{8,9},{9,8},{10,11... | collective-permute-start | bytes 786440 | tf_op jit(solution)/shard_map/ppermute | solution.py:33
  15.2 7.6 %collective-permute-start.3 = (bf16[8,64,256]{2,1,0:T(8,128)(2,1)S(1)}, bf16[8,64,256]{2,1,0:T(8,128)(2,1)S(1)}, u32[]{:S(2)}, u32[]{:S(2)}) collective-permute-start(bf16[8,64,256]{2,1,0:T(8,128)(2,1)S(1)} %add_convert_fusion.3), channel_id=1, source_target_pairs={{0,3},{1,2},{2,1},{3,0},{4,7},{5,6},{6,5},{7,4},{8,11},{9,10},{10,... | collective-permute-start | bytes 786440 | tf_op jit(solution)/shard_map/ppermute | solution.py:33
  19.8 6.2 %collective-permute-start.6 = (bf16[8,64,256]{2,1,0:T(8,128)(2,1)S(1)}, bf16[8,64,256]{2,1,0:T(8,128)(2,1)S(1)}, u32[]{:S(2)}, u32[]{:S(2)}) collective-permute-start(bf16[8,64,256]{2,1,0:T(8,128)(2,1)S(1)} %add_convert_fusion.1), channel_id=1, source_target_pairs={{0,1},{1,0},{2,3},{3,2},{4,5},{5,4},{6,7},{7,6},{8,9},{9,8},{10,11... | collective-permute-start | bytes 786440 | tf_op jit(solution)/shard_map/ppermute | solution.py:33
  19.9 9.6 %collective-permute-start.4 = (bf16[8,64,256]{2,1,0:T(8,128)(2,1)S(1)}, bf16[8,64,256]{2,1,0:T(8,128)(2,1)S(1)}, u32[]{:S(2)}, u32[]{:S(2)}) collective-permute-start(bf16[8,64,256]{2,1,0:T(8,128)(2,1)S(1)} %get-tuple-element.43), channel_id=1, source_target_pairs={{0,3},{1,2},{2,1},{3,0},{4,7},{5,6},{6,5},{7,4},{8,11},{9,10},{10,... | collective-permute-start | bytes 786440 | tf_op jit(solution)/shard_map/ppermute | solution.py:33
  30.4 22.4 %all-to-all-start = ((bf16[8,128,256]{2,1,0:T(8,128)(2,1)}), bf16[8,128,256]{2,1,0:T(8,128)(2,1)S(1)}, u32[]{:S(2)}, u32[]{:S(2)}) async-start(bf16[8,128,256]{2,1,0:T(8,128)(2,1)} %pad_maximum_fusion), calls=%async_computation | async-start | bytes 1048576 | tf_op jit(solution)/shard_map/all_to_all | solution.py:303
  54.4 21.0 %all-to-all-start.1 = ((bf16[8,432,128]{2,1,0:T(8,128)(2,1)}), bf16[8,432,128]{2,1,0:T(8,128)(2,1)S(1)}, u32[]{:S(2)}, u32[]{:S(2)}) async-start(bf16[8,432,128]{2,1,0:T(8,128)(2,1)} %copy-done.5), calls=%async_computation.1 | async-start | bytes 1769472 | tf_op jit(solution)/shard_map/all_to_all | solution.py:309
  78.6 7.6 %collective-permute-start.9 = (bf16[8,32,512]{2,1,0:T(8,128)(2,1)S(1)}, bf16[8,32,512]{2,1,0:T(8,128)(2,1)S(1)}, u32[]{:S(2)}, u32[]{:S(2)}) collective-permute-start(bf16[8,32,512]{2,1,0:T(8,128)(2,1)S(1)} %bitcast.64), channel_id=1, source_target_pairs={{0,1},{1,0},{2,3},{3,2},{4,5},{5,4},{6,7},{7,6},{8,9},{9,8},{10,11... | collective-permute-start | bytes 786440 | tf_op jit(solution)/shard_map/ppermute | solution.py:33
  78.9 10.2 %collective-permute-start.12 = (bf16[8,32,512]{2,1,0:T(8,128)(2,1)S(1)}, bf16[8,32,512]{2,1,0:T(8,128)(2,1)S(1)}, u32[]{:S(2)}, u32[]{:S(2)}) collective-permute-start(bf16[8,32,512]{2,1,0:T(8,128)(2,1)S(1)} %bitcast.62), channel_id=1, source_target_pairs={{0,3},{1,2},{2,1},{3,0},{4,7},{5,6},{6,5},{7,4},{8,11},{9,10},{10,... | collective-permute-start | bytes 786440 | tf_op jit(solution)/shard_map/ppermute | solution.py:33
  82.5 9.4 %collective-permute-start.8 = (bf16[8,32,512]{2,1,0:T(8,128)(2,1)S(1)}, bf16[8,32,512]{2,1,0:T(8,128)(2,1)S(1)}, u32[]{:S(2)}, u32[]{:S(2)}) collective-permute-start(bf16[8,32,512]{2,1,0:T(8,128)(2,1)S(1)} %bitcast.63), channel_id=1, source_target_pairs={{0,1},{1,0},{2,3},{3,2},{4,5},{5,4},{6,7},{7,6},{8,9},{9,8},{10,11... | collective-permute-start | bytes 786440 | tf_op jit(solution)/shard_map/ppermute | solution.py:33
  86.3 7.1 %collective-permute-start.10 = (bf16[8,32,512]{2,1,0:T(8,128)(2,1)S(1)}, bf16[8,32,512]{2,1,0:T(8,128)(2,1)S(1)}, u32[]{:S(2)}, u32[]{:S(2)}) collective-permute-start(bf16[8,32,512]{2,1,0:T(8,128)(2,1)S(1)} %fusion.3), channel_id=1, source_target_pairs={{0,3},{1,2},{2,1},{3,0},{4,7},{5,6},{6,5},{7,4},{8,11},{9,10},{10,... | collective-permute-start | bytes 786440 | tf_op jit(solution)/shard_map/ppermute | solution.py:33
  87.1 11.9 %collective-permute-start.11 = (bf16[8,32,512]{2,1,0:T(8,128)(2,1)S(1)}, bf16[8,32,512]{2,1,0:T(8,128)(2,1)S(1)}, u32[]{:S(2)}, u32[]{:S(2)}) collective-permute-start(bf16[8,32,512]{2,1,0:T(8,128)(2,1)S(1)} %bitcast.61), channel_id=1, source_target_pairs={{0,3},{1,2},{2,1},{3,0},{4,7},{5,6},{6,5},{7,4},{8,11},{9,10},{10,... | collective-permute-start | bytes 786440 | tf_op jit(solution)/shard_map/ppermute | solution.py:33
  89.1 9.8 %collective-permute-start.13 = (bf16[8,32,512]{2,1,0:T(8,128)(2,1)S(1)}, bf16[8,32,512]{2,1,0:T(8,128)(2,1)S(1)}, u32[]{:S(2)}, u32[]{:S(2)}) collective-permute-start(bf16[8,32,512]{2,1,0:T(8,128)(2,1)S(1)} %fusion), channel_id=1, source_target_pairs={{0,1},{1,0},{2,3},{3,2},{4,5},{5,4},{6,7},{7,6},{8,9},{9,8},{10,11... | collective-permute-start | bytes 786440 | tf_op jit(solution)/shard_map/ppermute | solution.py:33
  99.9 18.6 %all-to-all-start.2 = ((bf16[8,64,512]{2,1,0:T(8,128)(2,1)}), bf16[8,64,512]{2,1,0:T(8,128)(2,1)}, u32[]{:S(2)}, u32[]{:S(2)}) async-start(bf16[8,64,512]{2,1,0:T(8,128)(2,1)} %pad_maximum_fusion.1), calls=%async_computation.2 | async-start | bytes 1048576 | tf_op jit(solution)/shard_map/all_to_all | solution.py:319
  135.6 6.5 %collective-permute-start.15 = (bf16[256,512]{1,0:T(8,128)(2,1)S(1)}, bf16[256,512]{1,0:T(8,128)(2,1)S(1)}, u32[]{:S(2)}, u32[]{:S(2)}) collective-permute-start(bf16[256,512]{1,0:T(8,128)(2,1)S(1)} %bitcast.53), channel_id=1, source_target_pairs={{0,3},{1,2},{2,1},{3,0},{4,7},{5,6},{6,5},{7,4},{8,11},{9,10},{10,... | collective-permute-start | bytes 786440 | tf_op jit(solution)/shard_map/ppermute | solution.py:33
  136.4 5.7 %collective-permute-start.17 = (bf16[256,512]{1,0:T(8,128)(2,1)S(1)}, bf16[256,512]{1,0:T(8,128)(2,1)S(1)}, u32[]{:S(2)}, u32[]{:S(2)}) collective-permute-start(bf16[256,512]{1,0:T(8,128)(2,1)S(1)} %bitcast.50), channel_id=1, source_target_pairs={{0,1},{1,0},{2,3},{3,2},{4,5},{5,4},{6,7},{7,6},{8,9},{9,8},{10,11... | collective-permute-start | bytes 786440 | tf_op jit(solution)/shard_map/ppermute | solution.py:33
  136.4 8.0 %collective-permute-start.14 = (bf16[256,512]{1,0:T(8,128)(2,1)S(1)}, bf16[256,512]{1,0:T(8,128)(2,1)S(1)}, u32[]{:S(2)}, u32[]{:S(2)}) collective-permute-start(bf16[256,512]{1,0:T(8,128)(2,1)S(1)} %bitcast.54), channel_id=1, source_target_pairs={{0,1},{1,0},{2,3},{3,2},{4,5},{5,4},{6,7},{7,6},{8,9},{9,8},{10,11... | collective-permute-start | bytes 786440 | tf_op jit(solution)/shard_map/ppermute | solution.py:33
  137.9 7.1 %collective-permute-start.19 = (bf16[256,512]{1,0:T(8,128)(2,1)S(1)}, bf16[256,512]{1,0:T(8,128)(2,1)S(1)}, u32[]{:S(2)}, u32[]{:S(2)}) collective-permute-start(bf16[256,512]{1,0:T(8,128)(2,1)S(1)} %bitcast.51), channel_id=1, source_target_pairs={{0,3},{1,2},{2,1},{3,0},{4,7},{5,6},{6,5},{7,4},{8,11},{9,10},{10,... | collective-permute-start | bytes 786440 | tf_op jit(solution)/shard_map/ppermute | solution.py:33
  142.1 7.9 %collective-permute-start.16 = (bf16[256,512]{1,0:T(8,128)(2,1)S(1)}, bf16[256,512]{1,0:T(8,128)(2,1)S(1)}, u32[]{:S(2)}, u32[]{:S(2)}) collective-permute-start(bf16[256,512]{1,0:T(8,128)(2,1)S(1)} %collective-permute-done.15.refs_3_), channel_id=1, source_target_pairs={{0,1},{1,0},{2,3},{3,2},{4,5},{5,4},{6,7},{7,6},{8,9},{9,8},{10,11... | collective-permute-start | bytes 786440 | tf_op jit(solution)/shard_map/ppermute | solution.py:33
  142.1 9.5 %collective-permute-start.18 = (bf16[256,512]{1,0:T(8,128)(2,1)S(1)}, bf16[256,512]{1,0:T(8,128)(2,1)S(1)}, u32[]{:S(2)}, u32[]{:S(2)}) collective-permute-start(bf16[256,512]{1,0:T(8,128)(2,1)S(1)} %collective-permute-done.17.refs_5_), channel_id=1, source_target_pairs={{0,3},{1,2},{2,1},{3,0},{4,7},{5,6},{6,5},{7,4},{8,11},{9,10},{10,... | collective-permute-start | bytes 786440 | tf_op jit(solution)/shard_map/ppermute | solution.py:33
  (9 other events, 103.3 us)

commit v14 on v13

--- a/solution.py
+++ b/solution.py
@@ -41,6 +41,7 @@
     second_near = across(second_near, 3)
     first_last = across(add(first[3], first_far), 3)
     second_last = across(add(second[1], second_far), 1)
+    first_last, first_near, second_near = lax.optimization_barrier((first_last, first_near, second_near))
     if tie:
         second_last, *tie = lax.optimization_barrier((second_last, *tie))
     return (

time: 173 us -> 179 us (1.035)
  starting transfers between devices: 44.1 us -> 47.8 us
  waiting for transfers between devices: 68.5 us -> 70.4 us
    ppermute x18, starting transfers between devices: 18.9 us -> 22.6 us  [across(): return lax.ppermute(block, 'x', [(i, i ^ flip) for i in range(NX)])]
  transfers between devices with their start and end apart: 23 -> 23, of which waited for: 17 -> 15; matrix products, arithmetic and copies ran while one was open for 2% -> 2% of each run, Pallas kernels for 2% -> 2%
where the time goes in v14:
time: 179 us; the launch traced here: 178 us
  waiting for transfers between devices  70.4 us (39%)
  starting transfers between devices  47.8 us (27%)
  blocking collectives  32.8 us (18%)
  Pallas kernels  12.5 us (7%)
  local copies, waits for them, and re-layouts  10.3 us (6%)
  other arithmetic  3.54 us (2%)
    ppermute x18, waiting for transfers between devices, across(): return lax.ppermute(block, 'x', [(i, i ^ flip) for i in range(NX)])  32.1 us
    all_to_all x2, waiting for transfers between devices, local(): moved = lax.all_to_all(summed, 'z', 0, 0)  28.8 us
    ppermute x18, starting transfers between devices, across(): return lax.ppermute(block, 'x', [(i, i ^ flip) for i in range(NX)])  22.6 us
    all_to_all x1, blocking collectives, local(): tall = lax.all_to_all(grad, 'z', 0, 0)  16.6 us
    all_to_all x1, blocking collectives, local(): back = lax.all_to_all(sent, COLUMN, 0, 0)  16.2 us
    all_to_all x2, starting transfers between devices, local(): moved = lax.all_to_all(summed, 'z', 0, 0)  12.4 us
    all_to_all x1, waiting for transfers between devices, local(): got = lax.all_to_all(sent, COLUMN, 0, 0)  9.45 us
    all_to_all x1, starting transfers between devices, local(): got = lax.all_to_all(sent, COLUMN, 0, 0)  7.63 us
  transfers between devices with their start and end apart: 23, of which 15 were waited for; matrix products, arithmetic and copies ran while one was open for 2% of the time, Pallas kernels for 2%

profile of v14, /device:TPU:1, one launch (start us, length us, event | category | flops | bytes accessed | tf_op | source)
XLA Modules:
  0.0 178.3 jit_solution(10852390893600021526)
XLA Ops:
  0.6 3.8 %collective-permute-start = (bf16[64,256]{1,0:T(8,128)(2,1)}, bf16[64,256]{1,0:T(8,128)(2,1)S(1)}, u32[]{:S(2)}, u32[]{:S(2)}) collective-permute-start(bf16[64,256]{1,0:T(8,128)(2,1)} %own_ref.1), channel_id=1, source_target_pairs={{0,32},{32,0},{1,33},{33,1},{2,34},{34,2},{3,35},{35,3},{4,36},{36... | collective-permute-start | bytes 98312 | tf_op jit(solution)/shard_map/ppermute | solution.py:293
  4.5 2.2 %copy-done.2 = bf16[256,8192]{1,0:T(8,128)(2,1)S(1)} copy-done((bf16[256,8192]{1,0:T(8,128)(2,1)S(1)}, bf16[256,8192]{1,0:T(8,128)(2,1)}, u32[]{:S(2)}) %copy-start.2) | copy-done | bytes 4194328
  15.6 3.2 %collective-permute-start.2 = (bf16[8,64,256]{2,1,0:T(8,128)(2,1)S(1)}, bf16[8,64,256]{2,1,0:T(8,128)(2,1)S(1)}, u32[]{:S(2)}, u32[]{:S(2)}) collective-permute-start(bf16[8,64,256]{2,1,0:T(8,128)(2,1)S(1)} %add_convert_fusion.3), channel_id=1, source_target_pairs={{0,3},{1,2},{2,1},{3,0},{4,7},{5,6},{6,5},{7,4},{8,11},{9,10},{10,... | collective-permute-start | bytes 786440 | tf_op jit(solution)/shard_map/ppermute | solution.py:33
  20.4 2.8 %collective-permute-done.4 = bf16[8,64,256]{2,1,0:T(8,128)(2,1)S(1)} collective-permute-done((bf16[8,64,256]{2,1,0:T(8,128)(2,1)S(1)}, bf16[8,64,256]{2,1,0:T(8,128)(2,1)S(1)}, u32[]{:S(2)}, u32[]{:S(2)}) %collective-permute-start.4) | collective-permute-done | bytes 262176 | tf_op jit(solution)/shard_map/ppermute | solution.py:33
  23.2 5.6 %collective-permute-done.2 = bf16[8,64,256]{2,1,0:T(8,128)(2,1)S(1)} collective-permute-done((bf16[8,64,256]{2,1,0:T(8,128)(2,1)S(1)}, bf16[8,64,256]{2,1,0:T(8,128)(2,1)S(1)}, u32[]{:S(2)}, u32[]{:S(2)}) %collective-permute-start.2) | collective-permute-done | bytes 262176 | tf_op jit(solution)/shard_map/ppermute | solution.py:33
  29.9 8.2 %all-to-all-start = ((bf16[8,128,256]{2,1,0:T(8,128)(2,1)}), bf16[8,128,256]{2,1,0:T(8,128)(2,1)S(1)}, u32[]{:S(2)}, u32[]{:S(2)}) async-start(bf16[8,128,256]{2,1,0:T(8,128)(2,1)} %pad_maximum_fusion), calls=%async_computation | async-start | bytes 1048576 | tf_op jit(solution)/shard_map/all_to_all | solution.py:304
  39.1 13.5 %all-to-all-done.moved_ref = bf16[8,128,256]{2,1,0:T(8,128)(2,1)S(1)} async-done(((bf16[8,128,256]{2,1,0:T(8,128)(2,1)}), bf16[8,128,256]{2,1,0:T(8,128)(2,1)S(1)}, u32[]{:S(2)}, u32[]{:S(2)}) %all-to-all-start) | async-done | bytes 524320 | tf_op jit(solution)/shard_map/all_to_all | solution.py:304
  54.1 7.6 %all-to-all-start.1 = ((bf16[8,432,128]{2,1,0:T(8,128)(2,1)}), bf16[8,432,128]{2,1,0:T(8,128)(2,1)S(1)}, u32[]{:S(2)}, u32[]{:S(2)}) async-start(bf16[8,432,128]{2,1,0:T(8,128)(2,1)} %copy-done.5), calls=%async_computation.1 | async-start | bytes 1769472 | tf_op jit(solution)/shard_map/all_to_all | solution.py:310
  61.8 2.2 %copy-done.1 = bf16[256,8192]{1,0:T(8,128)(2,1)S(1)} copy-done((bf16[256,8192]{1,0:T(8,128)(2,1)S(1)}, bf16[256,8192]{1,0:T(8,128)(2,1)}, u32[]{:S(2)}) %copy-start.1) | copy-done | bytes 4194328
  65.6 9.5 %all-to-all-done.1.got_ref = bf16[8,432,128]{2,1,0:T(8,128)(2,1)S(1)} async-done(((bf16[8,432,128]{2,1,0:T(8,128)(2,1)}), bf16[8,432,128]{2,1,0:T(8,128)(2,1)S(1)}, u32[]{:S(2)}, u32[]{:S(2)}) %all-to-all-start.1) | async-done | bytes 884768 | tf_op jit(solution)/shard_map/all_to_all | solution.py:310
  78.3 2.5 %collective-permute-start.12 = (bf16[8,32,512]{2,1,0:T(8,128)(2,1)S(1)}, bf16[8,32,512]{2,1,0:T(8,128)(2,1)S(1)}, u32[]{:S(2)}, u32[]{:S(2)}) collective-permute-start(bf16[8,32,512]{2,1,0:T(8,128)(2,1)S(1)} %bitcast.62), channel_id=1, source_target_pairs={{0,3},{1,2},{2,1},{3,0},{4,7},{5,6},{6,5},{7,4},{8,11},{9,10},{10,... | collective-permute-start | bytes 786440 | tf_op jit(solution)/shard_map/ppermute | solution.py:33
  80.8 2.5 %shard_map.107 = (bf16[256,512]{1,0:T(8,128)(2,1)S(1)}, bf16[256,512]{1,0:T(8,128)(2,1)S(1)}, bf16[256,512]{1,0:T(8,128)(2,1)S(1)}, bf16[256,512]{1,0:T(8,128)(2...) custom-call(s32[3]{0:T(128)S(1)} %pad_add_fusion.place_ref, ...), custom_call_target="tpu_custom_call" | custom-call | flops 1415577600 | bytes 5242880 | tf_op jit(solution)/shard_map/pallas_call | solution.py:234
  85.9 2.5 %collective-permute-start.9 = (bf16[8,32,512]{2,1,0:T(8,128)(2,1)S(1)}, bf16[8,32,512]{2,1,0:T(8,128)(2,1)S(1)}, u32[]{:S(2)}, u32[]{:S(2)}) collective-permute-start(bf16[8,32,512]{2,1,0:T(8,128)(2,1)S(1)} %fusion.3), channel_id=1, source_target_pairs={{0,3},{1,2},{2,1},{3,0},{4,7},{5,6},{6,5},{7,4},{8,11},{9,10},{10,... | collective-permute-start | bytes 786440 | tf_op jit(solution)/shard_map/ppermute | solution.py:33
  88.7 3.0 %collective-permute-done.10 = bf16[8,32,512]{2,1,0:T(8,128)(2,1)S(1)} collective-permute-done((bf16[8,32,512]{2,1,0:T(8,128)(2,1)S(1)}, bf16[8,32,512]{2,1,0:T(8,128)(2,1)S(1)}, u32[]{:S(2)}, u32[]{:S(2)}) %collective-permute-start.10) | collective-permute-done | bytes 262176 | tf_op jit(solution)/shard_map/ppermute | solution.py:33
  91.9 5.6 %collective-permute-done.9 = bf16[8,32,512]{2,1,0:T(8,128)(2,1)S(1)} collective-permute-done((bf16[8,32,512]{2,1,0:T(8,128)(2,1)S(1)}, bf16[8,32,512]{2,1,0:T(8,128)(2,1)S(1)}, u32[]{:S(2)}, u32[]{:S(2)}) %collective-permute-start.9) | collective-permute-done | bytes 262176 | tf_op jit(solution)/shard_map/ppermute | solution.py:33
  98.6 4.1 %all-to-all-start.2 = ((bf16[8,64,512]{2,1,0:T(8,128)(2,1)}), bf16[8,64,512]{2,1,0:T(8,128)(2,1)}, u32[]{:S(2)}, u32[]{:S(2)}) async-start(bf16[8,64,512]{2,1,0:T(8,128)(2,1)} %pad_maximum_fusion.1), calls=%async_computation.2 | async-start | bytes 1048576 | tf_op jit(solution)/shard_map/all_to_all | solution.py:320
  102.9 15.4 %all-to-all-done.2.moved_ref = bf16[8,64,512]{2,1,0:T(8,128)(2,1)} async-done(((bf16[8,64,512]{2,1,0:T(8,128)(2,1)}), bf16[8,64,512]{2,1,0:T(8,128)(2,1)}, u32[]{:S(2)}, u32[]{:S(2)}) %all-to-all-start.2) | async-done | bytes 524320 | tf_op jit(solution)/shard_map/all_to_all | solution.py:320
  120.0 16.6 %all_to_all.25 = bf16[8,64,512]{2,1,0:T(8,128)(2,1)S(1)} all-to-all(bf16[8,64,512]{2,1,0:T(8,128)(2,1)S(1)} %shard_map.109), channel_id=1, replica_groups=mesh['ylo'=2,'core'=2,'seq'=2,'z'=8,'x'=4] {'z'}, dimensions={0} | all-to-all | bytes 1048576 | tf_op jit(solution)/shard_map/all_to_all | solution.py:323
  136.6 6.1 %collective-permute-start.15 = (bf16[256,512]{1,0:T(8,128)(2,1)S(1)}, bf16[256,512]{1,0:T(8,128)(2,1)S(1)}, u32[]{:S(2)}, u32[]{:S(2)}) collective-permute-start(bf16[256,512]{1,0:T(8,128)(2,1)S(1)} %bitcast.53), channel_id=1, source_target_pairs={{0,3},{1,2},{2,1},{3,0},{4,7},{5,6},{6,5},{7,4},{8,11},{9,10},{10,... | collective-permute-start | bytes 786440 | tf_op jit(solution)/shard_map/ppermute | solution.py:33
  144.3 2.2 %collective-permute-done.15.refs_3_ = bf16[256,512]{1,0:T(8,128)(2,1)S(1)} collective-permute-done((bf16[256,512]{1,0:T(8,128)(2,1)S(1)}, bf16[256,512]{1,0:T(8,128)(2,1)S(1)}, u32[]{:S(2)}, u32[]{:S(2)}) %collective-permute-start.15) | collective-permute-done | bytes 262176 | tf_op jit(solution)/shard_map/ppermute | solution.py:33
  149.1 3.7 %collective-permute-done.14.refs_1_ = bf16[256,512]{1,0:T(8,128)(2,1)S(1)} collective-permute-done((bf16[256,512]{1,0:T(8,128)(2,1)S(1)}, bf16[256,512]{1,0:T(8,128)(2,1)S(1)}, u32[]{:S(2)}, u32[]{:S(2)}) %collective-permute-start.14) | collective-permute-done | bytes 262176 | tf_op jit(solution)/shard_map/ppermute | solution.py:33
  153.0 5.4 %collective-permute-done.16.refs_2_ = bf16[256,512]{1,0:T(8,128)(2,1)S(1)} collective-permute-done((bf16[256,512]{1,0:T(8,128)(2,1)S(1)}, bf16[256,512]{1,0:T(8,128)(2,1)S(1)}, u32[]{:S(2)}, u32[]{:S(2)}) %collective-permute-start.16) | collective-permute-done | bytes 262176 | tf_op jit(solution)/shard_map/ppermute | solution.py:33
  158.5 2.2 %shard_map.110 = (bf16[4,256,128]{2,1,0:T(8,128)(2,1)S(1)}, bf16[16,128]{1,0:T(8,128)(2,1)S(1)}, bf16[128,1024]{1,0:T(8,128)(2,1)}) custom-call(s32[3]{0:T(128)S(1)} %pad_add_fusion.place_ref, bf16[256,512]{1,0:T(8,128)(2,1)S(1)} %bitcast.55, bf16[256,512]{1,0:T(8,128)(2,1)S(1)} %collective-permute-done.14.refs_1_, ...), custom_call_target="tpu_custom_call" | custom-call | flops 536870912 | bytes 5242880 | tf_op jit(solution)/shard_map/pallas_call | solution.py:273
  160.9 16.2 %all_to_all.26.back_ref = bf16[8,144,128]{2,1,0:T(8,128)(2,1)S(1)} all-to-all(bf16[8,144,128]{2,1,0:T(8,128)(2,1)S(1)} %pad_maximum_fusion.2), channel_id=1, replica_groups=mesh['ylo'=2,'core'=2,'seq'=2,'z'=8,'x'=4] {'ylo','core','seq'}, dimensions={0} | all-to-all | bytes 589824 | tf_op jit(solution)/shard_map/all_to_all | solution.py:330
  (84 shorter events, 30.7 us)
Async XLA Ops:
  0.6 7.1 %collective-permute-start = (bf16[64,256]{1,0:T(8,128)(2,1)}, bf16[64,256]{1,0:T(8,128)(2,1)S(1)}, u32[]{:S(2)}, u32[]{:S(2)}) collective-permute-start(bf16[64,256]{1,0:T(8,128)(2,1)} %own_ref.1), channel_id=1, source_target_pairs={{0,32},{32,0},{1,33},{33,1},{2,34},{34,2},{3,35},{35,3},{4,36},{36... | collective-permute-start | bytes 98312 | tf_op jit(solution)/shard_map/ppermute | solution.py:293
  9.1 43.5 %copy-start.6 = (bf16[128,256]{1,0:T(8,128)(2,1)S(1)}, bf16[128,256]{1,0:T(8,128)(2,1)}, u32[]{:S(2)}) copy-start(bf16[128,256]{1,0:T(8,128)(2,1)} %resid_ref.1) | copy-start | bytes 196612
  9.1 6.4 %collective-permute-start.1 = (bf16[8,64,256]{2,1,0:T(8,128)(2,1)S(1)}, bf16[8,64,256]{2,1,0:T(8,128)(2,1)S(1)}, u32[]{:S(2)}, u32[]{:S(2)}) collective-permute-start(bf16[8,64,256]{2,1,0:T(8,128)(2,1)S(1)} %get-tuple-element.42), channel_id=1, source_target_pairs={{0,1},{1,0},{2,3},{3,2},{4,5},{5,4},{6,7},{7,6},{8,9},{9,8},{10,11... | collective-permute-start | bytes 786440 | tf_op jit(solution)/shard_map/ppermute | solution.py:33
  10.4 8.4 %collective-permute-start.5 = (bf16[8,64,256]{2,1,0:T(8,128)(2,1)S(1)}, bf16[8,64,256]{2,1,0:T(8,128)(2,1)}, u32[]{:S(2)}, u32[]{:S(2)}) collective-permute-start(bf16[8,64,256]{2,1,0:T(8,128)(2,1)S(1)} %get-tuple-element.54), channel_id=1, source_target_pairs={{0,3},{1,2},{2,1},{3,0},{4,7},{5,6},{6,5},{7,4},{8,11},{9,10},{10,... | collective-permute-start | bytes 786440 | tf_op jit(solution)/shard_map/ppermute | solution.py:33
  13.3 15.7 %collective-permute-start.7 = (bf16[256,1024]{1,0:T(8,128)(2,1)S(1)}, bf16[256,1024]{1,0:T(8,128)(2,1)S(1)}, u32[]{:S(2)}, u32[]{:S(2)}) collective-permute-start(bf16[256,1024]{1,0:T(8,128)(2,1)S(1)} %constant_dynamic-slice_fusion), channel_id=1, source_target_pairs={{0,32},{32,0},{1,33},{33,1},{2,34},{34,2},{3,35},{35,3},{4,36},{36... | collective-permute-start | bytes 1572872 | tf_op jit(solution)/shard_map/ppermute | solution.py:301
  14.6 5.9 %collective-permute-start.3 = (bf16[8,64,256]{2,1,0:T(8,128)(2,1)S(1)}, bf16[8,64,256]{2,1,0:T(8,128)(2,1)S(1)}, u32[]{:S(2)}, u32[]{:S(2)}) collective-permute-start(bf16[8,64,256]{2,1,0:T(8,128)(2,1)S(1)} %get-tuple-element.47), channel_id=1, source_target_pairs={{0,1},{1,0},{2,3},{3,2},{4,5},{5,4},{6,7},{7,6},{8,9},{9,8},{10,11... | collective-permute-start | bytes 786440 | tf_op jit(solution)/shard_map/ppermute | solution.py:33
  14.9 8.3 %collective-permute-start.4 = (bf16[8,64,256]{2,1,0:T(8,128)(2,1)S(1)}, bf16[8,64,256]{2,1,0:T(8,128)(2,1)S(1)}, u32[]{:S(2)}, u32[]{:S(2)}) collective-permute-start(bf16[8,64,256]{2,1,0:T(8,128)(2,1)S(1)} %get-tuple-element.48), channel_id=1, source_target_pairs={{0,3},{1,2},{2,1},{3,0},{4,7},{5,6},{6,5},{7,4},{8,11},{9,10},{10,... | collective-permute-start | bytes 786440 | tf_op jit(solution)/shard_map/ppermute | solution.py:33
  15.6 13.3 %collective-permute-start.2 = (bf16[8,64,256]{2,1,0:T(8,128)(2,1)S(1)}, bf16[8,64,256]{2,1,0:T(8,128)(2,1)S(1)}, u32[]{:S(2)}, u32[]{:S(2)}) collective-permute-start(bf16[8,64,256]{2,1,0:T(8,128)(2,1)S(1)} %add_convert_fusion.3), channel_id=1, source_target_pairs={{0,3},{1,2},{2,1},{3,0},{4,7},{5,6},{6,5},{7,4},{8,11},{9,10},{10,... | collective-permute-start | bytes 786440 | tf_op jit(solution)/shard_map/ppermute | solution.py:33
  19.8 9.1 %collective-permute-start.6 = (bf16[8,64,256]{2,1,0:T(8,128)(2,1)S(1)}, bf16[8,64,256]{2,1,0:T(8,128)(2,1)S(1)}, u32[]{:S(2)}, u32[]{:S(2)}) collective-permute-start(bf16[8,64,256]{2,1,0:T(8,128)(2,1)S(1)} %add_convert_fusion.1), channel_id=1, source_target_pairs={{0,1},{1,0},{2,3},{3,2},{4,5},{5,4},{6,7},{7,6},{8,9},{9,8},{10,11... | collective-permute-start | bytes 786440 | tf_op jit(solution)/shard_map/ppermute | solution.py:33
  29.9 22.6 %all-to-all-start = ((bf16[8,128,256]{2,1,0:T(8,128)(2,1)}), bf16[8,128,256]{2,1,0:T(8,128)(2,1)S(1)}, u32[]{:S(2)}, u32[]{:S(2)}) async-start(bf16[8,128,256]{2,1,0:T(8,128)(2,1)} %pad_maximum_fusion), calls=%async_computation | async-start | bytes 1048576 | tf_op jit(solution)/shard_map/all_to_all | solution.py:304
  54.1 20.9 %all-to-all-start.1 = ((bf16[8,432,128]{2,1,0:T(8,128)(2,1)}), bf16[8,432,128]{2,1,0:T(8,128)(2,1)S(1)}, u32[]{:S(2)}, u32[]{:S(2)}) async-start(bf16[8,432,128]{2,1,0:T(8,128)(2,1)} %copy-done.5), calls=%async_computation.1 | async-start | bytes 1769472 | tf_op jit(solution)/shard_map/all_to_all | solution.py:310
  78.2 7.6 %collective-permute-start.8 = (bf16[8,32,512]{2,1,0:T(8,128)(2,1)S(1)}, bf16[8,32,512]{2,1,0:T(8,128)(2,1)S(1)}, u32[]{:S(2)}, u32[]{:S(2)}) collective-permute-start(bf16[8,32,512]{2,1,0:T(8,128)(2,1)S(1)} %bitcast.64), channel_id=1, source_target_pairs={{0,1},{1,0},{2,3},{3,2},{4,5},{5,4},{6,7},{7,6},{8,9},{9,8},{10,11... | collective-permute-start | bytes 786440 | tf_op jit(solution)/shard_map/ppermute | solution.py:33
  78.3 10.0 %collective-permute-start.12 = (bf16[8,32,512]{2,1,0:T(8,128)(2,1)S(1)}, bf16[8,32,512]{2,1,0:T(8,128)(2,1)S(1)}, u32[]{:S(2)}, u32[]{:S(2)}) collective-permute-start(bf16[8,32,512]{2,1,0:T(8,128)(2,1)S(1)} %bitcast.62), channel_id=1, source_target_pairs={{0,3},{1,2},{2,1},{3,0},{4,7},{5,6},{6,5},{7,4},{8,11},{9,10},{10,... | collective-permute-start | bytes 786440 | tf_op jit(solution)/shard_map/ppermute | solution.py:33
  83.3 8.5 %collective-permute-start.10 = (bf16[8,32,512]{2,1,0:T(8,128)(2,1)S(1)}, bf16[8,32,512]{2,1,0:T(8,128)(2,1)S(1)}, u32[]{:S(2)}, u32[]{:S(2)}) collective-permute-start(bf16[8,32,512]{2,1,0:T(8,128)(2,1)S(1)} %bitcast.63), channel_id=1, source_target_pairs={{0,1},{1,0},{2,3},{3,2},{4,5},{5,4},{6,7},{7,6},{8,9},{9,8},{10,11... | collective-permute-start | bytes 786440 | tf_op jit(solution)/shard_map/ppermute | solution.py:33
  84.1 7.8 %collective-permute-start.11 = (bf16[8,32,512]{2,1,0:T(8,128)(2,1)S(1)}, bf16[8,32,512]{2,1,0:T(8,128)(2,1)S(1)}, u32[]{:S(2)}, u32[]{:S(2)}) collective-permute-start(bf16[8,32,512]{2,1,0:T(8,128)(2,1)S(1)} %bitcast.61), channel_id=1, source_target_pairs={{0,3},{1,2},{2,1},{3,0},{4,7},{5,6},{6,5},{7,4},{8,11},{9,10},{10,... | collective-permute-start | bytes 786440 | tf_op jit(solution)/shard_map/ppermute | solution.py:33
  85.9 11.6 %collective-permute-start.9 = (bf16[8,32,512]{2,1,0:T(8,128)(2,1)S(1)}, bf16[8,32,512]{2,1,0:T(8,128)(2,1)S(1)}, u32[]{:S(2)}, u32[]{:S(2)}) collective-permute-start(bf16[8,32,512]{2,1,0:T(8,128)(2,1)S(1)} %fusion.3), channel_id=1, source_target_pairs={{0,3},{1,2},{2,1},{3,0},{4,7},{5,6},{6,5},{7,4},{8,11},{9,10},{10,... | collective-permute-start | bytes 786440 | tf_op jit(solution)/shard_map/ppermute | solution.py:33
  88.4 9.2 %collective-permute-start.13 = (bf16[8,32,512]{2,1,0:T(8,128)(2,1)S(1)}, bf16[8,32,512]{2,1,0:T(8,128)(2,1)S(1)}, u32[]{:S(2)}, u32[]{:S(2)}) collective-permute-start(bf16[8,32,512]{2,1,0:T(8,128)(2,1)S(1)} %fusion), channel_id=1, source_target_pairs={{0,1},{1,0},{2,3},{3,2},{4,5},{5,4},{6,7},{7,6},{8,9},{9,8},{10,11... | collective-permute-start | bytes 786440 | tf_op jit(solution)/shard_map/ppermute | solution.py:33
  98.6 19.7 %all-to-all-start.2 = ((bf16[8,64,512]{2,1,0:T(8,128)(2,1)}), bf16[8,64,512]{2,1,0:T(8,128)(2,1)}, u32[]{:S(2)}, u32[]{:S(2)}) async-start(bf16[8,64,512]{2,1,0:T(8,128)(2,1)} %pad_maximum_fusion.1), calls=%async_computation.2 | async-start | bytes 1048576 | tf_op jit(solution)/shard_map/all_to_all | solution.py:320
  136.6 9.8 %collective-permute-start.15 = (bf16[256,512]{1,0:T(8,128)(2,1)S(1)}, bf16[256,512]{1,0:T(8,128)(2,1)S(1)}, u32[]{:S(2)}, u32[]{:S(2)}) collective-permute-start(bf16[256,512]{1,0:T(8,128)(2,1)S(1)} %bitcast.53), channel_id=1, source_target_pairs={{0,3},{1,2},{2,1},{3,0},{4,7},{5,6},{6,5},{7,4},{8,11},{9,10},{10,... | collective-permute-start | bytes 786440 | tf_op jit(solution)/shard_map/ppermute | solution.py:33
  142.7 5.5 %collective-permute-start.17 = (bf16[256,512]{1,0:T(8,128)(2,1)S(1)}, bf16[256,512]{1,0:T(8,128)(2,1)S(1)}, u32[]{:S(2)}, u32[]{:S(2)}) collective-permute-start(bf16[256,512]{1,0:T(8,128)(2,1)S(1)} %bitcast.50), channel_id=1, source_target_pairs={{0,1},{1,0},{2,3},{3,2},{4,5},{5,4},{6,7},{7,6},{8,9},{9,8},{10,11... | collective-permute-start | bytes 786440 | tf_op jit(solution)/shard_map/ppermute | solution.py:33
  142.7 10.1 %collective-permute-start.14 = (bf16[256,512]{1,0:T(8,128)(2,1)S(1)}, bf16[256,512]{1,0:T(8,128)(2,1)S(1)}, u32[]{:S(2)}, u32[]{:S(2)}) collective-permute-start(bf16[256,512]{1,0:T(8,128)(2,1)S(1)} %bitcast.54), channel_id=1, source_target_pairs={{0,1},{1,0},{2,3},{3,2},{4,5},{5,4},{6,7},{7,6},{8,9},{9,8},{10,11... | collective-permute-start | bytes 786440 | tf_op jit(solution)/shard_map/ppermute | solution.py:33
  144.2 8.9 %collective-permute-start.19 = (bf16[256,512]{1,0:T(8,128)(2,1)S(1)}, bf16[256,512]{1,0:T(8,128)(2,1)S(1)}, u32[]{:S(2)}, u32[]{:S(2)}) collective-permute-start(bf16[256,512]{1,0:T(8,128)(2,1)S(1)} %bitcast.51), channel_id=1, source_target_pairs={{0,3},{1,2},{2,1},{3,0},{4,7},{5,6},{6,5},{7,4},{8,11},{9,10},{10,... | collective-permute-start | bytes 786440 | tf_op jit(solution)/shard_map/ppermute | solution.py:33
  146.5 12.0 %collective-permute-start.16 = (bf16[256,512]{1,0:T(8,128)(2,1)S(1)}, bf16[256,512]{1,0:T(8,128)(2,1)S(1)}, u32[]{:S(2)}, u32[]{:S(2)}) collective-permute-start(bf16[256,512]{1,0:T(8,128)(2,1)S(1)} %collective-permute-done.15.refs_3_), channel_id=1, source_target_pairs={{0,1},{1,0},{2,3},{3,2},{4,5},{5,4},{6,7},{7,6},{8,9},{9,8},{10,11... | collective-permute-start | bytes 786440 | tf_op jit(solution)/shard_map/ppermute | solution.py:33
  148.2 10.2 %collective-permute-start.18 = (bf16[256,512]{1,0:T(8,128)(2,1)S(1)}, bf16[256,512]{1,0:T(8,128)(2,1)S(1)}, u32[]{:S(2)}, u32[]{:S(2)}) collective-permute-start(bf16[256,512]{1,0:T(8,128)(2,1)S(1)} %collective-permute-done.17.refs_5_), channel_id=1, source_target_pairs={{0,3},{1,2},{2,1},{3,0},{4,7},{5,6},{6,5},{7,4},{8,11},{9,10},{10,... | collective-permute-start | bytes 786440 | tf_op jit(solution)/shard_map/ppermute | solution.py:33
  (9 other events, 102.6 us)
